TPU v7x, 32 devices: a whole 2x2x4 slice. The times are simulated.
32 devices in a mesh: req: 4 (over z), ctx: 4 (over x, core), kvh: 2 (over y).
Axes of the slice: x: 2, y: 2, z: 4, core: 2. Of those that a mesh axis runs over, the one named last changes fastest.
Arguments:
- query: bfloat16 [16, 8, 16, 128], P('req', 'kvh', 'ctx'), may hold values from -15 to 15
- kv_pool: bfloat16 [8192, 16, 8, 256], P(('req', 'ctx'), None, 'kvh'), may hold values from -4 to 4
- page_table: int32 [16, 512], P('req', 'ctx'), may hold values from 0 to 511, as said below
- context_len: int32 [16], P('req'), may hold values from 1024 to 8192
- fresh_kv: bfloat16 [1792, 16, 8, 256], P(('req', 'ctx'), None, 'kvh'), may hold values from -4 to 4
- fresh_bucket: int32 [1792], P(('req', 'ctx')), may hold values from 0 to 63, as said below
Outputs:
- attended: bfloat16 [16, 8, 16, 128], P('req', 'kvh', 'ctx')
Inputs may be any that keep to these rules, and one draw needn't show every extreme that they name: `page_table`: within the block of 4 requests and 128 logical pages that one device holds, the entries are a permutation of 0 to 511. `fresh_bucket`: the 112 entries of one device name no bucket more than 2 times.
All inputs are finite; a program needn't handle non-finite values.
Results may differ from a plain program's by a relative error of at most 0.0055.
Values may be sent and summed in bfloat16 or wider, within the bound.
No kernel may reach another device: no remote copies, remote signals or barrier semaphores. Data moves between devices by JAX's collectives and lax.ppermute only.
A program may use at most 128 MiB of HBM per device.

v0:
```python
import jax
import jax.numpy as jnp
from jax import lax
from jax.sharding import PartitionSpec as P

CAP = 2


NEG = -1e30


def from_behind(value, axis, steps):
    count = lax.axis_size(axis)
    pairs = [(source, (source + steps) % count) for source in range(count)]
    return lax.ppermute(value, axis, pairs)


def block_partial(visiting, keyvals, allowed, score_scale):
    head_dim = visiting.shape[-1]
    scores = (
        jnp.einsum(
            "jhrd,sjthd->jhrst",
            visiting,
            keyvals[..., :head_dim],
            preferred_element_type=jnp.float32,
        )
        * score_scale
    )
    allowed_rows = jnp.transpose(allowed, (1, 0, 2))[:, None, None]
    scores = jnp.where(allowed_rows, scores, NEG)
    row_top = jnp.max(scores, axis=(3, 4))
    weights = jnp.where(allowed_rows, jnp.exp(scores - row_top[..., None, None]), 0.0)
    totals = jnp.sum(weights, axis=(3, 4))
    weighted = jnp.einsum(
        "jhrst,sjthd->jhrd",
        weights.astype(jnp.bfloat16),
        keyvals[..., head_dim:],
        preferred_element_type=jnp.float32,
    )
    return (row_top, totals, weighted)


def pool_partial(visiting, pool_flat, allowed, score_scale):
    head_dim = visiting.shape[-1]
    scores = (
        jnp.einsum(
            "jhrd,thd->jhrt",
            visiting,
            pool_flat[..., :head_dim],
            preferred_element_type=jnp.float32,
        )
        * score_scale
    )
    allowed_rows = allowed[:, None, None, :]
    scores = jnp.where(allowed_rows, scores, NEG)
    row_top = jnp.max(scores, axis=3)
    weights = jnp.where(allowed_rows, jnp.exp(scores - row_top[..., None]), 0.0)
    totals = jnp.sum(weights, axis=3)
    weighted = jnp.einsum(
        "jhrt,thd->jhrd",
        weights.astype(jnp.bfloat16),
        pool_flat[..., head_dim:],
        preferred_element_type=jnp.float32,
    )
    return (row_top, totals, weighted)


def merge_parts(first, second):
    row_top = jnp.maximum(first[0], second[0])
    factor_one = jnp.exp(first[0] - row_top)
    factor_two = jnp.exp(second[0] - row_top)
    totals = first[1] * factor_one + second[1] * factor_two
    weighted = first[2] * factor_one[..., None] + second[2] * factor_two[..., None]
    return (row_top, totals, weighted)


def local(query, kv_pool, page_table, context_len, fresh_kv, fresh_bucket):
    ctx_size = lax.axis_size("ctx")
    ctx_place = lax.axis_index("ctx")
    req_size = lax.axis_size("req")
    req_dev, kvh_dev, group_dev, head_dim = query.shape
    page_len = kv_pool.shape[1]
    row_width = kv_pool.shape[3]
    pool_slots = kv_pool.shape[0]
    pages_dev = page_table.shape[1]
    local_tokens = pages_dev * page_len
    score_scale = head_dim ** (-0.5)
    sources = req_size * ctx_size
    pool_flat = kv_pool.reshape(pool_slots * page_len, kvh_dev, row_width)
    matches = (
        page_table[:, :, None] == jnp.arange(pool_slots, dtype=jnp.int32)[None, None, :]
    ).astype(jnp.int32)
    slot_owned = jnp.sum(matches, axis=1) > 0
    slot_page = jnp.sum(matches * jnp.arange(pages_dev, dtype=jnp.int32)[None, :, None], axis=1)
    in_page = jnp.arange(page_len, dtype=jnp.int32)
    slot_position = (
        ctx_place * local_tokens + slot_page[:, :, None] * page_len + in_page[None, None, :]
    )
    pool_allowed = slot_owned[:, :, None] & (slot_position < context_len[:, None, None])
    pool_allowed = pool_allowed.reshape(req_dev, pool_slots * page_len)
    arrived_set = None
    fresh_result = None
    request = fresh_bucket // ctx_size
    target = (request // req_dev * ctx_size + fresh_bucket % ctx_size) * req_dev + request % req_dev
    n_targets = sources * req_dev
    onehot = (target[:, None] == jnp.arange(n_targets, dtype=jnp.int32)[None, :]).astype(jnp.int32)
    earlier = jnp.cumsum(onehot, axis=0) - onehot
    rank_in = jnp.sum(earlier * onehot, axis=1)
    slot_index = target * CAP + rank_in
    selector = (
        jnp.arange(n_targets * CAP, dtype=jnp.int32)[:, None] == slot_index[None, :]
    ).astype(jnp.bfloat16)
    fresh_rows = fresh_kv.reshape(fresh_kv.shape[0], page_len * kvh_dev * row_width)
    outgoing = jnp.dot(selector, fresh_rows, preferred_element_type=jnp.float32).astype(
        jnp.bfloat16
    )
    outgoing = outgoing.reshape(sources, req_dev, CAP * page_len, kvh_dev, row_width)
    filled = jnp.sum(selector, axis=1).reshape(sources, req_dev, CAP)
    arrived, arrived_flags = (
        lax.all_to_all(outgoing, ("req", "ctx"), split_axis=0, concat_axis=0, tiled=True),
        lax.all_to_all(filled, ("req", "ctx"), split_axis=0, concat_axis=0, tiled=True),
    )
    arrived_live = jnp.repeat(arrived_flags > 0.5, page_len, axis=2)
    arrived_set = (arrived, arrived_live)

    def turn(turn_index, carry):
        visiting, row_top, totals, weighted = carry
        parts = pool_partial(visiting, pool_flat, pool_allowed, score_scale)
        parts = merge_parts(
            parts, block_partial(visiting, arrived_set[0], arrived_set[1], score_scale)
        )
        parts = merge_parts((row_top, totals, weighted), parts)
        visiting = from_behind(visiting, "ctx", 1)
        row_top, totals, weighted = from_behind((parts[0], parts[1], parts[2]), "ctx", 1)
        return (visiting, row_top, totals, weighted)

    start_top = jnp.full((req_dev, kvh_dev, group_dev), NEG, jnp.float32)
    start_totals = jnp.zeros((req_dev, kvh_dev, group_dev), jnp.float32)
    start_weighted = jnp.zeros((req_dev, kvh_dev, group_dev, head_dim), jnp.float32)
    carried = lax.fori_loop(0, ctx_size, turn, (query, start_top, start_totals, start_weighted))
    result = (carried[1], carried[2], carried[3])
    return (result[2] / result[1][..., None]).astype(jnp.bfloat16)


def solution(mesh):
    placed = (
        P("req", "kvh", "ctx", None),
        P(("req", "ctx"), None, "kvh", None),
        P("req", "ctx"),
        P("req"),
        P(("req", "ctx"), None, "kvh", None),
        P(("req", "ctx")),
    )
    return jax.shard_map(
        local, mesh=mesh, in_specs=placed, out_specs=P("req", "kvh", "ctx", None), check_vma=False
    )
```

profile of v0, /device:TPU:16, one launch (start us, length us, event | category | flops | bytes accessed | tf_op | source)
XLA Modules:
  0.0 237.0 jit_solution(5929846898265388910)
XLA Ops:
  2.9 6.2 %all-to-all-start = ((bf16[16,4,2]{1,2,0:T(2,128)(2,1)}), bf16[16,4,2]{1,2,0:T(2,128)(2,1)S(1)}, u32[]{:S(2)}, u32[]{:S(2)}) async-start(bf16[16,4,2]{1,2,0:T(2,128)(2,1)} %copy.59), calls=%async_computation | async-start | bytes 16384 | tf_op jit(solution)/shard_map/all_to_all | solution.py:121
  9.0 7.1 %reshape.51 = bf16[112,16384]{1,0:T(8,128)(2,1)} reshape(bf16[112,16,4,256]{3,2,1,0:T(4,128)(2,1)} %param.12) | data formatting | bytes 7340032 | tf_op jit(solution)/shard_map/reshape | solution.py:113
  16.1 5.3 %convolution_convert_fusion = bf16[128,16384]{1,0:T(8,128)(2,1)} fusion(bf16[112,16384]{1,0:T(8,128)(2,1)} %reshape.51, s32[112]{0:T(128)S(1)} %multiply_add_fusion.1), kind=kOutput, calls=%fused_computation.48 | convolution fusion | flops 471873536 | bytes 7864768 | tf_op jit(solution)/shard_map/dot_general | solution.py:114
  21.4 7.8 %reshape.52 = bf16[16,4,32,4,256]{4,3,2,1,0:T(4,128)(2,1)} reshape(bf16[128,16384]{1,0:T(8,128)(2,1)} %convolution_convert_fusion) | data formatting | bytes 8388608 | tf_op jit(solution)/shard_map/reshape | solution.py:117
  29.3 5.1 %copy.58 = bf16[16,4,32,4,256]{4,2,3,1,0:T(8,128)(2,1)} copy(bf16[16,4,32,4,256]{4,3,2,1,0:T(4,128)(2,1)} %reshape.52) | data formatting | bytes 8388608 | tf_op jit(solution)/shard_map/reshape | solution.py:117
  34.4 6.0 %all-to-all-start.1 = ((bf16[16,4,32,4,256]{4,2,3,1,0:T(8,128)(2,1)}), bf16[16,4,32,4,256]{4,2,3,1,0:T(8,128)(2,1)}, u32[]{:S(2)}, u32[]{:S(2)}) async-start(bf16[16,4,32,4,256]{4,2,3,1,0:T(8,128)(2,1)} %copy.58), calls=%async_computation.1 | async-start | bytes 8388608 | tf_op jit(solution)/shard_map/all_to_all | solution.py:120
  40.4 15.3 %copy.57 = bf16[512,16,4,256]{3,1,0,2:T(8,128)(2,1)} copy(bf16[512,16,4,256]{3,2,1,0:T(4,128)(2,1)} %param.9) | data formatting | bytes 33554432 | tf_op args[1]
  56.2 76.9 %all-to-all-done.1 = bf16[16,4,32,4,256]{4,2,3,1,0:T(8,128)(2,1)} async-done(((bf16[16,4,32,4,256]{4,2,3,1,0:T(8,128)(2,1)}), bf16[16,4,32,4,256]{4,2,3,1,0:T(8,128)(2,1)}, u32[]{:S(2)}, u32[]{:S(2)}) %all-to-all-start.1) | async-done | bytes 4194336 | tf_op jit(solution)/shard_map/all_to_all | solution.py:120
  133.1 4.8 %copy.60 = bf16[16,4,32,4,256]{4,2,0,3,1:T(8,128)(2,1)} copy(bf16[16,4,32,4,256]{4,2,3,1,0:T(8,128)(2,1)} %all-to-all-done.1) | data formatting | bytes 8388608
  137.9 98.4 %while.17 = (s32[]{:T(128)}, bf16[4,4,4,128]{3,2,1,0:T(4,128)(2,1)S(1)}, f32[4,4,4]{2,0,1:T(4,128)S(1)}, f32[4,4,4]{2,0,1:T(4,128)S(1)}, f32[4,4,4,128]{3,2,0,1:...) while((s32[]{:T(128)}, ...), condition=%wide.region_10.11_spmd.clone, body=%wide.region_5.10_spmd.clone.sunk | while | flops 290308608 | bytes 45256640 | solution.py:140
  139.4 4.5 %fusion.89 = (f32[4,4,4]{2,1,0:T(4,128)S(1)}, f32[4,4,4,16,32]{4,2,3,1,0:T(4,128)S(1)}) fusion(bf16[16,4,32,4,256]{4,2,0,3,1:T(8,128)(2,1)} %get-tuple-element.296, bf16[4,4,4,128]{3,2,1,0:T(4,128)(2,1)S(1)} %copy.123, pred[4,16,32]{2,1,0:T(8,128)(4,1)S(1)} %copy.116), kind=kOutput, calls=%fused_computation.77.clone.1 | convolution fusion | flops 8486848 | bytes 2246912 | tf_op jit(solution)/shard_map/while/body/eval_jaxpr/jhrd,sjthd->jhrst/dot_general | solution.py:21
  144.4 6.5 %fusion.92 = (f32[4,4,4]{2,0,1:T(4,128)S(1)}, f32[4,4,4,8192]{3,2,0,1:T(4,128)S(1)}) fusion(bf16[4,4,4,128]{3,2,1,0:T(4,128)(2,1)S(1)} %copy.123, bf16[8192,4,256]{2,0,1:T(8,128)(2,1)} %get-tuple-element.295, pred[4,8192]{1,0:T(4,128)(4,1)S(1)} %broadcast_in_dim.117), kind=kOutput, calls=%fused_computation.78.clone.1 | convolution fusion | flops 135790528 | bytes 10535168 | tf_op jit(solution)/shard_map/while/body/eval_jaxpr/jhrd,thd->jhrt/dot_general | solution.py:46
  152.6 5.5 %fusion.96 = f32[4,4,4,128]{3,2,0,1:T(4,128)S(1)} fusion(f32[4,4,4,128]{3,2,0,1:T(4,128)S(1)} %fusion.95, bf16[8192,4,256]{2,0,1:T(8,128)(2,1)} %get-tuple-element.295, f32[4,4,4,8192]{3,2,0,1:T(4,128)S(1)} %get-tuple-element.257, f32[4,4,4]{2,0,1:T(4,128)S(1)} %get-tuple-element.258, pred[4,8192]{1,0:T(4,128)(4,1)S(1)} %broadcast_in_dim.117, ...), kind=kOutput, calls=%fused_computation.24.clone.1 | convolution fusion | flops 135831552 | bytes 10617856 | tf_op jit(solution)/shard_map/while/body/eval_jaxpr/jhrt,thd->jhrd/dot_general | solution.py:59
  163.4 4.5 %fusion.89 = (f32[4,4,4]{2,1,0:T(4,128)S(1)}, f32[4,4,4,16,32]{4,2,3,1,0:T(4,128)S(1)}) fusion(bf16[16,4,32,4,256]{4,2,0,3,1:T(8,128)(2,1)} %get-tuple-element.296, bf16[4,4,4,128]{3,2,1,0:T(4,128)(2,1)S(1)} %copy.123, pred[4,16,32]{2,1,0:T(8,128)(4,1)S(1)} %copy.116), kind=kOutput, calls=%fused_computation.77.clone.1 | convolution fusion | flops 8486848 | bytes 2246912 | tf_op jit(solution)/shard_map/while/body/eval_jaxpr/jhrd,sjthd->jhrst/dot_general | solution.py:21
  168.4 6.5 %fusion.92 = (f32[4,4,4]{2,0,1:T(4,128)S(1)}, f32[4,4,4,8192]{3,2,0,1:T(4,128)S(1)}) fusion(bf16[4,4,4,128]{3,2,1,0:T(4,128)(2,1)S(1)} %copy.123, bf16[8192,4,256]{2,0,1:T(8,128)(2,1)} %get-tuple-element.295, pred[4,8192]{1,0:T(4,128)(4,1)S(1)} %broadcast_in_dim.117), kind=kOutput, calls=%fused_computation.78.clone.1 | convolution fusion | flops 135790528 | bytes 10535168 | tf_op jit(solution)/shard_map/while/body/eval_jaxpr/jhrd,thd->jhrt/dot_general | solution.py:46
  176.6 5.5 %fusion.96 = f32[4,4,4,128]{3,2,0,1:T(4,128)S(1)} fusion(f32[4,4,4,128]{3,2,0,1:T(4,128)S(1)} %fusion.95, bf16[8192,4,256]{2,0,1:T(8,128)(2,1)} %get-tuple-element.295, f32[4,4,4,8192]{3,2,0,1:T(4,128)S(1)} %get-tuple-element.257, f32[4,4,4]{2,0,1:T(4,128)S(1)} %get-tuple-element.258, pred[4,8192]{1,0:T(4,128)(4,1)S(1)} %broadcast_in_dim.117, ...), kind=kOutput, calls=%fused_computation.24.clone.1 | convolution fusion | flops 135831552 | bytes 10617856 | tf_op jit(solution)/shard_map/while/body/eval_jaxpr/jhrt,thd->jhrd/dot_general | solution.py:59
  184.5 2.5 %collective-permute-done.1 = f32[4,4,4]{2,0,1:T(4,128)S(1)} collective-permute-done((f32[4,4,4]{2,0,1:T(4,128)S(1)}, f32[4,4,4]{2,0,1:T(4,128)S(1)}, u32[]{:S(2)}, u32[]{:S(2)}) %collective-permute-start.1) | collective-permute-done | bytes 288 | tf_op jit(solution)/shard_map/while/body/eval_jaxpr/ppermute | solution.py:15
  188.6 4.5 %fusion.89 = (f32[4,4,4]{2,1,0:T(4,128)S(1)}, f32[4,4,4,16,32]{4,2,3,1,0:T(4,128)S(1)}) fusion(bf16[16,4,32,4,256]{4,2,0,3,1:T(8,128)(2,1)} %get-tuple-element.296, bf16[4,4,4,128]{3,2,1,0:T(4,128)(2,1)S(1)} %copy.123, pred[4,16,32]{2,1,0:T(8,128)(4,1)S(1)} %copy.116), kind=kOutput, calls=%fused_computation.77.clone.1 | convolution fusion | flops 8486848 | bytes 2246912 | tf_op jit(solution)/shard_map/while/body/eval_jaxpr/jhrd,sjthd->jhrst/dot_general | solution.py:21
  193.6 6.5 %fusion.92 = (f32[4,4,4]{2,0,1:T(4,128)S(1)}, f32[4,4,4,8192]{3,2,0,1:T(4,128)S(1)}) fusion(bf16[4,4,4,128]{3,2,1,0:T(4,128)(2,1)S(1)} %copy.123, bf16[8192,4,256]{2,0,1:T(8,128)(2,1)} %get-tuple-element.295, pred[4,8192]{1,0:T(4,128)(4,1)S(1)} %broadcast_in_dim.117), kind=kOutput, calls=%fused_computation.78.clone.1 | convolution fusion | flops 135790528 | bytes 10535168 | tf_op jit(solution)/shard_map/while/body/eval_jaxpr/jhrd,thd->jhrt/dot_general | solution.py:46
  201.8 5.5 %fusion.96 = f32[4,4,4,128]{3,2,0,1:T(4,128)S(1)} fusion(f32[4,4,4,128]{3,2,0,1:T(4,128)S(1)} %fusion.95, bf16[8192,4,256]{2,0,1:T(8,128)(2,1)} %get-tuple-element.295, f32[4,4,4,8192]{3,2,0,1:T(4,128)S(1)} %get-tuple-element.257, f32[4,4,4]{2,0,1:T(4,128)S(1)} %get-tuple-element.258, pred[4,8192]{1,0:T(4,128)(4,1)S(1)} %broadcast_in_dim.117, ...), kind=kOutput, calls=%fused_computation.24.clone.1 | convolution fusion | flops 135831552 | bytes 10617856 | tf_op jit(solution)/shard_map/while/body/eval_jaxpr/jhrt,thd->jhrd/dot_general | solution.py:59
  212.6 4.5 %fusion.89 = (f32[4,4,4]{2,1,0:T(4,128)S(1)}, f32[4,4,4,16,32]{4,2,3,1,0:T(4,128)S(1)}) fusion(bf16[16,4,32,4,256]{4,2,0,3,1:T(8,128)(2,1)} %get-tuple-element.296, bf16[4,4,4,128]{3,2,1,0:T(4,128)(2,1)S(1)} %copy.123, pred[4,16,32]{2,1,0:T(8,128)(4,1)S(1)} %copy.116), kind=kOutput, calls=%fused_computation.77.clone.1 | convolution fusion | flops 8486848 | bytes 2246912 | tf_op jit(solution)/shard_map/while/body/eval_jaxpr/jhrd,sjthd->jhrst/dot_general | solution.py:21
  217.6 6.5 %fusion.92 = (f32[4,4,4]{2,0,1:T(4,128)S(1)}, f32[4,4,4,8192]{3,2,0,1:T(4,128)S(1)}) fusion(bf16[4,4,4,128]{3,2,1,0:T(4,128)(2,1)S(1)} %copy.123, bf16[8192,4,256]{2,0,1:T(8,128)(2,1)} %get-tuple-element.295, pred[4,8192]{1,0:T(4,128)(4,1)S(1)} %broadcast_in_dim.117), kind=kOutput, calls=%fused_computation.78.clone.1 | convolution fusion | flops 135790528 | bytes 10535168 | tf_op jit(solution)/shard_map/while/body/eval_jaxpr/jhrd,thd->jhrt/dot_general | solution.py:46
  225.8 5.5 %fusion.96 = f32[4,4,4,128]{3,2,0,1:T(4,128)S(1)} fusion(f32[4,4,4,128]{3,2,0,1:T(4,128)S(1)} %fusion.95, bf16[8192,4,256]{2,0,1:T(8,128)(2,1)} %get-tuple-element.295, f32[4,4,4,8192]{3,2,0,1:T(4,128)S(1)} %get-tuple-element.257, f32[4,4,4]{2,0,1:T(4,128)S(1)} %get-tuple-element.258, pred[4,8192]{1,0:T(4,128)(4,1)S(1)} %broadcast_in_dim.117, ...), kind=kOutput, calls=%fused_computation.24.clone.1 | convolution fusion | flops 135831552 | bytes 10617856 | tf_op jit(solution)/shard_map/while/body/eval_jaxpr/jhrt,thd->jhrd/dot_general | solution.py:59
  233.7 2.5 %collective-permute-done.1 = f32[4,4,4]{2,0,1:T(4,128)S(1)} collective-permute-done((f32[4,4,4]{2,0,1:T(4,128)S(1)}, f32[4,4,4]{2,0,1:T(4,128)S(1)}, u32[]{:S(2)}, u32[]{:S(2)}) %collective-permute-start.1) | collective-permute-done | bytes 288 | tf_op jit(solution)/shard_map/while/body/eval_jaxpr/ppermute | solution.py:15
  (99 shorter events, 31.1 us)
Async XLA Ops:
  2.9 31.5 %all-to-all-start = ((bf16[16,4,2]{1,2,0:T(2,128)(2,1)}), bf16[16,4,2]{1,2,0:T(2,128)(2,1)S(1)}, u32[]{:S(2)}, u32[]{:S(2)}) async-start(bf16[16,4,2]{1,2,0:T(2,128)(2,1)} %copy.59), calls=%async_computation | async-start | bytes 16384 | tf_op jit(solution)/shard_map/all_to_all | solution.py:121
  34.4 98.7 %all-to-all-start.1 = ((bf16[16,4,32,4,256]{4,2,3,1,0:T(8,128)(2,1)}), bf16[16,4,32,4,256]{4,2,3,1,0:T(8,128)(2,1)}, u32[]{:S(2)}, u32[]{:S(2)}) async-start(bf16[16,4,32,4,256]{4,2,3,1,0:T(8,128)(2,1)} %copy.58), calls=%async_computation.1 | async-start | bytes 8388608 | tf_op jit(solution)/shard_map/all_to_all | solution.py:120
  40.4 15.3 %copy-start.3 = (s32[4,128]{1,0:T(4,128)S(1)}, s32[4,128]{1,0:T(4,128)}, u32[]{:S(2)}) copy-start(s32[4,128]{1,0:T(4,128)} %param.10) | copy-start | bytes 6148
  56.2 81.7 %copy-start.1 = (bf16[4,4,4,128]{3,2,1,0:T(4,128)(2,1)S(1)}, bf16[4,4,4,128]{3,2,1,0:T(4,128)(2,1)}, u32[]{:S(2)}) copy-start(bf16[4,4,4,128]{3,2,1,0:T(4,128)(2,1)} %param.8) | copy-start | bytes 49156
  56.2 81.7 %copy-start.2 = (s32[4]{0:T(128)S(1)}, s32[4]{0:T(128)}, u32[]{:S(2)}) copy-start(s32[4]{0:T(128)} %param.11) | copy-start | bytes 52
  144.4 7.8 %copy-start = (bf16[16,4,32,4,256]{4,2,0,3,1:T(8,128)(2,1)S(1)}, bf16[16,4,32,4,256]{4,2,0,3,1:T(8,128)(2,1)}, u32[]{:S(2)}) copy-start(bf16[16,4,32,4,256]{4,2,0,3,1:T(8,128)(2,1)} %get-tuple-element.296) | copy-start | bytes 12582916 | tf_op jit(solution)/shard_map/while
  158.2 3.8 %collective-permute-start.3 = (f32[4,4,4,128]{3,2,0,1:T(4,128)S(1)}, f32[4,4,4,128]{3,2,0,1:T(4,128)S(1)}, u32[]{:S(2)}, u32[]{:S(2)}) collective-permute-start(f32[4,4,4,128]{3,2,0,1:T(4,128)S(1)} %fusion.96), channel_id=1, source_target_pairs={{0,2},{2,4},{4,6},{6,0},{1,3},{3,5},{5,7},{7,1},{8,10},{10,12},{12... | collective-permute-start | bytes 98312 | tf_op jit(solution)/shard_map/while/body/eval_jaxpr/ppermute | solution.py:15
  158.2 3.7 %collective-permute-start = (bf16[4,4,4,128]{3,2,1,0:T(4,128)(2,1)S(1)}, bf16[4,4,4,128]{3,2,1,0:T(4,128)(2,1)S(1)}, u32[]{:S(2)}, u32[]{:S(2)}) collective-permute-start(bf16[4,4,4,128]{3,2,1,0:T(4,128)(2,1)S(1)} %copy.123), channel_id=1, source_target_pairs={{0,2},{2,4},{4,6},{6,0},{1,3},{3,5},{5,7},{7,1},{8,10},{10,12},{12... | collective-permute-start | bytes 49160 | tf_op jit(solution)/shard_map/while/body/eval_jaxpr/ppermute | solution.py:15
  158.3 3.5 %collective-permute-start.1 = (f32[4,4,4]{2,0,1:T(4,128)S(1)}, f32[4,4,4]{2,0,1:T(4,128)S(1)}, u32[]{:S(2)}, u32[]{:S(2)}) collective-permute-start(f32[4,4,4]{2,0,1:T(4,128)S(1)} %get-tuple-element.259), channel_id=1, source_target_pairs={{0,2},{2,4},{4,6},{6,0},{1,3},{3,5},{5,7},{7,1},{8,10},{10,12},{12... | collective-permute-start | bytes 776 | tf_op jit(solution)/shard_map/while/body/eval_jaxpr/ppermute | solution.py:15
  158.4 3.5 %collective-permute-start.2 = (f32[4,4,4]{2,0,1:T(4,128)S(1)}, f32[4,4,4]{2,0,1:T(4,128)S(1)}, u32[]{:S(2)}, u32[]{:S(2)}) collective-permute-start(f32[4,4,4]{2,0,1:T(4,128)S(1)} %get-tuple-element.260), channel_id=1, source_target_pairs={{0,2},{2,4},{4,6},{6,0},{1,3},{3,5},{5,7},{7,1},{8,10},{10,12},{12... | collective-permute-start | bytes 776 | tf_op jit(solution)/shard_map/while/body/eval_jaxpr/ppermute | solution.py:15
  168.4 7.7 %copy-start = (bf16[16,4,32,4,256]{4,2,0,3,1:T(8,128)(2,1)S(1)}, bf16[16,4,32,4,256]{4,2,0,3,1:T(8,128)(2,1)}, u32[]{:S(2)}) copy-start(bf16[16,4,32,4,256]{4,2,0,3,1:T(8,128)(2,1)} %get-tuple-element.296) | copy-start | bytes 12582916 | tf_op jit(solution)/shard_map/while
  182.2 5.0 %collective-permute-start.3 = (f32[4,4,4,128]{3,2,0,1:T(4,128)S(1)}, f32[4,4,4,128]{3,2,0,1:T(4,128)S(1)}, u32[]{:S(2)}, u32[]{:S(2)}) collective-permute-start(f32[4,4,4,128]{3,2,0,1:T(4,128)S(1)} %fusion.96), channel_id=1, source_target_pairs={{0,2},{2,4},{4,6},{6,0},{1,3},{3,5},{5,7},{7,1},{8,10},{10,12},{12... | collective-permute-start | bytes 98312 | tf_op jit(solution)/shard_map/while/body/eval_jaxpr/ppermute | solution.py:15
  182.2 4.9 %collective-permute-start = (bf16[4,4,4,128]{3,2,1,0:T(4,128)(2,1)S(1)}, bf16[4,4,4,128]{3,2,1,0:T(4,128)(2,1)S(1)}, u32[]{:S(2)}, u32[]{:S(2)}) collective-permute-start(bf16[4,4,4,128]{3,2,1,0:T(4,128)(2,1)S(1)} %copy.123), channel_id=1, source_target_pairs={{0,2},{2,4},{4,6},{6,0},{1,3},{3,5},{5,7},{7,1},{8,10},{10,12},{12... | collective-permute-start | bytes 49160 | tf_op jit(solution)/shard_map/while/body/eval_jaxpr/ppermute | solution.py:15
  184.0 3.1 %collective-permute-start.1 = (f32[4,4,4]{2,0,1:T(4,128)S(1)}, f32[4,4,4]{2,0,1:T(4,128)S(1)}, u32[]{:S(2)}, u32[]{:S(2)}) collective-permute-start(f32[4,4,4]{2,0,1:T(4,128)S(1)} %get-tuple-element.259), channel_id=1, source_target_pairs={{0,2},{2,4},{4,6},{6,0},{1,3},{3,5},{5,7},{7,1},{8,10},{10,12},{12... | collective-permute-start | bytes 776 | tf_op jit(solution)/shard_map/while/body/eval_jaxpr/ppermute | solution.py:15
  184.0 3.1 %collective-permute-start.2 = (f32[4,4,4]{2,0,1:T(4,128)S(1)}, f32[4,4,4]{2,0,1:T(4,128)S(1)}, u32[]{:S(2)}, u32[]{:S(2)}) collective-permute-start(f32[4,4,4]{2,0,1:T(4,128)S(1)} %get-tuple-element.260), channel_id=1, source_target_pairs={{0,2},{2,4},{4,6},{6,0},{1,3},{3,5},{5,7},{7,1},{8,10},{10,12},{12... | collective-permute-start | bytes 776 | tf_op jit(solution)/shard_map/while/body/eval_jaxpr/ppermute | solution.py:15
  193.6 7.7 %copy-start = (bf16[16,4,32,4,256]{4,2,0,3,1:T(8,128)(2,1)S(1)}, bf16[16,4,32,4,256]{4,2,0,3,1:T(8,128)(2,1)}, u32[]{:S(2)}) copy-start(bf16[16,4,32,4,256]{4,2,0,3,1:T(8,128)(2,1)} %get-tuple-element.296) | copy-start | bytes 12582916 | tf_op jit(solution)/shard_map/while
  207.4 3.8 %collective-permute-start.3 = (f32[4,4,4,128]{3,2,0,1:T(4,128)S(1)}, f32[4,4,4,128]{3,2,0,1:T(4,128)S(1)}, u32[]{:S(2)}, u32[]{:S(2)}) collective-permute-start(f32[4,4,4,128]{3,2,0,1:T(4,128)S(1)} %fusion.96), channel_id=1, source_target_pairs={{0,2},{2,4},{4,6},{6,0},{1,3},{3,5},{5,7},{7,1},{8,10},{10,12},{12... | collective-permute-start | bytes 98312 | tf_op jit(solution)/shard_map/while/body/eval_jaxpr/ppermute | solution.py:15
  207.5 3.7 %collective-permute-start = (bf16[4,4,4,128]{3,2,1,0:T(4,128)(2,1)S(1)}, bf16[4,4,4,128]{3,2,1,0:T(4,128)(2,1)S(1)}, u32[]{:S(2)}, u32[]{:S(2)}) collective-permute-start(bf16[4,4,4,128]{3,2,1,0:T(4,128)(2,1)S(1)} %copy.123), channel_id=1, source_target_pairs={{0,2},{2,4},{4,6},{6,0},{1,3},{3,5},{5,7},{7,1},{8,10},{10,12},{12... | collective-permute-start | bytes 49160 | tf_op jit(solution)/shard_map/while/body/eval_jaxpr/ppermute | solution.py:15
  208.0 3.1 %collective-permute-start.1 = (f32[4,4,4]{2,0,1:T(4,128)S(1)}, f32[4,4,4]{2,0,1:T(4,128)S(1)}, u32[]{:S(2)}, u32[]{:S(2)}) collective-permute-start(f32[4,4,4]{2,0,1:T(4,128)S(1)} %get-tuple-element.259), channel_id=1, source_target_pairs={{0,2},{2,4},{4,6},{6,0},{1,3},{3,5},{5,7},{7,1},{8,10},{10,12},{12... | collective-permute-start | bytes 776 | tf_op jit(solution)/shard_map/while/body/eval_jaxpr/ppermute | solution.py:15
  208.0 3.1 %collective-permute-start.2 = (f32[4,4,4]{2,0,1:T(4,128)S(1)}, f32[4,4,4]{2,0,1:T(4,128)S(1)}, u32[]{:S(2)}, u32[]{:S(2)}) collective-permute-start(f32[4,4,4]{2,0,1:T(4,128)S(1)} %get-tuple-element.260), channel_id=1, source_target_pairs={{0,2},{2,4},{4,6},{6,0},{1,3},{3,5},{5,7},{7,1},{8,10},{10,12},{12... | collective-permute-start | bytes 776 | tf_op jit(solution)/shard_map/while/body/eval_jaxpr/ppermute | solution.py:15
  231.4 5.0 %collective-permute-start.3 = (f32[4,4,4,128]{3,2,0,1:T(4,128)S(1)}, f32[4,4,4,128]{3,2,0,1:T(4,128)S(1)}, u32[]{:S(2)}, u32[]{:S(2)}) collective-permute-start(f32[4,4,4,128]{3,2,0,1:T(4,128)S(1)} %fusion.96), channel_id=1, source_target_pairs={{0,2},{2,4},{4,6},{6,0},{1,3},{3,5},{5,7},{7,1},{8,10},{10,12},{12... | collective-permute-start | bytes 98312 | tf_op jit(solution)/shard_map/while/body/eval_jaxpr/ppermute | solution.py:15
  231.5 4.9 %collective-permute-start = (bf16[4,4,4,128]{3,2,1,0:T(4,128)(2,1)S(1)}, bf16[4,4,4,128]{3,2,1,0:T(4,128)(2,1)S(1)}, u32[]{:S(2)}, u32[]{:S(2)}) collective-permute-start(bf16[4,4,4,128]{3,2,1,0:T(4,128)(2,1)S(1)} %copy.123), channel_id=1, source_target_pairs={{0,2},{2,4},{4,6},{6,0},{1,3},{3,5},{5,7},{7,1},{8,10},{10,12},{12... | collective-permute-start | bytes 49160 | tf_op jit(solution)/shard_map/while/body/eval_jaxpr/ppermute | solution.py:15
  233.2 3.1 %collective-permute-start.1 = (f32[4,4,4]{2,0,1:T(4,128)S(1)}, f32[4,4,4]{2,0,1:T(4,128)S(1)}, u32[]{:S(2)}, u32[]{:S(2)}) collective-permute-start(f32[4,4,4]{2,0,1:T(4,128)S(1)} %get-tuple-element.259), channel_id=1, source_target_pairs={{0,2},{2,4},{4,6},{6,0},{1,3},{3,5},{5,7},{7,1},{8,10},{10,12},{12... | collective-permute-start | bytes 776 | tf_op jit(solution)/shard_map/while/body/eval_jaxpr/ppermute | solution.py:15
  233.2 3.1 %collective-permute-start.2 = (f32[4,4,4]{2,0,1:T(4,128)S(1)}, f32[4,4,4]{2,0,1:T(4,128)S(1)}, u32[]{:S(2)}, u32[]{:S(2)}) collective-permute-start(f32[4,4,4]{2,0,1:T(4,128)S(1)} %get-tuple-element.260), channel_id=1, source_target_pairs={{0,2},{2,4},{4,6},{6,0},{1,3},{3,5},{5,7},{7,1},{8,10},{10,12},{12... | collective-permute-start | bytes 776 | tf_op jit(solution)/shard_map/while/body/eval_jaxpr/ppermute | solution.py:15
  (1 other events, 7.7 us)
where the time goes:
time: 238 us; the launch traced here: 237 us
  waiting for transfers between devices  85.1 us (36%)
  matrix products  73.3 us (31%)
  local copies, waits for them, and re-layouts  43.9 us (18%)
  starting transfers between devices  21.4 us (9%)
  other arithmetic  13 us (5%)
    all_to_all x1, waiting for transfers between devices, local(): lax.all_to_all(outgoing, ('req', 'ctx'), split_axis=0, concat_axis=0, til...  76.9 us
    dot_general x4, matrix products, pool_partial(): jnp.einsum('jhrd,thd->jhrt', visiting, pool_flat[..., :head_dim], preferr...  25.8 us
    dot_general x4, matrix products, pool_partial(): jnp.einsum('jhrt,thd->jhrd', weights.astype(jnp.bfloat16), pool_flat[...,...  22.1 us
    unnamed x9, local copies, waits for them, and re-layouts  20.2 us
    dot_general x4, matrix products, block_partial(): jnp.einsum('jhrd,sjthd->jhrst', visiting, keyvals[..., :head_dim], prefer...  18 us
    reshape x2, local copies, waits for them, and re-layouts, local(): outgoing.reshape(sources, req_dev, CAP * page_len, kvh_dev, row_width)  12.9 us
    ppermute x16, starting transfers between devices, from_behind(): return lax.ppermute(value, axis, pairs)  9.19 us
    ppermute x16, waiting for transfers between devices, from_behind(): return lax.ppermute(value, axis, pairs)  8.16 us
  transfers between devices with their start and end apart: 18, of which 9 were waited for; matrix products, arithmetic and copies ran while one was open for 17% of the time, Pallas kernels for 0%

commit v1 on v0

v1 whole, which is shorter than its diff:
```python
import functools
import math

import jax
import jax.numpy as jnp
from jax import lax
from jax.experimental import pallas as pl
from jax.experimental.pallas import tpu as pltpu
from jax.sharding import PartitionSpec as P

NEG = -1e30
CAP = 2
LOG2E = math.log2(math.e)
LANES = 128


def attend_kernel(
    dims, own_ref, table_ref, left_ref, slots_ref, counts_ref, q_ref, kpool_ref, vpool_ref,
    kfresh_ref, vfresh_ref, out_ref, lse_ref, kb, vb, kf, vf, acc_s, top_s, tot_s, sem,
):
    (n_req, n_ctx, req_dev, heads, group, page, slots, pages_dev, split, chunk_pages) = dims
    n_reqs = n_req * req_dev
    rows = n_ctx * heads * group
    block = heads * group
    page_rows = page * heads
    scale = LOG2E / math.sqrt(LANES)

    def copy(index, source, target, half):
        where = source.at[:, :, :, pl.ds(half * LANES, LANES)] if split else source
        return pltpu.make_async_copy(where, target, sem.at[index])

    copies = [
        copy(0, kfresh_ref, kf, 0), copy(1, vfresh_ref, vf, 1),
        copy(2, kpool_ref, kb, 0), copy(3, vpool_ref, vb, 1),
    ]
    for one in copies:
        one.start()

    def page_of(ref, index):
        return ref[index].reshape(page_rows, LANES)

    def query_of(request):
        return q_ref[request]

    def scores_of(request, keys, limit, per):
        s = lax.dot_general(
            query_of(request), keys, (((1,), (1,)), ((), ())), preferred_element_type=jnp.float32
        )
        row = lax.broadcasted_iota(jnp.int32, s.shape, 0)
        col = lax.broadcasted_iota(jnp.int32, s.shape, 1)
        keep = ((row // group) % heads == col % heads) & (col < limit * per)
        return jnp.where(keep, s * scale, NEG)

    def fold(state, s, values):
        top, tot, acc = state
        new_top = jnp.maximum(top, jnp.max(s, axis=1, keepdims=True))
        p = jnp.exp2(s - new_top)
        fade = jnp.exp2(top - new_top)
        tot = tot * fade + jnp.sum(p, axis=1, keepdims=True)
        acc = acc * fade + jnp.dot(
            p.astype(jnp.bfloat16), values, preferred_element_type=jnp.float32
        )
        return new_top, tot, acc

    start = (
        jnp.full((rows, 1), NEG, jnp.float32),
        jnp.zeros((rows, 1), jnp.float32),
        jnp.zeros((rows, LANES), jnp.float32),
    )

    copies[0].wait()
    copies[1].wait()

    def fresh_step(request, _):
        places = [slots_ref[request * slots + n] for n in range(slots)]
        keys = jnp.concatenate([page_of(kf, n) for n in places], axis=0)
        values = jnp.concatenate([page_of(vf, n) for n in places], axis=0)
        s = scores_of(request, keys, counts_ref[request], page_rows)
        top, tot, acc = fold(start, s, values)
        acc_s[request] = acc
        top_s[request] = jnp.broadcast_to(top, (rows, LANES))
        tot_s[request] = jnp.broadcast_to(tot, (rows, LANES))
        return 0

    lax.fori_loop(0, n_reqs, fresh_step, 0)

    copies[2].wait()
    copies[3].wait()

    def resident_step(i, _):
        request = own_ref[0] * req_dev + i

        def chunk_step(chunk, state):
            first = chunk * chunk_pages
            places = [table_ref[i * pages_dev + first + n] for n in range(chunk_pages)]
            keys = jnp.concatenate([page_of(kb, n) for n in places], axis=0)
            values = jnp.concatenate([page_of(vb, n) for n in places], axis=0)
            s = scores_of(request, keys, left_ref[i] - first * page, heads)
            return fold(state, s, values)

        state = (top_s[request][:, :1], tot_s[request][:, :1], acc_s[request])
        top, tot, acc = lax.fori_loop(0, pages_dev // chunk_pages, chunk_step, state)
        acc_s[request] = acc
        top_s[request] = jnp.broadcast_to(top, (rows, LANES))
        tot_s[request] = jnp.broadcast_to(tot, (rows, LANES))
        return 0

    lax.fori_loop(0, req_dev, resident_step, 0)

    lane = lax.broadcasted_iota(jnp.int32, (rows, LANES), 1)
    lse = jnp.zeros((rows, LANES), jnp.float32)
    for request in range(n_reqs):
        tot = tot_s[request]
        out_ref[request] = (acc_s[request] / tot).astype(jnp.bfloat16)
        lse = jnp.where(lane == request, top_s[request] + jnp.log2(tot), lse)
    lse_ref[...] = lse


def merge_kernel(dims, own_ref, got_ref, lse_ref, out_ref, w_s):
    n_src, req_dev, block, n_ctx = dims
    base = pl.multiple_of(own_ref[0] * block, block)
    lse = lse_ref[...]
    top = jnp.max(lse, axis=0, keepdims=True)
    w = jnp.exp2(lse - top)
    w = w / jnp.sum(w, axis=0, keepdims=True)
    for i in range(req_dev):
        total = jnp.zeros((block, LANES), jnp.float32)
        for s in range(n_src):
            total += w[s, i * block:(i + 1) * block, :] * got_ref[s, i * block:(i + 1) * block, :].astype(jnp.float32)
        out_ref[i] = total.astype(jnp.bfloat16)


def local(query, kv_pool, page_table, context_len, fresh_kv, fresh_bucket):
    n_ctx = lax.axis_size("ctx")
    n_req = lax.axis_size("req")
    ctx_place = lax.axis_index("ctx")
    req_place = lax.axis_index("req")
    req_dev, heads, group, head_dim = query.shape
    pool_slots, page = kv_pool.shape[:2]
    new_dev = fresh_kv.shape[0]
    pages_dev = page_table.shape[1]
    n_reqs = n_req * req_dev
    slots = CAP * n_ctx
    rows = n_ctx * heads * group
    block = heads * group
    n_src = n_req * n_ctx

    gathered = lax.all_gather(query, ("req", "ctx"))
    q_all = gathered.reshape(n_req, n_ctx, req_dev, block, head_dim)
    q_all = q_all.transpose(0, 2, 1, 3, 4).reshape(n_reqs, rows, head_dim)

    left = context_len - ctx_place * (pages_dev * page)
    request = fresh_bucket // n_ctx
    order = jnp.arange(new_dev, dtype=jnp.int32)
    same = (request[:, None] == request[None, :]) & (order[None, :] < order[:, None])
    place = request * slots + jnp.sum(same.astype(jnp.int32), axis=1)
    spots = jnp.arange(n_reqs * slots, dtype=jnp.int32)
    slot_table = jnp.sum(jnp.where(place[None, :] == spots[:, None], order[None, :], 0), axis=1)
    counts = jnp.sum((request[None, :] == jnp.arange(n_reqs)[:, None]).astype(jnp.int32), axis=1)

    split = heads % 4 == 0
    if split:
        pools = (kv_pool, kv_pool, fresh_kv, fresh_kv)
        shape = (page, heads, LANES)
    else:
        pools = tuple(
            a[..., h * LANES:(h + 1) * LANES].reshape(a.shape[0], page * heads, LANES)
            for a in (kv_pool, fresh_kv) for h in (0, 1)
        )
        shape = (page * heads, LANES)
    dims = (n_req, n_ctx, req_dev, heads, group, page, slots, pages_dev, split, 16)
    smem = pl.BlockSpec(memory_space=pltpu.SMEM)
    vmem = pl.BlockSpec(memory_space=pltpu.VMEM)
    hbm = pl.BlockSpec(memory_space=pl.ANY)
    out, lse = pl.pallas_call(
        functools.partial(attend_kernel, dims),
        out_shape=(
            jax.ShapeDtypeStruct((n_reqs, rows, LANES), jnp.bfloat16),
            jax.ShapeDtypeStruct((rows, LANES), jnp.float32),
        ),
        in_specs=[smem] * 5 + [vmem] + [hbm] * 4,
        out_specs=(vmem, vmem),
        scratch_shapes=[
            pltpu.VMEM((pool_slots,) + shape, jnp.bfloat16),
            pltpu.VMEM((pool_slots,) + shape, jnp.bfloat16),
            pltpu.VMEM((new_dev,) + shape, jnp.bfloat16),
            pltpu.VMEM((new_dev,) + shape, jnp.bfloat16),
            pltpu.VMEM((n_reqs, rows, LANES), jnp.float32),
            pltpu.VMEM((n_reqs, rows, LANES), jnp.float32),
            pltpu.VMEM((n_reqs, rows, LANES), jnp.float32),
            pltpu.SemaphoreType.DMA((4,)),
        ],
        compiler_params=pltpu.CompilerParams(vmem_limit_bytes=48 * 2**20),
        name="attend",
    )(
        req_place.astype(jnp.int32).reshape(1), page_table.reshape(-1), left, slot_table, counts,
        q_all, *pools,
    )
    sends = out.reshape(n_req, req_dev, n_ctx, block, LANES).transpose(0, 2, 1, 3, 4)
    sends = sends.reshape(n_src, req_dev * block, LANES)
    lse = lse[:, :n_reqs].T.reshape(n_req, req_dev, n_ctx, block).transpose(0, 2, 1, 3)
    lse = lse.reshape(n_src, req_dev * block)
    got = lax.all_to_all(sends, ("req", "ctx"), split_axis=0, concat_axis=0, tiled=True)
    got_lse = lax.all_to_all(lse, ("req", "ctx"), split_axis=0, concat_axis=0, tiled=True)
    top = jnp.max(got_lse, axis=0)
    w = jnp.exp2(got_lse - top)
    w = w / jnp.sum(w, axis=0)
    merged = jnp.sum(got.astype(jnp.float32) * w[:, :, None], axis=0)
    return merged.astype(jnp.bfloat16).reshape(req_dev, heads, group, head_dim)


def solution(mesh):
    placed = (
        P("req", "kvh", "ctx", None),
        P(("req", "ctx"), None, "kvh", None),
        P("req", "ctx"),
        P("req"),
        P(("req", "ctx"), None, "kvh", None),
        P(("req", "ctx")),
    )
    return jax.shard_map(
        local, mesh=mesh, in_specs=placed, out_specs=P("req", "kvh", "ctx", None), check_vma=False
    )
```

time: 238 us -> 81.5 us (0.34)
  the two profiles are of different devices: /device:TPU:16 before, /device:TPU:0 now
where the time goes in v1:
time: 81.5 us; the launch traced here: 81.2 us
  Pallas kernels  27 us (33%)
  blocking collectives  24 us (29%)
  waiting for transfers between devices  15.5 us (19%)
  starting transfers between devices  7 us (9%)
  local copies, waits for them, and re-layouts  4.3 us (5%)
  other arithmetic  3.26 us (4%)
    pallas_call x1, Pallas kernels, local(): pl.pallas_call(functools.partial(attend_kernel, dims), out_shape=(jax.Sha...  27 us
    all_gather x1, blocking collectives, local(): gathered = lax.all_gather(query, ('req', 'ctx'))  24 us
    all_to_all x1, waiting for transfers between devices, local(): lax.all_to_all(sends, ('req', 'ctx'), split_axis=0, concat_axis=0, tiled=...  9.92 us
    all_to_all x1, waiting for transfers between devices, local(): lax.all_to_all(lse, ('req', 'ctx'), split_axis=0, concat_axis=0, tiled=True)  5.57 us
    all_to_all x1, starting transfers between devices, local(): lax.all_to_all(sends, ('req', 'ctx'), split_axis=0, concat_axis=0, tiled=...  3.53 us
    all_to_all x1, starting transfers between devices, local(): lax.all_to_all(lse, ('req', 'ctx'), split_axis=0, concat_axis=0, tiled=True)  3.47 us
    unnamed x4, local copies, waits for them, and re-layouts  2.72 us
  transfers between devices with their start and end apart: 2, of which 2 were waited for; matrix products, arithmetic and copies ran while one was open for 1% of the time, Pallas kernels for 0%

profile of v1, /device:TPU:0, one launch (start us, length us, event | category | flops | bytes accessed | tf_op | source)
XLA Modules:
  0.0 81.2 jit_solution(7758379831120712826)
XLA Ops:
  0.0 0.7 and_select_fusion
  0.7 0.2 convert_reduce_fusion
  0.8 0.1 convert_reduce_fusion.1.counts_ref
  1.0 0.7 multiply_add_fusion
  1.6 0.1 select_reduce_fusion.slots_ref
  1.7 24.0 %all-gather = bf16[64,4,4,128]{3,2,1,0:T(4,128)(2,1)S(1)} all-gather(bf16[4,4,4,128]{3,2,1,0:T(4,128)(2,1)} %param.6), channel_id=2, replica_groups=mesh['req'=4,'ctx'=4,'kvh'=2] {'req','ctx'}, dimensions={0}, use_global_device_ids=true | all-gather | bytes 278528 | tf_op jit(solution)/shard_map/all_gather | solution.py:148
  25.8 0.7 broadcast_subtract_fusion.left_ref
  26.4 0.0 copy-start
  26.4 2.0 %copy-done = bf16[112,16,4,256]{3,2,1,0:T(4,128)(2,1)S(1)} copy-done((bf16[112,16,4,256]{3,2,1,0:T(4,128)(2,1)S(1)}, bf16[112,16,4,256]{3,2,1,0:T(4,128)(2,1)}, u32[]{:S(2)}) %copy-start) | copy-done | bytes 3670040
  28.5 0.0 copy-start.1
  28.5 0.7 copy-done.1
  29.2 27.0 %attend.1 = (bf16[16,64,128]{2,1,0:T(8,128)(2,1)S(1)}, f32[64,128]{1,0:T(8,128)S(1)}) custom-call(s32[1]{0:T(128)} %bitcast.own_ref, s32[512]{0:T(512)S(1)} %bitcast.18, s32[4]{0:T(128)S(1)} %broadcast_subtract_fusion.left_ref, s32[128]{0:T(128)S(1)} %select_reduce_fusion.slots_ref, s32[16]{0:T(128)S(1)} %convert_reduce_fusion.1.counts_ref, ...), custom_call_target="tpu_custom_call" | custom-call | tf_op jit(solution)/shard_map/attend/pallas_call | solution.py:175
  56.2 0.1 copy.19
  56.2 0.1 reshape.67
  56.3 0.7 all_to_all.12
  57.0 3.5 %all-to-all-start.1 = ((f32[16,1,64]{2,1,0:T(1,128)}), f32[16,1,64]{2,1,0:T(1,128)S(1)}, u32[]{:S(2)}, u32[]{:S(2)}) async-start(f32[16,1,64]{2,1,0:T(1,128)} %bitcast.10), calls=%async_computation.1 | async-start | bytes 16384 | tf_op jit(solution)/shard_map/all_to_all | solution.py:204
  60.5 0.7 copy.18
  61.2 5.6 %all-to-all-done.1 = f32[16,1,64]{2,1,0:T(1,128)S(1)} async-done(((f32[16,1,64]{2,1,0:T(1,128)}), f32[16,1,64]{2,1,0:T(1,128)S(1)}, u32[]{:S(2)}, u32[]{:S(2)}) %all-to-all-start.1) | async-done | bytes 4128 | tf_op jit(solution)/shard_map/all_to_all | solution.py:204
  66.8 3.5 %all-to-all-start = ((bf16[16,64,128]{2,1,0:T(8,128)(2,1)}), bf16[16,64,128]{2,1,0:T(8,128)(2,1)S(1)}, u32[]{:S(2)}, u32[]{:S(2)}) async-start(bf16[16,64,128]{2,1,0:T(8,128)(2,1)} %bitcast.7), calls=%async_computation | async-start | bytes 524288 | tf_op jit(solution)/shard_map/all_to_all | solution.py:203
  70.4 9.9 %all-to-all-done = bf16[16,64,128]{2,1,0:T(8,128)(2,1)S(1)} async-done(((bf16[16,64,128]{2,1,0:T(8,128)(2,1)}), bf16[16,64,128]{2,1,0:T(8,128)(2,1)S(1)}, u32[]{:S(2)}, u32[]{:S(2)}) %all-to-all-start) | async-done | bytes 262176 | tf_op jit(solution)/shard_map/all_to_all | solution.py:203
  80.3 0.8 multiply_reduce_fusion
  (6 shorter events, 0.1 us)
Async XLA Ops:
  26.4 2.0 %copy-start = (bf16[112,16,4,256]{3,2,1,0:T(4,128)(2,1)S(1)}, bf16[112,16,4,256]{3,2,1,0:T(4,128)(2,1)}, u32[]{:S(2)}) copy-start(bf16[112,16,4,256]{3,2,1,0:T(4,128)(2,1)} %vfresh_ref.1) | copy-start | bytes 11010052
  28.5 0.7 copy-start.1
  57.0 9.8 %all-to-all-start.1 = ((f32[16,1,64]{2,1,0:T(1,128)}), f32[16,1,64]{2,1,0:T(1,128)S(1)}, u32[]{:S(2)}, u32[]{:S(2)}) async-start(f32[16,1,64]{2,1,0:T(1,128)} %bitcast.10), calls=%async_computation.1 | async-start | bytes 16384 | tf_op jit(solution)/shard_map/all_to_all | solution.py:204
  66.8 13.5 %all-to-all-start = ((bf16[16,64,128]{2,1,0:T(8,128)(2,1)}), bf16[16,64,128]{2,1,0:T(8,128)(2,1)S(1)}, u32[]{:S(2)}, u32[]{:S(2)}) async-start(bf16[16,64,128]{2,1,0:T(8,128)(2,1)} %bitcast.7), calls=%async_computation | async-start | bytes 524288 | tf_op jit(solution)/shard_map/all_to_all | solution.py:203

commit v2 on v0

v2 whole, which is shorter than its diff:
```python
import functools
import math

import jax
import jax.numpy as jnp
from jax import lax
from jax.experimental import pallas as pl
from jax.experimental.pallas import tpu as pltpu
from jax.sharding import PartitionSpec as P

NEG = -1e30
CAP = 2
LANES = 128
SCALE = math.log2(math.e) / math.sqrt(LANES)
WIDE = 1024
VMEM = pl.BlockSpec(memory_space=pltpu.VMEM)
SMEM = pl.BlockSpec(memory_space=pltpu.SMEM)
HBM = pl.BlockSpec(memory_space=pl.ANY)


def shift(value, axis, steps):
    count = lax.axis_size(axis)
    pairs = [(source, (source + steps) % count) for source in range(count)]
    return lax.ppermute(value, axis, pairs)


def stage_kernel(pieces, pool_ref, fresh_ref, kb, vb, kf, vf, sem):
    each = pool_ref.shape[0] // pieces
    copies = []
    for half, (pool_to, fresh_to) in enumerate(((kb, kf), (vb, vf))):
        lanes = pl.ds(half * LANES, LANES)
        copies.append(pltpu.make_async_copy(
            fresh_ref.at[:, :, :, lanes], fresh_to, sem.at[len(copies)]))
        for n in range(pieces):
            some = pl.ds(n * each, each)
            copies.append(pltpu.make_async_copy(
                pool_ref.at[some, :, :, lanes], pool_to.at[some], sem.at[len(copies)]))
    for one in copies:
        one.start()
    for one in copies:
        one.wait()


def tools(heads, page_rows):
    def page_of(ref, index):
        return ref[index].reshape(page_rows, LANES)

    def class_reduce(x, op):
        step = heads
        while step < LANES:
            x = op(x, pltpu.roll(x, step, 1))
            step *= 2
        return x

    def scores(q, keys, sub, lane, limit, first):
        s = lax.dot_general(q, keys, (((1,), (1,)), ((), ())), preferred_element_type=jnp.float32)
        out = []
        for j in range(s.shape[1] // LANES):
            part = s[:, j * LANES:(j + 1) * LANES]
            one = part[:sub]
            for h in range(1, heads):
                one = jnp.where(lane % heads == h, part[h * sub:(h + 1) * sub], one)
            one = jnp.where(lane < limit - (first + j * LANES), one * SCALE, NEG)
            out.append(one)
        return out

    def spread(p, onehots):
        p = p.astype(jnp.bfloat16)
        return jnp.concatenate([p * one for one in onehots], axis=0)

    def rows_of(x, h):
        return jnp.broadcast_to(x[:, h:h + 1], x.shape)

    return page_of, class_reduce, scores, spread, rows_of


def fold_max(parts):
    top = parts[0]
    for part in parts[1:]:
        top = jnp.maximum(top, part)
    return top


def resident_kernel(
    dims, table_ref, left_ref, q_ref, kb, vb, acc_ref, top_ref, tot_ref, t_s,
):
    heads, page_rows, pages_dev, sub = dims
    page_of, class_reduce, scores, spread, rows_of = tools(heads, page_rows)
    columns = pages_dev * page_rows
    wide = min(WIDE, columns)
    per = wide // page_rows
    lane = lax.broadcasted_iota(jnp.int32, (sub, LANES), 1)
    onehots = [(lane % heads == h).astype(jnp.bfloat16) for h in range(heads)]

    def step(i, _):
        q = q_ref[i]
        limit = left_ref[i] * heads
        base = i * pages_dev
        top = jnp.full((sub, LANES), NEG, jnp.float32)
        for c in range(columns // wide):
            keys = jnp.concatenate(
                [page_of(kb, table_ref[base + c * per + n]) for n in range(per)], axis=0)
            parts = scores(q, keys, sub, lane, limit, c * wide)
            for j, part in enumerate(parts):
                t_s[:, c * wide + j * LANES:c * wide + (j + 1) * LANES] = part
            top = jnp.maximum(top, fold_max(parts))
        top = class_reduce(top, jnp.maximum)
        tot = jnp.zeros((sub, LANES), jnp.float32)
        acc = jnp.zeros((heads * sub, LANES), jnp.float32)
        for c in range(columns // wide):
            weights = []
            for j in range(wide // LANES):
                at = c * wide + j * LANES
                p = jnp.exp2(t_s[:, at:at + LANES] - top)
                tot = tot + p
                weights.append(spread(p, onehots))
            values = jnp.concatenate(
                [page_of(vb, table_ref[base + c * per + n]) for n in range(per)], axis=0)
            acc = acc + jnp.dot(
                jnp.concatenate(weights, axis=1), values, preferred_element_type=jnp.float32)
        acc_ref[i] = acc
        top_ref[i] = top
        tot_ref[i] = class_reduce(tot, jnp.add)
        return 0

    lax.fori_loop(0, q_ref.shape[0], step, 0)


def fresh_kernel(
    dims, own_ref, slots_ref, counts_ref, qown_ref, qfar_ref, kf, vf, acc_ref, top_ref, tot_ref,
    out_ref,
):
    heads, page_rows, slots, sub, n_req, req_dev = dims
    page_of, class_reduce, scores, spread, rows_of = tools(heads, page_rows)
    lane = lax.broadcasted_iota(jnp.int32, (sub, LANES), 1)
    onehots = [(lane % heads == h).astype(jnp.bfloat16) for h in range(heads)]
    n_reqs = n_req * req_dev
    unit = 4 * heads
    fill = LANES // unit
    kind = (lane % unit) // heads
    slabs = [jnp.zeros((sub, LANES), jnp.float32) for _ in range(-(-n_reqs // fill))]
    for k in range(n_req):
        place = lax.rem(own_ref[0] + k, n_req)
        for i in range(req_dev):
            n = k * req_dev + i
            request = place * req_dev + i
            q = qown_ref[i] if k == 0 else qfar_ref[n - req_dev]
            spots = [slots_ref[request * slots + m] for m in range(slots)]
            keys = jnp.concatenate([page_of(kf, m) for m in spots], axis=0)
            values = jnp.concatenate([page_of(vf, m) for m in spots], axis=0)
            parts = scores(q, keys, sub, lane, counts_ref[request] * page_rows, 0)
            top = class_reduce(fold_max(parts), jnp.maximum)
            if k == 0:
                top = jnp.maximum(top, top_ref[i])
            weights = []
            tot = jnp.zeros((sub, LANES), jnp.float32)
            for part in parts:
                p = jnp.exp2(part - top)
                tot = tot + p
                weights.append(spread(p, onehots))
            tot = class_reduce(tot, jnp.add)
            acc = jnp.dot(
                jnp.concatenate(weights, axis=1), values, preferred_element_type=jnp.float32)
            if k == 0:
                fade = jnp.exp2(top_ref[i] - top)
                tot = tot + fade * tot_ref[i]
            whole = 1.0 / tot
            for h in range(heads):
                some = acc[h * sub:(h + 1) * sub]
                if k == 0:
                    some = some + acc_ref[i, h * sub:(h + 1) * sub, :] * rows_of(fade, h)
                out_ref[n * heads + h] = (some * rows_of(whole, h)).astype(jnp.bfloat16)
            lse = top + jnp.log2(tot)
            slab = n // fill
            slabs[slab] = jnp.where(lane // unit == n % fill, lse, slabs[slab])
    for n, lse in enumerate(slabs):
        out_ref[n_reqs * heads + n] = pieces_of(lse, kind)


def pieces_of(lse, kind):
    high = lse.astype(jnp.bfloat16)
    rest = lse - high.astype(jnp.float32)
    mid = rest.astype(jnp.bfloat16)
    low = (rest - mid.astype(jnp.float32)).astype(jnp.bfloat16)
    both = jnp.where(kind == 1, mid.astype(jnp.float32), low.astype(jnp.float32))
    return jnp.where(kind == 0, high.astype(jnp.float32), both).astype(jnp.bfloat16)


def whole_of(pieces, heads):
    x = pieces.astype(jnp.float32)
    return x + pltpu.roll(x, LANES - heads, 1) + pltpu.roll(x, LANES - 2 * heads, 1)


def merge_lse(refs, slab, heads):
    lses = [whole_of(ref[slab], heads) for ref in refs]
    top = fold_max(lses)
    shares = [jnp.exp2(lse - top) for lse in lses]
    tot = sum(shares)
    return [share / tot for share in shares], top + jnp.log2(tot)


def ctx_merge_kernel(dims, *refs):
    heads, n_req, req_dev = dims
    refs, out_ref = refs[:-1], refs[-1]
    n_reqs = n_req * req_dev
    unit = 4 * heads
    fill = LANES // unit
    group = out_ref.shape[2]
    lane = lax.broadcasted_iota(jnp.int32, (group, LANES), 1)
    spread_lse = []
    for slab in range(-(-n_reqs // fill)):
        shares, lse = merge_lse(refs, n_reqs * heads + slab, heads)
        kind = (lane % unit) // heads
        same = lse
        for m in (1, 2):
            same = jnp.where(kind == m, pltpu.roll(lse, m * heads, 1), same)
        spread_lse.append(pieces_of(same, kind))
        for n in range(slab * fill, min(n_reqs, (slab + 1) * fill)):
            for h in range(heads):
                at = (n % fill) * unit + h
                total = 0.0
                for ref, share in zip(refs, shares):
                    total = total + ref[n * heads + h].astype(jnp.float32) * jnp.broadcast_to(
                        share[:, at:at + 1], (group, LANES))
                out_ref[n // req_dev, (n % req_dev) * heads + h] = total.astype(jnp.bfloat16)
    for k in range(n_req):
        slab = spread_lse[k * req_dev // fill].astype(jnp.float32)
        at = (k * req_dev) % fill * unit
        if at:
            slab = pltpu.roll(slab, LANES - at, 1)
        out_ref[k, req_dev * heads] = slab.astype(jnp.bfloat16)


def req_merge_kernel(dims, *refs):
    heads, req_dev = dims
    refs, out_ref = refs[:-1], refs[-1]
    group = out_ref.shape[2]
    shares, _ = merge_lse(refs, req_dev * heads, heads)
    for i in range(req_dev):
        for h in range(heads):
            at = i * 4 * heads + h
            total = 0.0
            for ref, share in zip(refs, shares):
                total = total + ref[i * heads + h].astype(jnp.float32) * jnp.broadcast_to(
                    share[:, at:at + 1], (group, LANES))
            out_ref[i, h] = total.astype(jnp.bfloat16)


def params(mib):
    return pltpu.CompilerParams(vmem_limit_bytes=mib * 2**20)


def local(query, kv_pool, page_table, context_len, fresh_kv, fresh_bucket):
    n_ctx = lax.axis_size("ctx")
    n_req = lax.axis_size("req")
    ctx_place = lax.axis_index("ctx")
    req_place = lax.axis_index("req")
    req_dev, heads, group, head_dim = query.shape
    pool_slots, page = kv_pool.shape[:2]
    new_dev = fresh_kv.shape[0]
    pages_dev = page_table.shape[1]
    n_reqs = n_req * req_dev
    slots = CAP * n_ctx
    sub = n_ctx * group
    rows = heads * sub
    page_rows = page * heads

    near = [query] + [shift(query, "ctx", -k) for k in range(1, n_ctx)]
    ahead = jnp.stack([shift(query, "req", -k) for k in range(1, n_req)])

    if heads % 4 == 0:
        pieces = 8
        half = lambda count: jax.ShapeDtypeStruct((count, page, heads, LANES), jnp.bfloat16)
        kb, vb, kf, vf = pl.pallas_call(
            functools.partial(stage_kernel, pieces),
            out_shape=(half(pool_slots), half(pool_slots), half(new_dev), half(new_dev)),
            in_specs=[HBM, HBM],
            out_specs=(VMEM,) * 4,
            scratch_shapes=[pltpu.SemaphoreType.DMA((2 * pieces + 2,))],
            compiler_params=params(2),
            cost_estimate=pl.CostEstimate(
                flops=0, transcendentals=0, bytes_accessed=2 * (kv_pool.size + fresh_kv.size)),
            name="stage",
        )(kv_pool, fresh_kv)
    else:
        kb, vb, kf, vf = (
            a[..., h * LANES:(h + 1) * LANES].reshape(a.shape[0], page_rows, LANES)
            for a in (kv_pool, fresh_kv) for h in (0, 1)
        )

    far = [ahead] + [shift(ahead, "ctx", -k) for k in range(1, n_ctx)]
    q_own = jnp.stack(near).transpose(1, 2, 0, 3, 4).reshape(req_dev, rows, head_dim)
    q_far = jnp.stack(far).transpose(1, 2, 3, 0, 4, 5).reshape(n_reqs - req_dev, rows, head_dim)

    left = context_len - ctx_place * (pages_dev * page)
    request = fresh_bucket // n_ctx
    order = jnp.arange(new_dev, dtype=jnp.int32)
    same = (request[:, None] == request[None, :]) & (order[None, :] < order[:, None])
    place = request * slots + jnp.sum(same.astype(jnp.int32), axis=1)
    spots = jnp.arange(n_reqs * slots, dtype=jnp.int32)
    slot_table = jnp.sum(jnp.where(place[None, :] == spots[:, None], order[None, :], 0), axis=1)
    counts = jnp.sum((request[None, :] == jnp.arange(n_reqs)[:, None]).astype(jnp.int32), axis=1)

    f32 = lambda *shape: jax.ShapeDtypeStruct(shape, jnp.float32)
    bf16 = lambda *shape: jax.ShapeDtypeStruct(shape, jnp.bfloat16)
    columns = pages_dev * page_rows
    acc, top, tot = pl.pallas_call(
        functools.partial(resident_kernel, (heads, page_rows, pages_dev, sub)),
        out_shape=(
            f32(req_dev, rows, LANES), f32(req_dev, sub, LANES), f32(req_dev, sub, LANES)),
        in_specs=[SMEM] * 2 + [VMEM] * 3,
        out_specs=(VMEM,) * 3,
        scratch_shapes=[pltpu.VMEM((sub, columns), jnp.float32)],
        compiler_params=params(8),
        cost_estimate=pl.CostEstimate(
            flops=4 * req_dev * rows * columns * LANES, transcendentals=req_dev * sub * columns,
            bytes_accessed=2 * kv_pool.size),
        name="resident",
    )(page_table.reshape(-1), left, q_own, kb, vb)

    fill = LANES // (4 * heads)
    slabs = n_reqs * heads + -(-n_reqs // fill)
    parts = pl.pallas_call(
        functools.partial(fresh_kernel, (heads, page_rows, slots, sub, n_req, req_dev)),
        out_shape=bf16(slabs, sub, LANES),
        in_specs=[SMEM] * 3 + [VMEM] * 7,
        out_specs=VMEM,
        compiler_params=params(8),
        cost_estimate=pl.CostEstimate(
            flops=4 * n_reqs * rows * slots * page_rows * LANES,
            transcendentals=n_reqs * sub * slots * page_rows, bytes_accessed=2 * fresh_kv.size),
        name="fresh",
    )(
        req_place.astype(jnp.int32).reshape(1), slot_table, counts, q_own, q_far, kf, vf,
        acc, top, tot,
    )
    sends = parts.reshape(slabs, n_ctx, group, LANES).transpose(1, 0, 2, 3)
    got = [sends[0]] + [shift(sends[k], "ctx", k) for k in range(1, n_ctx)]
    merged = pl.pallas_call(
        functools.partial(ctx_merge_kernel, (heads, n_req, req_dev)),
        out_shape=bf16(n_req, req_dev * heads + 1, group, LANES),
        in_specs=[VMEM] * n_ctx,
        out_specs=VMEM,
        compiler_params=params(8),
        name="ctx_merge",
    )(*got)
    got = [merged[0]] + [shift(merged[k], "req", k) for k in range(1, n_req)]
    return pl.pallas_call(
        functools.partial(req_merge_kernel, (heads, req_dev)),
        out_shape=bf16(req_dev, heads, group, LANES),
        in_specs=[VMEM] * n_req,
        out_specs=VMEM,
        compiler_params=params(8),
        name="req_merge",
    )(*got)


def solution(mesh):
    placed = (
        P("req", "kvh", "ctx", None),
        P(("req", "ctx"), None, "kvh", None),
        P("req", "ctx"),
        P("req"),
        P(("req", "ctx"), None, "kvh", None),
        P(("req", "ctx")),
    )
    return jax.shard_map(
        local, mesh=mesh, in_specs=placed, out_specs=P("req", "kvh", "ctx", None), check_vma=False
    )
```

time: 238 us -> 65.7 us (0.28)
  the two profiles are of different devices: /device:TPU:16 before, /device:TPU:0 now
where the time goes in v2:
time: 65.7 us; the launch traced here: 65.4 us
  Pallas kernels  29.9 us (46%)
  starting transfers between devices  17.8 us (27%)
  local copies, waits for them, and re-layouts  8.14 us (12%)
  waiting for transfers between devices  6.79 us (10%)
  other arithmetic  2.69 us (4%)
    ppermute x15, starting transfers between devices, shift(): return lax.ppermute(value, axis, pairs)  17.8 us
    pallas_call x1, Pallas kernels, local(): pl.pallas_call(functools.partial(fresh_kernel, (heads, page_rows, slots,...  12.7 us
    pallas_call x1, Pallas kernels, local(): pl.pallas_call(functools.partial(resident_kernel, (heads, page_rows, page...  8.53 us
    unnamed x8, local copies, waits for them, and re-layouts  7.81 us
    pallas_call x1, Pallas kernels, local(): pl.pallas_call(functools.partial(stage_kernel, pieces), out_shape=(half(p...  7.21 us
    ppermute x15, waiting for transfers between devices, shift(): return lax.ppermute(value, axis, pairs)  6.79 us
  transfers between devices with their start and end apart: 15, of which 7 were waited for; matrix products, arithmetic and copies ran while one was open for 4% of the time, Pallas kernels for 24%

profile of v2, /device:TPU:0, one launch (start us, length us, event | category | flops | bytes accessed | tf_op | source)
XLA Modules:
  0.0 65.4 jit_solution(1910869252196076095)
XLA Ops:
  0.0 5.0 %collective-permute-start.3 = (bf16[4,4,4,128]{3,2,1,0:T(4,128)(2,1)}, bf16[4,4,4,128]{3,2,1,0:T(4,128)(2,1)S(1)}, u32[]{:S(2)}, u32[]{:S(2)}) collective-permute-start(bf16[4,4,4,128]{3,2,1,0:T(4,128)(2,1)} %param.6), channel_id=1, source_target_pairs={{0,24},{8,0},{16,8},{24,16},{1,25},{9,1},{17,9},{25,17},{2,26},{10... | collective-permute-start | bytes 49160 | tf_op jit(solution)/shard_map/ppermute | solution.py:24
  5.1 1.0 %collective-permute-start.5 = (bf16[4,4,4,128]{3,2,1,0:T(4,128)(2,1)}, bf16[4,4,4,128]{3,2,1,0:T(4,128)(2,1)S(1)}, u32[]{:S(2)}, u32[]{:S(2)}) collective-permute-start(bf16[4,4,4,128]{3,2,1,0:T(4,128)(2,1)} %param.6), channel_id=1, source_target_pairs={{0,8},{8,16},{16,24},{24,0},{1,9},{9,17},{17,25},{25,1},{2,10},{10... | collective-permute-start | bytes 49160 | tf_op jit(solution)/shard_map/ppermute | solution.py:24
  6.2 1.4 %collective-permute-start.1 = (bf16[4,4,4,128]{3,2,1,0:T(4,128)(2,1)}, bf16[4,4,4,128]{3,2,1,0:T(4,128)(2,1)S(1)}, u32[]{:S(2)}, u32[]{:S(2)}) collective-permute-start(bf16[4,4,4,128]{3,2,1,0:T(4,128)(2,1)} %param.6), channel_id=1, source_target_pairs={{0,4},{2,6},{4,0},{6,2},{1,5},{3,7},{5,1},{7,3},{8,12},{10,14},{12... | collective-permute-start | bytes 49160 | tf_op jit(solution)/shard_map/ppermute | solution.py:24
  7.6 0.7 %and_select_fusion = s32[112]{0:T(128)S(1)} fusion(s32[112]{0:T(128)} %param.11), kind=kLoop, calls=%fused_computation.19 | loop fusion | flops 1680 | bytes 896 | tf_op jit(solution)/shard_map/jit(floor_divide)/jit(_where)/select_n | solution.py:296
  8.4 0.7 %multiply_add_fusion = s32[112]{0:T(128)S(1)} fusion(s32[112]{0:T(128)S(1)} %convert_reduce_fusion, s32[112]{0:T(128)} %param.11), kind=kLoop, calls=%fused_computation.23 | loop fusion | flops 1904 | bytes 1344 | tf_op jit(solution)/shard_map/add | solution.py:299
  9.2 0.7 %broadcast_subtract_fusion.left_ref = s32[4]{0:T(128)S(1)} fusion(s32[4]{0:T(128)} %param.9, s32[]{:T(128)S(6)} %mul.11), kind=kLoop, calls=%fused_computation.24 | loop fusion | flops 4 | bytes 36 | tf_op jit(solution)/shard_map/sub | solution.py:295
  10.0 5.8 %copy-done = bf16[512,16,4,256]{3,2,1,0:T(4,128)(2,1)S(1)} copy-done((bf16[512,16,4,256]{3,2,1,0:T(4,128)(2,1)S(1)}, bf16[512,16,4,256]{3,2,1,0:T(4,128)(2,1)}, u32[]{:S(2)}) %copy-start) | copy-done | bytes 16777240
  15.7 2.0 %copy-done.1 = bf16[112,16,4,256]{3,2,1,0:T(4,128)(2,1)S(1)} copy-done((bf16[112,16,4,256]{3,2,1,0:T(4,128)(2,1)S(1)}, bf16[112,16,4,256]{3,2,1,0:T(4,128)(2,1)}, u32[]{:S(2)}) %copy-start.1) | copy-done | bytes 3670040
  17.8 7.2 %stage.1 = (bf16[512,16,4,128]{3,2,1,0:T(4,128)(2,1)S(1)}, bf16[512,16,4,128]{3,2,1,0:T(4,128)(2,1)S(1)}, bf16[112,16,4,128]{3,2,1,0:T(4,128)(2,1)S(1)}, bf16[112,16,4,128]{3,2,1,0:T(4,128)(2,1)S(1)}) custom-call(bf16[512,16,4,256]{3,2,1,0:T(4,128)(2,1)S(1)} %copy-done, bf16[112,16,4,256]{3,2,1,0:T(4,128)(2,1)S(1)} %copy-done.1), custom_call_target="tpu_custom_call" | custom-call | bytes 20447232 | tf_op jit(solution)/shard_map/stage/pallas_call | solution.py:274
  25.3 1.6 %collective-permute-start.6 = (bf16[3,4,4,4,128]{4,3,2,1,0:T(4,128)(2,1)S(1)}, bf16[3,4,4,4,128]{4,3,2,1,0:T(4,128)(2,1)S(1)}, u32[]{:S(2)}, u32[]{:S(2)}) collective-permute-start(bf16[3,4,4,4,128]{4,3,2,1,0:T(4,128)(2,1)S(1)} %pad_maximum_fusion), channel_id=1, source_target_pairs={{0,6},{2,0},{4,2},{6,4},{1,7},{3,1},{5,3},{7,5},{8,14},{10,8},{12,... | collective-permute-start | bytes 147464 | tf_op jit(solution)/shard_map/ppermute | solution.py:24
  26.9 0.6 collective-permute-start.7
  28.3 8.5 %resident.1 = (f32[4,64,128]{2,1,0:T(8,128)S(1)}, f32[4,16,128]{2,1,0:T(8,128)S(1)}, f32[4,16,128]{2,1,0:T(8,128)S(1)}) custom-call(s32[512]{0:T(512)S(1)} %bitcast.44, s32[4]{0:T(128)S(1)} %broadcast_subtract_fusion.left_ref, bf16[4,64,128]{2,1,0:T(8,128)(2,1)S(1)} %bitcast.42, bf16[512,16,4,128]{3,2,1,0:T(4,128)(2,1)S(1)} %get-tuple-element.14.kb, ...), custom_call_target="tpu_custom_call" | custom-call | flops 1073741824 | bytes 16777216 | tf_op jit(solution)/shard_map/resident/pallas_call | solution.py:307
  37.2 12.7 %fresh.1 = bf16[66,16,128]{2,1,0:T(8,128)(2,1)S(1)} custom-call(s32[1]{0:T(128)} %bitcast.own_ref, s32[128]{0:T(128)S(1)} %select_reduce_fusion.slots_ref, s32[16]{0:T(128)S(1)} %convert_reduce_fusion.1.counts_ref, bf16[4,64,128]{2,1,0:T(8,128)(2,1)S(1)} %bitcast.43, bf16[12,64,128]{2,1,0:T(8,128)(2,1)S(1)} %bitcast.41, ...), custom_call_target="tpu_custom_call" | custom-call | flops 268435456 | bytes 3670016 | tf_op jit(solution)/shard_map/fresh/pallas_call | solution.py:323
  50.0 1.1 %collective-permute-start.10 = (bf16[66,4,128]{2,1,0:T(4,128)(2,1)S(1)}, bf16[66,4,128]{2,1,0:T(4,128)(2,1)S(1)}, u32[]{:S(2)}, u32[]{:S(2)}) collective-permute-start(bf16[66,4,128]{2,1,0:T(4,128)(2,1)S(1)} %get-tuple-element.20), channel_id=1, source_target_pairs={{0,4},{2,6},{4,0},{6,2},{1,5},{3,7},{5,1},{7,3},{8,12},{10,14},{12... | collective-permute-start | bytes 202760 | tf_op jit(solution)/shard_map/ppermute | solution.py:24
  51.1 1.4 %collective-permute-start.11 = (bf16[66,4,128]{2,1,0:T(4,128)(2,1)S(1)}, bf16[66,4,128]{2,1,0:T(4,128)(2,1)S(1)}, u32[]{:S(2)}, u32[]{:S(2)}) collective-permute-start(bf16[66,4,128]{2,1,0:T(4,128)(2,1)S(1)} %get-tuple-element.19), channel_id=1, source_target_pairs={{0,6},{2,0},{4,2},{6,4},{1,7},{3,1},{5,3},{7,5},{8,14},{10,8},{12,... | collective-permute-start | bytes 202760 | tf_op jit(solution)/shard_map/ppermute | solution.py:24
  52.6 2.4 %collective-permute-done.10.refs_2_ = bf16[66,4,128]{2,1,0:T(4,128)(2,1)S(1)} collective-permute-done((bf16[66,4,128]{2,1,0:T(4,128)(2,1)S(1)}, bf16[66,4,128]{2,1,0:T(4,128)(2,1)S(1)}, u32[]{:S(2)}, u32[]{:S(2)}) %collective-permute-start.10) | collective-permute-done | bytes 67616 | tf_op jit(solution)/shard_map/ppermute | solution.py:24
  55.0 1.5 %collective-permute-done.9.refs_1_ = bf16[66,4,128]{2,1,0:T(4,128)(2,1)S(1)} collective-permute-done((bf16[66,4,128]{2,1,0:T(4,128)(2,1)S(1)}, bf16[66,4,128]{2,1,0:T(4,128)(2,1)S(1)}, u32[]{:S(2)}, u32[]{:S(2)}) %collective-permute-start.9) | collective-permute-done | bytes 67616 | tf_op jit(solution)/shard_map/ppermute | solution.py:24
  56.5 0.6 ctx_merge.1
  57.2 2.5 %collective-permute-start.12 = (bf16[17,4,128]{2,1,0:T(4,128)(2,1)S(1)}, bf16[17,4,128]{2,1,0:T(4,128)(2,1)S(1)}, u32[]{:S(2)}, u32[]{:S(2)}) collective-permute-start(bf16[17,4,128]{2,1,0:T(4,128)(2,1)S(1)} %get-tuple-element.25), channel_id=1, source_target_pairs={{0,8},{8,16},{16,24},{24,0},{1,9},{9,17},{17,25},{25,1},{2,10},{10... | collective-permute-start | bytes 52232 | tf_op jit(solution)/shard_map/ppermute | solution.py:24
  59.7 0.9 %collective-permute-start.13 = (bf16[17,4,128]{2,1,0:T(4,128)(2,1)S(1)}, bf16[17,4,128]{2,1,0:T(4,128)(2,1)S(1)}, u32[]{:S(2)}, u32[]{:S(2)}) collective-permute-start(bf16[17,4,128]{2,1,0:T(4,128)(2,1)S(1)} %get-tuple-element.24), channel_id=1, source_target_pairs={{0,16},{8,24},{16,0},{24,8},{1,17},{9,25},{17,1},{25,9},{2,18},{10... | collective-permute-start | bytes 52232 | tf_op jit(solution)/shard_map/ppermute | solution.py:24
  60.7 1.5 %collective-permute-start.14 = (bf16[17,4,128]{2,1,0:T(4,128)(2,1)S(1)}, bf16[17,4,128]{2,1,0:T(4,128)(2,1)S(1)}, u32[]{:S(2)}, u32[]{:S(2)}) collective-permute-start(bf16[17,4,128]{2,1,0:T(4,128)(2,1)S(1)} %get-tuple-element.23), channel_id=1, source_target_pairs={{0,24},{8,0},{16,8},{24,16},{1,25},{9,1},{17,9},{25,17},{2,26},{10... | collective-permute-start | bytes 52232 | tf_op jit(solution)/shard_map/ppermute | solution.py:24
  62.2 0.8 %collective-permute-done.12.refs_1_ = bf16[17,4,128]{2,1,0:T(4,128)(2,1)S(1)} collective-permute-done((bf16[17,4,128]{2,1,0:T(4,128)(2,1)S(1)}, bf16[17,4,128]{2,1,0:T(4,128)(2,1)S(1)}, u32[]{:S(2)}, u32[]{:S(2)}) %collective-permute-start.12) | collective-permute-done | bytes 17440 | tf_op jit(solution)/shard_map/ppermute | solution.py:24
  63.0 1.4 %collective-permute-done.13.refs_2_ = bf16[17,4,128]{2,1,0:T(4,128)(2,1)S(1)} collective-permute-done((bf16[17,4,128]{2,1,0:T(4,128)(2,1)S(1)}, bf16[17,4,128]{2,1,0:T(4,128)(2,1)S(1)}, u32[]{:S(2)}, u32[]{:S(2)}) %collective-permute-start.13) | collective-permute-done | bytes 17440 | tf_op jit(solution)/shard_map/ppermute | solution.py:24
  64.6 0.9 %req_merge.1 = bf16[4,4,4,128]{3,2,1,0:T(4,128)(2,1)} custom-call(bf16[17,4,128]{2,1,0:T(4,128)(2,1)S(1)} %get-tuple-element.26.refs_0_, bf16[17,4,128]{2,1,0:T(4,128)(2,1)S(1)} %collective-permute-done.12.refs_1_, bf16[17,4,128]{2,1,0:T(4,128)(2,1)S(1)} %collective-permute-done.13.refs_2_, bf16[17,4,128]{2,1,0:T(4,128)(2,1)S(1)} %collective-permute-done.14.refs_3_), custom_call_target="tpu_custom_call" | custom-call | tf_op jit(solution)/shard_map/req_merge/pallas_call | solution.py:348
  (34 shorter events, 2.3 us)
Async XLA Ops:
  0.0 25.0 %collective-permute-start.3 = (bf16[4,4,4,128]{3,2,1,0:T(4,128)(2,1)}, bf16[4,4,4,128]{3,2,1,0:T(4,128)(2,1)S(1)}, u32[]{:S(2)}, u32[]{:S(2)}) collective-permute-start(bf16[4,4,4,128]{3,2,1,0:T(4,128)(2,1)} %param.6), channel_id=1, source_target_pairs={{0,24},{8,0},{16,8},{24,16},{1,25},{9,1},{17,9},{25,17},{2,26},{10... | collective-permute-start | bytes 49160 | tf_op jit(solution)/shard_map/ppermute | solution.py:24
  5.0 20.2 %collective-permute-start.4 = (bf16[4,4,4,128]{3,2,1,0:T(4,128)(2,1)}, bf16[4,4,4,128]{3,2,1,0:T(4,128)(2,1)S(1)}, u32[]{:S(2)}, u32[]{:S(2)}) collective-permute-start(bf16[4,4,4,128]{3,2,1,0:T(4,128)(2,1)} %param.6), channel_id=1, source_target_pairs={{0,16},{8,24},{16,0},{24,8},{1,17},{9,25},{17,1},{25,9},{2,18},{10... | collective-permute-start | bytes 49160 | tf_op jit(solution)/shard_map/ppermute | solution.py:24
  5.1 20.2 %collective-permute-start.5 = (bf16[4,4,4,128]{3,2,1,0:T(4,128)(2,1)}, bf16[4,4,4,128]{3,2,1,0:T(4,128)(2,1)S(1)}, u32[]{:S(2)}, u32[]{:S(2)}) collective-permute-start(bf16[4,4,4,128]{3,2,1,0:T(4,128)(2,1)} %param.6), channel_id=1, source_target_pairs={{0,8},{8,16},{16,24},{24,0},{1,9},{9,17},{17,25},{25,1},{2,10},{10... | collective-permute-start | bytes 49160 | tf_op jit(solution)/shard_map/ppermute | solution.py:24
  6.1 21.5 %collective-permute-start = (bf16[4,4,4,128]{3,2,1,0:T(4,128)(2,1)}, bf16[4,4,4,128]{3,2,1,0:T(4,128)(2,1)S(1)}, u32[]{:S(2)}, u32[]{:S(2)}) collective-permute-start(bf16[4,4,4,128]{3,2,1,0:T(4,128)(2,1)} %param.6), channel_id=1, source_target_pairs={{0,6},{2,0},{4,2},{6,4},{1,7},{3,1},{5,3},{7,5},{8,14},{10,8},{12,... | collective-permute-start | bytes 49160 | tf_op jit(solution)/shard_map/ppermute | solution.py:24
  6.2 21.7 %collective-permute-start.1 = (bf16[4,4,4,128]{3,2,1,0:T(4,128)(2,1)}, bf16[4,4,4,128]{3,2,1,0:T(4,128)(2,1)S(1)}, u32[]{:S(2)}, u32[]{:S(2)}) collective-permute-start(bf16[4,4,4,128]{3,2,1,0:T(4,128)(2,1)} %param.6), channel_id=1, source_target_pairs={{0,4},{2,6},{4,0},{6,2},{1,5},{3,7},{5,1},{7,3},{8,12},{10,14},{12... | collective-permute-start | bytes 49160 | tf_op jit(solution)/shard_map/ppermute | solution.py:24
  9.9 5.8 %copy-start = (bf16[512,16,4,256]{3,2,1,0:T(4,128)(2,1)S(1)}, bf16[512,16,4,256]{3,2,1,0:T(4,128)(2,1)}, u32[]{:S(2)}) copy-start(bf16[512,16,4,256]{3,2,1,0:T(4,128)(2,1)} %pool_ref.1) | copy-start | bytes 50331652
  15.7 2.0 %copy-start.1 = (bf16[112,16,4,256]{3,2,1,0:T(4,128)(2,1)S(1)}, bf16[112,16,4,256]{3,2,1,0:T(4,128)(2,1)}, u32[]{:S(2)}) copy-start(bf16[112,16,4,256]{3,2,1,0:T(4,128)(2,1)} %fresh_ref.1) | copy-start | bytes 11010052
  17.8 7.2 %copy-start.3 = (bf16[4,4,4,128]{3,2,1,0:T(4,128)(2,1)S(1)}, bf16[4,4,4,128]{3,2,1,0:T(4,128)(2,1)}, u32[]{:S(2)}) copy-start(bf16[4,4,4,128]{3,2,1,0:T(4,128)(2,1)} %param.6) | copy-start | bytes 49156
  17.8 10.5 %copy-start.2 = (s32[4,128]{1,0:T(4,128)S(1)}, s32[4,128]{1,0:T(4,128)}, u32[]{:S(2)}) copy-start(s32[4,128]{1,0:T(4,128)} %param.8) | copy-start | bytes 6148
  25.0 3.2 %collective-permute-start.2 = (bf16[4,4,4,128]{3,2,1,0:T(4,128)(2,1)S(1)}, bf16[4,4,4,128]{3,2,1,0:T(4,128)(2,1)S(1)}, u32[]{:S(2)}, u32[]{:S(2)}) collective-permute-start(bf16[4,4,4,128]{3,2,1,0:T(4,128)(2,1)S(1)} %copy-done.3), channel_id=1, source_target_pairs={{0,2},{2,4},{4,6},{6,0},{1,3},{3,5},{5,7},{7,1},{8,10},{10,12},{12... | collective-permute-start | bytes 49160 | tf_op jit(solution)/shard_map/ppermute | solution.py:24
  25.3 11.5 %collective-permute-start.6 = (bf16[3,4,4,4,128]{4,3,2,1,0:T(4,128)(2,1)S(1)}, bf16[3,4,4,4,128]{4,3,2,1,0:T(4,128)(2,1)S(1)}, u32[]{:S(2)}, u32[]{:S(2)}) collective-permute-start(bf16[3,4,4,4,128]{4,3,2,1,0:T(4,128)(2,1)S(1)} %pad_maximum_fusion), channel_id=1, source_target_pairs={{0,6},{2,0},{4,2},{6,4},{1,7},{3,1},{5,3},{7,5},{8,14},{10,8},{12,... | collective-permute-start | bytes 147464 | tf_op jit(solution)/shard_map/ppermute | solution.py:24
  26.9 10.0 %collective-permute-start.7 = (bf16[3,4,4,4,128]{4,3,2,1,0:T(4,128)(2,1)S(1)}, bf16[3,4,4,4,128]{4,3,2,1,0:T(4,128)(2,1)S(1)}, u32[]{:S(2)}, u32[]{:S(2)}) collective-permute-start(bf16[3,4,4,4,128]{4,3,2,1,0:T(4,128)(2,1)S(1)} %pad_maximum_fusion), channel_id=1, source_target_pairs={{0,4},{2,6},{4,0},{6,2},{1,5},{3,7},{5,1},{7,3},{8,12},{10,14},{12... | collective-permute-start | bytes 147464 | tf_op jit(solution)/shard_map/ppermute | solution.py:24
  27.6 9.3 %collective-permute-start.8 = (bf16[3,4,4,4,128]{4,3,2,1,0:T(4,128)(2,1)S(1)}, bf16[3,4,4,4,128]{4,3,2,1,0:T(4,128)(2,1)S(1)}, u32[]{:S(2)}, u32[]{:S(2)}) collective-permute-start(bf16[3,4,4,4,128]{4,3,2,1,0:T(4,128)(2,1)S(1)} %pad_maximum_fusion), channel_id=1, source_target_pairs={{0,2},{2,4},{4,6},{6,0},{1,3},{3,5},{5,7},{7,1},{8,10},{10,12},{12... | collective-permute-start | bytes 147464 | tf_op jit(solution)/shard_map/ppermute | solution.py:24
  50.0 4.9 %collective-permute-start.10 = (bf16[66,4,128]{2,1,0:T(4,128)(2,1)S(1)}, bf16[66,4,128]{2,1,0:T(4,128)(2,1)S(1)}, u32[]{:S(2)}, u32[]{:S(2)}) collective-permute-start(bf16[66,4,128]{2,1,0:T(4,128)(2,1)S(1)} %get-tuple-element.20), channel_id=1, source_target_pairs={{0,4},{2,6},{4,0},{6,2},{1,5},{3,7},{5,1},{7,3},{8,12},{10,14},{12... | collective-permute-start | bytes 202760 | tf_op jit(solution)/shard_map/ppermute | solution.py:24
  51.1 3.9 %collective-permute-start.11 = (bf16[66,4,128]{2,1,0:T(4,128)(2,1)S(1)}, bf16[66,4,128]{2,1,0:T(4,128)(2,1)S(1)}, u32[]{:S(2)}, u32[]{:S(2)}) collective-permute-start(bf16[66,4,128]{2,1,0:T(4,128)(2,1)S(1)} %get-tuple-element.19), channel_id=1, source_target_pairs={{0,6},{2,0},{4,2},{6,4},{1,7},{3,1},{5,3},{7,5},{8,14},{10,8},{12,... | collective-permute-start | bytes 202760 | tf_op jit(solution)/shard_map/ppermute | solution.py:24
  52.6 4.0 %collective-permute-start.9 = (bf16[66,4,128]{2,1,0:T(4,128)(2,1)S(1)}, bf16[66,4,128]{2,1,0:T(4,128)(2,1)S(1)}, u32[]{:S(2)}, u32[]{:S(2)}) collective-permute-start(bf16[66,4,128]{2,1,0:T(4,128)(2,1)S(1)} %get-tuple-element.21), channel_id=1, source_target_pairs={{0,2},{2,4},{4,6},{6,0},{1,3},{3,5},{5,7},{7,1},{8,10},{10,12},{12... | collective-permute-start | bytes 202760 | tf_op jit(solution)/shard_map/ppermute | solution.py:24
  57.2 5.7 %collective-permute-start.12 = (bf16[17,4,128]{2,1,0:T(4,128)(2,1)S(1)}, bf16[17,4,128]{2,1,0:T(4,128)(2,1)S(1)}, u32[]{:S(2)}, u32[]{:S(2)}) collective-permute-start(bf16[17,4,128]{2,1,0:T(4,128)(2,1)S(1)} %get-tuple-element.25), channel_id=1, source_target_pairs={{0,8},{8,16},{16,24},{24,0},{1,9},{9,17},{17,25},{25,1},{2,10},{10... | collective-permute-start | bytes 52232 | tf_op jit(solution)/shard_map/ppermute | solution.py:24
  59.7 4.7 %collective-permute-start.13 = (bf16[17,4,128]{2,1,0:T(4,128)(2,1)S(1)}, bf16[17,4,128]{2,1,0:T(4,128)(2,1)S(1)}, u32[]{:S(2)}, u32[]{:S(2)}) collective-permute-start(bf16[17,4,128]{2,1,0:T(4,128)(2,1)S(1)} %get-tuple-element.24), channel_id=1, source_target_pairs={{0,16},{8,24},{16,0},{24,8},{1,17},{9,25},{17,1},{25,9},{2,18},{10... | collective-permute-start | bytes 52232 | tf_op jit(solution)/shard_map/ppermute | solution.py:24
  60.7 3.9 %collective-permute-start.14 = (bf16[17,4,128]{2,1,0:T(4,128)(2,1)S(1)}, bf16[17,4,128]{2,1,0:T(4,128)(2,1)S(1)}, u32[]{:S(2)}, u32[]{:S(2)}) collective-permute-start(bf16[17,4,128]{2,1,0:T(4,128)(2,1)S(1)} %get-tuple-element.23), channel_id=1, source_target_pairs={{0,24},{8,0},{16,8},{24,16},{1,25},{9,1},{17,9},{25,17},{2,26},{10... | collective-permute-start | bytes 52232 | tf_op jit(solution)/shard_map/ppermute | solution.py:24

commit v3 on v2

v3 whole, which is shorter than its diff:
```python
import functools
import math

import jax
import jax.numpy as jnp
from jax import lax
from jax.experimental import pallas as pl
from jax.experimental.pallas import tpu as pltpu
from jax.sharding import PartitionSpec as P

NEG = -1e30
CAP = 2
LANES = 128
SCALE = math.log2(math.e) / math.sqrt(LANES)
WIDE = 1024
VMEM = pl.BlockSpec(memory_space=pltpu.VMEM)
SMEM = pl.BlockSpec(memory_space=pltpu.SMEM)
HBM = pl.BlockSpec(memory_space=pltpu.HBM)


def stage_kernel(
    pieces, n_ctx, slots, bucket_ref, pool_ref, fresh_ref, kb, vb, kf, vf, slots_ref, counts_ref,
    sem,
):
    each = pool_ref.shape[0] // pieces
    copies = []
    for half, (pool_to, fresh_to) in enumerate(((kb, kf), (vb, vf))):
        lanes = pl.ds(half * LANES, LANES)
        copies.append(pltpu.make_async_copy(
            fresh_ref.at[:, :, :, lanes], fresh_to, sem.at[len(copies)]))
        for n in range(pieces):
            some = pl.ds(n * each, each)
            copies.append(pltpu.make_async_copy(
                pool_ref.at[some, :, :, lanes], pool_to.at[some], sem.at[len(copies)]))
    for one in copies:
        one.start()
    list_fresh(n_ctx, slots, bucket_ref, slots_ref, counts_ref)
    for one in copies:
        one.wait()


def list_kernel(n_ctx, slots, bucket_ref, slots_ref, counts_ref):
    list_fresh(n_ctx, slots, bucket_ref, slots_ref, counts_ref)


def list_fresh(n_ctx, slots, bucket_ref, slots_ref, counts_ref):
    for n in range(counts_ref.shape[0]):
        counts_ref[n] = 0
    for n in range(slots_ref.shape[0]):
        slots_ref[n] = 0

    def put(page, _):
        request = bucket_ref[page] // n_ctx
        count = counts_ref[request]
        slots_ref[request * slots + count] = page
        counts_ref[request] = count + 1
        return 0

    lax.fori_loop(0, bucket_ref.shape[0], put, 0)


def class_reduce(x, op, heads):
    step = heads
    while step < LANES:
        x = op(x, pltpu.roll(x, step, 1))
        step *= 2
    return x


def pages_of(ref, table_ref, first, count):
    return jnp.concatenate([ref[table_ref[first + n]] for n in range(count)], axis=0)


def score_parts(q, keys, lane, limit, first, heads, sub):
    s = lax.dot_general(q, keys, (((1,), (1,)), ((), ())), preferred_element_type=jnp.float32)
    out = []
    for j in range(s.shape[1] // LANES):
        part = s[:, j * LANES:(j + 1) * LANES]
        one = part[:sub]
        for h in range(1, heads):
            one = jnp.where(lane % heads == h, part[h * sub:(h + 1) * sub], one)
        out.append(jnp.where(lane < limit - (first + j * LANES), one * SCALE, NEG))
    return out


def spread(p, onehots):
    p = p.astype(jnp.bfloat16)
    return jnp.concatenate([p * one for one in onehots], axis=0)


def rows_of(x, h):
    return jnp.broadcast_to(x[:, h:h + 1], x.shape)


def fold_max(parts):
    top = parts[0]
    for part in parts[1:]:
        top = jnp.maximum(top, part)
    return top


def resident_kernel(
    dims, table_ref, left_ref, q_ref, kb, vb, acc_ref, top_ref, tot_ref, t_s,
):
    heads, page_rows, pages_dev, sub = dims
    columns = pages_dev * page_rows
    wide = min(WIDE, columns)
    per = wide // page_rows
    chunks = columns // wide
    count = q_ref.shape[0]
    lane = lax.broadcasted_iota(jnp.int32, (sub, LANES), 1)
    onehots = [(lane % heads == h).astype(jnp.bfloat16) for h in range(heads)]

    def score_chunk(i, c, top):
        keys = pages_of(kb, table_ref, i * pages_dev + c * per, per)
        parts = score_parts(q_ref[i], keys, lane, left_ref[i] * heads, c * wide, heads, sub)
        for j, part in enumerate(parts):
            t_s[:, c * wide + j * LANES:c * wide + (j + 1) * LANES] = part
        return jnp.maximum(top, fold_max(parts))

    def value_chunk(i, c, top, tot, acc):
        weights = []
        for j in range(wide // LANES):
            at = c * wide + j * LANES
            p = jnp.exp2(t_s[:, at:at + LANES] - top)
            tot = tot + p
            weights.append(spread(p, onehots))
        values = pages_of(vb, table_ref, i * pages_dev + c * per, per)
        return tot, acc + jnp.dot(
            jnp.concatenate(weights, axis=1), values, preferred_element_type=jnp.float32)

    def finish(i, top, tot, acc):
        acc_ref[i] = acc
        top_ref[i] = top
        tot_ref[i] = class_reduce(tot, jnp.add, heads)

    low = jnp.full((sub, LANES), NEG, jnp.float32)
    none = jnp.zeros((sub, LANES), jnp.float32)
    empty = jnp.zeros((heads * sub, LANES), jnp.float32)

    def step(i, top):
        top = class_reduce(top, jnp.maximum, heads)
        later, tot, acc = low, none, empty
        for c in range(chunks):
            tot, acc = value_chunk(i, c, top, tot, acc)
            later = score_chunk(i + 1, c, later)
        finish(i, top, tot, acc)
        return later

    top = low
    for c in range(chunks):
        top = score_chunk(0, c, top)
    top = lax.fori_loop(0, count - 1, step, top)
    top = class_reduce(top, jnp.maximum, heads)
    tot, acc = none, empty
    for c in range(chunks):
        tot, acc = value_chunk(count - 1, c, top, tot, acc)
    finish(count - 1, top, tot, acc)


def fresh_kernel(
    dims, own_ref, slots_ref, counts_ref, q_ref, kf, vf, acc_ref, top_ref, tot_ref,
    out_ref, t_s, p_s,
):
    heads, page_rows, slots, sub, n_req, req_dev = dims
    lane = lax.broadcasted_iota(jnp.int32, (sub, LANES), 1)
    onehots = [(lane % heads == h).astype(jnp.bfloat16) for h in range(heads)]
    n_reqs = n_req * req_dev
    unit = 4 * heads
    fill = LANES // unit
    kind = (lane % unit) // heads
    columns = slots * page_rows
    requests = [
        lax.rem(own_ref[0] + k, n_req) * req_dev + i for k in range(n_req) for i in range(req_dev)
    ]
    tops = []
    for n, request in enumerate(requests):
        keys = pages_of(kf, slots_ref, request * slots, slots)
        parts = score_parts(
            q_ref[request], keys, lane, counts_ref[request] * page_rows, 0, heads, sub)
        for j, part in enumerate(parts):
            t_s[n, :, j * LANES:(j + 1) * LANES] = part
        tops.append(fold_max(parts))
    tops = class_reduce(jnp.concatenate(tops, axis=0), jnp.maximum, heads)
    tops = [tops[n * sub:(n + 1) * sub] for n in range(n_reqs)]
    for i in range(req_dev):
        tops[i] = jnp.maximum(tops[i], top_ref[i])
    tots = []
    for n in range(n_reqs):
        tot = jnp.zeros((sub, LANES), jnp.float32)
        for j in range(columns // LANES):
            p = jnp.exp2(t_s[n, :, j * LANES:(j + 1) * LANES] - tops[n])
            tot = tot + p
            p_s[n, :, j * LANES:(j + 1) * LANES] = spread(p, onehots)
        tots.append(tot)
    tots = class_reduce(jnp.concatenate(tots, axis=0), jnp.add, heads)
    tots = [tots[n * sub:(n + 1) * sub] for n in range(n_reqs)]
    fades = [jnp.exp2(top_ref[i] - tops[i]) for i in range(req_dev)]
    for i in range(req_dev):
        tots[i] = tots[i] + fades[i] * tot_ref[i]
    slabs = [jnp.zeros((sub, LANES), jnp.float32) for _ in range(-(-n_reqs // fill))]
    for n, request in enumerate(requests):
        values = pages_of(vf, slots_ref, request * slots, slots)
        acc = jnp.dot(p_s[n], values, preferred_element_type=jnp.float32)
        whole = 1.0 / tots[n]
        for h in range(heads):
            some = acc[h * sub:(h + 1) * sub]
            if n < req_dev:
                some = some + acc_ref[n, h * sub:(h + 1) * sub, :] * rows_of(fades[n], h)
            out_ref[request * heads + h] = (some * rows_of(whole, h)).astype(jnp.bfloat16)
        lse = tops[n] + jnp.log2(tots[n])
        for m in range(len(slabs)):
            slabs[m] = jnp.where(lane // unit == request - m * fill, lse, slabs[m])
    for n, lse in enumerate(slabs):
        out_ref[n_reqs * heads + n] = pieces_of(lse, kind)


def pieces_of(lse, kind):
    high = lse.astype(jnp.bfloat16)
    rest = lse - high.astype(jnp.float32)
    mid = rest.astype(jnp.bfloat16)
    low = (rest - mid.astype(jnp.float32)).astype(jnp.bfloat16)
    both = jnp.where(kind == 1, mid.astype(jnp.float32), low.astype(jnp.float32))
    return jnp.where(kind == 0, high.astype(jnp.float32), both).astype(jnp.bfloat16)


def whole_of(pieces, heads):
    x = pieces.astype(jnp.float32)
    return x + pltpu.roll(x, LANES - heads, 1) + pltpu.roll(x, LANES - 2 * heads, 1)


def merge_lse(refs, slab, heads):
    lses = [whole_of(ref[slab], heads) for ref in refs]
    top = fold_max(lses)
    shares = [jnp.exp2(lse - top) for lse in lses]
    tot = sum(shares)
    return [share / tot for share in shares], top + jnp.log2(tot)


def ctx_merge_kernel(dims, got_ref, out_ref):
    heads, n_req, req_dev = dims
    refs = [got_ref.at[n] for n in range(got_ref.shape[0])]
    n_reqs = n_req * req_dev
    unit = 4 * heads
    fill = LANES // unit
    group = out_ref.shape[2]
    lane = lax.broadcasted_iota(jnp.int32, (group, LANES), 1)
    spread_lse = []
    for slab in range(-(-n_reqs // fill)):
        shares, lse = merge_lse(refs, n_reqs * heads + slab, heads)
        kind = (lane % unit) // heads
        same = lse
        for m in (1, 2):
            same = jnp.where(kind == m, pltpu.roll(lse, m * heads, 1), same)
        spread_lse.append(pieces_of(same, kind))
        for n in range(slab * fill, min(n_reqs, (slab + 1) * fill)):
            for h in range(heads):
                at = (n % fill) * unit + h
                total = 0.0
                for ref, share in zip(refs, shares):
                    total = total + ref[n * heads + h].astype(jnp.float32) * jnp.broadcast_to(
                        share[:, at:at + 1], (group, LANES))
                out_ref[n // req_dev, (n % req_dev) * heads + h] = total.astype(jnp.bfloat16)
    for k in range(n_req):
        slab = spread_lse[k * req_dev // fill].astype(jnp.float32)
        at = (k * req_dev) % fill * unit
        if at:
            slab = pltpu.roll(slab, LANES - at, 1)
        out_ref[k, req_dev * heads] = slab.astype(jnp.bfloat16)


def req_merge_kernel(dims, got_ref, out_ref):
    heads, req_dev = dims
    refs = [got_ref.at[n] for n in range(got_ref.shape[0])]
    group = out_ref.shape[2]
    shares, _ = merge_lse(refs, req_dev * heads, heads)
    for i in range(req_dev):
        for h in range(heads):
            at = i * 4 * heads + h
            total = 0.0
            for ref, share in zip(refs, shares):
                total = total + ref[i * heads + h].astype(jnp.float32) * jnp.broadcast_to(
                    share[:, at:at + 1], (group, LANES))
            out_ref[i, h] = total.astype(jnp.bfloat16)


def params(mib):
    return pltpu.CompilerParams(vmem_limit_bytes=mib * 2**20)


def local(query, kv_pool, page_table, context_len, fresh_kv, fresh_bucket):
    n_ctx = lax.axis_size("ctx")
    n_req = lax.axis_size("req")
    ctx_place = lax.axis_index("ctx")
    req_place = lax.axis_index("req")
    req_dev, heads, group, head_dim = query.shape
    pool_slots, page = kv_pool.shape[:2]
    new_dev = fresh_kv.shape[0]
    pages_dev = page_table.shape[1]
    n_reqs = n_req * req_dev
    slots = CAP * n_ctx
    sub = n_ctx * group
    rows = heads * sub
    page_rows = page * heads

    smem = lambda count: jax.ShapeDtypeStruct((count,), jnp.int32)
    near = lax.all_to_all(
        jnp.broadcast_to(query, (n_ctx,) + query.shape), "ctx", split_axis=0, concat_axis=0,
        tiled=True)
    if heads % 4 == 0:
        pieces = 8
        half = lambda count: jax.ShapeDtypeStruct((count, page, heads, LANES), jnp.bfloat16)
        kb, vb, kf, vf, slot_table, counts = pl.pallas_call(
            functools.partial(stage_kernel, pieces, n_ctx, slots),
            out_shape=(
                half(pool_slots), half(pool_slots), half(new_dev), half(new_dev),
                smem(n_reqs * slots), smem(n_reqs)),
            in_specs=[SMEM, HBM, HBM],
            out_specs=(VMEM,) * 4 + (SMEM,) * 2,
            scratch_shapes=[pltpu.SemaphoreType.DMA((2 * pieces + 2,))],
            compiler_params=params(2),
            cost_estimate=pl.CostEstimate(
                flops=0, transcendentals=0, bytes_accessed=2 * (kv_pool.size + fresh_kv.size)),
            name="stage",
        )(
            fresh_bucket, pltpu.with_memory_space_constraint(kv_pool, pltpu.HBM),
            pltpu.with_memory_space_constraint(fresh_kv, pltpu.HBM))
        kb, vb, kf, vf = (a.reshape(a.shape[0], page_rows, LANES) for a in (kb, vb, kf, vf))
    else:
        kb, vb, kf, vf = (
            a[..., h * LANES:(h + 1) * LANES].reshape(a.shape[0], page_rows, LANES)
            for a in (kv_pool, fresh_kv) for h in (0, 1)
        )
        slot_table, counts = pl.pallas_call(
            functools.partial(list_kernel, n_ctx, slots),
            out_shape=(smem(n_reqs * slots), smem(n_reqs)),
            in_specs=[SMEM],
            out_specs=(SMEM,) * 2,
            name="list",
        )(fresh_bucket)

    far = lax.all_to_all(
        jnp.broadcast_to(near, (n_req,) + near.shape), "req", split_axis=0, concat_axis=0,
        tiled=True)
    q_own = near.transpose(1, 2, 0, 3, 4).reshape(req_dev, rows, head_dim)
    q_all = far.transpose(0, 2, 3, 1, 4, 5).reshape(n_reqs, rows, head_dim)
    left = context_len - ctx_place * (pages_dev * page)

    f32 = lambda *shape: jax.ShapeDtypeStruct(shape, jnp.float32)
    bf16 = lambda *shape: jax.ShapeDtypeStruct(shape, jnp.bfloat16)
    columns = pages_dev * page_rows
    acc, top, tot = pl.pallas_call(
        functools.partial(resident_kernel, (heads, page_rows, pages_dev, sub)),
        out_shape=(
            f32(req_dev, rows, LANES), f32(req_dev, sub, LANES), f32(req_dev, sub, LANES)),
        in_specs=[SMEM] * 2 + [VMEM] * 3,
        out_specs=(VMEM,) * 3,
        scratch_shapes=[pltpu.VMEM((sub, columns), jnp.float32)],
        compiler_params=params(8),
        cost_estimate=pl.CostEstimate(
            flops=4 * req_dev * rows * columns * LANES, transcendentals=req_dev * sub * columns,
            bytes_accessed=2 * kv_pool.size),
        name="resident",
    )(page_table.reshape(-1), left, q_own, kb, vb)

    fill = LANES // (4 * heads)
    slabs = n_reqs * heads + -(-n_reqs // fill)
    parts = pl.pallas_call(
        functools.partial(fresh_kernel, (heads, page_rows, slots, sub, n_req, req_dev)),
        out_shape=bf16(slabs, sub, LANES),
        in_specs=[SMEM] * 3 + [VMEM] * 6,
        out_specs=VMEM,
        scratch_shapes=[
            pltpu.VMEM((n_reqs, sub, slots * page_rows), jnp.float32),
            pltpu.VMEM((n_reqs, rows, slots * page_rows), jnp.bfloat16),
        ],
        compiler_params=params(8),
        cost_estimate=pl.CostEstimate(
            flops=4 * n_reqs * rows * slots * page_rows * LANES,
            transcendentals=n_reqs * sub * slots * page_rows, bytes_accessed=2 * fresh_kv.size),
        name="fresh",
    )(
        req_place.astype(jnp.int32).reshape(1), slot_table, counts, q_all, kf, vf, acc, top, tot,
    )
    sends = parts.reshape(slabs, n_ctx, group, LANES).transpose(1, 0, 2, 3)
    got = lax.all_to_all(sends, "ctx", split_axis=0, concat_axis=0, tiled=True)
    merged = pl.pallas_call(
        functools.partial(ctx_merge_kernel, (heads, n_req, req_dev)),
        out_shape=bf16(n_req, req_dev * heads + 1, group, LANES),
        in_specs=[VMEM],
        out_specs=VMEM,
        compiler_params=params(8),
        name="ctx_merge",
    )(got)
    got = lax.all_to_all(merged, "req", split_axis=0, concat_axis=0, tiled=True)
    return pl.pallas_call(
        functools.partial(req_merge_kernel, (heads, req_dev)),
        out_shape=bf16(req_dev, heads, group, LANES),
        in_specs=[VMEM],
        out_specs=VMEM,
        compiler_params=params(8),
        name="req_merge",
    )(got)


def solution(mesh):
    placed = (
        P("req", "kvh", "ctx", None),
        P(("req", "ctx"), None, "kvh", None),
        P("req", "ctx"),
        P("req"),
        P(("req", "ctx"), None, "kvh", None),
        P(("req", "ctx")),
    )
    return jax.shard_map(
        local, mesh=mesh, in_specs=placed, out_specs=P("req", "kvh", "ctx", None), check_vma=False
    )
```

time: 65.7 us -> 56.7 us (0.86)
  blocking collectives: 0 us -> 27.3 us
  starting transfers between devices: 17.8 us -> 4.87 us
  Pallas kernels: 29.9 us -> 19 us
  waiting for transfers between devices: 6.79 us -> 0.01 us
  local copies, waits for them, and re-layouts: 8.14 us -> 5.09 us
  other arithmetic: 2.69 us -> 0.01 us
    all_to_all x0 -> x3, blocking collectives: none -> 27.3 us  [the longest x1 10.6 us: local(): got = lax.all_to_all(merged, 'req', split_axis=0, concat_axis=0, tiled=True)]
    ppermute x15 -> x0, starting transfers between devices: 17.8 us -> none  [shift(): return lax.ppermute(value, axis, pairs)]
    pallas_call x1, Pallas kernels: 12.7 us -> 2.59 us  [local(): pl.pallas_call(functools.partial(fresh_kernel, (heads, page_rows, slots,...]
    ppermute x15 -> x0, waiting for transfers between devices: 6.79 us -> none  [shift(): return lax.ppermute(value, axis, pairs)]
    all_to_all x0 -> x1, starting transfers between devices: none -> 4.87 us  [local(): lax.all_to_all(jnp.broadcast_to(near, (n_req,) + near.shape), 'req', spli...]
    unnamed x8 -> x10, local copies, waits for them, and re-layouts: 7.81 us -> 3.39 us
    pallas_call x1, Pallas kernels: 8.53 us -> 6.81 us  [local(): pl.pallas_call(functools.partial(resident_kernel, (heads, page_rows, page...]
    broadcast_in_dim x0 -> x2, local copies, waits for them, and re-layouts: none -> 1.55 us  [the longest x1 0.82 us: local(): jnp.broadcast_to(near, (n_req,) + near.shape)]
  transfers between devices with their start and end apart: 15 -> 1, of which waited for: 7 -> 0; matrix products, arithmetic and copies ran while one was open for 4% -> 0% of each run, Pallas kernels for 24% -> 27%
where the time goes in v3:
time: 56.7 us; the launch traced here: 56.3 us
  blocking collectives  27.3 us (48%)
  Pallas kernels  19 us (34%)
  local copies, waits for them, and re-layouts  5.09 us (9%)
  starting transfers between devices  4.87 us (9%)
    all_to_all x1, blocking collectives, local(): got = lax.all_to_all(merged, 'req', split_axis=0, concat_axis=0, tiled=True)  10.6 us
    all_to_all x1, blocking collectives, local(): got = lax.all_to_all(sends, 'ctx', split_axis=0, concat_axis=0, tiled=True)  8.51 us
    all_to_all x1, blocking collectives, local(): lax.all_to_all(jnp.broadcast_to(query, (n_ctx,) + query.shape), 'ctx', sp...  8.13 us
    pallas_call x1, Pallas kernels, local(): pl.pallas_call(functools.partial(stage_kernel, pieces, n_ctx, slots), out...  8.12 us
    pallas_call x1, Pallas kernels, local(): pl.pallas_call(functools.partial(resident_kernel, (heads, page_rows, page...  6.81 us
    all_to_all x1, starting transfers between devices, local(): lax.all_to_all(jnp.broadcast_to(near, (n_req,) + near.shape), 'req', spli...  4.87 us
    unnamed x10, local copies, waits for them, and re-layouts  3.39 us
    pallas_call x1, Pallas kernels, local(): pl.pallas_call(functools.partial(fresh_kernel, (heads, page_rows, slots,...  2.59 us
  transfers between devices with their start and end apart: 1, of which 0 were waited for; matrix products, arithmetic and copies ran while one was open for 0% of the time, Pallas kernels for 27%

profile of v3, /device:TPU:0, one launch (start us, length us, event | category | flops | bytes accessed | tf_op | source)
XLA Modules:
  0.0 56.3 jit_solution(8556671190204489563)
XLA Ops:
  0.0 0.7 %broadcast_in_dim.6 = bf16[4,4,4,4,128]{4,3,2,1,0:T(4,128)(2,1)S(1)} broadcast(bf16[4,4,4,128]{3,2,1,0:T(4,128)(2,1)} %param.6), dimensions={1,2,3,4} | broadcast | bytes 81920 | tf_op jit(solution)/shard_map/broadcast_in_dim | solution.py:308
  0.7 8.1 %all_to_all.20 = bf16[4,4,4,4,128]{4,3,2,1,0:T(4,128)(2,1)S(1)} all-to-all(bf16[4,4,4,4,128]{4,3,2,1,0:T(4,128)(2,1)S(1)} %broadcast_in_dim.6), channel_id=1, replica_groups=mesh['req'=4,'ctx'=4,'kvh'=2] {'ctx'}, dimensions={0} | all-to-all | bytes 131072 | tf_op jit(solution)/shard_map/all_to_all | solution.py:307
  8.9 0.8 %broadcast_in_dim.7 = bf16[4,4,4,4,4,128]{5,4,1,3,2,0:T(4,128)(2,1)} broadcast(bf16[4,4,4,4,128]{4,3,0,2,1:T(4,128)(2,1)S(1)} %copy.8), dimensions={1,2,3,4,5} | broadcast | bytes 327680 | tf_op jit(solution)/shard_map/broadcast_in_dim | solution.py:343
  9.7 4.9 %all-to-all-start.1 = ((bf16[4,4,4,4,4,128]{5,4,1,3,2,0:T(4,128)(2,1)}), bf16[4,4,4,4,4,128]{5,4,1,3,2,0:T(4,128)(2,1)S(1)}, u32[]{:S(2)}, u32[]{:S(2)}) async-start(bf16[4,4,4,4,4,128]{5,4,1,3,2,0:T(4,128)(2,1)} %broadcast_in_dim.7), calls=%async_computation.1 | async-start | bytes 524288 | tf_op jit(solution)/shard_map/all_to_all | solution.py:342
  14.6 0.0 copy-start.3
  14.6 0.7 %copy-done.3 = s32[112]{0:T(128)S(1)} copy-done((s32[112]{0:T(128)S(1)}, s32[112]{0:T(128)}, u32[]{:S(2)}) %copy-start.3) | copy-done | bytes 472
  15.2 0.0 copy-start.4
  15.2 0.0 copy-start.2
  15.2 8.1 %stage.1 = (bf16[512,16,4,128]{3,2,1,0:T(4,128)(2,1)S(1)}, bf16[512,16,4,128]{3,2,1,0:T(4,128)(2,1)S(1)}, bf16[112,16,4,128]{3,2,1,0:T(4,128)(2,1)S(1)}, bf16[11...) custom-call(s32[112]{0:T(128)S(1)} %copy-done.3, bf16[512,16,4,256]{3,2,1,0:T(4,128)(2,1)} %pool_ref.1, ...), custom_call_target="tpu_custom_call" | custom-call | bytes 20447232 | tf_op jit(solution)/shard_map/stage/pallas_call | solution.py:313
  23.4 0.0 copy-start
  23.4 1.2 %copy-done = bf16[112,16,4,128]{3,2,1,0:T(4,128)(2,1)} copy-done((bf16[112,16,4,128]{3,2,1,0:T(4,128)(2,1)}, bf16[112,16,4,128]{3,2,1,0:T(4,128)(2,1)S(1)}, u32[]{:S(2)}) %copy-start) | copy-done | bytes 1835032
  24.6 0.0 copy-done.4
  24.7 0.0 copy-done.2
  24.7 6.8 %resident.1 = (f32[4,64,128]{2,1,0:T(8,128)S(1)}, f32[4,16,128]{2,1,0:T(8,128)S(1)}, f32[4,16,128]{2,1,0:T(8,128)S(1)}) custom-call(s32[512]{0:T(512)S(1)} %bitcast.22, s32[4]{0:T(128)S(1)} %broadcast_subtract_fusion.left_ref, bf16[4,64,128]{2,1,0:T(8,128)(2,1)S(1)} %bitcast.21, bf16[512,64,128]{2,1,0:T(8,128)(2,1)S(1)} %bitcast.15, ...), custom_call_target="tpu_custom_call" | custom-call | flops 1073741824 | bytes 16777216 | tf_op jit(solution)/shard_map/resident/pallas_call | solution.py:352
  31.5 0.0 all-to-all-done.1
  31.5 0.0 copy-start.1
  31.5 1.5 %copy-done.1 = bf16[112,16,4,128]{3,2,1,0:T(4,128)(2,1)S(1)} copy-done((bf16[112,16,4,128]{3,2,1,0:T(4,128)(2,1)S(1)}, bf16[112,16,4,128]{3,2,1,0:T(4,128)(2,1)}, u32[]{:S(2)}) %copy-start.1) | copy-done | bytes 1835032
  33.0 2.6 %fresh.1 = bf16[66,16,128]{2,1,0:T(8,128)(2,1)S(1)} custom-call(s32[1]{0:T(128)} %bitcast.own_ref, s32[128]{0:T(128)S(1)} %get-tuple-element.14.slots_ref, s32[16]{0:T(128)S(1)} %get-tuple-element.15.counts_ref, bf16[16,64,128]{2,1,0:T(8,128)(2,1)S(1)} %bitcast.20, bf16[112,64,128]{2,1,0:T(8,128)(2,1)S(1)} %bitcast.17, bf16[112,64,128]{2,1,0:T(8,128)(2,1)S(1)} %bitcast.18, ...), custom_call_target="tpu_custom_call" | custom-call | flops 268435456 | bytes 3670016 | tf_op jit(solution)/shard_map/fresh/pallas_call | solution.py:368
  35.6 0.1 copy.12
  35.7 8.5 %all_to_all.21.got_ref = bf16[4,66,4,128]{3,2,1,0:T(4,128)(2,1)S(1)} all-to-all(bf16[4,66,4,128]{3,2,1,0:T(4,128)(2,1)S(1)} %bitcast.23), channel_id=1, replica_groups=mesh['req'=4,'ctx'=4,'kvh'=2] {'ctx'}, dimensions={0} | all-to-all | bytes 540672 | tf_op jit(solution)/shard_map/all_to_all | solution.py:386
  44.2 0.6 %ctx_merge.1 = bf16[4,17,4,128]{3,2,1,0:T(4,128)(2,1)S(1)} custom-call(bf16[4,66,4,128]{3,2,1,0:T(4,128)(2,1)S(1)} %all_to_all.21.got_ref), custom_call_target="tpu_custom_call" | custom-call | tf_op jit(solution)/shard_map/ctx_merge/pallas_call | solution.py:387
  44.8 10.6 %all_to_all.22.got_ref = bf16[4,17,4,128]{3,2,1,0:T(4,128)(2,1)S(1)} all-to-all(bf16[4,17,4,128]{3,2,1,0:T(4,128)(2,1)S(1)} %ctx_merge.1), channel_id=1, replica_groups=mesh['req'=4,'ctx'=4,'kvh'=2] {'req'}, dimensions={0} | all-to-all | bytes 139264 | tf_op jit(solution)/shard_map/all_to_all | solution.py:395
  55.5 0.9 %req_merge.1 = bf16[4,4,4,128]{3,2,1,0:T(4,128)(2,1)} custom-call(bf16[4,17,4,128]{3,2,1,0:T(4,128)(2,1)S(1)} %all_to_all.22.got_ref), custom_call_target="tpu_custom_call" | custom-call | tf_op jit(solution)/shard_map/req_merge/pallas_call | solution.py:396
  (3 shorter events, 0.1 us)
Async XLA Ops:
  9.7 21.8 %all-to-all-start.1 = ((bf16[4,4,4,4,4,128]{5,4,1,3,2,0:T(4,128)(2,1)}), bf16[4,4,4,4,4,128]{5,4,1,3,2,0:T(4,128)(2,1)S(1)}, u32[]{:S(2)}, u32[]{:S(2)}) async-start(bf16[4,4,4,4,4,128]{5,4,1,3,2,0:T(4,128)(2,1)} %broadcast_in_dim.7), calls=%async_computation.1 | async-start | bytes 524288 | tf_op jit(solution)/shard_map/all_to_all | solution.py:342
  14.6 0.7 %copy-start.3 = (s32[112]{0:T(128)S(1)}, s32[112]{0:T(128)}, u32[]{:S(2)}) copy-start(s32[112]{0:T(128)} %bucket_ref.1) | copy-start | bytes 1348
  15.2 9.4 %copy-start.4 = (s32[4]{0:T(128)S(1)}, s32[4]{0:T(128)}, u32[]{:S(2)}) copy-start(s32[4]{0:T(128)} %param.9) | copy-start | bytes 52
  15.2 9.4 %copy-start.2 = (s32[4,128]{1,0:T(4,128)S(1)}, s32[4,128]{1,0:T(4,128)}, u32[]{:S(2)}) copy-start(s32[4,128]{1,0:T(4,128)} %param.8) | copy-start | bytes 6148
  23.4 1.2 %copy-start = (bf16[112,16,4,128]{3,2,1,0:T(4,128)(2,1)}, bf16[112,16,4,128]{3,2,1,0:T(4,128)(2,1)S(1)}, u32[]{:S(2)}) copy-start(bf16[112,16,4,128]{3,2,1,0:T(4,128)(2,1)S(1)} %get-tuple-element.17) | copy-start | bytes 5505028
  31.5 1.5 %copy-start.1 = (bf16[112,16,4,128]{3,2,1,0:T(4,128)(2,1)S(1)}, bf16[112,16,4,128]{3,2,1,0:T(4,128)(2,1)}, u32[]{:S(2)}) copy-start(bf16[112,16,4,128]{3,2,1,0:T(4,128)(2,1)} %copy-done) | copy-start | bytes 5505028

commit v4 on v3

--- a/solution.py
+++ b/solution.py
@@ -18,25 +18,34 @@
 HBM = pl.BlockSpec(memory_space=pltpu.HBM)
 
 
+def shift(value, axis, steps):
+    count = lax.axis_size(axis)
+    pairs = [(source, (source + steps) % count) for source in range(count)]
+    return lax.ppermute(value, axis, pairs)
+
+
 def stage_kernel(
-    pieces, n_ctx, slots, bucket_ref, pool_ref, fresh_ref, kb, vb, kf, vf, slots_ref, counts_ref,
-    sem,
+    pieces, n_ctx, slots, bucket_ref, pool_ref, fresh_ref, kb, kf, vf, slots_ref, counts_ref, sem,
 ):
-    each = pool_ref.shape[0] // pieces
-    copies = []
-    for half, (pool_to, fresh_to) in enumerate(((kb, kf), (vb, vf))):
-        lanes = pl.ds(half * LANES, LANES)
-        copies.append(pltpu.make_async_copy(
-            fresh_ref.at[:, :, :, lanes], fresh_to, sem.at[len(copies)]))
-        for n in range(pieces):
-            some = pl.ds(n * each, each)
-            copies.append(pltpu.make_async_copy(
-                pool_ref.at[some, :, :, lanes], pool_to.at[some], sem.at[len(copies)]))
+    copies = [
+        pltpu.make_async_copy(fresh_ref.at[:, :, :, pl.ds(half * LANES, LANES)], to, sem.at[half])
+        for half, to in enumerate((kf, vf))
+    ] + half_copies(pool_ref, kb, sem, 2, 0, pieces)
     for one in copies:
         one.start()
     list_fresh(n_ctx, slots, bucket_ref, slots_ref, counts_ref)
     for one in copies:
         one.wait()
+
+
+def half_copies(pool_ref, target, sem, first, half, pieces):
+    each = pool_ref.shape[0] // pieces
+    return [
+        pltpu.make_async_copy(
+            pool_ref.at[pl.ds(n * each, each), :, :, pl.ds(half * LANES, LANES)],
+            target.at[pl.ds(n * each, each)], sem.at[first + n])
+        for n in range(pieces)
+    ]
 
 
 def list_kernel(n_ctx, slots, bucket_ref, slots_ref, counts_ref):
@@ -100,66 +109,64 @@
 
 
 def resident_kernel(
-    dims, table_ref, left_ref, q_ref, kb, vb, acc_ref, top_ref, tot_ref, t_s,
+    dims, table_ref, left_ref, q_ref, kb, pool_ref, acc_ref, top_ref, tot_ref, t_s, *held,
 ):
-    heads, page_rows, pages_dev, sub = dims
+    heads, page_rows, pages_dev, sub, pieces = dims
+    copies = []
+    vb = pool_ref
+    if held:
+        copies = half_copies(pool_ref, held[0], held[1], 0, 1, pieces)
+        vb = held[0].reshape(held[0].shape[0], page_rows, LANES)
+    for one in copies:
+        one.start()
     columns = pages_dev * page_rows
     wide = min(WIDE, columns)
     per = wide // page_rows
     chunks = columns // wide
-    count = q_ref.shape[0]
     lane = lax.broadcasted_iota(jnp.int32, (sub, LANES), 1)
     onehots = [(lane % heads == h).astype(jnp.bfloat16) for h in range(heads)]
 
-    def score_chunk(i, c, top):
-        keys = pages_of(kb, table_ref, i * pages_dev + c * per, per)
-        parts = score_parts(q_ref[i], keys, lane, left_ref[i] * heads, c * wide, heads, sub)
-        for j, part in enumerate(parts):
-            t_s[:, c * wide + j * LANES:c * wide + (j + 1) * LANES] = part
-        return jnp.maximum(top, fold_max(parts))
-
-    def value_chunk(i, c, top, tot, acc):
-        weights = []
-        for j in range(wide // LANES):
-            at = c * wide + j * LANES
-            p = jnp.exp2(t_s[:, at:at + LANES] - top)
-            tot = tot + p
-            weights.append(spread(p, onehots))
-        values = pages_of(vb, table_ref, i * pages_dev + c * per, per)
-        return tot, acc + jnp.dot(
-            jnp.concatenate(weights, axis=1), values, preferred_element_type=jnp.float32)
-
-    def finish(i, top, tot, acc):
+    def score_step(i, _):
+        top = jnp.full((sub, LANES), NEG, jnp.float32)
+        for c in range(chunks):
+            keys = pages_of(kb, table_ref, i * pages_dev + c * per, per)
+            parts = score_parts(q_ref[i], keys, lane, left_ref[i] * heads, c * wide, heads, sub)
+            for j, part in enumerate(parts):
+                t_s[i, :, c * wide + j * LANES:c * wide + (j + 1) * LANES] = part
+            top = jnp.maximum(top, fold_max(parts))
+        top_ref[i] = top
+        return 0
+
+    def value_step(i, _):
+        tot = jnp.zeros((sub, LANES), jnp.float32)
+        acc = jnp.zeros((heads * sub, LANES), jnp.float32)
+        top = top_ref[i]
+        for c in range(chunks):
+            weights = []
+            for j in range(wide // LANES):
+                at = c * wide + j * LANES
+                p = jnp.exp2(t_s[i, :, at:at + LANES] - top)
+                tot = tot + p
+                weights.append(spread(p, onehots))
+            values = pages_of(vb, table_ref, i * pages_dev + c * per, per)
+            acc = acc + jnp.dot(
+                jnp.concatenate(weights, axis=1), values, preferred_element_type=jnp.float32)
         acc_ref[i] = acc
-        top_ref[i] = top
-        tot_ref[i] = class_reduce(tot, jnp.add, heads)
-
-    low = jnp.full((sub, LANES), NEG, jnp.float32)
-    none = jnp.zeros((sub, LANES), jnp.float32)
-    empty = jnp.zeros((heads * sub, LANES), jnp.float32)
-
-    def step(i, top):
-        top = class_reduce(top, jnp.maximum, heads)
-        later, tot, acc = low, none, empty
-        for c in range(chunks):
-            tot, acc = value_chunk(i, c, top, tot, acc)
-            later = score_chunk(i + 1, c, later)
-        finish(i, top, tot, acc)
-        return later
-
-    top = low
-    for c in range(chunks):
-        top = score_chunk(0, c, top)
-    top = lax.fori_loop(0, count - 1, step, top)
-    top = class_reduce(top, jnp.maximum, heads)
-    tot, acc = none, empty
-    for c in range(chunks):
-        tot, acc = value_chunk(count - 1, c, top, tot, acc)
-    finish(count - 1, top, tot, acc)
+        tot_ref[i] = tot
+        return 0
+
+    shape = top_ref.shape
+    flat = (shape[0] * shape[1], LANES)
+    lax.fori_loop(0, shape[0], score_step, 0)
+    top_ref[...] = class_reduce(top_ref[...].reshape(flat), jnp.maximum, heads).reshape(shape)
+    for one in copies:
+        one.wait()
+    lax.fori_loop(0, shape[0], value_step, 0)
+    tot_ref[...] = class_reduce(tot_ref[...].reshape(flat), jnp.add, heads).reshape(shape)
 
 
 def fresh_kernel(
-    dims, own_ref, slots_ref, counts_ref, q_ref, kf, vf, acc_ref, top_ref, tot_ref,
+    dims, own_ref, slots_ref, counts_ref, qown_ref, qfar_ref, kf, vf, acc_ref, top_ref, tot_ref,
     out_ref, t_s, p_s,
 ):
     heads, page_rows, slots, sub, n_req, req_dev = dims
@@ -176,8 +183,8 @@
     tops = []
     for n, request in enumerate(requests):
         keys = pages_of(kf, slots_ref, request * slots, slots)
-        parts = score_parts(
-            q_ref[request], keys, lane, counts_ref[request] * page_rows, 0, heads, sub)
+        q = qown_ref[n] if n < req_dev else qfar_ref[n - req_dev]
+        parts = score_parts(q, keys, lane, counts_ref[request] * page_rows, 0, heads, sub)
         for j, part in enumerate(parts):
             t_s[n, :, j * LANES:(j + 1) * LANES] = part
         tops.append(fold_max(parts))
@@ -207,10 +214,9 @@
             some = acc[h * sub:(h + 1) * sub]
             if n < req_dev:
                 some = some + acc_ref[n, h * sub:(h + 1) * sub, :] * rows_of(fades[n], h)
-            out_ref[request * heads + h] = (some * rows_of(whole, h)).astype(jnp.bfloat16)
+            out_ref[n * heads + h] = (some * rows_of(whole, h)).astype(jnp.bfloat16)
         lse = tops[n] + jnp.log2(tots[n])
-        for m in range(len(slabs)):
-            slabs[m] = jnp.where(lane // unit == request - m * fill, lse, slabs[m])
+        slabs[n // fill] = jnp.where(lane // unit == n % fill, lse, slabs[n // fill])
     for n, lse in enumerate(slabs):
         out_ref[n_reqs * heads + n] = pieces_of(lse, kind)
 
@@ -237,9 +243,9 @@
     return [share / tot for share in shares], top + jnp.log2(tot)
 
 
-def ctx_merge_kernel(dims, got_ref, out_ref):
+def ctx_merge_kernel(dims, *refs):
     heads, n_req, req_dev = dims
-    refs = [got_ref.at[n] for n in range(got_ref.shape[0])]
+    refs, out_ref = refs[:-1], refs[-1]
     n_reqs = n_req * req_dev
     unit = 4 * heads
     fill = LANES // unit
@@ -269,9 +275,9 @@
         out_ref[k, req_dev * heads] = slab.astype(jnp.bfloat16)
 
 
-def req_merge_kernel(dims, got_ref, out_ref):
+def req_merge_kernel(dims, *refs):
     heads, req_dev = dims
-    refs = [got_ref.at[n] for n in range(got_ref.shape[0])]
+    refs, out_ref = refs[:-1], refs[-1]
     group = out_ref.shape[2]
     shares, _ = merge_lse(refs, req_dev * heads, heads)
     for i in range(req_dev):
@@ -304,33 +310,34 @@
     page_rows = page * heads
 
     smem = lambda count: jax.ShapeDtypeStruct((count,), jnp.int32)
-    near = lax.all_to_all(
-        jnp.broadcast_to(query, (n_ctx,) + query.shape), "ctx", split_axis=0, concat_axis=0,
-        tiled=True)
+    near = jnp.stack([query] + [shift(query, "ctx", -k) for k in range(1, n_ctx)])
     if heads % 4 == 0:
         pieces = 8
         half = lambda count: jax.ShapeDtypeStruct((count, page, heads, LANES), jnp.bfloat16)
-        kb, vb, kf, vf, slot_table, counts = pl.pallas_call(
+        pool = pltpu.with_memory_space_constraint(kv_pool, pltpu.HBM)
+        kb, kf, vf, slot_table, counts = pl.pallas_call(
             functools.partial(stage_kernel, pieces, n_ctx, slots),
             out_shape=(
-                half(pool_slots), half(pool_slots), half(new_dev), half(new_dev),
-                smem(n_reqs * slots), smem(n_reqs)),
+                half(pool_slots), half(new_dev), half(new_dev), smem(n_reqs * slots), smem(n_reqs)),
             in_specs=[SMEM, HBM, HBM],
-            out_specs=(VMEM,) * 4 + (SMEM,) * 2,
-            scratch_shapes=[pltpu.SemaphoreType.DMA((2 * pieces + 2,))],
+            out_specs=(VMEM,) * 3 + (SMEM,) * 2,
+            scratch_shapes=[pltpu.SemaphoreType.DMA((pieces + 2,))],
             compiler_params=params(2),
             cost_estimate=pl.CostEstimate(
                 flops=0, transcendentals=0, bytes_accessed=2 * (kv_pool.size + fresh_kv.size)),
             name="stage",
-        )(
-            fresh_bucket, pltpu.with_memory_space_constraint(kv_pool, pltpu.HBM),
-            pltpu.with_memory_space_constraint(fresh_kv, pltpu.HBM))
-        kb, vb, kf, vf = (a.reshape(a.shape[0], page_rows, LANES) for a in (kb, vb, kf, vf))
+        )(fresh_bucket, pool, pltpu.with_memory_space_constraint(fresh_kv, pltpu.HBM))
+        kb, kf, vf = (a.reshape(a.shape[0], page_rows, LANES) for a in (kb, kf, vf))
+        vb, held = pool, [
+            pltpu.VMEM((pool_slots, page, heads, LANES), jnp.bfloat16),
+            pltpu.SemaphoreType.DMA((pieces,)),
+        ]
     else:
         kb, vb, kf, vf = (
             a[..., h * LANES:(h + 1) * LANES].reshape(a.shape[0], page_rows, LANES)
             for a in (kv_pool, fresh_kv) for h in (0, 1)
         )
+        held = []
         slot_table, counts = pl.pallas_call(
             functools.partial(list_kernel, n_ctx, slots),
             out_shape=(smem(n_reqs * slots), smem(n_reqs)),
@@ -339,24 +346,22 @@
             name="list",
         )(fresh_bucket)
 
-    far = lax.all_to_all(
-        jnp.broadcast_to(near, (n_req,) + near.shape), "req", split_axis=0, concat_axis=0,
-        tiled=True)
+    far = jnp.stack([shift(near, "req", -k) for k in range(1, n_req)])
     q_own = near.transpose(1, 2, 0, 3, 4).reshape(req_dev, rows, head_dim)
-    q_all = far.transpose(0, 2, 3, 1, 4, 5).reshape(n_reqs, rows, head_dim)
+    q_far = far.transpose(0, 2, 3, 1, 4, 5).reshape(n_reqs - req_dev, rows, head_dim)
     left = context_len - ctx_place * (pages_dev * page)
 
     f32 = lambda *shape: jax.ShapeDtypeStruct(shape, jnp.float32)
     bf16 = lambda *shape: jax.ShapeDtypeStruct(shape, jnp.bfloat16)
     columns = pages_dev * page_rows
     acc, top, tot = pl.pallas_call(
-        functools.partial(resident_kernel, (heads, page_rows, pages_dev, sub)),
+        functools.partial(resident_kernel, (heads, page_rows, pages_dev, sub, 8)),
         out_shape=(
             f32(req_dev, rows, LANES), f32(req_dev, sub, LANES), f32(req_dev, sub, LANES)),
-        in_specs=[SMEM] * 2 + [VMEM] * 3,
+        in_specs=[SMEM] * 2 + [VMEM] * 2 + [HBM if held else VMEM],
         out_specs=(VMEM,) * 3,
-        scratch_shapes=[pltpu.VMEM((sub, columns), jnp.float32)],
-        compiler_params=params(8),
+        scratch_shapes=[pltpu.VMEM((req_dev, sub, columns), jnp.float32)] + held,
+        compiler_params=params(14),
         cost_estimate=pl.CostEstimate(
             flops=4 * req_dev * rows * columns * LANES, transcendentals=req_dev * sub * columns,
             bytes_accessed=2 * kv_pool.size),
@@ -368,7 +373,7 @@
     parts = pl.pallas_call(
         functools.partial(fresh_kernel, (heads, page_rows, slots, sub, n_req, req_dev)),
         out_shape=bf16(slabs, sub, LANES),
-        in_specs=[SMEM] * 3 + [VMEM] * 6,
+        in_specs=[SMEM] * 3 + [VMEM] * 7,
         out_specs=VMEM,
         scratch_shapes=[
             pltpu.VMEM((n_reqs, sub, slots * page_rows), jnp.float32),
@@ -380,27 +385,27 @@
             transcendentals=n_reqs * sub * slots * page_rows, bytes_accessed=2 * fresh_kv.size),
         name="fresh",
     )(
-        req_place.astype(jnp.int32).reshape(1), slot_table, counts, q_all, kf, vf, acc, top, tot,
+        req_place.astype(jnp.int32).reshape(1), slot_table, counts, q_own, q_far, kf, vf, acc, top, tot,
     )
     sends = parts.reshape(slabs, n_ctx, group, LANES).transpose(1, 0, 2, 3)
-    got = lax.all_to_all(sends, "ctx", split_axis=0, concat_axis=0, tiled=True)
+    got = [sends[0]] + [shift(sends[k], "ctx", k) for k in range(1, n_ctx)]
     merged = pl.pallas_call(
         functools.partial(ctx_merge_kernel, (heads, n_req, req_dev)),
         out_shape=bf16(n_req, req_dev * heads + 1, group, LANES),
-        in_specs=[VMEM],
+        in_specs=[VMEM] * n_ctx,
         out_specs=VMEM,
         compiler_params=params(8),
         name="ctx_merge",
-    )(got)
-    got = lax.all_to_all(merged, "req", split_axis=0, concat_axis=0, tiled=True)
+    )(*got)
+    got = [merged[0]] + [shift(merged[k], "req", k) for k in range(1, n_req)]
     return pl.pallas_call(
         functools.partial(req_merge_kernel, (heads, req_dev)),
         out_shape=bf16(req_dev, heads, group, LANES),
-        in_specs=[VMEM],
+        in_specs=[VMEM] * n_req,
         out_specs=VMEM,
         compiler_params=params(8),
         name="req_merge",
-    )(got)
+    )(*got)
 
 
 def solution(mesh):

time: 56.7 us -> 43 us (0.76)
  blocking collectives: 27.3 us -> 0 us
  waiting for transfers between devices: 0.01 us -> 9.35 us
  starting transfers between devices: 4.87 us -> 13.6 us
  local copies, waits for them, and re-layouts: 5.09 us -> 0.99 us
  Pallas kernels: 19 us -> 17.9 us
  other arithmetic: 0.01 us -> 0.93 us
    all_to_all x3 -> x0, blocking collectives: 27.3 us -> none  [the longest x1 10.6 us: local(): got = lax.all_to_all(merged, 'req', split_axis=0, concat_axis=0, tiled=True)]
    ppermute x0 -> x12, starting transfers between devices: none -> 13.6 us  [shift(): return lax.ppermute(value, axis, pairs)]
    ppermute x0 -> x12, waiting for transfers between devices: none -> 9.35 us  [shift(): return lax.ppermute(value, axis, pairs)]
    all_to_all x1 -> x0, starting transfers between devices: 4.87 us -> none  [local(): lax.all_to_all(jnp.broadcast_to(near, (n_req,) + near.shape), 'req', spli...]
    unnamed x10 -> x6, local copies, waits for them, and re-layouts: 3.39 us -> 0.66 us
    pallas_call x1, Pallas kernels: 8.12 us -> 5.69 us  [local(): pl.pallas_call(functools.partial(stage_kernel, pieces, n_ctx, slots), out...]
    broadcast_in_dim x2 -> x0, local copies, waits for them, and re-layouts: 1.55 us -> none  [the longest x1 0.82 us: local(): jnp.broadcast_to(near, (n_req,) + near.shape)]
    pallas_call x1, Pallas kernels: 6.81 us -> 8.07 us  [local(): pl.pallas_call(functools.partial(resident_kernel, (heads, page_rows, page...]
  transfers between devices with their start and end apart: 1 -> 12, of which waited for: 0 -> 5; matrix products, arithmetic and copies ran while one was open for 0% -> 2% of each run, Pallas kernels for 27% -> 32%
where the time goes in v4:
time: 43 us; the launch traced here: 42.9 us
  Pallas kernels  17.9 us (42%)
  starting transfers between devices  13.6 us (32%)
  waiting for transfers between devices  9.35 us (22%)
  local copies, waits for them, and re-layouts  0.99 us (2%)
  other arithmetic  0.93 us (2%)
    ppermute x12, starting transfers between devices, shift(): return lax.ppermute(value, axis, pairs)  13.6 us
    ppermute x12, waiting for transfers between devices, shift(): return lax.ppermute(value, axis, pairs)  9.35 us
    pallas_call x1, Pallas kernels, local(): pl.pallas_call(functools.partial(resident_kernel, (heads, page_rows, page...  8.07 us
    pallas_call x1, Pallas kernels, local(): pl.pallas_call(functools.partial(stage_kernel, pieces, n_ctx, slots), out...  5.69 us
    pallas_call x1, Pallas kernels, local(): pl.pallas_call(functools.partial(fresh_kernel, (heads, page_rows, slots,...  2.62 us
    pallas_call x1, Pallas kernels, local(): pl.pallas_call(functools.partial(req_merge_kernel, (heads, req_dev)), out...  0.87 us
  transfers between devices with their start and end apart: 12, of which 5 were waited for; matrix products, arithmetic and copies ran while one was open for 2% of the time, Pallas kernels for 32%

profile of v4, /device:TPU:0, one launch (start us, length us, event | category | flops | bytes accessed | tf_op | source)
XLA Modules:
  0.0 42.9 jit_solution(8396503352186719494)
XLA Ops:
  0.0 2.4 %collective-permute-start = (bf16[4,4,4,128]{3,2,1,0:T(4,128)(2,1)}, bf16[4,4,4,128]{3,2,1,0:T(4,128)(2,1)S(1)}, u32[]{:S(2)}, u32[]{:S(2)}) collective-permute-start(bf16[4,4,4,128]{3,2,1,0:T(4,128)(2,1)} %param.6), channel_id=1, source_target_pairs={{0,6},{2,0},{4,2},{6,4},{1,7},{3,1},{5,3},{7,5},{8,14},{10,8},{12,... | collective-permute-start | bytes 49160 | tf_op jit(solution)/shard_map/ppermute | solution.py:24
  2.4 1.1 %collective-permute-start.1 = (bf16[4,4,4,128]{3,2,1,0:T(4,128)(2,1)}, bf16[4,4,4,128]{3,2,1,0:T(4,128)(2,1)S(1)}, u32[]{:S(2)}, u32[]{:S(2)}) collective-permute-start(bf16[4,4,4,128]{3,2,1,0:T(4,128)(2,1)} %param.6), channel_id=1, source_target_pairs={{0,4},{2,6},{4,0},{6,2},{1,5},{3,7},{5,1},{7,3},{8,12},{10,14},{12... | collective-permute-start | bytes 49160 | tf_op jit(solution)/shard_map/ppermute | solution.py:24
  3.5 0.7 %broadcast_subtract_fusion.left_ref = s32[4]{0:T(128)S(1)} fusion(s32[4]{0:T(128)} %param.9, s32[]{:T(128)S(6)} %mul.3), kind=kLoop, calls=%fused_computation.11 | loop fusion | flops 4 | bytes 36 | tf_op jit(solution)/shard_map/sub | solution.py:352
  4.1 0.7 %copy-done.1 = s32[112]{0:T(128)S(1)} copy-done((s32[112]{0:T(128)S(1)}, s32[112]{0:T(128)}, u32[]{:S(2)}) %copy-start.1) | copy-done | bytes 472
  4.8 5.7 %stage.1 = (bf16[512,16,4,128]{3,2,1,0:T(4,128)(2,1)S(1)}, bf16[112,16,4,128]{3,2,1,0:T(4,128)(2,1)S(1)}, bf16[112,16,4,128]{3,2,1,0:T(4,128)(2,1)S(1)}, s32[128]{0:T(128)S(1)}, s32[16]{0:T(128)S(1)}) custom-call(s32[112]{0:T(128)S(1)} %copy-done.1, bf16[512,16,4,256]{3,2,1,0:T(4,128)(2,1)} %pool_ref.3, bf16[112,16,4,256]{3,2,1,0:T(4,128)(2,1)} %fresh_ref.1), custom_call_target="tpu_custom_call" | custom-call | bytes 20447232 | tf_op jit(solution)/shard_map/stage/pallas_call | solution.py:318
  10.6 2.7 %collective-permute-start.4 = (bf16[4,4,4,4,128]{4,3,2,1,0:T(4,128)(2,1)S(1)}, bf16[4,4,4,4,128]{4,3,2,1,0:T(4,128)(2,1)S(1)}, u32[]{:S(2)}, u32[]{:S(2)}) collective-permute-start(bf16[4,4,4,4,128]{4,3,2,1,0:T(4,128)(2,1)S(1)} %pad_maximum_fusion), channel_id=1, source_target_pairs={{0,16},{8,24},{16,0},{24,8},{1,17},{9,25},{17,1},{25,9},{2,18},{10... | collective-permute-start | bytes 196616 | tf_op jit(solution)/shard_map/ppermute | solution.py:24
  13.3 1.3 %collective-permute-start.3 = (bf16[4,4,4,4,128]{4,3,2,1,0:T(4,128)(2,1)S(1)}, bf16[4,4,4,4,128]{4,3,2,1,0:T(4,128)(2,1)S(1)}, u32[]{:S(2)}, u32[]{:S(2)}) collective-permute-start(bf16[4,4,4,4,128]{4,3,2,1,0:T(4,128)(2,1)S(1)} %pad_maximum_fusion), channel_id=1, source_target_pairs={{0,24},{8,0},{16,8},{24,16},{1,25},{9,1},{17,9},{25,17},{2,26},{10... | collective-permute-start | bytes 196616 | tf_op jit(solution)/shard_map/ppermute | solution.py:24
  14.6 0.7 %collective-permute-start.5 = (bf16[4,4,4,4,128]{4,3,2,1,0:T(4,128)(2,1)S(1)}, bf16[4,4,4,4,128]{4,3,2,1,0:T(4,128)(2,1)S(1)}, u32[]{:S(2)}, u32[]{:S(2)}) collective-permute-start(bf16[4,4,4,4,128]{4,3,2,1,0:T(4,128)(2,1)S(1)} %pad_maximum_fusion), channel_id=1, source_target_pairs={{0,8},{8,16},{16,24},{24,0},{1,9},{9,17},{17,25},{25,1},{2,10},{10... | collective-permute-start | bytes 196616 | tf_op jit(solution)/shard_map/ppermute | solution.py:24
  15.4 8.1 %resident.1 = (f32[4,64,128]{2,1,0:T(8,128)S(1)}, f32[4,16,128]{2,1,0:T(8,128)S(1)}, f32[4,16,128]{2,1,0:T(8,128)S(1)}) custom-call(s32[512]{0:T(512)S(1)} %bitcast.45, s32[4]{0:T(128)S(1)} %broadcast_subtract_fusion.left_ref, bf16[4,64,128]{2,1,0:T(8,128)(2,1)S(1)} %bitcast.43, bf16[512,64,128]{2,1,0:T(8,128)(2,1)S(1)} %bitcast.38, ...), custom_call_target="tpu_custom_call" | custom-call | flops 1073741824 | bytes 16777216 | tf_op jit(solution)/shard_map/resident/pallas_call | solution.py:357
  23.5 0.2 maximum_bitcast_fusion
  23.7 2.6 %fresh.1 = bf16[66,16,128]{2,1,0:T(8,128)(2,1)S(1)} custom-call(s32[1]{0:T(128)} %bitcast.own_ref, s32[128]{0:T(128)S(1)} %get-tuple-element.13.slots_ref, s32[16]{0:T(128)S(1)} %get-tuple-element.14.counts_ref, bf16[4,64,128]{2,1,0:T(8,128)(2,1)S(1)} %bitcast.44, bf16[12,64,128]{2,1,0:T(8,128)(2,1)S(1)} %bitcast.42, bf16[112,64,128]{2,1,0:T(8,128)(2,1)S(1)} %bitcast.39, ...), custom_call_target="tpu_custom_call" | custom-call | flops 268435456 | bytes 3670016 | tf_op jit(solution)/shard_map/fresh/pallas_call | solution.py:373
  26.3 0.1 copy.13
  26.4 0.1 slice_bitcast_fusion
  26.5 0.1 collective-permute-start.8
  26.7 1.5 %collective-permute-start.7 = (bf16[66,4,128]{2,1,0:T(4,128)(2,1)S(1)}, bf16[66,4,128]{2,1,0:T(4,128)(2,1)S(1)}, u32[]{:S(2)}, u32[]{:S(2)}) collective-permute-start(bf16[66,4,128]{2,1,0:T(4,128)(2,1)S(1)} %get-tuple-element.22), channel_id=1, source_target_pairs={{0,4},{2,6},{4,0},{6,2},{1,5},{3,7},{5,1},{7,3},{8,12},{10,14},{12... | collective-permute-start | bytes 202760 | tf_op jit(solution)/shard_map/ppermute | solution.py:24
  28.2 0.7 %collective-permute-done.8.refs_3_ = bf16[66,4,128]{2,1,0:T(4,128)(2,1)S(1)} collective-permute-done((bf16[66,4,128]{2,1,0:T(4,128)(2,1)S(1)}, bf16[66,4,128]{2,1,0:T(4,128)(2,1)S(1)}, u32[]{:S(2)}, u32[]{:S(2)}) %collective-permute-start.8) | collective-permute-done | bytes 67616 | tf_op jit(solution)/shard_map/ppermute | solution.py:24
  28.9 3.7 %collective-permute-done.7.refs_2_ = bf16[66,4,128]{2,1,0:T(4,128)(2,1)S(1)} collective-permute-done((bf16[66,4,128]{2,1,0:T(4,128)(2,1)S(1)}, bf16[66,4,128]{2,1,0:T(4,128)(2,1)S(1)}, u32[]{:S(2)}, u32[]{:S(2)}) %collective-permute-start.7) | collective-permute-done | bytes 67616 | tf_op jit(solution)/shard_map/ppermute | solution.py:24
  32.6 0.6 %ctx_merge.1 = bf16[4,17,4,128]{3,2,1,0:T(4,128)(2,1)S(1)} custom-call(bf16[66,4,128]{2,1,0:T(4,128)(2,1)S(1)} %get-tuple-element.24.refs_0_, bf16[66,4,128]{2,1,0:T(4,128)(2,1)S(1)} %collective-permute-done.6.refs_1_, bf16[66,4,128]{2,1,0:T(4,128)(2,1)S(1)} %collective-permute-done.7.refs_2_, bf16[66,4,128]{2,1,0:T(4,128)(2,1)S(1)} %collective-permute-done.8.refs_3_), custom_call_target="tpu_custom_call" | custom-call | tf_op jit(solution)/shard_map/ctx_merge/pallas_call | solution.py:392
  33.3 3.2 %collective-permute-start.11 = (bf16[17,4,128]{2,1,0:T(4,128)(2,1)S(1)}, bf16[17,4,128]{2,1,0:T(4,128)(2,1)S(1)}, u32[]{:S(2)}, u32[]{:S(2)}) collective-permute-start(bf16[17,4,128]{2,1,0:T(4,128)(2,1)S(1)} %get-tuple-element.25), channel_id=1, source_target_pairs={{0,24},{8,0},{16,8},{24,16},{1,25},{9,1},{17,9},{25,17},{2,26},{10... | collective-permute-start | bytes 52232 | tf_op jit(solution)/shard_map/ppermute | solution.py:24
  36.5 0.6 %collective-permute-start.9 = (bf16[17,4,128]{2,1,0:T(4,128)(2,1)S(1)}, bf16[17,4,128]{2,1,0:T(4,128)(2,1)S(1)}, u32[]{:S(2)}, u32[]{:S(2)}) collective-permute-start(bf16[17,4,128]{2,1,0:T(4,128)(2,1)S(1)} %get-tuple-element.27), channel_id=1, source_target_pairs={{0,8},{8,16},{16,24},{24,0},{1,9},{9,17},{17,25},{25,1},{2,10},{10... | collective-permute-start | bytes 52232 | tf_op jit(solution)/shard_map/ppermute | solution.py:24
  37.1 0.8 %collective-permute-done.11.refs_3_ = bf16[17,4,128]{2,1,0:T(4,128)(2,1)S(1)} collective-permute-done((bf16[17,4,128]{2,1,0:T(4,128)(2,1)S(1)}, bf16[17,4,128]{2,1,0:T(4,128)(2,1)S(1)}, u32[]{:S(2)}, u32[]{:S(2)}) %collective-permute-start.11) | collective-permute-done | bytes 17440 | tf_op jit(solution)/shard_map/ppermute | solution.py:24
  37.9 3.2 %collective-permute-done.10.refs_2_ = bf16[17,4,128]{2,1,0:T(4,128)(2,1)S(1)} collective-permute-done((bf16[17,4,128]{2,1,0:T(4,128)(2,1)S(1)}, bf16[17,4,128]{2,1,0:T(4,128)(2,1)S(1)}, u32[]{:S(2)}, u32[]{:S(2)}) %collective-permute-start.10) | collective-permute-done | bytes 17440 | tf_op jit(solution)/shard_map/ppermute | solution.py:24
  41.1 0.9 %collective-permute-done.9.refs_1_ = bf16[17,4,128]{2,1,0:T(4,128)(2,1)S(1)} collective-permute-done((bf16[17,4,128]{2,1,0:T(4,128)(2,1)S(1)}, bf16[17,4,128]{2,1,0:T(4,128)(2,1)S(1)}, u32[]{:S(2)}, u32[]{:S(2)}) %collective-permute-start.9) | collective-permute-done | bytes 17440 | tf_op jit(solution)/shard_map/ppermute | solution.py:24
  42.0 0.9 %req_merge.1 = bf16[4,4,4,128]{3,2,1,0:T(4,128)(2,1)} custom-call(bf16[17,4,128]{2,1,0:T(4,128)(2,1)S(1)} %get-tuple-element.28.refs_0_, bf16[17,4,128]{2,1,0:T(4,128)(2,1)S(1)} %collective-permute-done.9.refs_1_, bf16[17,4,128]{2,1,0:T(4,128)(2,1)S(1)} %collective-permute-done.10.refs_2_, bf16[17,4,128]{2,1,0:T(4,128)(2,1)S(1)} %collective-permute-done.11.refs_3_), custom_call_target="tpu_custom_call" | custom-call | tf_op jit(solution)/shard_map/req_merge/pallas_call | solution.py:401
  (20 shorter events, 0.3 us)
Async XLA Ops:
  0.0 10.5 %collective-permute-start = (bf16[4,4,4,128]{3,2,1,0:T(4,128)(2,1)}, bf16[4,4,4,128]{3,2,1,0:T(4,128)(2,1)S(1)}, u32[]{:S(2)}, u32[]{:S(2)}) collective-permute-start(bf16[4,4,4,128]{3,2,1,0:T(4,128)(2,1)} %param.6), channel_id=1, source_target_pairs={{0,6},{2,0},{4,2},{6,4},{1,7},{3,1},{5,3},{7,5},{8,14},{10,8},{12,... | collective-permute-start | bytes 49160 | tf_op jit(solution)/shard_map/ppermute | solution.py:24
  2.4 8.1 %collective-permute-start.2 = (bf16[4,4,4,128]{3,2,1,0:T(4,128)(2,1)}, bf16[4,4,4,128]{3,2,1,0:T(4,128)(2,1)S(1)}, u32[]{:S(2)}, u32[]{:S(2)}) collective-permute-start(bf16[4,4,4,128]{3,2,1,0:T(4,128)(2,1)} %param.6), channel_id=1, source_target_pairs={{0,2},{2,4},{4,6},{6,0},{1,3},{3,5},{5,7},{7,1},{8,10},{10,12},{12... | collective-permute-start | bytes 49160 | tf_op jit(solution)/shard_map/ppermute | solution.py:24
  2.4 8.1 %collective-permute-start.1 = (bf16[4,4,4,128]{3,2,1,0:T(4,128)(2,1)}, bf16[4,4,4,128]{3,2,1,0:T(4,128)(2,1)S(1)}, u32[]{:S(2)}, u32[]{:S(2)}) collective-permute-start(bf16[4,4,4,128]{3,2,1,0:T(4,128)(2,1)} %param.6), channel_id=1, source_target_pairs={{0,4},{2,6},{4,0},{6,2},{1,5},{3,7},{5,1},{7,3},{8,12},{10,14},{12... | collective-permute-start | bytes 49160 | tf_op jit(solution)/shard_map/ppermute | solution.py:24
  4.1 0.7 %copy-start.1 = (s32[112]{0:T(128)S(1)}, s32[112]{0:T(128)}, u32[]{:S(2)}) copy-start(s32[112]{0:T(128)} %bucket_ref.1) | copy-start | bytes 1348
  4.8 5.7 %copy-start.2 = (bf16[4,4,4,128]{3,2,1,0:T(4,128)(2,1)S(1)}, bf16[4,4,4,128]{3,2,1,0:T(4,128)(2,1)}, u32[]{:S(2)}) copy-start(bf16[4,4,4,128]{3,2,1,0:T(4,128)(2,1)} %param.6) | copy-start | bytes 49156
  4.8 10.6 %copy-start = (s32[4,128]{1,0:T(4,128)S(1)}, s32[4,128]{1,0:T(4,128)}, u32[]{:S(2)}) copy-start(s32[4,128]{1,0:T(4,128)} %param.8) | copy-start | bytes 6148
  10.6 12.8 %collective-permute-start.4 = (bf16[4,4,4,4,128]{4,3,2,1,0:T(4,128)(2,1)S(1)}, bf16[4,4,4,4,128]{4,3,2,1,0:T(4,128)(2,1)S(1)}, u32[]{:S(2)}, u32[]{:S(2)}) collective-permute-start(bf16[4,4,4,4,128]{4,3,2,1,0:T(4,128)(2,1)S(1)} %pad_maximum_fusion), channel_id=1, source_target_pairs={{0,16},{8,24},{16,0},{24,8},{1,17},{9,25},{17,1},{25,9},{2,18},{10... | collective-permute-start | bytes 196616 | tf_op jit(solution)/shard_map/ppermute | solution.py:24
  13.3 10.2 %collective-permute-start.3 = (bf16[4,4,4,4,128]{4,3,2,1,0:T(4,128)(2,1)S(1)}, bf16[4,4,4,4,128]{4,3,2,1,0:T(4,128)(2,1)S(1)}, u32[]{:S(2)}, u32[]{:S(2)}) collective-permute-start(bf16[4,4,4,4,128]{4,3,2,1,0:T(4,128)(2,1)S(1)} %pad_maximum_fusion), channel_id=1, source_target_pairs={{0,24},{8,0},{16,8},{24,16},{1,25},{9,1},{17,9},{25,17},{2,26},{10... | collective-permute-start | bytes 196616 | tf_op jit(solution)/shard_map/ppermute | solution.py:24
  14.6 8.8 %collective-permute-start.5 = (bf16[4,4,4,4,128]{4,3,2,1,0:T(4,128)(2,1)S(1)}, bf16[4,4,4,4,128]{4,3,2,1,0:T(4,128)(2,1)S(1)}, u32[]{:S(2)}, u32[]{:S(2)}) collective-permute-start(bf16[4,4,4,4,128]{4,3,2,1,0:T(4,128)(2,1)S(1)} %pad_maximum_fusion), channel_id=1, source_target_pairs={{0,8},{8,16},{16,24},{24,0},{1,9},{9,17},{17,25},{25,1},{2,10},{10... | collective-permute-start | bytes 196616 | tf_op jit(solution)/shard_map/ppermute | solution.py:24
  26.5 2.3 %collective-permute-start.8 = (bf16[66,4,128]{2,1,0:T(4,128)(2,1)S(1)}, bf16[66,4,128]{2,1,0:T(4,128)(2,1)S(1)}, u32[]{:S(2)}, u32[]{:S(2)}) collective-permute-start(bf16[66,4,128]{2,1,0:T(4,128)(2,1)S(1)} %get-tuple-element.21), channel_id=1, source_target_pairs={{0,6},{2,0},{4,2},{6,4},{1,7},{3,1},{5,3},{7,5},{8,14},{10,8},{12,... | collective-permute-start | bytes 202760 | tf_op jit(solution)/shard_map/ppermute | solution.py:24
  26.7 5.9 %collective-permute-start.7 = (bf16[66,4,128]{2,1,0:T(4,128)(2,1)S(1)}, bf16[66,4,128]{2,1,0:T(4,128)(2,1)S(1)}, u32[]{:S(2)}, u32[]{:S(2)}) collective-permute-start(bf16[66,4,128]{2,1,0:T(4,128)(2,1)S(1)} %get-tuple-element.22), channel_id=1, source_target_pairs={{0,4},{2,6},{4,0},{6,2},{1,5},{3,7},{5,1},{7,3},{8,12},{10,14},{12... | collective-permute-start | bytes 202760 | tf_op jit(solution)/shard_map/ppermute | solution.py:24
  28.2 4.4 %collective-permute-start.6 = (bf16[66,4,128]{2,1,0:T(4,128)(2,1)S(1)}, bf16[66,4,128]{2,1,0:T(4,128)(2,1)S(1)}, u32[]{:S(2)}, u32[]{:S(2)}) collective-permute-start(bf16[66,4,128]{2,1,0:T(4,128)(2,1)S(1)} %get-tuple-element.23), channel_id=1, source_target_pairs={{0,2},{2,4},{4,6},{6,0},{1,3},{3,5},{5,7},{7,1},{8,10},{10,12},{12... | collective-permute-start | bytes 202760 | tf_op jit(solution)/shard_map/ppermute | solution.py:24
  33.3 4.6 %collective-permute-start.11 = (bf16[17,4,128]{2,1,0:T(4,128)(2,1)S(1)}, bf16[17,4,128]{2,1,0:T(4,128)(2,1)S(1)}, u32[]{:S(2)}, u32[]{:S(2)}) collective-permute-start(bf16[17,4,128]{2,1,0:T(4,128)(2,1)S(1)} %get-tuple-element.25), channel_id=1, source_target_pairs={{0,24},{8,0},{16,8},{24,16},{1,25},{9,1},{17,9},{25,17},{2,26},{10... | collective-permute-start | bytes 52232 | tf_op jit(solution)/shard_map/ppermute | solution.py:24
  36.4 4.6 %collective-permute-start.10 = (bf16[17,4,128]{2,1,0:T(4,128)(2,1)S(1)}, bf16[17,4,128]{2,1,0:T(4,128)(2,1)S(1)}, u32[]{:S(2)}, u32[]{:S(2)}) collective-permute-start(bf16[17,4,128]{2,1,0:T(4,128)(2,1)S(1)} %get-tuple-element.26), channel_id=1, source_target_pairs={{0,16},{8,24},{16,0},{24,8},{1,17},{9,25},{17,1},{25,9},{2,18},{10... | collective-permute-start | bytes 52232 | tf_op jit(solution)/shard_map/ppermute | solution.py:24
  36.5 5.5 %collective-permute-start.9 = (bf16[17,4,128]{2,1,0:T(4,128)(2,1)S(1)}, bf16[17,4,128]{2,1,0:T(4,128)(2,1)S(1)}, u32[]{:S(2)}, u32[]{:S(2)}) collective-permute-start(bf16[17,4,128]{2,1,0:T(4,128)(2,1)S(1)} %get-tuple-element.27), channel_id=1, source_target_pairs={{0,8},{8,16},{16,24},{24,0},{1,9},{9,17},{17,25},{25,1},{2,10},{10... | collective-permute-start | bytes 52232 | tf_op jit(solution)/shard_map/ppermute | solution.py:24

commit v5 on v4

v5 whole, which is shorter than its diff:
```python
import functools
import math

import jax
import jax.numpy as jnp
from jax import lax
from jax.experimental import pallas as pl
from jax.experimental.pallas import tpu as pltpu
from jax.sharding import PartitionSpec as P

NEG = -1e30
CAP = 2
LANES = 128
SCALE = math.log2(math.e) / math.sqrt(LANES)
SCORE_WIDE = 256
VALUE_WIDE = 512
VMEM = pl.BlockSpec(memory_space=pltpu.VMEM)
SMEM = pl.BlockSpec(memory_space=pltpu.SMEM)
HBM = pl.BlockSpec(memory_space=pltpu.HBM)


def swap(value, axis, bit):
    return lax.ppermute(value, axis, [(n, n ^ bit) for n in range(lax.axis_size(axis))])


def bits_of(axis):
    bit = lax.axis_size(axis) // 2
    while bit:
        yield bit
        bit //= 2


def after(value, done):
    return lax.optimization_barrier((value, done))[0]


def half_copies(pool_ref, target, sem, half, pieces):
    each = pool_ref.shape[0] // pieces
    return [
        pltpu.make_async_copy(
            pool_ref.at[pl.ds(n * each, each), :, :, pl.ds(half * LANES, LANES)],
            target.at[pl.ds(n * each, each)], sem.at[n])
        for n in range(pieces)
    ]


def stage_fresh_kernel(
    n_ctx, slots, bucket_hbm, fresh_ref, kf, vf, slots_ref, counts_ref, bucket_ref, sem, bucket_sem,
):
    copies = [
        half_copies(fresh_ref, kf, sem.at[0], 0, 1)[0], half_copies(fresh_ref, vf, sem.at[1], 1, 1)[0],
    ]
    listed = pltpu.make_async_copy(bucket_hbm, bucket_ref, bucket_sem)
    listed.start()
    for one in copies:
        one.start()
    listed.wait()
    list_fresh(n_ctx, slots, bucket_ref, slots_ref, counts_ref)
    for one in copies:
        one.wait()


def stage_keys_kernel(pieces, pool_ref, kb, done_ref, sem):
    copies = half_copies(pool_ref, kb, sem, 0, pieces)
    for one in copies:
        one.start()
    done_ref[0] = 0
    for one in copies:
        one.wait()


def list_kernel(n_ctx, slots, bucket_ref, slots_ref, counts_ref):
    list_fresh(n_ctx, slots, bucket_ref, slots_ref, counts_ref)


def list_fresh(n_ctx, slots, bucket_ref, slots_ref, counts_ref):
    for n in range(counts_ref.shape[0]):
        counts_ref[n] = 0
    for n in range(slots_ref.shape[0]):
        slots_ref[n] = 0

    def put(page, _):
        request = bucket_ref[page] // n_ctx
        count = counts_ref[request]
        slots_ref[request * slots + count] = page
        counts_ref[request] = count + 1
        return 0

    lax.fori_loop(0, bucket_ref.shape[0], put, 0)


def class_reduce(x, op, heads):
    step = heads
    while step < LANES:
        x = op(x, pltpu.roll(x, step, 1))
        step *= 2
    return x


def pages_of(ref, table_ref, first, count):
    return jnp.concatenate([ref[table_ref[first + n]] for n in range(count)], axis=0)


def score_parts(q, keys, lane, limit, first, heads, sub):
    s = lax.dot_general(q, keys, (((1,), (1,)), ((), ())), preferred_element_type=jnp.float32)
    out = []
    for j in range(s.shape[1] // LANES):
        part = s[:, j * LANES:(j + 1) * LANES]
        one = part[:sub]
        for h in range(1, heads):
            one = jnp.where(lane % heads == h, part[h * sub:(h + 1) * sub], one)
        out.append(jnp.where(lane < limit - (first + j * LANES), one * SCALE, NEG))
    return out


def spread(p, onehots):
    p = p.astype(jnp.bfloat16)
    return jnp.concatenate([p * one for one in onehots], axis=0)


def rows_of(x, h):
    return jnp.broadcast_to(x[:, h:h + 1], x.shape)


def fold_max(parts):
    top = parts[0]
    for part in parts[1:]:
        top = jnp.maximum(top, part)
    return top


def score_kernel(dims, table_ref, len_ref, q_ref, kb, *refs):
    heads, page_rows, pages_dev, sub, pieces = dims
    copies = []
    if pieces:
        pool_ref, t_ref, top_ref, vb, sem = refs
        copies = half_copies(pool_ref, vb, sem, 1, pieces)
    else:
        t_ref, top_ref = refs
    for one in copies:
        one.start()
    columns = pages_dev * page_rows
    wide = min(SCORE_WIDE, columns)
    per = wide // page_rows
    lane = lax.broadcasted_iota(jnp.int32, (sub, LANES), 1)
    start = lax.axis_index("ctx") * (pages_dev * page_rows)

    def step(i, _):
        top = jnp.full((sub, LANES), NEG, jnp.float32)
        limit = len_ref[i] * heads - start
        for c in range(columns // wide):
            keys = pages_of(kb, table_ref, i * pages_dev + c * per, per)
            parts = score_parts(q_ref[i], keys, lane, limit, c * wide, heads, sub)
            for j, part in enumerate(parts):
                t_ref[i, :, c * wide + j * LANES:c * wide + (j + 1) * LANES] = part
            top = jnp.maximum(top, fold_max(parts))
        top_ref[i] = top
        return 0

    shape = top_ref.shape
    flat = (shape[0] * shape[1], LANES)
    lax.fori_loop(0, shape[0], step, 0)
    top_ref[...] = class_reduce(top_ref[...].reshape(flat), jnp.maximum, heads).reshape(shape)
    for one in copies:
        one.wait()


def value_kernel(dims, table_ref, t_ref, top_ref, vb, acc_ref, tot_ref):
    heads, page_rows, pages_dev, sub = dims
    columns = pages_dev * page_rows
    wide = min(VALUE_WIDE, columns)
    per = wide // page_rows
    lane = lax.broadcasted_iota(jnp.int32, (sub, LANES), 1)
    onehots = [(lane % heads == h).astype(jnp.bfloat16) for h in range(heads)]

    def step(i, _):
        tot = jnp.zeros((sub, LANES), jnp.float32)
        acc = jnp.zeros((heads * sub, LANES), jnp.float32)
        top = top_ref[i]
        for c in range(columns // wide):
            weights = []
            for j in range(wide // LANES):
                at = c * wide + j * LANES
                p = jnp.exp2(t_ref[i, :, at:at + LANES] - top)
                tot = tot + p
                weights.append(spread(p, onehots))
            values = pages_of(vb, table_ref, i * pages_dev + c * per, per)
            acc = acc + jnp.dot(
                jnp.concatenate(weights, axis=1), values, preferred_element_type=jnp.float32)
        acc_ref[i] = acc
        tot_ref[i] = tot
        return 0

    shape = tot_ref.shape
    flat = (shape[0] * shape[1], LANES)
    lax.fori_loop(0, shape[0], step, 0)
    tot_ref[...] = class_reduce(tot_ref[...].reshape(flat), jnp.add, heads).reshape(shape)


def fresh_kernel(
    dims, slots_ref, counts_ref, q_refs, kf, vf, acc_ref, top_ref, tot_ref, keep_ref, send_ref,
    t_s, p_s,
):
    heads, page_rows, slots, sub, offsets, req_dev = dims
    lane = lax.broadcasted_iota(jnp.int32, (sub, LANES), 1)
    onehots = [(lane % heads == h).astype(jnp.bfloat16) for h in range(heads)]
    unit = 4 * heads
    columns = slots * page_rows
    wide = min(SCORE_WIDE, columns)
    per = wide // page_rows
    own = lax.axis_index("req")
    requests = [(own ^ offset) * req_dev + i for offset in offsets for i in range(req_dev)]
    n_reqs = len(requests)
    tops = []
    for n, request in enumerate(requests):
        limit = counts_ref[request] * page_rows
        top = jnp.full((sub, LANES), NEG, jnp.float32)
        for c in range(columns // wide):
            keys = pages_of(kf, slots_ref, request * slots + c * per, per)
            q = q_refs[n // req_dev][n % req_dev]
            parts = score_parts(q, keys, lane, limit, c * wide, heads, sub)
            for j, part in enumerate(parts):
                t_s[n, :, c * wide + j * LANES:c * wide + (j + 1) * LANES] = part
            top = jnp.maximum(top, fold_max(parts))
        tops.append(top)
    tops = class_reduce(jnp.concatenate(tops, axis=0), jnp.maximum, heads)
    tops = [tops[n * sub:(n + 1) * sub] for n in range(n_reqs)]
    for i in range(req_dev):
        tops[i] = jnp.maximum(tops[i], top_ref[i])
    tots = []
    for n in range(n_reqs):
        tot = jnp.zeros((sub, LANES), jnp.float32)
        for j in range(columns // LANES):
            p = jnp.exp2(t_s[n, :, j * LANES:(j + 1) * LANES] - tops[n])
            tot = tot + p
            p_s[n, :, j * LANES:(j + 1) * LANES] = spread(p, onehots)
        tots.append(tot)
    tots = class_reduce(jnp.concatenate(tots, axis=0), jnp.add, heads)
    tots = [tots[n * sub:(n + 1) * sub] for n in range(n_reqs)]
    fades = [jnp.exp2(top_ref[i] - tops[i]) for i in range(req_dev)]
    for i in range(req_dev):
        tots[i] = tots[i] + fades[i] * tot_ref[i]
    lses = [jnp.zeros((sub, LANES), jnp.float32) for _ in offsets]
    for n, request in enumerate(requests):
        values = pages_of(vf, slots_ref, request * slots, slots)
        acc = jnp.dot(p_s[n], values, preferred_element_type=jnp.float32)
        whole = 1.0 / tots[n]
        block, i = n // req_dev, n % req_dev
        for h in range(heads):
            some = acc[h * sub:(h + 1) * sub]
            if n < req_dev:
                some = some + acc_ref[n, h * sub:(h + 1) * sub, :] * rows_of(fades[n], h)
            some = some * rows_of(whole, h)
            keep_ref[block, i * heads + h] = some[:sub // 2]
            send_ref[block, i * heads + h] = some[sub // 2:].astype(jnp.bfloat16)
        lse = tops[n] + jnp.log2(tots[n])
        lses[block] = jnp.where(lane // unit == i, lse, lses[block])
    for block, lse in enumerate(lses):
        keep_ref[block, req_dev * heads] = lse[:sub // 2]
        send_ref[block, req_dev * heads] = pieces_of(lse[sub // 2:], heads)


def pieces_of(lse, heads):
    lane = lax.broadcasted_iota(jnp.int32, lse.shape, 1)
    kind = lane % (4 * heads) // heads
    high = lse.astype(jnp.bfloat16).astype(jnp.float32)
    rest = lse - high
    mid = rest.astype(jnp.bfloat16).astype(jnp.float32)
    both = jnp.where(kind == 1, mid, rest - mid)
    return jnp.where(kind == 0, high, both).astype(jnp.bfloat16)


def whole_of(pieces, heads):
    x = pieces.astype(jnp.float32)
    lane = lax.broadcasted_iota(jnp.int32, x.shape, 1)
    kind = lane % (4 * heads) // heads
    x = x + pltpu.roll(x, LANES - heads, 1) + pltpu.roll(x, LANES - 2 * heads, 1)
    same = x
    for m in (1, 2):
        same = jnp.where(kind == m, pltpu.roll(x, m * heads, 1), same)
    return same


def merge_kernel(split, heads, keep_ref, got_ref, *outs):
    blocks, slabs, rows, _ = keep_ref.shape
    slabs -= 1
    half = rows // 2

    def put(block, slab, value, coded):
        if split == "rows":
            outs[0][block, slab] = value[:half]
            outs[1][block, slab] = coded(value[half:])
        elif split == "blocks" and block < blocks // 2:
            outs[0][block, slab] = value
        elif split == "blocks":
            outs[1][block - blocks // 2, slab] = coded(value)
        elif slab < slabs:
            outs[0][slab // heads, slab % heads] = coded(value)

    for block in range(blocks):
        own = keep_ref[block, slabs]
        other = whole_of(got_ref[block, slabs], heads)
        top = jnp.maximum(own, other)
        share = jnp.exp2(own - top)
        tot = share + jnp.exp2(other - top)
        share = share / tot
        for slab in range(slabs):
            at = slab // heads * 4 * heads + slab % heads
            part = jnp.broadcast_to(share[:, at:at + 1], (rows, LANES))
            kept, got = keep_ref[block, slab], got_ref[block, slab].astype(jnp.float32)
            put(block, slab, part * kept + (1.0 - part) * got, lambda x: x.astype(jnp.bfloat16))
        put(block, slabs, top + jnp.log2(tot), lambda x: pieces_of(x, heads))


def params(mib):
    return pltpu.CompilerParams(vmem_limit_bytes=mib * 2**20)


def local(query, kv_pool, page_table, context_len, fresh_kv, fresh_bucket):
    n_ctx = lax.axis_size("ctx")
    n_req = lax.axis_size("req")
    req_dev, heads, group, head_dim = query.shape
    pool_slots, page = kv_pool.shape[:2]
    new_dev = fresh_kv.shape[0]
    pages_dev = page_table.shape[1]
    n_reqs = n_req * req_dev
    slots = CAP * n_ctx
    sub = n_ctx * group
    rows = heads * sub
    page_rows = page * heads

    smem = lambda count: jax.ShapeDtypeStruct((count,), jnp.int32)
    bf16 = lambda *shape: jax.ShapeDtypeStruct(shape, jnp.bfloat16)
    f32 = lambda *shape: jax.ShapeDtypeStruct(shape, jnp.float32)
    columns = pages_dev * page_rows
    split = heads % 4 == 0
    pieces = 8 if split else 0

    near = query[None]
    offsets = [0]
    ctx_bits = list(bits_of("ctx"))
    if split:
        keep_hbm = lambda a: pltpu.with_memory_space_constraint(a, pltpu.HBM)
        pool, fresh = keep_hbm(kv_pool), keep_hbm(fresh_kv)
        arrived = swap(near, "ctx", ctx_bits[0])
        kf, vf, slot_table, counts = pl.pallas_call(
            functools.partial(stage_fresh_kernel, n_ctx, slots),
            out_shape=(
                bf16(new_dev, page, heads, LANES), bf16(new_dev, page, heads, LANES),
                smem(n_reqs * slots), smem(n_reqs)),
            in_specs=[HBM, HBM],
            out_specs=(VMEM,) * 2 + (SMEM,) * 2,
            scratch_shapes=[
                pltpu.SMEM((new_dev,), jnp.int32), pltpu.SemaphoreType.DMA((2, 1)),
                pltpu.SemaphoreType.DMA],
            compiler_params=params(2),
            cost_estimate=pl.CostEstimate(
                flops=0, transcendentals=0, bytes_accessed=4 * fresh_kv.size),
            name="stage_fresh",
        )(keep_hbm(fresh_bucket), fresh)
        near = jnp.concatenate([near, after(arrived, counts)])
        for bit in ctx_bits[1:-1]:
            near = jnp.concatenate([near, swap(near, "ctx", bit)])
        arrived = swap(near, "ctx", ctx_bits[-1])
        kb, done = pl.pallas_call(
            functools.partial(stage_keys_kernel, pieces),
            out_shape=(bf16(pool_slots, page, heads, LANES), smem(1)),
            in_specs=[HBM],
            out_specs=(VMEM, SMEM),
            scratch_shapes=[pltpu.SemaphoreType.DMA((pieces,))],
            compiler_params=params(2),
            cost_estimate=pl.CostEstimate(
                flops=0, transcendentals=0, bytes_accessed=2 * kv_pool.size),
            name="stage_keys",
        )(pool)
        near = jnp.concatenate([near, after(arrived, done)])
        kb, kf, vf = (a.reshape(a.shape[0], page_rows, LANES) for a in (kb, kf, vf))
        score_in, score_specs = (pool,), [HBM]
        score_out = (bf16(pool_slots, page, heads, LANES),)
        score_scratch = [pltpu.SemaphoreType.DMA((pieces,))]
    else:
        for bit in ctx_bits:
            near = jnp.concatenate([near, swap(near, "ctx", bit)])
        kb, vb, kf, vf = (
            a[..., h * LANES:(h + 1) * LANES].reshape(a.shape[0], page_rows, LANES)
            for a in (kv_pool, fresh_kv) for h in (0, 1)
        )
        slot_table, counts = pl.pallas_call(
            functools.partial(list_kernel, n_ctx, slots),
            out_shape=(smem(n_reqs * slots), smem(n_reqs)),
            in_specs=[SMEM],
            out_specs=(SMEM,) * 2,
            name="list",
        )(fresh_bucket)
        score_in, score_specs, score_out, score_scratch = (), [], (), []

    rows_first = lambda a: a.transpose(1, 2, 0, 3, 4).reshape(req_dev, rows, head_dim)
    req_bits = list(bits_of("req"))
    far = [rows_first(near)[None]]
    table = page_table.reshape(-1)
    far.append(swap(far[0], "req", req_bits[0]))
    offsets = [0, req_bits[0]]
    t, top, *staged = pl.pallas_call(
        functools.partial(score_kernel, (heads, page_rows, pages_dev, sub, pieces)),
        out_shape=(f32(req_dev, sub, columns), f32(req_dev, sub, LANES)) + score_out,
        in_specs=[SMEM] * 2 + [VMEM] * 2 + score_specs,
        out_specs=(VMEM,) * (2 + len(score_out)),
        scratch_shapes=score_scratch,
        compiler_params=params(4),
        cost_estimate=pl.CostEstimate(
            flops=2 * req_dev * rows * columns * LANES, transcendentals=0,
            bytes_accessed=kv_pool.size),
        name="scores",
    )(table, context_len, far[0][0], kb, *score_in)
    if staged:
        vb = staged[0].reshape(pool_slots, page_rows, LANES)
    far[1] = after(far[1], top)
    for bit in req_bits[1:]:
        far.append(swap(jnp.concatenate(far), "req", bit))
        offsets += [offset ^ bit for offset in offsets]
    acc, tot = pl.pallas_call(
        functools.partial(value_kernel, (heads, page_rows, pages_dev, sub)),
        out_shape=(f32(req_dev, rows, LANES), f32(req_dev, sub, LANES)),
        in_specs=[SMEM] + [VMEM] * 3,
        out_specs=(VMEM,) * 2,
        compiler_params=params(4),
        cost_estimate=pl.CostEstimate(
            flops=2 * req_dev * rows * columns * LANES, transcendentals=req_dev * sub * columns,
            bytes_accessed=kv_pool.size),
        name="values",
    )(table, t, top, vb)

    slabs = req_dev * heads + 1
    blocks = n_req

    def fresh_call(slots_ref, counts_ref, *refs):
        q_refs = [ref.at[n] for ref in refs[:len(far)] for n in range(ref.shape[0])]
        fresh_kernel(
            (heads, page_rows, slots, sub, offsets, req_dev), slots_ref, counts_ref, q_refs,
            *refs[len(far):])

    keep, send = pl.pallas_call(
        fresh_call,
        out_shape=(
            f32(blocks, slabs, sub // 2, LANES), bf16(blocks, slabs, sub // 2, LANES)),
        in_specs=[SMEM] * 2 + [VMEM] * (5 + len(far)),
        out_specs=(VMEM,) * 2,
        scratch_shapes=[
            pltpu.VMEM((n_reqs, sub, slots * page_rows), jnp.float32),
            pltpu.VMEM((n_reqs, rows, slots * page_rows), jnp.bfloat16),
        ],
        compiler_params=params(8),
        cost_estimate=pl.CostEstimate(
            flops=4 * n_reqs * rows * slots * page_rows * LANES,
            transcendentals=n_reqs * sub * slots * page_rows, bytes_accessed=2 * fresh_kv.size),
        name="fresh",
    )(slot_table, counts, *far, kf, vf, acc, top, tot)

    left = sub // 2
    for axis, bit in [("ctx", b) for b in ctx_bits[::-1]] + [("req", b) for b in req_bits[::-1]]:
        got = swap(send, axis, bit)
        if left > group:
            how, left = "rows", left // 2
        elif blocks > 1:
            how, blocks = "blocks", blocks // 2
        else:
            how = "last"
        shape = (blocks, slabs, left, LANES)
        out = pl.pallas_call(
            functools.partial(merge_kernel, how, heads),
            out_shape=[bf16(req_dev, heads, group, LANES)] if how == "last" else [f32(*shape), bf16(*shape)],
            in_specs=[VMEM] * 2,
            out_specs=[VMEM] if how == "last" else [VMEM] * 2,
            compiler_params=params(8),
            name="merge_" + how,
        )(keep, got)
        if how == "last":
            return out[0]
        keep, send = out


def solution(mesh):
    placed = (
        P("req", "kvh", "ctx", None),
        P(("req", "ctx"), None, "kvh", None),
        P("req", "ctx"),
        P("req"),
        P(("req", "ctx"), None, "kvh", None),
        P(("req", "ctx")),
    )
    return jax.shard_map(
        local, mesh=mesh, in_specs=placed, out_specs=P("req", "kvh", "ctx", None), check_vma=False
    )
```

time: 43 us -> 43.5 us (1.012)
  waiting for transfers between devices: 9.35 us -> 13.9 us
  starting transfers between devices: 13.6 us -> 10.1 us
  Pallas kernels: 17.9 us -> 19.1 us
  local copies, waits for them, and re-layouts: 0.99 us -> 0.04 us
  other arithmetic: 0.93 us -> 0.09 us
    ppermute x12 -> x8, waiting for transfers between devices: 9.35 us -> 13.9 us  [swap(): lax.ppermute(value, axis, [(n, n ^ bit) for n in range(lax.axis_size(axis...]
    ppermute x12 -> x8, starting transfers between devices: 13.6 us -> 10.1 us  [swap(): lax.ppermute(value, axis, [(n, n ^ bit) for n in range(lax.axis_size(axis...]
    pallas_call x5 -> x9, Pallas kernels: 17.9 us -> 19.1 us  [the longest x1 4.42 us: local(): pl.pallas_call(functools.partial(score_kernel, (heads, page_rows, pages_d...]
    sub x1 -> x0, other arithmetic: 0.66 us -> none  [local(): left = context_len - ctx_place * (pages_dev * page)]
    unnamed x6, local copies, waits for them, and re-layouts: 0.66 us -> 0.02 us
  transfers between devices with their start and end apart: 12 -> 8, of which waited for: 5 -> 6; matrix products, arithmetic and copies ran while one was open for 2% -> 0% of each run, Pallas kernels for 32% -> 34%
where the time goes in v5:
time: 43.5 us; the launch traced here: 43.4 us
  Pallas kernels  19.1 us (44%)
  waiting for transfers between devices  13.9 us (32%)
  starting transfers between devices  10.1 us (23%)
    ppermute x8, waiting for transfers between devices, swap(): lax.ppermute(value, axis, [(n, n ^ bit) for n in range(lax.axis_size(axis...  13.9 us
    ppermute x8, starting transfers between devices, swap(): lax.ppermute(value, axis, [(n, n ^ bit) for n in range(lax.axis_size(axis...  10.1 us
    pallas_call x1, Pallas kernels, local(): pl.pallas_call(functools.partial(score_kernel, (heads, page_rows, pages_d...  4.42 us
    pallas_call x1, Pallas kernels, local(): pl.pallas_call(functools.partial(stage_keys_kernel, pieces), out_shape=(b...  3.99 us
    pallas_call x1, Pallas kernels, local(): pl.pallas_call(functools.partial(stage_fresh_kernel, n_ctx, slots), out_s...  3.56 us
    pallas_call x1, Pallas kernels, local(): pl.pallas_call(functools.partial(value_kernel, (heads, page_rows, pages_d...  2.75 us
    pallas_call x1, Pallas kernels, local(): pl.pallas_call(fresh_call, out_shape=(f32(blocks, slabs, sub // 2, LANES)...  2.62 us
    pallas_call x4, Pallas kernels, local(): pl.pallas_call(functools.partial(merge_kernel, how, heads), out_shape=[bf...  1.81 us
  transfers between devices with their start and end apart: 8, of which 6 were waited for; matrix products, arithmetic and copies ran while one was open for 0% of the time, Pallas kernels for 34%

profile of v5, /device:TPU:0, one launch (start us, length us, event | category | flops | bytes accessed | tf_op | source)
XLA Modules:
  0.0 43.4 jit_solution(11053797786021892156)
XLA Ops:
  0.0 2.9 %collective-permute-start = (bf16[1,4,4,4,128]{4,3,2,1,0:T(4,128)(2,1)}, bf16[1,4,4,4,128]{4,3,2,1,0:T(4,128)(2,1)S(1)}, u32[]{:S(2)}, u32[]{:S(2)}) collective-permute-start(bf16[1,4,4,4,128]{4,3,2,1,0:T(4,128)(2,1)} %bitcast.20), channel_id=1, source_target_pairs={{0,4},{2,6},{4,0},{6,2},{1,5},{3,7},{5,1},{7,3},{8,12},{10,14},{12... | collective-permute-start | bytes 49160 | tf_op jit(solution)/shard_map/ppermute | solution.py:23
  2.9 3.6 %stage_fresh.1 = (bf16[112,16,4,128]{3,2,1,0:T(4,128)(2,1)S(1)}, bf16[112,16,4,128]{3,2,1,0:T(4,128)(2,1)S(1)}, s32[128]{0:T(128)S(1)}, s32[16]{0:T(128)S(1)}) custom-call(s32[112]{0:T(128)} %bucket_hbm.1, bf16[112,16,4,256]{3,2,1,0:T(4,128)(2,1)} %fresh_ref.1), custom_call_target="tpu_custom_call" | custom-call | bytes 7340032 | tf_op jit(solution)/shard_map/stage_fresh/pallas_call | solution.py:346
  6.6 0.1 collective-permute-start.1
  6.6 1.2 %collective-permute-done.1 = bf16[2,4,4,4,128]{4,3,2,1,0:T(4,128)(2,1)S(1)} collective-permute-done((bf16[2,4,4,4,128]{4,3,2,1,0:T(4,128)(2,1)S(1)}, bf16[2,4,4,4,128]{4,3,2,1,0:T(4,128)(2,1)S(1)}, u32[]{:S(2)}, u32[]{:S(2)}) %collective-permute-start.1) | collective-permute-done | bytes 32800 | tf_op jit(solution)/shard_map/ppermute | solution.py:23
  7.8 0.1 maximum_bitcast_fusion
  8.0 2.7 %collective-permute-start.2 = (bf16[1,4,64,128]{3,2,1,0:T(8,128)(2,1)S(1)}, bf16[1,4,64,128]{3,2,1,0:T(8,128)(2,1)S(1)}, u32[]{:S(2)}, u32[]{:S(2)}) collective-permute-start(bf16[1,4,64,128]{3,2,1,0:T(8,128)(2,1)S(1)} %bitcast.14), channel_id=1, source_target_pairs={{0,16},{8,24},{16,0},{24,8},{1,17},{9,25},{17,1},{25,9},{2,18},{10... | collective-permute-start | bytes 196616 | tf_op jit(solution)/shard_map/ppermute | solution.py:23
  10.6 4.0 %stage_keys.1 = (bf16[512,16,4,128]{3,2,1,0:T(4,128)(2,1)S(1)}, s32[1]{0:T(128)}) custom-call(bf16[512,16,4,256]{3,2,1,0:T(4,128)(2,1)} %refs_0_.1), custom_call_target="tpu_custom_call" | custom-call | bytes 16777216 | tf_op jit(solution)/shard_map/stage_keys/pallas_call | solution.py:365
  14.6 4.4 %scores.1 = (f32[4,16,8192]{2,1,0:T(8,128)S(1)}, f32[4,16,128]{2,1,0:T(8,128)S(1)}, bf16[512,16,4,128]{3,2,1,0:T(4,128)(2,1)S(1)}) custom-call(s32[512]{0:T(512)S(1)} %bitcast.18, s32[4]{0:T(128)S(1)} %copy-done.1, bf16[4,64,128]{2,1,0:T(8,128)(2,1)S(1)} %bitcast.15, bf16[512,64,128]{2,1,0:T(8,128)(2,1)S(1)} %bitcast.11, bf16[512,16,4,256]{3,2,1,0:T(4,128)(2,1)} %refs_0_.1), custom_call_target="tpu_custom_call" | custom-call | flops 536870912 | bytes 8388608 | tf_op jit(solution)/shard_map/scores/pallas_call | solution.py:403
  19.1 1.7 %collective-permute-start.3 = (bf16[2,4,64,128]{3,2,1,0:T(8,128)(2,1)S(1)}, bf16[2,4,64,128]{3,2,1,0:T(8,128)(2,1)S(1)}, u32[]{:S(2)}, u32[]{:S(2)}) collective-permute-start(bf16[2,4,64,128]{3,2,1,0:T(8,128)(2,1)S(1)} %pad_maximum_fusion), channel_id=1, source_target_pairs={{0,8},{8,0},{16,24},{24,16},{1,9},{9,1},{17,25},{25,17},{2,10},{10... | collective-permute-start | bytes 393224 | tf_op jit(solution)/shard_map/ppermute | solution.py:23
  20.7 2.8 %values.1 = (f32[4,64,128]{2,1,0:T(8,128)S(1)}, f32[4,16,128]{2,1,0:T(8,128)S(1)}) custom-call(s32[512]{0:T(512)S(1)} %bitcast.19, f32[4,16,8192]{2,1,0:T(8,128)S(1)} %get-tuple-element.33.t_ref, f32[4,16,128]{2,1,0:T(8,128)S(1)} %get-tuple-element.29.top_ref.refs_6_, bf16[512,64,128]{2,1,0:T(8,128)(2,1)S(1)} %bitcast.10), custom_call_target="tpu_custom_call" | custom-call | flops 536870912 | bytes 8388608 | tf_op jit(solution)/shard_map/values/pallas_call | solution.py:421
  23.5 0.9 %collective-permute-done.3.refs_2_ = bf16[2,4,64,128]{3,2,1,0:T(8,128)(2,1)S(1)} collective-permute-done((bf16[2,4,64,128]{3,2,1,0:T(8,128)(2,1)S(1)}, bf16[2,4,64,128]{3,2,1,0:T(8,128)(2,1)S(1)}, u32[]{:S(2)}, u32[]{:S(2)}) %collective-permute-start.3) | collective-permute-done | bytes 131104 | tf_op jit(solution)/shard_map/ppermute | solution.py:23
  24.4 2.6 %fresh.1 = (f32[4,17,8,128]{3,2,1,0:T(8,128)S(1)}, bf16[4,17,8,128]{3,2,1,0:T(8,128)(2,1)S(1)}) custom-call(s32[128]{0:T(128)S(1)} %get-tuple-element.25.slots_ref, s32[16]{0:T(128)S(1)} %get-tuple-element.26.counts_ref, bf16[1,4,64,128]{3,2,1,0:T(8,128)(2,1)S(1)} %bitcast.17, bf16[1,4,64,128]{3,2,1,0:T(8,128)(2,1)S(1)} %collective-permute-done.2.refs_1_, ...), custom_call_target="tpu_custom_call" | custom-call | flops 268435456 | bytes 3670016 | tf_op jit(solution)/shard_map/fresh/pallas_call | solution.py:442
  27.1 0.1 collective-permute-start.4
  27.1 1.3 %collective-permute-done.4.got_ref = bf16[4,17,8,128]{3,2,1,0:T(8,128)(2,1)S(1)} collective-permute-done((bf16[4,17,8,128]{3,2,1,0:T(8,128)(2,1)S(1)}, bf16[4,17,8,128]{3,2,1,0:T(8,128)(2,1)S(1)}, u32[]{:S(2)}, u32[]{:S(2)}) %collective-permute-start.4) | collective-permute-done | bytes 139296 | tf_op jit(solution)/shard_map/ppermute | solution.py:23
  28.5 0.3 merge_rows.1
  28.8 0.6 %collective-permute-start.5 = (bf16[4,17,4,128]{3,2,1,0:T(4,128)(2,1)S(1)}, bf16[4,17,4,128]{3,2,1,0:T(4,128)(2,1)S(1)}, u32[]{:S(2)}, u32[]{:S(2)}) collective-permute-start(bf16[4,17,4,128]{3,2,1,0:T(4,128)(2,1)S(1)} %get-tuple-element.40), channel_id=1, source_target_pairs={{0,4},{2,6},{4,0},{6,2},{1,5},{3,7},{5,1},{7,3},{8,12},{10,14},{12... | collective-permute-start | bytes 208904 | tf_op jit(solution)/shard_map/ppermute | solution.py:23
  29.4 3.8 %collective-permute-done.5.got_ref = bf16[4,17,4,128]{3,2,1,0:T(4,128)(2,1)S(1)} collective-permute-done((bf16[4,17,4,128]{3,2,1,0:T(4,128)(2,1)S(1)}, bf16[4,17,4,128]{3,2,1,0:T(4,128)(2,1)S(1)}, u32[]{:S(2)}, u32[]{:S(2)}) %collective-permute-start.5) | collective-permute-done | bytes 69664 | tf_op jit(solution)/shard_map/ppermute | solution.py:23
  33.2 0.3 merge_blocks.2
  33.5 1.6 %collective-permute-start.6 = (bf16[2,17,4,128]{3,2,1,0:T(4,128)(2,1)S(1)}, bf16[2,17,4,128]{3,2,1,0:T(4,128)(2,1)S(1)}, u32[]{:S(2)}, u32[]{:S(2)}) collective-permute-start(bf16[2,17,4,128]{3,2,1,0:T(4,128)(2,1)S(1)} %get-tuple-element.42), channel_id=1, source_target_pairs={{0,8},{8,0},{16,24},{24,16},{1,9},{9,1},{17,25},{25,17},{2,10},{10... | collective-permute-start | bytes 104456 | tf_op jit(solution)/shard_map/ppermute | solution.py:23
  35.2 2.4 %collective-permute-done.6.got_ref = bf16[2,17,4,128]{3,2,1,0:T(4,128)(2,1)S(1)} collective-permute-done((bf16[2,17,4,128]{3,2,1,0:T(4,128)(2,1)S(1)}, bf16[2,17,4,128]{3,2,1,0:T(4,128)(2,1)S(1)}, u32[]{:S(2)}, u32[]{:S(2)}) %collective-permute-start.6) | collective-permute-done | bytes 34848 | tf_op jit(solution)/shard_map/ppermute | solution.py:23
  37.5 0.3 merge_blocks.3
  37.8 0.4 collective-permute-start.7
  38.2 4.3 %collective-permute-done.7.got_ref = bf16[1,17,4,128]{3,2,1,0:T(4,128)(2,1)S(1)} collective-permute-done((bf16[1,17,4,128]{3,2,1,0:T(4,128)(2,1)S(1)}, bf16[1,17,4,128]{3,2,1,0:T(4,128)(2,1)S(1)}, u32[]{:S(2)}, u32[]{:S(2)}) %collective-permute-start.7) | collective-permute-done | bytes 17440 | tf_op jit(solution)/shard_map/ppermute | solution.py:23
  42.5 0.9 %merge_last.1 = bf16[4,4,4,128]{3,2,1,0:T(4,128)(2,1)} custom-call(f32[1,17,4,128]{3,2,1,0:T(4,128)S(1)} %get-tuple-element.43.keep_ref, bf16[1,17,4,128]{3,2,1,0:T(4,128)(2,1)S(1)} %collective-permute-done.7.got_ref), custom_call_target="tpu_custom_call" | custom-call | tf_op jit(solution)/shard_map/merge_last/pallas_call | solution.py:469
  (11 shorter events, 0.1 us)
Async XLA Ops:
  0.0 6.5 %copy-start.2 = (bf16[4,4,4,128]{3,2,1,0:T(4,128)(2,1)S(1)}, bf16[4,4,4,128]{3,2,1,0:T(4,128)(2,1)}, u32[]{:S(2)}) copy-start(bf16[4,4,4,128]{3,2,1,0:T(4,128)(2,1)} %param.6) | copy-start | bytes 49156
  0.0 6.5 %collective-permute-start = (bf16[1,4,4,4,128]{4,3,2,1,0:T(4,128)(2,1)}, bf16[1,4,4,4,128]{4,3,2,1,0:T(4,128)(2,1)S(1)}, u32[]{:S(2)}, u32[]{:S(2)}) collective-permute-start(bf16[1,4,4,4,128]{4,3,2,1,0:T(4,128)(2,1)} %bitcast.20), channel_id=1, source_target_pairs={{0,4},{2,6},{4,0},{6,2},{1,5},{3,7},{5,1},{7,3},{8,12},{10,14},{12... | collective-permute-start | bytes 49160 | tf_op jit(solution)/shard_map/ppermute | solution.py:23
  6.6 1.3 %collective-permute-start.1 = (bf16[2,4,4,4,128]{4,3,2,1,0:T(4,128)(2,1)S(1)}, bf16[2,4,4,4,128]{4,3,2,1,0:T(4,128)(2,1)S(1)}, u32[]{:S(2)}, u32[]{:S(2)}) collective-permute-start(bf16[2,4,4,4,128]{4,3,2,1,0:T(4,128)(2,1)S(1)} %pad_maximum_fusion.1), channel_id=1, source_target_pairs={{0,2},{2,0},{4,6},{6,4},{1,3},{3,1},{5,7},{7,5},{8,10},{10,8},{12,... | collective-permute-start | bytes 98312 | tf_op jit(solution)/shard_map/ppermute | solution.py:23
  7.9 6.7 %copy-start = (s32[4,128]{1,0:T(4,128)S(1)}, s32[4,128]{1,0:T(4,128)}, u32[]{:S(2)}) copy-start(s32[4,128]{1,0:T(4,128)} %param.8) | copy-start | bytes 6148
  7.9 6.7 %copy-start.1 = (s32[4]{0:T(128)S(1)}, s32[4]{0:T(128)}, u32[]{:S(2)}) copy-start(s32[4]{0:T(128)} %len_ref.1) | copy-start | bytes 52
  8.0 11.1 %collective-permute-start.2 = (bf16[1,4,64,128]{3,2,1,0:T(8,128)(2,1)S(1)}, bf16[1,4,64,128]{3,2,1,0:T(8,128)(2,1)S(1)}, u32[]{:S(2)}, u32[]{:S(2)}) collective-permute-start(bf16[1,4,64,128]{3,2,1,0:T(8,128)(2,1)S(1)} %bitcast.14), channel_id=1, source_target_pairs={{0,16},{8,24},{16,0},{24,8},{1,17},{9,25},{17,1},{25,9},{2,18},{10... | collective-permute-start | bytes 196616 | tf_op jit(solution)/shard_map/ppermute | solution.py:23
  19.1 5.4 %collective-permute-start.3 = (bf16[2,4,64,128]{3,2,1,0:T(8,128)(2,1)S(1)}, bf16[2,4,64,128]{3,2,1,0:T(8,128)(2,1)S(1)}, u32[]{:S(2)}, u32[]{:S(2)}) collective-permute-start(bf16[2,4,64,128]{3,2,1,0:T(8,128)(2,1)S(1)} %pad_maximum_fusion), channel_id=1, source_target_pairs={{0,8},{8,0},{16,24},{24,16},{1,9},{9,1},{17,25},{25,17},{2,10},{10... | collective-permute-start | bytes 393224 | tf_op jit(solution)/shard_map/ppermute | solution.py:23
  27.1 1.4 %collective-permute-start.4 = (bf16[4,17,8,128]{3,2,1,0:T(8,128)(2,1)S(1)}, bf16[4,17,8,128]{3,2,1,0:T(8,128)(2,1)S(1)}, u32[]{:S(2)}, u32[]{:S(2)}) collective-permute-start(bf16[4,17,8,128]{3,2,1,0:T(8,128)(2,1)S(1)} %get-tuple-element.38), channel_id=1, source_target_pairs={{0,2},{2,0},{4,6},{6,4},{1,3},{3,1},{5,7},{7,5},{8,10},{10,8},{12,... | collective-permute-start | bytes 417800 | tf_op jit(solution)/shard_map/ppermute | solution.py:23
  28.8 4.4 %collective-permute-start.5 = (bf16[4,17,4,128]{3,2,1,0:T(4,128)(2,1)S(1)}, bf16[4,17,4,128]{3,2,1,0:T(4,128)(2,1)S(1)}, u32[]{:S(2)}, u32[]{:S(2)}) collective-permute-start(bf16[4,17,4,128]{3,2,1,0:T(4,128)(2,1)S(1)} %get-tuple-element.40), channel_id=1, source_target_pairs={{0,4},{2,6},{4,0},{6,2},{1,5},{3,7},{5,1},{7,3},{8,12},{10,14},{12... | collective-permute-start | bytes 208904 | tf_op jit(solution)/shard_map/ppermute | solution.py:23
  33.5 4.0 %collective-permute-start.6 = (bf16[2,17,4,128]{3,2,1,0:T(4,128)(2,1)S(1)}, bf16[2,17,4,128]{3,2,1,0:T(4,128)(2,1)S(1)}, u32[]{:S(2)}, u32[]{:S(2)}) collective-permute-start(bf16[2,17,4,128]{3,2,1,0:T(4,128)(2,1)S(1)} %get-tuple-element.42), channel_id=1, source_target_pairs={{0,8},{8,0},{16,24},{24,16},{1,9},{9,1},{17,25},{25,17},{2,10},{10... | collective-permute-start | bytes 104456 | tf_op jit(solution)/shard_map/ppermute | solution.py:23
  37.8 4.7 %collective-permute-start.7 = (bf16[1,17,4,128]{3,2,1,0:T(4,128)(2,1)S(1)}, bf16[1,17,4,128]{3,2,1,0:T(4,128)(2,1)S(1)}, u32[]{:S(2)}, u32[]{:S(2)}) collective-permute-start(bf16[1,17,4,128]{3,2,1,0:T(4,128)(2,1)S(1)} %get-tuple-element.44), channel_id=1, source_target_pairs={{0,16},{8,24},{16,0},{24,8},{1,17},{9,25},{17,1},{25,9},{2,18},{10... | collective-permute-start | bytes 52232 | tf_op jit(solution)/shard_map/ppermute | solution.py:23

commit v6 on v4

v6 whole, which is shorter than its diff:
```python
import functools
import math

import jax
import jax.numpy as jnp
from jax import lax
from jax.experimental import pallas as pl
from jax.experimental.pallas import tpu as pltpu
from jax.sharding import PartitionSpec as P

NEG = -1e30
CAP = 2
LANES = 128
SCALE = math.log2(math.e) / math.sqrt(LANES)
SCORE_WIDE = 256
VALUE_WIDE = 512
VMEM = pl.BlockSpec(memory_space=pltpu.VMEM)
SMEM = pl.BlockSpec(memory_space=pltpu.SMEM)
HBM = pl.BlockSpec(memory_space=pltpu.HBM)


def swap(value, axis, bit):
    return lax.ppermute(value, axis, [(n, n ^ bit) for n in range(lax.axis_size(axis))])


def half_copies(pool_ref, target, sem, half, pieces):
    each = pool_ref.shape[0] // pieces
    return [
        pltpu.make_async_copy(
            pool_ref.at[pl.ds(n * each, each), :, :, pl.ds(half * LANES, LANES)],
            target.at[pl.ds(n * each, each)], sem.at[n])
        for n in range(pieces)
    ]


def stage_kernel(
    pieces, n_ctx, slots, bucket_hbm, pool_ref, fresh_ref, kb, vb, kf, vf, slots_ref, counts_ref,
    bucket_ref, sem, fresh_sem, bucket_sem,
):
    listed = pltpu.make_async_copy(bucket_hbm, bucket_ref, bucket_sem)
    copies = []
    for half, (pool_to, fresh_to) in enumerate(((kb, kf), (vb, vf))):
        copies += half_copies(fresh_ref, fresh_to, fresh_sem.at[half], half, 1)
        copies += half_copies(pool_ref, pool_to, sem.at[half], half, pieces)
    listed.start()
    for one in copies:
        one.start()
    listed.wait()
    list_fresh(n_ctx, slots, bucket_ref, slots_ref, counts_ref)
    for one in copies:
        one.wait()


def list_kernel(n_ctx, slots, bucket_ref, slots_ref, counts_ref):
    list_fresh(n_ctx, slots, bucket_ref, slots_ref, counts_ref)


def list_fresh(n_ctx, slots, bucket_ref, slots_ref, counts_ref):
    for n in range(counts_ref.shape[0]):
        counts_ref[n] = 0
    for n in range(slots_ref.shape[0]):
        slots_ref[n] = 0

    def put(page, _):
        request = bucket_ref[page] // n_ctx
        count = counts_ref[request]
        slots_ref[request * slots + count] = page
        counts_ref[request] = count + 1
        return 0

    lax.fori_loop(0, bucket_ref.shape[0], put, 0)


def class_reduce(x, op, heads):
    step = heads
    while step < LANES:
        x = op(x, pltpu.roll(x, step, 1))
        step *= 2
    return x


def pages_of(ref, table_ref, first, count):
    return jnp.concatenate([ref[table_ref[first + n]] for n in range(count)], axis=0)


def score_parts(q, keys, lane, limit, first, heads, sub):
    s = lax.dot_general(q, keys, (((1,), (1,)), ((), ())), preferred_element_type=jnp.float32)
    out = []
    for j in range(s.shape[1] // LANES):
        part = s[:, j * LANES:(j + 1) * LANES]
        one = part[:sub]
        for h in range(1, heads):
            one = jnp.where(lane % heads == h, part[h * sub:(h + 1) * sub], one)
        out.append(jnp.where(lane < limit - (first + j * LANES), one * SCALE, NEG))
    return out


def spread(p, onehots):
    p = p.astype(jnp.bfloat16)
    return jnp.concatenate([p * one for one in onehots], axis=0)


def rows_of(x, h):
    return jnp.broadcast_to(x[:, h:h + 1], x.shape)


def fold_max(parts):
    top = parts[0]
    for part in parts[1:]:
        top = jnp.maximum(top, part)
    return top


def resident_kernel(dims, table_ref, len_ref, q_ref, kb, vb, out_ref, t_s, top_s, tot_s, acc_s):
    heads, page_rows, pages_dev, sub, req_dev, n_ctx = dims
    columns = pages_dev * page_rows
    lane = lax.broadcasted_iota(jnp.int32, (sub, LANES), 1)
    onehots = [(lane % heads == h).astype(jnp.bfloat16) for h in range(heads)]
    ctx = lax.axis_index("ctx")
    first = lax.axis_index("req") * req_dev
    start = ctx * columns

    def score_step(i, _):
        wide = min(SCORE_WIDE, columns)
        per = wide // page_rows
        top = jnp.full((sub, LANES), NEG, jnp.float32)
        limit = len_ref[i] * heads - start
        for c in range(columns // wide):
            keys = pages_of(kb, table_ref, i * pages_dev + c * per, per)
            parts = score_parts(q_ref[first + i], keys, lane, limit, c * wide, heads, sub)
            for j, part in enumerate(parts):
                t_s[i, :, c * wide + j * LANES:c * wide + (j + 1) * LANES] = part
            top = jnp.maximum(top, fold_max(parts))
        top_s[i] = top
        return 0

    def value_step(i, _):
        wide = min(VALUE_WIDE, columns)
        per = wide // page_rows
        tot = jnp.zeros((sub, LANES), jnp.float32)
        acc = jnp.zeros((heads * sub, LANES), jnp.float32)
        top = top_s[i]
        for c in range(columns // wide):
            weights = []
            for j in range(wide // LANES):
                at = c * wide + j * LANES
                p = jnp.exp2(t_s[i, :, at:at + LANES] - top)
                tot = tot + p
                weights.append(spread(p, onehots))
            values = pages_of(vb, table_ref, i * pages_dev + c * per, per)
            acc = acc + jnp.dot(
                jnp.concatenate(weights, axis=1), values, preferred_element_type=jnp.float32)
        acc_s[i] = acc
        tot_s[i] = tot
        return 0

    flat = (req_dev * sub, LANES)
    lax.fori_loop(0, req_dev, score_step, 0)
    top_s[...] = class_reduce(top_s[...].reshape(flat), jnp.maximum, heads).reshape(top_s.shape)
    lax.fori_loop(0, req_dev, value_step, 0)
    tots = class_reduce(tot_s[...].reshape(flat), jnp.add, heads)
    whole = 1.0 / tots
    lses = top_s[...].reshape(flat) + jnp.log2(tots)
    group = sub // n_ctx

    def put(slab, value, coded):
        for place in range(n_ctx):
            out_ref[place ^ ctx, slab] = coded(value[place * group:(place + 1) * group])

    lse = jnp.zeros((sub, LANES), jnp.float32)
    for i in range(req_dev):
        rows = slice(i * sub, (i + 1) * sub)
        for h in range(heads):
            some = acc_s[i, h * sub:(h + 1) * sub, :] * rows_of(whole[rows], h)
            put(i * heads + h, some, lambda x: x.astype(jnp.bfloat16))
        lse = jnp.where(lane // (4 * heads) == i, lses[rows], lse)
    put(req_dev * heads, lse, lambda x: pieces_of(x, heads))


def fresh_kernel(dims, slots_ref, counts_ref, q_ref, kf, vf, out_ref, t_s, p_s):
    heads, page_rows, slots, sub, n_req, req_dev = dims
    lane = lax.broadcasted_iota(jnp.int32, (sub, LANES), 1)
    onehots = [(lane % heads == h).astype(jnp.bfloat16) for h in range(heads)]
    columns = slots * page_rows
    wide = min(SCORE_WIDE, columns)
    per = wide // page_rows
    n_reqs = n_req * req_dev
    tops = []
    for n in range(n_reqs):
        limit = counts_ref[n] * page_rows
        top = jnp.full((sub, LANES), NEG, jnp.float32)
        for c in range(columns // wide):
            keys = pages_of(kf, slots_ref, n * slots + c * per, per)
            parts = score_parts(q_ref[n], keys, lane, limit, c * wide, heads, sub)
            for j, part in enumerate(parts):
                t_s[n, :, c * wide + j * LANES:c * wide + (j + 1) * LANES] = part
            top = jnp.maximum(top, fold_max(parts))
        tops.append(top)
    tops = class_reduce(jnp.concatenate(tops, axis=0), jnp.maximum, heads)
    tots = []
    for n in range(n_reqs):
        tot = jnp.zeros((sub, LANES), jnp.float32)
        for j in range(columns // LANES):
            p = jnp.exp2(
                t_s[n, :, j * LANES:(j + 1) * LANES] - tops[n * sub:(n + 1) * sub])
            tot = tot + p
            p_s[n, :, j * LANES:(j + 1) * LANES] = spread(p, onehots)
        tots.append(tot)
    tots = class_reduce(jnp.concatenate(tots, axis=0), jnp.add, heads)
    whole = 1.0 / tots
    lses = tops + jnp.log2(tots)
    for block in range(n_req):
        lse = jnp.zeros((sub, LANES), jnp.float32)
        for i in range(req_dev):
            n = block * req_dev + i
            values = pages_of(vf, slots_ref, n * slots, slots)
            acc = jnp.dot(p_s[n], values, preferred_element_type=jnp.float32)
            rows = slice(n * sub, (n + 1) * sub)
            for h in range(heads):
                some = acc[h * sub:(h + 1) * sub] * rows_of(whole[rows], h)
                out_ref[block, i * heads + h] = some.astype(jnp.bfloat16)
            lse = jnp.where(lane // (4 * heads) == i, lses[rows], lse)
        out_ref[block, req_dev * heads] = pieces_of(lse, heads)


def pieces_of(lse, heads):
    lane = lax.broadcasted_iota(jnp.int32, lse.shape, 1)
    kind = lane % (4 * heads) // heads
    high = lse.astype(jnp.bfloat16).astype(jnp.float32)
    rest = lse - high
    mid = rest.astype(jnp.bfloat16).astype(jnp.float32)
    both = jnp.where(kind == 1, mid, rest - mid)
    return jnp.where(kind == 0, high, both).astype(jnp.bfloat16)


def whole_of(pieces, heads):
    x = pieces.astype(jnp.float32)
    return x + pltpu.roll(x, LANES - heads, 1) + pltpu.roll(x, LANES - 2 * heads, 1)


def merge_kernel(*refs):
    many, *ones, out_ref = refs
    parts = [many.at[n] for n in range(many.shape[0])] + ones
    req_dev, heads, group, _ = out_ref.shape
    lses = [whole_of(part[req_dev * heads], heads) for part in parts]
    top = fold_max(lses)
    shares = [jnp.exp2(lse - top) for lse in lses]
    tot = shares[0]
    for share in shares[1:]:
        tot = tot + share
    shares = [share / tot for share in shares]
    for i in range(req_dev):
        for h in range(heads):
            at = i * 4 * heads + h
            total = jnp.zeros((group, LANES), jnp.float32)
            for part, share in zip(parts, shares):
                total = total + part[i * heads + h].astype(jnp.float32) * jnp.broadcast_to(
                    share[:, at:at + 1], (group, LANES))
            out_ref[i, h] = total.astype(jnp.bfloat16)


def params(mib):
    return pltpu.CompilerParams(vmem_limit_bytes=mib * 2**20)


def local(query, kv_pool, page_table, context_len, fresh_kv, fresh_bucket):
    n_ctx = lax.axis_size("ctx")
    n_req = lax.axis_size("req")
    req_dev, heads, group, head_dim = query.shape
    pool_slots, page = kv_pool.shape[:2]
    new_dev = fresh_kv.shape[0]
    pages_dev = page_table.shape[1]
    n_reqs = n_req * req_dev
    slots = CAP * n_ctx
    sub = n_ctx * group
    rows = heads * sub
    page_rows = page * heads

    smem = lambda count: jax.ShapeDtypeStruct((count,), jnp.int32)
    bf16 = lambda *shape: jax.ShapeDtypeStruct(shape, jnp.bfloat16)
    f32 = lambda *shape: jax.ShapeDtypeStruct(shape, jnp.float32)
    columns = pages_dev * page_rows
    split = heads % 4 == 0
    pieces = 8 if split else 0

    n_src = n_req * n_ctx
    everyone = ("req", "ctx")
    arrived = lax.all_to_all(
        jnp.broadcast_to(query, (n_src,) + query.shape), everyone, split_axis=0, concat_axis=0,
        tiled=True)
    if split:
        in_hbm = lambda a: pltpu.with_memory_space_constraint(a, pltpu.HBM)
        half = lambda count: bf16(count, page, heads, LANES)
        kb, vb, kf, vf, slot_table, counts = pl.pallas_call(
            functools.partial(stage_kernel, pieces, n_ctx, slots),
            out_shape=(
                half(pool_slots), half(pool_slots), half(new_dev), half(new_dev),
                smem(n_reqs * slots), smem(n_reqs)),
            in_specs=[HBM] * 3,
            out_specs=(VMEM,) * 4 + (SMEM,) * 2,
            scratch_shapes=[
                pltpu.SMEM((new_dev,), jnp.int32), pltpu.SemaphoreType.DMA((2, pieces)),
                pltpu.SemaphoreType.DMA((2, 1)), pltpu.SemaphoreType.DMA],
            compiler_params=params(2),
            cost_estimate=pl.CostEstimate(
                flops=0, transcendentals=0, bytes_accessed=4 * (kv_pool.size + fresh_kv.size)),
            name="stage",
        )(in_hbm(fresh_bucket), in_hbm(kv_pool), in_hbm(fresh_kv))
        kb, vb, kf, vf = (a.reshape(a.shape[0], page_rows, LANES) for a in (kb, vb, kf, vf))
    else:
        kb, vb, kf, vf = (
            a[..., h * LANES:(h + 1) * LANES].reshape(a.shape[0], page_rows, LANES)
            for a in (kv_pool, fresh_kv) for h in (0, 1)
        )
        slot_table, counts = pl.pallas_call(
            functools.partial(list_kernel, n_ctx, slots),
            out_shape=(smem(n_reqs * slots), smem(n_reqs)),
            in_specs=[SMEM],
            out_specs=(SMEM,) * 2,
            name="list",
        )(fresh_bucket)

    queries = arrived.reshape((n_req, n_ctx) + query.shape).transpose(0, 2, 3, 1, 4, 5)
    queries = queries.reshape(n_reqs, rows, head_dim)
    slabs = req_dev * heads + 1
    parts = pl.pallas_call(
        functools.partial(fresh_kernel, (heads, page_rows, slots, sub, n_req, req_dev)),
        out_shape=bf16(n_req, slabs, sub, LANES),
        in_specs=[SMEM] * 2 + [VMEM] * 3,
        out_specs=VMEM,
        scratch_shapes=[
            pltpu.VMEM((n_reqs, sub, slots * page_rows), jnp.float32),
            pltpu.VMEM((n_reqs, rows, slots * page_rows), jnp.bfloat16),
        ],
        compiler_params=params(8),
        cost_estimate=pl.CostEstimate(
            flops=4 * n_reqs * rows * slots * page_rows * LANES,
            transcendentals=n_reqs * sub * slots * page_rows, bytes_accessed=2 * fresh_kv.size),
        name="fresh",
    )(slot_table, counts, queries, kf, vf)
    sends = parts.reshape(n_req, slabs, n_ctx, group, LANES).transpose(0, 2, 1, 3, 4)
    sends = sends.reshape(n_src, slabs, group, LANES)
    sends, queries = lax.optimization_barrier((sends, queries))
    got = lax.all_to_all(sends, everyone, split_axis=0, concat_axis=0, tiled=True)

    mine = pl.pallas_call(
        functools.partial(
            resident_kernel, (heads, page_rows, pages_dev, sub, req_dev, n_ctx)),
        out_shape=bf16(n_ctx, slabs, group, LANES),
        in_specs=[SMEM] * 2 + [VMEM] * 3,
        out_specs=VMEM,
        scratch_shapes=[
            pltpu.VMEM((req_dev, sub, columns), jnp.float32),
            pltpu.VMEM((req_dev, sub, LANES), jnp.float32),
            pltpu.VMEM((req_dev, sub, LANES), jnp.float32),
            pltpu.VMEM((req_dev, rows, LANES), jnp.float32),
        ],
        compiler_params=params(5),
        cost_estimate=pl.CostEstimate(
            flops=4 * req_dev * rows * columns * LANES, transcendentals=req_dev * sub * columns,
            bytes_accessed=2 * kv_pool.size),
        name="resident",
    )(page_table.reshape(-1), context_len, queries, kb, vb)
    ones = [mine[0]] + [swap(mine[bits], "ctx", bits) for bits in range(1, n_ctx)]
    return pl.pallas_call(
        merge_kernel,
        out_shape=bf16(req_dev, heads, group, LANES),
        in_specs=[VMEM] * (1 + n_ctx),
        out_specs=VMEM,
        compiler_params=params(8),
        name="merge",
    )(got, *ones)


def solution(mesh):
    placed = (
        P("req", "kvh", "ctx", None),
        P(("req", "ctx"), None, "kvh", None),
        P("req", "ctx"),
        P("req"),
        P(("req", "ctx"), None, "kvh", None),
        P(("req", "ctx")),
    )
    return jax.shard_map(
        local, mesh=mesh, in_specs=placed, out_specs=P("req", "kvh", "ctx", None), check_vma=False
    )
```

time: 43 us -> 56.1 us (1.30)
  local copies, waits for them, and re-layouts: 0.99 us -> 17.9 us
  waiting for transfers between devices: 9.35 us -> 3.38 us
  starting transfers between devices: 13.6 us -> 15.5 us
    unnamed x6 -> x16, local copies, waits for them, and re-layouts: 0.66 us -> 16 us
    all_to_all x0 -> x2, starting transfers between devices: none -> 13.4 us  [the longest x1 7.36 us: local(): lax.all_to_all(jnp.broadcast_to(query, (n_src,) + query.shape), everyone,...]
    ppermute x12 -> x3, starting transfers between devices: 13.6 us -> 2.13 us  [swap(): lax.ppermute(value, axis, [(n, n ^ bit) for n in range(lax.axis_size(axis...]
    ppermute x12 -> x3, waiting for transfers between devices: 9.35 us -> 3.37 us  [swap(): lax.ppermute(value, axis, [(n, n ^ bit) for n in range(lax.axis_size(axis...]
    pallas_call x1, Pallas kernels: 5.69 us -> 7.61 us  [local(): pl.pallas_call(functools.partial(stage_kernel, pieces, n_ctx, slots), out...]
    broadcast_in_dim x0 -> x1, local copies, waits for them, and re-layouts: none -> 1.54 us  [local(): jnp.broadcast_to(query, (n_src,) + query.shape)]
    pallas_call x1, Pallas kernels: 8.07 us -> 6.62 us  [local(): pl.pallas_call(functools.partial(resident_kernel, (heads, page_rows, page...]
    concatenate x0 -> x1, other arithmetic: none -> 0.92 us
  transfers between devices with their start and end apart: 12 -> 5, of which waited for: 5 -> 2; matrix products, arithmetic and copies ran while one was open for 2% -> 0% of each run, Pallas kernels for 32% -> 26%
where the time goes in v6:
time: 56.1 us; the launch traced here: 55.7 us
  local copies, waits for them, and re-layouts  17.9 us (32%)
  Pallas kernels  17.9 us (32%)
  starting transfers between devices  15.5 us (28%)
  waiting for transfers between devices  3.38 us (6%)
  other arithmetic  0.92 us (2%)
    unnamed x16, local copies, waits for them, and re-layouts  16 us
    pallas_call x1, Pallas kernels, local(): pl.pallas_call(functools.partial(stage_kernel, pieces, n_ctx, slots), out...  7.61 us
    all_to_all x1, starting transfers between devices, local(): lax.all_to_all(jnp.broadcast_to(query, (n_src,) + query.shape), everyone,...  7.36 us
    pallas_call x1, Pallas kernels, local(): pl.pallas_call(functools.partial(resident_kernel, (heads, page_rows, page...  6.62 us
    all_to_all x1, starting transfers between devices, local(): lax.all_to_all(sends, everyone, split_axis=0, concat_axis=0, tiled=True)  6 us
    ppermute x3, waiting for transfers between devices, swap(): lax.ppermute(value, axis, [(n, n ^ bit) for n in range(lax.axis_size(axis...  3.37 us
    pallas_call x1, Pallas kernels, local(): pl.pallas_call(functools.partial(fresh_kernel, (heads, page_rows, slots,...  2.46 us
    ppermute x3, starting transfers between devices, swap(): lax.ppermute(value, axis, [(n, n ^ bit) for n in range(lax.axis_size(axis...  2.13 us
  transfers between devices with their start and end apart: 5, of which 2 were waited for; matrix products, arithmetic and copies ran while one was open for 0% of the time, Pallas kernels for 26%

profile of v6, /device:TPU:0, one launch (start us, length us, event | category | flops | bytes accessed | tf_op | source)
XLA Modules:
  0.0 55.7 jit_solution(6757184420147765747)
XLA Ops:
  0.0 1.5 %broadcast_in_dim.3 = bf16[16,4,4,4,128]{4,3,2,1,0:T(4,128)(2,1)} broadcast(bf16[4,4,4,128]{3,2,1,0:T(4,128)(2,1)} %param.6), dimensions={1,2,3,4} | broadcast | bytes 278528 | tf_op jit(solution)/shard_map/broadcast_in_dim | solution.py:289
  1.5 7.4 %all-to-all-start = ((bf16[16,4,4,4,128]{4,3,2,1,0:T(4,128)(2,1)}), bf16[16,4,4,4,128]{4,3,2,1,0:T(4,128)(2,1)S(1)}, u32[]{:S(2)}, u32[]{:S(2)}) async-start(bf16[16,4,4,4,128]{4,3,2,1,0:T(4,128)(2,1)} %broadcast_in_dim.3), calls=%async_computation | async-start | bytes 524288 | tf_op jit(solution)/shard_map/all_to_all | solution.py:288
  8.9 0.0 copy-start.6
  8.9 0.0 copy-start.7
  8.9 7.6 %stage.1 = (bf16[512,16,4,128]{3,2,1,0:T(4,128)(2,1)S(1)}, bf16[512,16,4,128]{3,2,1,0:T(4,128)(2,1)S(1)}, bf16[112,16,4,128]{3,2,1,0:T(4,128)(2,1)S(1)}, bf16[11...) custom-call(s32[112]{0:T(128)} %bucket_hbm.1, bf16[512,16,4,256]{3,2,1,0:T(4,128)(2,1)} %pool_ref.1, ...), custom_call_target="tpu_custom_call" | custom-call | bytes 40894464 | tf_op jit(solution)/shard_map/stage/pallas_call | solution.py:294
  16.6 3.2 %copy-done = bf16[512,16,4,128]{3,2,1,0:T(4,128)(2,1)} copy-done((bf16[512,16,4,128]{3,2,1,0:T(4,128)(2,1)}, bf16[512,16,4,128]{3,2,1,0:T(4,128)(2,1)S(1)}, u32[]{:S(2)}) %copy-start) | copy-done | bytes 8388632
  19.8 3.2 %copy-done.2 = bf16[512,16,4,128]{3,2,1,0:T(4,128)(2,1)} copy-done((bf16[512,16,4,128]{3,2,1,0:T(4,128)(2,1)}, bf16[512,16,4,128]{3,2,1,0:T(4,128)(2,1)S(1)}, u32[]{:S(2)}) %copy-start.2) | copy-done | bytes 8388632
  23.0 1.3 %copy-done.4 = bf16[112,16,4,128]{3,2,1,0:T(4,128)(2,1)} copy-done((bf16[112,16,4,128]{3,2,1,0:T(4,128)(2,1)}, bf16[112,16,4,128]{3,2,1,0:T(4,128)(2,1)S(1)}, u32[]{:S(2)}) %copy-start.4) | copy-done | bytes 1835032
  24.3 0.0 all-to-all-done
  24.3 0.2 copy.8
  24.5 0.1 copy.9
  24.6 1.5 %copy-done.5 = bf16[112,16,4,128]{3,2,1,0:T(4,128)(2,1)S(1)} copy-done((bf16[112,16,4,128]{3,2,1,0:T(4,128)(2,1)S(1)}, bf16[112,16,4,128]{3,2,1,0:T(4,128)(2,1)}, u32[]{:S(2)}) %copy-start.5) | copy-done | bytes 1835032
  26.1 2.5 %fresh.1 = bf16[4,17,16,128]{3,2,1,0:T(8,128)(2,1)S(1)} custom-call(s32[128]{0:T(128)S(1)} %get-tuple-element.13.slots_ref, s32[16]{0:T(128)S(1)} %get-tuple-element.14.counts_ref, bf16[16,64,128]{2,1,0:T(8,128)(2,1)S(1)} %bitcast.20, bf16[112,64,128]{2,1,0:T(8,128)(2,1)S(1)} %bitcast.22, bf16[112,64,128]{2,1,0:T(8,128)(2,1)S(1)} %bitcast.23), custom_call_target="tpu_custom_call" | custom-call | flops 268435456 | bytes 3670016 | tf_op jit(solution)/shard_map/fresh/pallas_call | solution.py:326
  28.6 0.1 fusion
  28.7 0.9 %pad_maximum_fusion = bf16[4,68,4,128]{3,2,1,0:T(4,128)(2,1)} fusion(bf16[4,17,4,128]{3,2,1,0:T(4,128)(2,1)S(1)} %get-tuple-element.22, bf16[4,17,4,128]{3,2,1,0:T(4,128)(2,1)S(1)} %get-tuple-element.23, bf16[4,17,4,128]{3,2,1,0:T(4,128)(2,1)S(1)} %get-tuple-element.24, bf16[4,17,4,128]{3,2,1,0:T(4,128)(2,1)S(1)} %get-tuple-element.21), kind=kLoop, calls=%fused_computation | loop fusion | flops 417792 | bytes 557056 | tf_op jit(solution)/shard_map/concatenate
  29.6 6.0 %all-to-all-start.1 = ((bf16[16,17,4,128]{3,2,1,0:T(4,128)(2,1)}), bf16[16,17,4,128]{3,2,1,0:T(4,128)(2,1)S(1)}, u32[]{:S(2)}, u32[]{:S(2)}) async-start(bf16[16,17,4,128]{3,2,1,0:T(4,128)(2,1)} %bitcast.5), calls=%async_computation.1 | async-start | bytes 557056 | tf_op jit(solution)/shard_map/all_to_all | solution.py:344
  35.6 3.4 %copy-done.1 = bf16[512,16,4,128]{3,2,1,0:T(4,128)(2,1)S(1)} copy-done((bf16[512,16,4,128]{3,2,1,0:T(4,128)(2,1)S(1)}, bf16[512,16,4,128]{3,2,1,0:T(4,128)(2,1)}, u32[]{:S(2)}) %copy-start.1) | copy-done | bytes 8388632
  39.0 3.4 %copy-done.3 = bf16[512,16,4,128]{3,2,1,0:T(4,128)(2,1)S(1)} copy-done((bf16[512,16,4,128]{3,2,1,0:T(4,128)(2,1)S(1)}, bf16[512,16,4,128]{3,2,1,0:T(4,128)(2,1)}, u32[]{:S(2)}) %copy-start.3) | copy-done | bytes 8388632
  42.4 6.6 %resident.1 = bf16[4,17,4,128]{3,2,1,0:T(4,128)(2,1)S(1)} custom-call(s32[512]{0:T(512)S(1)} %bitcast.24, s32[4]{0:T(128)S(1)} %copy-done.7, bf16[16,64,128]{2,1,0:T(8,128)(2,1)S(1)} %bitcast.21, bf16[512,64,128]{2,1,0:T(8,128)(2,1)S(1)} %bitcast.18, bf16[512,64,128]{2,1,0:T(8,128)(2,1)S(1)} %bitcast.19), custom_call_target="tpu_custom_call" | custom-call | flops 1073741824 | bytes 16777216 | tf_op jit(solution)/shard_map/resident/pallas_call | solution.py:346
  49.0 1.7 %collective-permute-start.2 = (bf16[17,4,128]{2,1,0:T(4,128)(2,1)S(1)}, bf16[17,4,128]{2,1,0:T(4,128)(2,1)S(1)}, u32[]{:S(2)}, u32[]{:S(2)}) collective-permute-start(bf16[17,4,128]{2,1,0:T(4,128)(2,1)S(1)} %get-tuple-element.25), channel_id=1, source_target_pairs={{0,6},{2,4},{4,2},{6,0},{1,7},{3,5},{5,3},{7,1},{8,14},{10,12},{12... | collective-permute-start | bytes 52232 | tf_op jit(solution)/shard_map/ppermute | solution.py:23
  50.8 0.4 collective-permute-start.1
  51.1 1.1 %collective-permute-done.2.refs_4_ = bf16[17,4,128]{2,1,0:T(4,128)(2,1)S(1)} collective-permute-done((bf16[17,4,128]{2,1,0:T(4,128)(2,1)S(1)}, bf16[17,4,128]{2,1,0:T(4,128)(2,1)S(1)}, u32[]{:S(2)}, u32[]{:S(2)}) %collective-permute-start.2) | collective-permute-done | bytes 17440 | tf_op jit(solution)/shard_map/ppermute | solution.py:23
  52.3 2.3 %collective-permute-done.1.refs_3_ = bf16[17,4,128]{2,1,0:T(4,128)(2,1)S(1)} collective-permute-done((bf16[17,4,128]{2,1,0:T(4,128)(2,1)S(1)}, bf16[17,4,128]{2,1,0:T(4,128)(2,1)S(1)}, u32[]{:S(2)}, u32[]{:S(2)}) %collective-permute-start.1) | collective-permute-done | bytes 17440 | tf_op jit(solution)/shard_map/ppermute | solution.py:23
  54.5 1.2 %merge.1 = bf16[4,4,4,128]{3,2,1,0:T(4,128)(2,1)} custom-call(bf16[16,17,4,128]{3,2,1,0:T(4,128)(2,1)S(1)} %all-to-all-done.1.refs_0_, bf16[17,4,128]{2,1,0:T(4,128)(2,1)S(1)} %get-tuple-element.28.refs_1_, bf16[17,4,128]{2,1,0:T(4,128)(2,1)S(1)} %collective-permute-done.refs_2_, bf16[17,4,128]{2,1,0:T(4,128)(2,1)S(1)} %collective-permute-done.1.refs_3_, ...), custom_call_target="tpu_custom_call" | custom-call | tf_op jit(solution)/shard_map/merge/pallas_call | solution.py:365
  (12 shorter events, 0.1 us)
Async XLA Ops:
  1.5 22.7 %all-to-all-start = ((bf16[16,4,4,4,128]{4,3,2,1,0:T(4,128)(2,1)}), bf16[16,4,4,4,128]{4,3,2,1,0:T(4,128)(2,1)S(1)}, u32[]{:S(2)}, u32[]{:S(2)}) async-start(bf16[16,4,4,4,128]{4,3,2,1,0:T(4,128)(2,1)} %broadcast_in_dim.3), calls=%async_computation | async-start | bytes 524288 | tf_op jit(solution)/shard_map/all_to_all | solution.py:288
  8.9 26.7 %copy-start.6 = (s32[4,128]{1,0:T(4,128)S(1)}, s32[4,128]{1,0:T(4,128)}, u32[]{:S(2)}) copy-start(s32[4,128]{1,0:T(4,128)} %param.8) | copy-start | bytes 6148
  8.9 26.7 %copy-start.7 = (s32[4]{0:T(128)S(1)}, s32[4]{0:T(128)}, u32[]{:S(2)}) copy-start(s32[4]{0:T(128)} %len_ref.1) | copy-start | bytes 52
  16.6 3.2 %copy-start = (bf16[512,16,4,128]{3,2,1,0:T(4,128)(2,1)}, bf16[512,16,4,128]{3,2,1,0:T(4,128)(2,1)S(1)}, u32[]{:S(2)}) copy-start(bf16[512,16,4,128]{3,2,1,0:T(4,128)(2,1)S(1)} %get-tuple-element.19) | copy-start | bytes 25165828
  19.8 3.2 %copy-start.2 = (bf16[512,16,4,128]{3,2,1,0:T(4,128)(2,1)}, bf16[512,16,4,128]{3,2,1,0:T(4,128)(2,1)S(1)}, u32[]{:S(2)}) copy-start(bf16[512,16,4,128]{3,2,1,0:T(4,128)(2,1)S(1)} %get-tuple-element.20) | copy-start | bytes 25165828
  23.0 1.3 %copy-start.4 = (bf16[112,16,4,128]{3,2,1,0:T(4,128)(2,1)}, bf16[112,16,4,128]{3,2,1,0:T(4,128)(2,1)S(1)}, u32[]{:S(2)}) copy-start(bf16[112,16,4,128]{3,2,1,0:T(4,128)(2,1)S(1)} %get-tuple-element.16) | copy-start | bytes 5505028
  24.6 1.5 %copy-start.5 = (bf16[112,16,4,128]{3,2,1,0:T(4,128)(2,1)S(1)}, bf16[112,16,4,128]{3,2,1,0:T(4,128)(2,1)}, u32[]{:S(2)}) copy-start(bf16[112,16,4,128]{3,2,1,0:T(4,128)(2,1)} %copy-done.4) | copy-start | bytes 5505028
  29.6 25.0 %all-to-all-start.1 = ((bf16[16,17,4,128]{3,2,1,0:T(4,128)(2,1)}), bf16[16,17,4,128]{3,2,1,0:T(4,128)(2,1)S(1)}, u32[]{:S(2)}, u32[]{:S(2)}) async-start(bf16[16,17,4,128]{3,2,1,0:T(4,128)(2,1)} %bitcast.5), calls=%async_computation.1 | async-start | bytes 557056 | tf_op jit(solution)/shard_map/all_to_all | solution.py:344
  35.6 3.4 %copy-start.1 = (bf16[512,16,4,128]{3,2,1,0:T(4,128)(2,1)S(1)}, bf16[512,16,4,128]{3,2,1,0:T(4,128)(2,1)}, u32[]{:S(2)}) copy-start(bf16[512,16,4,128]{3,2,1,0:T(4,128)(2,1)} %copy-done) | copy-start | bytes 25165828
  39.0 3.4 %copy-start.3 = (bf16[512,16,4,128]{3,2,1,0:T(4,128)(2,1)S(1)}, bf16[512,16,4,128]{3,2,1,0:T(4,128)(2,1)}, u32[]{:S(2)}) copy-start(bf16[512,16,4,128]{3,2,1,0:T(4,128)(2,1)} %copy-done.2) | copy-start | bytes 25165828
  49.0 3.2 %collective-permute-start.2 = (bf16[17,4,128]{2,1,0:T(4,128)(2,1)S(1)}, bf16[17,4,128]{2,1,0:T(4,128)(2,1)S(1)}, u32[]{:S(2)}, u32[]{:S(2)}) collective-permute-start(bf16[17,4,128]{2,1,0:T(4,128)(2,1)S(1)} %get-tuple-element.25), channel_id=1, source_target_pairs={{0,6},{2,4},{4,2},{6,0},{1,7},{3,5},{5,3},{7,1},{8,14},{10,12},{12... | collective-permute-start | bytes 52232 | tf_op jit(solution)/shard_map/ppermute | solution.py:23
  50.8 3.8 %collective-permute-start.1 = (bf16[17,4,128]{2,1,0:T(4,128)(2,1)S(1)}, bf16[17,4,128]{2,1,0:T(4,128)(2,1)S(1)}, u32[]{:S(2)}, u32[]{:S(2)}) collective-permute-start(bf16[17,4,128]{2,1,0:T(4,128)(2,1)S(1)} %get-tuple-element.26), channel_id=1, source_target_pairs={{0,4},{2,6},{4,0},{6,2},{1,5},{3,7},{5,1},{7,3},{8,12},{10,14},{12... | collective-permute-start | bytes 52232 | tf_op jit(solution)/shard_map/ppermute | solution.py:23
  51.1 3.4 %collective-permute-start = (bf16[17,4,128]{2,1,0:T(4,128)(2,1)S(1)}, bf16[17,4,128]{2,1,0:T(4,128)(2,1)S(1)}, u32[]{:S(2)}, u32[]{:S(2)}) collective-permute-start(bf16[17,4,128]{2,1,0:T(4,128)(2,1)S(1)} %get-tuple-element.27), channel_id=1, source_target_pairs={{0,2},{2,0},{4,6},{6,4},{1,3},{3,1},{5,7},{7,5},{8,10},{10,8},{12,... | collective-permute-start | bytes 52232 | tf_op jit(solution)/shard_map/ppermute | solution.py:23

commit v7 on v5

v7 whole, which is shorter than its diff:
```python
import functools
import math

import jax
import jax.numpy as jnp
from jax import lax
from jax.experimental import pallas as pl
from jax.experimental.pallas import tpu as pltpu
from jax.sharding import PartitionSpec as P

NEG = -1e30
CAP = 2
LANES = 128
SCALE = math.log2(math.e) / math.sqrt(LANES)
SCORE_WIDE = 256
VALUE_WIDE = 512
VMEM = pl.BlockSpec(memory_space=pltpu.VMEM)
SMEM = pl.BlockSpec(memory_space=pltpu.SMEM)
HBM = pl.BlockSpec(memory_space=pltpu.HBM)


def swap(value, axis, bit):
    return lax.ppermute(value, axis, [(n, n ^ bit) for n in range(lax.axis_size(axis))])


def bits_of(axis):
    bit = lax.axis_size(axis) // 2
    while bit:
        yield bit
        bit //= 2


def half_copies(pool_ref, target, sem, half, pieces):
    each = pool_ref.shape[0] // pieces
    return [
        pltpu.make_async_copy(
            pool_ref.at[pl.ds(n * each, each), :, :, pl.ds(half * LANES, LANES)],
            target.at[pl.ds(n * each, each)], sem.at[n])
        for n in range(pieces)
    ]


def stage_fresh_kernel(fresh_ref, kf, vf, sem):
    copies = []
    for half, to in enumerate((kf, vf)):
        copies += half_copies(fresh_ref, to, sem.at[half], half, sem.shape[1])
    for one in copies:
        one.start()
    for one in copies:
        one.wait()


def stage_keys_kernel(
    n_ctx, slots, bucket_hbm, pool_ref, kb, slots_ref, counts_ref, bucket_ref, sem, bucket_sem,
):
    listed = pltpu.make_async_copy(bucket_hbm, bucket_ref, bucket_sem)
    copies = half_copies(pool_ref, kb, sem, 0, sem.shape[0])
    listed.start()
    for one in copies:
        one.start()
    listed.wait()
    list_fresh(n_ctx, slots, bucket_ref, slots_ref, counts_ref)
    for one in copies:
        one.wait()


def list_kernel(n_ctx, slots, bucket_ref, slots_ref, counts_ref):
    list_fresh(n_ctx, slots, bucket_ref, slots_ref, counts_ref)


def list_fresh(n_ctx, slots, bucket_ref, slots_ref, counts_ref):
    for n in range(counts_ref.shape[0]):
        counts_ref[n] = 0
    for n in range(slots_ref.shape[0]):
        slots_ref[n] = 0

    def put(page, _):
        request = bucket_ref[page] // n_ctx
        count = counts_ref[request]
        slots_ref[request * slots + count] = page
        counts_ref[request] = count + 1
        return 0

    lax.fori_loop(0, bucket_ref.shape[0], put, 0)


def class_reduce(x, op, heads):
    step = heads
    while step < LANES:
        x = op(x, pltpu.roll(x, step, 1))
        step *= 2
    return x


def pages_of(ref, table_ref, first, count):
    return jnp.concatenate([ref[table_ref[first + n]] for n in range(count)], axis=0)


def score_parts(q, keys, lane, limit, first, heads, sub):
    s = lax.dot_general(q, keys, (((1,), (1,)), ((), ())), preferred_element_type=jnp.float32)
    out = []
    for j in range(s.shape[1] // LANES):
        part = s[:, j * LANES:(j + 1) * LANES]
        one = part[:sub]
        for h in range(1, heads):
            one = jnp.where(lane % heads == h, part[h * sub:(h + 1) * sub], one)
        out.append(jnp.where(lane < limit - (first + j * LANES), one * SCALE, NEG))
    return out


def spread(p, onehots):
    p = p.astype(jnp.bfloat16)
    return jnp.concatenate([p * one for one in onehots], axis=0)


def rows_of(x, h):
    return jnp.broadcast_to(x[:, h:h + 1], x.shape)


def fold_max(parts):
    top = parts[0]
    for part in parts[1:]:
        top = jnp.maximum(top, part)
    return top


def score_kernel(dims, table_ref, len_ref, q_ref, kb, *refs):
    heads, page_rows, pages_dev, sub, pieces = dims
    copies = []
    if pieces:
        pool_ref, t_ref, top_ref, vb, sem = refs
        copies = half_copies(pool_ref, vb, sem, 1, pieces)
    else:
        t_ref, top_ref = refs
    for one in copies:
        one.start()
    columns = pages_dev * page_rows
    wide = min(SCORE_WIDE, columns)
    per = wide // page_rows
    lane = lax.broadcasted_iota(jnp.int32, (sub, LANES), 1)
    start = lax.axis_index("ctx") * (pages_dev * page_rows)

    def step(i, _):
        top = jnp.full((sub, LANES), NEG, jnp.float32)
        limit = len_ref[i] * heads - start
        for c in range(columns // wide):
            keys = pages_of(kb, table_ref, i * pages_dev + c * per, per)
            parts = score_parts(q_ref[i], keys, lane, limit, c * wide, heads, sub)
            for j, part in enumerate(parts):
                t_ref[i, :, c * wide + j * LANES:c * wide + (j + 1) * LANES] = part
            top = jnp.maximum(top, fold_max(parts))
        top_ref[i] = top
        return 0

    shape = top_ref.shape
    flat = (shape[0] * shape[1], LANES)
    lax.fori_loop(0, shape[0], step, 0)
    top_ref[...] = class_reduce(top_ref[...].reshape(flat), jnp.maximum, heads).reshape(shape)
    for one in copies:
        one.wait()


def value_kernel(
    dims, table_ref, t_ref, top_ref, vb, acc_ref, ftop_ref, ftot_ref, keep_ref, send_ref,
    acc_s, tot_s,
):
    heads, page_rows, pages_dev, sub = dims
    req_dev = t_ref.shape[0]
    columns = pages_dev * page_rows
    wide = min(VALUE_WIDE, columns)
    per = wide // page_rows
    lane = lax.broadcasted_iota(jnp.int32, (sub, LANES), 1)
    onehots = [(lane % heads == h).astype(jnp.bfloat16) for h in range(heads)]

    def step(i, _):
        tot = jnp.zeros((sub, LANES), jnp.float32)
        acc = jnp.zeros((heads * sub, LANES), jnp.float32)
        top = top_ref[i]
        for c in range(columns // wide):
            weights = []
            for j in range(wide // LANES):
                at = c * wide + j * LANES
                p = jnp.exp2(t_ref[i, :, at:at + LANES] - top)
                tot = tot + p
                weights.append(spread(p, onehots))
            values = pages_of(vb, table_ref, i * pages_dev + c * per, per)
            acc = acc + jnp.dot(
                jnp.concatenate(weights, axis=1), values, preferred_element_type=jnp.float32)
        acc_s[i] = acc
        tot_s[i] = tot
        return 0

    lax.fori_loop(0, req_dev, step, 0)
    flat = (req_dev * sub, LANES)
    tots = class_reduce(tot_s[...].reshape(flat), jnp.add, heads)
    top, ftop = top_ref[...].reshape(flat), ftop_ref[...].reshape(flat)
    both = jnp.maximum(top, ftop)
    fade, ffade = jnp.exp2(top - both), jnp.exp2(ftop - both)
    tots = tots * fade + ftot_ref[...].reshape(flat) * ffade
    fade, ffade = fade / tots, ffade / tots
    lses = both + jnp.log2(tots)
    for i in range(req_dev):
        rows = slice(i * sub, (i + 1) * sub)
        for h in range(heads):
            part = slice(h * sub, (h + 1) * sub)
            some = acc_s[i, part, :] * rows_of(fade[rows], h)
            some = some + acc_ref[i, part, :] * rows_of(ffade[rows], h)
            put_rows(keep_ref, send_ref, (0, i * heads + h), some)
    lse = by_request(lses, heads, sub, range(req_dev))
    put_rows(keep_ref, send_ref, (0, req_dev * heads), lse, heads)


def put_rows(keep_ref, send_ref, place, value, heads=0):
    half = value.shape[0] // 2
    send = value[half:]
    keep_ref[place] = value[:half]
    send_ref[place] = pieces_of(send, heads) if heads else send.astype(jnp.bfloat16)


def by_request(lses, heads, sub, requests):
    lane = lax.broadcasted_iota(jnp.int32, (sub, LANES), 1)
    out = jnp.zeros((sub, LANES), jnp.float32)
    for i, n in enumerate(requests):
        out = jnp.where(lane // (4 * heads) == i, lses[n * sub:(n + 1) * sub], out)
    return out


def fresh_kernel(
    dims, slots_ref, counts_ref, *refs,
):
    heads, page_rows, slots, sub, req_dev = dims
    *q_refs, kf, vf, keep_ref, send_ref, acc_ref, top_ref, tot_ref, t_s, p_s = refs
    lane = lax.broadcasted_iota(jnp.int32, (sub, LANES), 1)
    onehots = [(lane % heads == h).astype(jnp.bfloat16) for h in range(heads)]
    columns = slots * page_rows
    wide = min(SCORE_WIDE, columns)
    per = wide // page_rows
    own = lax.axis_index("req")
    requests = [(own ^ k) * req_dev + i for k in range(len(q_refs)) for i in range(req_dev)]
    n_reqs = len(requests)
    tops = []
    for n, request in enumerate(requests):
        limit = counts_ref[request] * page_rows
        top = jnp.full((sub, LANES), NEG, jnp.float32)
        for c in range(columns // wide):
            keys = pages_of(kf, slots_ref, request * slots + c * per, per)
            q = q_refs[n // req_dev][n % req_dev]
            parts = score_parts(q, keys, lane, limit, c * wide, heads, sub)
            for j, part in enumerate(parts):
                t_s[n, :, c * wide + j * LANES:c * wide + (j + 1) * LANES] = part
            top = jnp.maximum(top, fold_max(parts))
        tops.append(top)
    tops = class_reduce(jnp.concatenate(tops, axis=0), jnp.maximum, heads)
    tots = []
    for n in range(n_reqs):
        tot = jnp.zeros((sub, LANES), jnp.float32)
        for j in range(columns // LANES):
            p = jnp.exp2(
                t_s[n, :, j * LANES:(j + 1) * LANES] - tops[n * sub:(n + 1) * sub])
            tot = tot + p
            p_s[n, :, j * LANES:(j + 1) * LANES] = spread(p, onehots)
        tots.append(tot)
    tots = class_reduce(jnp.concatenate(tots, axis=0), jnp.add, heads)
    whole = 1.0 / tots
    lses = tops + jnp.log2(tots)
    for n, request in enumerate(requests):
        values = pages_of(vf, slots_ref, request * slots, slots)
        acc = jnp.dot(p_s[n], values, preferred_element_type=jnp.float32)
        rows = slice(n * sub, (n + 1) * sub)
        block, i = n // req_dev - 1, n % req_dev
        if block < 0:
            acc_ref[i] = acc
            top_ref[i] = tops[rows]
            tot_ref[i] = tots[rows]
            continue
        for h in range(heads):
            some = acc[h * sub:(h + 1) * sub] * rows_of(whole[rows], h)
            put_rows(keep_ref, send_ref, (block, i * heads + h), some)
    for block in range(len(q_refs) - 1):
        first = (block + 1) * req_dev
        lse = by_request(lses, heads, sub, range(first, first + req_dev))
        put_rows(keep_ref, send_ref, (block, req_dev * heads), lse, heads)


def pieces_of(lse, heads):
    lane = lax.broadcasted_iota(jnp.int32, lse.shape, 1)
    kind = lane % (4 * heads) // heads
    high = lse.astype(jnp.bfloat16).astype(jnp.float32)
    rest = lse - high
    mid = rest.astype(jnp.bfloat16).astype(jnp.float32)
    both = jnp.where(kind == 1, mid, rest - mid)
    return jnp.where(kind == 0, high, both).astype(jnp.bfloat16)


def whole_of(pieces, heads):
    x = pieces.astype(jnp.float32)
    lane = lax.broadcasted_iota(jnp.int32, x.shape, 1)
    kind = lane % (4 * heads) // heads
    x = x + pltpu.roll(x, LANES - heads, 1) + pltpu.roll(x, LANES - 2 * heads, 1)
    same = x
    for m in (1, 2):
        same = jnp.where(kind == m, pltpu.roll(x, m * heads, 1), same)
    return same


def merge_kernel(heads, skip, goals, keep_ref, got_ref, *outs):
    blocks, slabs, rows, _ = keep_ref.shape
    slabs -= 1

    def put(block, slab, value, coded=0):
        if goals[block] is None:
            put_rows(outs[0], outs[1], (block, slab), value, coded)
        else:
            which, place = goals[block]
            if outs[which].dtype == jnp.bfloat16:
                value = pieces_of(value, coded) if coded else value.astype(jnp.bfloat16)
            outs[which][place, slab] = value

    for block in range(blocks):
        own = keep_ref[block, slabs]
        other = whole_of(got_ref[block + skip, slabs], heads)
        top = jnp.maximum(own, other)
        share = jnp.exp2(own - top)
        tot = share + jnp.exp2(other - top)
        share = share / tot
        for slab in range(slabs):
            at = slab // heads * 4 * heads + slab % heads
            part = jnp.broadcast_to(share[:, at:at + 1], (rows, LANES))
            kept = keep_ref[block, slab]
            got = got_ref[block + skip, slab].astype(jnp.float32)
            put(block, slab, part * kept + (1.0 - part) * got)
        put(block, slabs, top + jnp.log2(tot), heads)


def last_kernel(keep_ref, *refs):
    *got_refs, out_ref = refs
    req_dev, heads, group, _ = out_ref.shape
    slabs = req_dev * heads
    parts = [keep_ref.at[0]] + [ref.at[0] for ref in got_refs]
    lses = [keep_ref[0, slabs]] + [whole_of(ref[0, slabs], heads) for ref in got_refs]
    top = fold_max(lses)
    shares = [jnp.exp2(lse - top) for lse in lses]
    tot = shares[0]
    for share in shares[1:]:
        tot = tot + share
    shares = [share / tot for share in shares]
    for slab in range(slabs):
        at = slab // heads * 4 * heads + slab % heads
        total = jnp.zeros((group, LANES), jnp.float32)
        for part, share in zip(parts, shares):
            total = total + part[slab].astype(jnp.float32) * jnp.broadcast_to(
                share[:, at:at + 1], (group, LANES))
        out_ref[slab // heads, slab % heads] = total.astype(jnp.bfloat16)


def params(mib):
    return pltpu.CompilerParams(vmem_limit_bytes=mib * 2**20)


def local(query, kv_pool, page_table, context_len, fresh_kv, fresh_bucket):
    n_ctx = lax.axis_size("ctx")
    n_req = lax.axis_size("req")
    req_dev, heads, group, head_dim = query.shape
    pool_slots, page = kv_pool.shape[:2]
    new_dev = fresh_kv.shape[0]
    pages_dev = page_table.shape[1]
    n_reqs = n_req * req_dev
    slots = CAP * n_ctx
    sub = n_ctx * group
    rows = heads * sub
    page_rows = page * heads

    smem = lambda count: jax.ShapeDtypeStruct((count,), jnp.int32)
    bf16 = lambda *shape: jax.ShapeDtypeStruct(shape, jnp.bfloat16)
    f32 = lambda *shape: jax.ShapeDtypeStruct(shape, jnp.float32)
    columns = pages_dev * page_rows
    split = heads % 4 == 0
    pieces = 8 if split else 0

    near = query[None]
    first, *others = bits_of("ctx")
    arrived = swap(near, "ctx", first)
    if split:
        in_hbm = lambda a: pltpu.with_memory_space_constraint(a, pltpu.HBM)
        pool = in_hbm(kv_pool)
        half = lambda count: bf16(count, page, heads, LANES)
        kf, vf = pl.pallas_call(
            stage_fresh_kernel,
            out_shape=(half(new_dev), half(new_dev)),
            in_specs=[HBM],
            out_specs=(VMEM,) * 2,
            scratch_shapes=[pltpu.SemaphoreType.DMA((2, 4))],
            compiler_params=params(2),
            cost_estimate=pl.CostEstimate(
                flops=0, transcendentals=0, bytes_accessed=4 * fresh_kv.size),
            name="stage_fresh",
        )(in_hbm(fresh_kv))
        arrived, kf = lax.optimization_barrier((arrived, kf))
        kb, slot_table, counts = pl.pallas_call(
            functools.partial(stage_keys_kernel, n_ctx, slots),
            out_shape=(half(pool_slots), smem(n_reqs * slots), smem(n_reqs)),
            in_specs=[HBM] * 2,
            out_specs=(VMEM, SMEM, SMEM),
            scratch_shapes=[
                pltpu.SMEM((new_dev,), jnp.int32), pltpu.SemaphoreType.DMA((pieces,)),
                pltpu.SemaphoreType.DMA],
            compiler_params=params(2),
            cost_estimate=pl.CostEstimate(
                flops=0, transcendentals=0, bytes_accessed=2 * kv_pool.size),
            name="stage_keys",
        )(in_hbm(fresh_bucket), pool)
        kb, kf, vf = (a.reshape(a.shape[0], page_rows, LANES) for a in (kb, kf, vf))
        score_in, score_specs, score_out = (pool,), [HBM], (half(pool_slots),)
        score_scratch = [pltpu.SemaphoreType.DMA((pieces,))]
    else:
        kb, vb, kf, vf = (
            a[..., h * LANES:(h + 1) * LANES].reshape(a.shape[0], page_rows, LANES)
            for a in (kv_pool, fresh_kv) for h in (0, 1)
        )
        slot_table, counts = pl.pallas_call(
            functools.partial(list_kernel, n_ctx, slots),
            out_shape=(smem(n_reqs * slots), smem(n_reqs)),
            in_specs=[SMEM],
            out_specs=(SMEM,) * 2,
            name="list",
        )(fresh_bucket)
        score_in, score_specs, score_out, score_scratch = (), [], (), []

    near = jnp.concatenate([near, arrived])
    for bit in others:
        near = jnp.concatenate([near, swap(near, "ctx", bit)])
    q_own = near.transpose(1, 2, 0, 3, 4).reshape(req_dev, rows, head_dim)
    far = [q_own] + [swap(q_own, "req", k) for k in range(n_req - 1, 0, -1)][::-1]

    slabs = req_dev * heads + 1
    left = sub // 2
    keep, send, acc, ftop, ftot = pl.pallas_call(
        functools.partial(fresh_kernel, (heads, page_rows, slots, sub, req_dev)),
        out_shape=(
            f32(n_req - 1, slabs, left, LANES), bf16(n_req - 1, slabs, left, LANES),
            f32(req_dev, rows, LANES), f32(req_dev, sub, LANES), f32(req_dev, sub, LANES)),
        in_specs=[SMEM] * 2 + [VMEM] * (2 + n_req),
        out_specs=(VMEM,) * 5,
        scratch_shapes=[
            pltpu.VMEM((n_reqs, sub, slots * page_rows), jnp.float32),
            pltpu.VMEM((n_reqs, rows, slots * page_rows), jnp.bfloat16),
        ],
        compiler_params=params(8),
        cost_estimate=pl.CostEstimate(
            flops=4 * n_reqs * rows * slots * page_rows * LANES,
            transcendentals=n_reqs * sub * slots * page_rows, bytes_accessed=2 * fresh_kv.size),
        name="fresh",
    )(slot_table, counts, *far, kf, vf)

    def merge(keep, got, skip, goals, shapes):
        return pl.pallas_call(
            functools.partial(merge_kernel, heads, skip, goals),
            out_shape=shapes,
            in_specs=[VMEM] * 2,
            out_specs=[VMEM] * len(shapes),
            compiler_params=params(8),
            name="merge",
        )(keep, got)

    def halved(keep, got):
        shape = (keep.shape[0], slabs, keep.shape[2] // 2, LANES)
        return merge(keep, got, 0, [None] * keep.shape[0], [f32(*shape), bf16(*shape)])

    def sorted_by(keep, got, skip, offsets, bit):
        sends = [offset for offset in offsets if offset & bit]
        keeps = [offset for offset in offsets if not offset & bit]
        goals = [
            (0, sends.index(o)) if o in sends else (1, keeps.index(o)) for o in offsets]
        shape = lambda count: (count, slabs, group, LANES)
        shapes = [bf16(*shape(len(sends)))] + ([f32(*shape(len(keeps)))] if keeps else [])
        return merge(keep, got, skip, goals, shapes), keeps

    ctx_bits = list(bits_of("ctx"))[::-1]
    req_bits = list(bits_of("req"))[::-1]
    table = page_table.reshape(-1)
    send, q_own = lax.optimization_barrier((send, q_own))
    got = swap(send, "ctx", ctx_bits[0])
    t, top, *staged = pl.pallas_call(
        functools.partial(score_kernel, (heads, page_rows, pages_dev, sub, pieces)),
        out_shape=(f32(req_dev, sub, columns), f32(req_dev, sub, LANES)) + score_out,
        in_specs=[SMEM] * 2 + [VMEM] * 2 + score_specs,
        out_specs=(VMEM,) * (2 + len(score_out)),
        scratch_shapes=score_scratch,
        compiler_params=params(4),
        cost_estimate=pl.CostEstimate(
            flops=2 * req_dev * rows * columns * LANES, transcendentals=0,
            bytes_accessed=kv_pool.size),
        name="scores",
    )(table, context_len, q_own, kb, *score_in)
    if staged:
        vb = staged[0].reshape(pool_slots, page_rows, LANES)
    got, top = lax.optimization_barrier((got, top))
    for bit in ctx_bits[1:]:
        keep, send = halved(keep, got)
        send, top = lax.optimization_barrier((send, top))
        got = swap(send, "ctx", bit)
    own_keep, own_send = pl.pallas_call(
        functools.partial(value_kernel, (heads, page_rows, pages_dev, sub)),
        out_shape=(f32(1, slabs, left, LANES), bf16(1, slabs, left, LANES)),
        in_specs=[SMEM] + [VMEM] * 6,
        out_specs=(VMEM,) * 2,
        scratch_shapes=[
            pltpu.VMEM((req_dev, rows, LANES), jnp.float32),
            pltpu.VMEM((req_dev, sub, LANES), jnp.float32)],
        compiler_params=params(4),
        cost_estimate=pl.CostEstimate(
            flops=2 * req_dev * rows * columns * LANES, transcendentals=req_dev * sub * columns,
            bytes_accessed=kv_pool.size),
        name="values",
    )(table, t, top, vb, acc, ftop, ftot)
    own_got = swap(own_send, "ctx", ctx_bits[0])
    got, own_keep = lax.optimization_barrier((got, own_keep))
    offsets, skip, arrived = list(range(1, n_req)), 0, []
    for bit in req_bits:
        if offsets:
            (send, *kept), offsets = sorted_by(keep, got, skip, offsets, bit)
        keep = kept[0] if kept else None
        if bit == req_bits[0]:
            for ctx_bit in ctx_bits[1:]:
                own_keep, own_send = halved(own_keep, own_got)
                own_got = swap(own_send, "ctx", ctx_bit)
        got = swap(send, "req", bit)
        arrived.append(got)
        skip = 1
    return pl.pallas_call(
        last_kernel,
        out_shape=bf16(req_dev, heads, group, LANES),
        in_specs=[VMEM] * (2 + len(arrived)),
        out_specs=VMEM,
        compiler_params=params(8),
        name="last",
    )(own_keep, own_got, *arrived)


def solution(mesh):
    placed = (
        P("req", "kvh", "ctx", None),
        P(("req", "ctx"), None, "kvh", None),
        P("req", "ctx"),
        P("req"),
        P(("req", "ctx"), None, "kvh", None),
        P(("req", "ctx")),
    )
    return jax.shard_map(
        local, mesh=mesh, in_specs=placed, out_specs=P("req", "kvh", "ctx", None), check_vma=False
    )
```

time: 43.5 us -> 38.9 us (0.89)
  waiting for transfers between devices: 13.9 us -> 7.14 us
  starting transfers between devices: 10.1 us -> 13.2 us
  Pallas kernels: 19.1 us -> 18.1 us
    ppermute x8 -> x11, waiting for transfers between devices: 13.9 us -> 7.14 us  [swap(): lax.ppermute(value, axis, [(n, n ^ bit) for n in range(lax.axis_size(axis...]
    ppermute x8 -> x11, starting transfers between devices: 10.1 us -> 13.2 us  [swap(): lax.ppermute(value, axis, [(n, n ^ bit) for n in range(lax.axis_size(axis...]
    pallas_call x7 -> x8, Pallas kernels: 12 us -> 10.7 us  [the longest x1 4.08 us: local(): pl.pallas_call(functools.partial(stage_keys_kernel, n_ctx, slots), out_sh...]
  transfers between devices with their start and end apart: 8 -> 11, of which waited for: 6 -> 4; matrix products, arithmetic and copies ran while one was open for 0% -> 0% of each run, Pallas kernels for 34% -> 37%
where the time goes in v7:
time: 38.9 us; the launch traced here: 38.7 us
  Pallas kernels  18.1 us (47%)
  starting transfers between devices  13.2 us (34%)
  waiting for transfers between devices  7.14 us (18%)
    ppermute x11, starting transfers between devices, swap(): lax.ppermute(value, axis, [(n, n ^ bit) for n in range(lax.axis_size(axis...  13.2 us
    ppermute x11, waiting for transfers between devices, swap(): lax.ppermute(value, axis, [(n, n ^ bit) for n in range(lax.axis_size(axis...  7.14 us
    pallas_call x1, Pallas kernels, local(): pl.pallas_call(functools.partial(score_kernel, (heads, page_rows, pages_d...  4.45 us
    pallas_call x1, Pallas kernels, local(): pl.pallas_call(functools.partial(stage_keys_kernel, n_ctx, slots), out_sh...  4.08 us
    pallas_call x1, Pallas kernels, local(): pl.pallas_call(functools.partial(value_kernel, (heads, page_rows, pages_d...  2.93 us
    pallas_call x1, Pallas kernels, local(): pl.pallas_call(functools.partial(fresh_kernel, (heads, page_rows, slots,...  2.53 us
    pallas_call x1, Pallas kernels, local(): pl.pallas_call(stage_fresh_kernel, out_shape=(half(new_dev), half(new_dev...  2.05 us
    pallas_call x4, Pallas kernels, merge(): pl.pallas_call(functools.partial(merge_kernel, heads, skip, goals), out_s...  1.12 us
  transfers between devices with their start and end apart: 11, of which 4 were waited for; matrix products, arithmetic and copies ran while one was open for 0% of the time, Pallas kernels for 37%

profile of v7, /device:TPU:0, one launch (start us, length us, event | category | flops | bytes accessed | tf_op | source)
XLA Modules:
  0.0 38.7 jit_solution(4884018906819760549)
XLA Ops:
  0.0 2.9 %collective-permute-start = (bf16[1,4,4,4,128]{4,3,2,1,0:T(4,128)(2,1)}, bf16[1,4,4,4,128]{4,3,2,1,0:T(4,128)(2,1)S(1)}, u32[]{:S(2)}, u32[]{:S(2)}) collective-permute-start(bf16[1,4,4,4,128]{4,3,2,1,0:T(4,128)(2,1)} %bitcast.20), channel_id=1, source_target_pairs={{0,4},{2,6},{4,0},{6,2},{1,5},{3,7},{5,1},{7,3},{8,12},{10,14},{12... | collective-permute-start | bytes 49160 | tf_op jit(solution)/shard_map/ppermute | solution.py:23
  2.9 2.1 %stage_fresh.1 = (bf16[112,16,4,128]{3,2,1,0:T(4,128)(2,1)S(1)}, bf16[112,16,4,128]{3,2,1,0:T(4,128)(2,1)S(1)}) custom-call(bf16[112,16,4,256]{3,2,1,0:T(4,128)(2,1)} %fresh_ref.1), custom_call_target="tpu_custom_call" | custom-call | bytes 7340032 | tf_op jit(solution)/shard_map/stage_fresh/pallas_call | solution.py:387
  5.1 0.1 collective-permute-start.1
  5.1 1.2 %collective-permute-done.1 = bf16[2,4,4,4,128]{4,3,2,1,0:T(4,128)(2,1)S(1)} collective-permute-done((bf16[2,4,4,4,128]{4,3,2,1,0:T(4,128)(2,1)S(1)}, bf16[2,4,4,4,128]{4,3,2,1,0:T(4,128)(2,1)S(1)}, u32[]{:S(2)}, u32[]{:S(2)}) %collective-permute-start.1) | collective-permute-done | bytes 32800 | tf_op jit(solution)/shard_map/ppermute | solution.py:23
  6.4 4.0 %collective-permute-start.4 = (bf16[4,64,128]{2,1,0:T(8,128)(2,1)S(1)}, bf16[4,64,128]{2,1,0:T(8,128)(2,1)S(1)}, u32[]{:S(2)}, u32[]{:S(2)}) collective-permute-start(bf16[4,64,128]{2,1,0:T(8,128)(2,1)S(1)} %bitcast.13), channel_id=1, source_target_pairs={{0,24},{8,16},{16,8},{24,0},{1,25},{9,17},{17,9},{25,1},{2,26},{10... | collective-permute-start | bytes 196616 | tf_op jit(solution)/shard_map/ppermute | solution.py:23
  10.5 0.6 %collective-permute-start.2 = (bf16[4,64,128]{2,1,0:T(8,128)(2,1)S(1)}, bf16[4,64,128]{2,1,0:T(8,128)(2,1)S(1)}, u32[]{:S(2)}, u32[]{:S(2)}) collective-permute-start(bf16[4,64,128]{2,1,0:T(8,128)(2,1)S(1)} %bitcast.15), channel_id=1, source_target_pairs={{0,8},{8,0},{16,24},{24,16},{1,9},{9,1},{17,25},{25,17},{2,10},{10... | collective-permute-start | bytes 196616 | tf_op jit(solution)/shard_map/ppermute | solution.py:23
  11.1 4.1 %stage_keys.1 = (bf16[512,16,4,128]{3,2,1,0:T(4,128)(2,1)S(1)}, s32[128]{0:T(128)S(1)}, s32[16]{0:T(128)S(1)}) custom-call(s32[112]{0:T(128)} %bucket_hbm.1, bf16[512,16,4,256]{3,2,1,0:T(4,128)(2,1)} %refs_0_.1), custom_call_target="tpu_custom_call" | custom-call | bytes 16777216 | tf_op jit(solution)/shard_map/stage_keys/pallas_call | solution.py:399
  15.2 1.1 %collective-permute-done.3.refs_2_ = bf16[4,64,128]{2,1,0:T(8,128)(2,1)S(1)} collective-permute-done((bf16[4,64,128]{2,1,0:T(8,128)(2,1)S(1)}, bf16[4,64,128]{2,1,0:T(8,128)(2,1)S(1)}, u32[]{:S(2)}, u32[]{:S(2)}) %collective-permute-start.3) | collective-permute-done | bytes 65568 | tf_op jit(solution)/shard_map/ppermute | solution.py:23
  16.4 2.5 %fresh.1 = (f32[3,17,8,128]{3,2,1,0:T(8,128)S(1)}, bf16[3,17,8,128]{3,2,1,0:T(8,128)(2,1)S(1)}, f32[4,64,128]{2,1,0:T(8,128)S(1)}, f32[4,16,128]{2,1,0:T(8,128)S(1)}, f32[4,16,128]{2,1,0:T(8,128)S(1)}) custom-call(s32[128]{0:T(128)S(1)} %get-tuple-element.36.slots_ref, s32[16]{0:T(128)S(1)} %get-tuple-element.37.counts_ref, ...), custom_call_target="tpu_custom_call" | custom-call | flops 268435456 | bytes 3670016 | tf_op jit(solution)/shard_map/fresh/pallas_call | solution.py:437
  18.9 0.1 collective-permute-start.5
  19.0 4.4 %scores.1 = (f32[4,16,8192]{2,1,0:T(8,128)S(1)}, f32[4,16,128]{2,1,0:T(8,128)S(1)}, bf16[512,16,4,128]{3,2,1,0:T(4,128)(2,1)S(1)}) custom-call(s32[512]{0:T(512)S(1)} %bitcast.18, s32[4]{0:T(128)S(1)} %copy-done.1, bf16[4,64,128]{2,1,0:T(8,128)(2,1)S(1)} %bitcast.17, bf16[512,64,128]{2,1,0:T(8,128)(2,1)S(1)} %bitcast.9, bf16[512,16,4,256]{3,2,1,0:T(4,128)(2,1)} %refs_0_.1), custom_call_target="tpu_custom_call" | custom-call | flops 536870912 | bytes 8388608 | tf_op jit(solution)/shard_map/scores/pallas_call | solution.py:483
  23.4 0.3 merge.4
  23.8 1.5 %collective-permute-start.6 = (bf16[3,17,4,128]{3,2,1,0:T(4,128)(2,1)S(1)}, bf16[3,17,4,128]{3,2,1,0:T(4,128)(2,1)S(1)}, u32[]{:S(2)}, u32[]{:S(2)}) collective-permute-start(bf16[3,17,4,128]{3,2,1,0:T(4,128)(2,1)S(1)} %get-tuple-element.51), channel_id=1, source_target_pairs={{0,4},{2,6},{4,0},{6,2},{1,5},{3,7},{5,1},{7,3},{8,12},{10,14},{12... | collective-permute-start | bytes 156680 | tf_op jit(solution)/shard_map/ppermute | solution.py:23
  25.3 2.9 %values.1 = (f32[1,17,8,128]{3,2,1,0:T(8,128)S(1)}, bf16[1,17,8,128]{3,2,1,0:T(8,128)(2,1)S(1)}) custom-call(s32[512]{0:T(512)S(1)} %bitcast.19, f32[4,16,8192]{2,1,0:T(8,128)S(1)} %get-tuple-element.52.t_ref, f32[4,16,128]{2,1,0:T(8,128)S(1)} %get-tuple-element.53.top_ref, bf16[512,64,128]{2,1,0:T(8,128)(2,1)S(1)} %bitcast.10, ...), custom_call_target="tpu_custom_call" | custom-call | flops 536870912 | bytes 8388608 | tf_op jit(solution)/shard_map/values/pallas_call | solution.py:502
  28.2 0.3 collective-permute-start.7
  28.5 0.3 merge.6
  28.8 1.2 %collective-permute-start.9 = (bf16[2,17,4,128]{3,2,1,0:T(4,128)(2,1)S(1)}, bf16[2,17,4,128]{3,2,1,0:T(4,128)(2,1)S(1)}, u32[]{:S(2)}, u32[]{:S(2)}) collective-permute-start(bf16[2,17,4,128]{3,2,1,0:T(4,128)(2,1)S(1)} %get-tuple-element.65), channel_id=1, source_target_pairs={{0,8},{8,0},{16,24},{24,16},{1,9},{9,1},{17,25},{25,17},{2,10},{10... | collective-permute-start | bytes 104456 | tf_op jit(solution)/shard_map/ppermute | solution.py:23
  30.0 0.3 merge.5
  30.3 1.1 %collective-permute-start.8 = (bf16[1,17,4,128]{3,2,1,0:T(4,128)(2,1)S(1)}, bf16[1,17,4,128]{3,2,1,0:T(4,128)(2,1)S(1)}, u32[]{:S(2)}, u32[]{:S(2)}) collective-permute-start(bf16[1,17,4,128]{3,2,1,0:T(4,128)(2,1)S(1)} %get-tuple-element.62), channel_id=1, source_target_pairs={{0,4},{2,6},{4,0},{6,2},{1,5},{3,7},{5,1},{7,3},{8,12},{10,14},{12... | collective-permute-start | bytes 52232 | tf_op jit(solution)/shard_map/ppermute | solution.py:23
  31.3 1.5 %collective-permute-done.9.got_ref.refs_1_ = bf16[2,17,4,128]{3,2,1,0:T(4,128)(2,1)S(1)} collective-permute-done((bf16[2,17,4,128]{3,2,1,0:T(4,128)(2,1)S(1)}, bf16[2,17,4,128]{3,2,1,0:T(4,128)(2,1)S(1)}, u32[]{:S(2)}, u32[]{:S(2)}) %collective-permute-start.9) | collective-permute-done | bytes 34848 | tf_op jit(solution)/shard_map/ppermute | solution.py:23
  32.8 0.3 merge.7
  33.1 1.4 %collective-permute-start.10 = (bf16[1,17,4,128]{3,2,1,0:T(4,128)(2,1)S(1)}, bf16[1,17,4,128]{3,2,1,0:T(4,128)(2,1)S(1)}, u32[]{:S(2)}, u32[]{:S(2)}) collective-permute-start(bf16[1,17,4,128]{3,2,1,0:T(4,128)(2,1)S(1)} %merge.7), channel_id=1, source_target_pairs={{0,16},{8,24},{16,0},{24,8},{1,17},{9,25},{17,1},{25,9},{2,18},{10... | collective-permute-start | bytes 52232 | tf_op jit(solution)/shard_map/ppermute | solution.py:23
  34.5 3.3 %collective-permute-done.10.refs_2_ = bf16[1,17,4,128]{3,2,1,0:T(4,128)(2,1)S(1)} collective-permute-done((bf16[1,17,4,128]{3,2,1,0:T(4,128)(2,1)S(1)}, bf16[1,17,4,128]{3,2,1,0:T(4,128)(2,1)S(1)}, u32[]{:S(2)}, u32[]{:S(2)}) %collective-permute-start.10) | collective-permute-done | bytes 17440 | tf_op jit(solution)/shard_map/ppermute | solution.py:23
  37.8 0.9 %last.1 = bf16[4,4,4,128]{3,2,1,0:T(4,128)(2,1)} custom-call(f32[1,17,4,128]{3,2,1,0:T(4,128)S(1)} %get-tuple-element.61.keep_ref, bf16[1,17,4,128]{3,2,1,0:T(4,128)(2,1)S(1)} %collective-permute-done.8.refs_0_, bf16[2,17,4,128]{3,2,1,0:T(4,128)(2,1)S(1)} %collective-permute-done.9.got_ref.refs_1_, bf16[1,17,4,128]{3,2,1,0:T(4,128)(2,1)S(1)} %collective-permute-done.10.refs_2_), custom_call_target="tpu_custom_call" | custom-call | tf_op jit(solution)/shard_map/last/pallas_call | solution.py:530
  (17 shorter events, 0.1 us)
Async XLA Ops:
  0.0 5.0 %copy-start.2 = (bf16[4,4,4,128]{3,2,1,0:T(4,128)(2,1)S(1)}, bf16[4,4,4,128]{3,2,1,0:T(4,128)(2,1)}, u32[]{:S(2)}) copy-start(bf16[4,4,4,128]{3,2,1,0:T(4,128)(2,1)} %param.6) | copy-start | bytes 49156
  0.0 5.0 %collective-permute-start = (bf16[1,4,4,4,128]{4,3,2,1,0:T(4,128)(2,1)}, bf16[1,4,4,4,128]{4,3,2,1,0:T(4,128)(2,1)S(1)}, u32[]{:S(2)}, u32[]{:S(2)}) collective-permute-start(bf16[1,4,4,4,128]{4,3,2,1,0:T(4,128)(2,1)} %bitcast.20), channel_id=1, source_target_pairs={{0,4},{2,6},{4,0},{6,2},{1,5},{3,7},{5,1},{7,3},{8,12},{10,14},{12... | collective-permute-start | bytes 49160 | tf_op jit(solution)/shard_map/ppermute | solution.py:23
  5.1 1.3 %collective-permute-start.1 = (bf16[2,4,4,4,128]{4,3,2,1,0:T(4,128)(2,1)S(1)}, bf16[2,4,4,4,128]{4,3,2,1,0:T(4,128)(2,1)S(1)}, u32[]{:S(2)}, u32[]{:S(2)}) collective-permute-start(bf16[2,4,4,4,128]{4,3,2,1,0:T(4,128)(2,1)S(1)} %pad_maximum_fusion), channel_id=1, source_target_pairs={{0,2},{2,0},{4,6},{6,4},{1,3},{3,1},{5,7},{7,5},{8,10},{10,8},{12,... | collective-permute-start | bytes 98312 | tf_op jit(solution)/shard_map/ppermute | solution.py:23
  6.4 8.8 %collective-permute-start.4 = (bf16[4,64,128]{2,1,0:T(8,128)(2,1)S(1)}, bf16[4,64,128]{2,1,0:T(8,128)(2,1)S(1)}, u32[]{:S(2)}, u32[]{:S(2)}) collective-permute-start(bf16[4,64,128]{2,1,0:T(8,128)(2,1)S(1)} %bitcast.13), channel_id=1, source_target_pairs={{0,24},{8,16},{16,8},{24,0},{1,25},{9,17},{17,9},{25,1},{2,26},{10... | collective-permute-start | bytes 196616 | tf_op jit(solution)/shard_map/ppermute | solution.py:23
  10.5 5.9 %collective-permute-start.3 = (bf16[4,64,128]{2,1,0:T(8,128)(2,1)S(1)}, bf16[4,64,128]{2,1,0:T(8,128)(2,1)S(1)}, u32[]{:S(2)}, u32[]{:S(2)}) collective-permute-start(bf16[4,64,128]{2,1,0:T(8,128)(2,1)S(1)} %bitcast.14), channel_id=1, source_target_pairs={{0,16},{8,24},{16,0},{24,8},{1,17},{9,25},{17,1},{25,9},{2,18},{10... | collective-permute-start | bytes 196616 | tf_op jit(solution)/shard_map/ppermute | solution.py:23
  10.5 5.9 %collective-permute-start.2 = (bf16[4,64,128]{2,1,0:T(8,128)(2,1)S(1)}, bf16[4,64,128]{2,1,0:T(8,128)(2,1)S(1)}, u32[]{:S(2)}, u32[]{:S(2)}) collective-permute-start(bf16[4,64,128]{2,1,0:T(8,128)(2,1)S(1)} %bitcast.15), channel_id=1, source_target_pairs={{0,8},{8,0},{16,24},{24,16},{1,9},{9,1},{17,25},{25,17},{2,10},{10... | collective-permute-start | bytes 196616 | tf_op jit(solution)/shard_map/ppermute | solution.py:23
  15.2 3.8 %copy-start = (s32[4,128]{1,0:T(4,128)S(1)}, s32[4,128]{1,0:T(4,128)}, u32[]{:S(2)}) copy-start(s32[4,128]{1,0:T(4,128)} %param.8) | copy-start | bytes 6148
  15.2 3.8 %copy-start.1 = (s32[4]{0:T(128)S(1)}, s32[4]{0:T(128)}, u32[]{:S(2)}) copy-start(s32[4]{0:T(128)} %len_ref.1) | copy-start | bytes 52
  18.9 4.6 %collective-permute-start.5 = (bf16[3,17,8,128]{3,2,1,0:T(8,128)(2,1)S(1)}, bf16[3,17,8,128]{3,2,1,0:T(8,128)(2,1)S(1)}, u32[]{:S(2)}, u32[]{:S(2)}) collective-permute-start(bf16[3,17,8,128]{3,2,1,0:T(8,128)(2,1)S(1)} %get-tuple-element.44), channel_id=1, source_target_pairs={{0,2},{2,0},{4,6},{6,4},{1,3},{3,1},{5,7},{7,5},{8,10},{10,8},{12,... | collective-permute-start | bytes 313352 | tf_op jit(solution)/shard_map/ppermute | solution.py:23
  23.8 4.7 %collective-permute-start.6 = (bf16[3,17,4,128]{3,2,1,0:T(4,128)(2,1)S(1)}, bf16[3,17,4,128]{3,2,1,0:T(4,128)(2,1)S(1)}, u32[]{:S(2)}, u32[]{:S(2)}) collective-permute-start(bf16[3,17,4,128]{3,2,1,0:T(4,128)(2,1)S(1)} %get-tuple-element.51), channel_id=1, source_target_pairs={{0,4},{2,6},{4,0},{6,2},{1,5},{3,7},{5,1},{7,3},{8,12},{10,14},{12... | collective-permute-start | bytes 156680 | tf_op jit(solution)/shard_map/ppermute | solution.py:23
  28.2 1.8 %collective-permute-start.7 = (bf16[1,17,8,128]{3,2,1,0:T(8,128)(2,1)S(1)}, bf16[1,17,8,128]{3,2,1,0:T(8,128)(2,1)S(1)}, u32[]{:S(2)}, u32[]{:S(2)}) collective-permute-start(bf16[1,17,8,128]{3,2,1,0:T(8,128)(2,1)S(1)} %get-tuple-element.60), channel_id=1, source_target_pairs={{0,2},{2,0},{4,6},{6,4},{1,3},{3,1},{5,7},{7,5},{8,10},{10,8},{12,... | collective-permute-start | bytes 104456 | tf_op jit(solution)/shard_map/ppermute | solution.py:23
  28.8 4.0 %collective-permute-start.9 = (bf16[2,17,4,128]{3,2,1,0:T(4,128)(2,1)S(1)}, bf16[2,17,4,128]{3,2,1,0:T(4,128)(2,1)S(1)}, u32[]{:S(2)}, u32[]{:S(2)}) collective-permute-start(bf16[2,17,4,128]{3,2,1,0:T(4,128)(2,1)S(1)} %get-tuple-element.65), channel_id=1, source_target_pairs={{0,8},{8,0},{16,24},{24,16},{1,9},{9,1},{17,25},{25,17},{2,10},{10... | collective-permute-start | bytes 104456 | tf_op jit(solution)/shard_map/ppermute | solution.py:23
  30.3 4.2 %collective-permute-start.8 = (bf16[1,17,4,128]{3,2,1,0:T(4,128)(2,1)S(1)}, bf16[1,17,4,128]{3,2,1,0:T(4,128)(2,1)S(1)}, u32[]{:S(2)}, u32[]{:S(2)}) collective-permute-start(bf16[1,17,4,128]{3,2,1,0:T(4,128)(2,1)S(1)} %get-tuple-element.62), channel_id=1, source_target_pairs={{0,4},{2,6},{4,0},{6,2},{1,5},{3,7},{5,1},{7,3},{8,12},{10,14},{12... | collective-permute-start | bytes 52232 | tf_op jit(solution)/shard_map/ppermute | solution.py:23
  33.1 4.7 %collective-permute-start.10 = (bf16[1,17,4,128]{3,2,1,0:T(4,128)(2,1)S(1)}, bf16[1,17,4,128]{3,2,1,0:T(4,128)(2,1)S(1)}, u32[]{:S(2)}, u32[]{:S(2)}) collective-permute-start(bf16[1,17,4,128]{3,2,1,0:T(4,128)(2,1)S(1)} %merge.7), channel_id=1, source_target_pairs={{0,16},{8,24},{16,0},{24,8},{1,17},{9,25},{17,1},{25,9},{2,18},{10... | collective-permute-start | bytes 52232 | tf_op jit(solution)/shard_map/ppermute | solution.py:23

commit v8 on v7

--- a/solution.py
+++ b/solution.py
@@ -30,14 +30,33 @@
         bit //= 2
 
 
-def half_copies(pool_ref, target, sem, half, pieces):
+def half_copies(pool_ref, target, sem, half, pieces, tokens=None):
     each = pool_ref.shape[0] // pieces
+    tokens = tokens or pl.ds(0, pool_ref.shape[1])
     return [
         pltpu.make_async_copy(
-            pool_ref.at[pl.ds(n * each, each), :, :, pl.ds(half * LANES, LANES)],
+            pool_ref.at[pl.ds(n * each, each), tokens, :, pl.ds(half * LANES, LANES)],
             target.at[pl.ds(n * each, each)], sem.at[n])
         for n in range(pieces)
     ]
+
+
+class ValueCopies:
+    def __init__(self, refs, part, pieces):
+        self.copies = []
+        if pieces:
+            pool_ref, target, sem = refs
+            count = pool_ref.shape[1] // 2
+            self.copies = half_copies(
+                pool_ref, target, sem, 1, pieces, pl.ds(part * count, count))
+
+    def start(self):
+        for one in self.copies:
+            one.start()
+
+    def wait(self):
+        for one in self.copies:
+            one.wait()
 
 
 def stage_fresh_kernel(fresh_ref, kf, vf, sem):
@@ -75,13 +94,13 @@
         slots_ref[n] = 0
 
     def put(page, _):
-        request = bucket_ref[page] // n_ctx
+        request = bucket_ref[page] >> (n_ctx.bit_length() - 1)
         count = counts_ref[request]
         slots_ref[request * slots + count] = page
         counts_ref[request] = count + 1
         return 0
 
-    lax.fori_loop(0, bucket_ref.shape[0], put, 0)
+    lax.fori_loop(0, bucket_ref.shape[0], put, 0, unroll=16)
 
 
 def class_reduce(x, op, heads):
@@ -92,8 +111,9 @@
     return x
 
 
-def pages_of(ref, table_ref, first, count):
-    return jnp.concatenate([ref[table_ref[first + n]] for n in range(count)], axis=0)
+def pages_of(refs, table_ref, first, count):
+    pages = [table_ref[first + n] for n in range(count)]
+    return jnp.concatenate([ref[page] for page in pages for ref in refs], axis=0)
 
 
 def score_parts(q, keys, lane, limit, first, heads, sub):
@@ -124,87 +144,115 @@
     return top
 
 
-def score_kernel(dims, table_ref, len_ref, q_ref, kb, *refs):
-    heads, page_rows, pages_dev, sub, pieces = dims
-    copies = []
-    if pieces:
-        pool_ref, t_ref, top_ref, vb, sem = refs
-        copies = half_copies(pool_ref, vb, sem, 1, pieces)
-    else:
-        t_ref, top_ref = refs
-    for one in copies:
-        one.start()
+def score_request(dims, i, table_ref, len_ref, q_ref, kb, t_ref, top_ref, at):
+    heads, page_rows, pages_dev, sub = dims
     columns = pages_dev * page_rows
     wide = min(SCORE_WIDE, columns)
     per = wide // page_rows
     lane = lax.broadcasted_iota(jnp.int32, (sub, LANES), 1)
-    start = lax.axis_index("ctx") * (pages_dev * page_rows)
-
-    def step(i, _):
-        top = jnp.full((sub, LANES), NEG, jnp.float32)
-        limit = len_ref[i] * heads - start
-        for c in range(columns // wide):
-            keys = pages_of(kb, table_ref, i * pages_dev + c * per, per)
-            parts = score_parts(q_ref[i], keys, lane, limit, c * wide, heads, sub)
-            for j, part in enumerate(parts):
-                t_ref[i, :, c * wide + j * LANES:c * wide + (j + 1) * LANES] = part
-            top = jnp.maximum(top, fold_max(parts))
-        top_ref[i] = top
-        return 0
-
-    shape = top_ref.shape
-    flat = (shape[0] * shape[1], LANES)
-    lax.fori_loop(0, shape[0], step, 0)
-    top_ref[...] = class_reduce(top_ref[...].reshape(flat), jnp.maximum, heads).reshape(shape)
-    for one in copies:
-        one.wait()
-
-
-def value_kernel(
-    dims, table_ref, t_ref, top_ref, vb, acc_ref, ftop_ref, ftot_ref, keep_ref, send_ref,
-    acc_s, tot_s,
-):
+    top = jnp.full((sub, LANES), NEG, jnp.float32)
+    limit = len_ref[i] * heads - lax.axis_index("ctx") * columns
+    for c in range(columns // wide):
+        keys = pages_of([kb], table_ref, i * pages_dev + c * per, per)
+        parts = score_parts(q_ref[0, i], keys, lane, limit, c * wide, heads, sub)
+        for j, part in enumerate(parts):
+            t_ref[at, :, c * wide + j * LANES:c * wide + (j + 1) * LANES] = part
+        top = jnp.maximum(top, fold_max(parts))
+    top_ref[at] = top
+
+
+def value_request(dims, i, table_ref, t_ref, top_ref, at, vbs, acc_ref, tot_ref):
     heads, page_rows, pages_dev, sub = dims
-    req_dev = t_ref.shape[0]
     columns = pages_dev * page_rows
     wide = min(VALUE_WIDE, columns)
     per = wide // page_rows
     lane = lax.broadcasted_iota(jnp.int32, (sub, LANES), 1)
     onehots = [(lane % heads == h).astype(jnp.bfloat16) for h in range(heads)]
+    tot = jnp.zeros((sub, LANES), jnp.float32)
+    acc = jnp.zeros((heads * sub, LANES), jnp.float32)
+    top = top_ref[at]
+    for c in range(columns // wide):
+        weights = []
+        for j in range(wide // LANES):
+            where = c * wide + j * LANES
+            p = jnp.exp2(t_ref[at, :, where:where + LANES] - top)
+            tot = tot + p
+            weights.append(spread(p, onehots))
+        values = pages_of(vbs, table_ref, i * pages_dev + c * per, per)
+        acc = acc + jnp.dot(
+            jnp.concatenate(weights, axis=1), values, preferred_element_type=jnp.float32)
+    acc_ref[at] = acc
+    tot_ref[at] = tot
+
+
+def reduce_rows(ref, op, heads):
+    flat = ref[...].reshape(ref.shape[0] * ref.shape[1], LANES)
+    return class_reduce(flat, op, heads)
+
+
+def first_kernel(dims, pieces, table_ref, len_ref, q_ref, kb, *refs):
+    refs = list(refs)
+    pool = [refs.pop(0)] if pieces else []
+    t_ref, top_ref, *refs = refs
+    copies = ValueCopies(pool + refs, 1, pieces)
+    copies.start()
 
     def step(i, _):
-        tot = jnp.zeros((sub, LANES), jnp.float32)
-        acc = jnp.zeros((heads * sub, LANES), jnp.float32)
-        top = top_ref[i]
-        for c in range(columns // wide):
-            weights = []
-            for j in range(wide // LANES):
-                at = c * wide + j * LANES
-                p = jnp.exp2(t_ref[i, :, at:at + LANES] - top)
-                tot = tot + p
-                weights.append(spread(p, onehots))
-            values = pages_of(vb, table_ref, i * pages_dev + c * per, per)
-            acc = acc + jnp.dot(
-                jnp.concatenate(weights, axis=1), values, preferred_element_type=jnp.float32)
-        acc_s[i] = acc
-        tot_s[i] = tot
+        score_request(dims, i, table_ref, len_ref, q_ref, kb, t_ref, top_ref, i)
         return 0
 
-    lax.fori_loop(0, req_dev, step, 0)
+    lax.fori_loop(0, t_ref.shape[0], step, 0)
+    top_ref[...] = reduce_rows(top_ref, jnp.maximum, dims[0]).reshape(top_ref.shape)
+    copies.wait()
+
+
+def middle_kernel(dims, table_ref, len_ref, q_ref, kb, t_ref, top_ref, *refs):
+    *vbs, later_ref, later_top_ref, acc_ref, tot_ref = refs
+    half = t_ref.shape[0]
+
+    def step(i, _):
+        score_request(
+            dims, half + i, table_ref, len_ref, q_ref, kb, later_ref, later_top_ref, i)
+        value_request(dims, i, table_ref, t_ref, top_ref, i, vbs, acc_ref, tot_ref)
+        return 0
+
+    lax.fori_loop(0, half, step, 0)
+    later_top_ref[...] = reduce_rows(
+        later_top_ref, jnp.maximum, dims[0]).reshape(later_top_ref.shape)
+
+
+def second_kernel(
+    dims, table_ref, t_ref, top_ref, first_top_ref, first_acc_ref, first_tot_ref, facc_ref,
+    ftop_ref, ftot_ref, *refs,
+):
+    *vbs, keep_ref, send_ref, acc_s, tot_s = refs
+    heads, page_rows, pages_dev, sub = dims
+    half = t_ref.shape[0]
+    req_dev = ftop_ref.shape[0]
+
+    def step(i, _):
+        value_request(dims, half + i, table_ref, t_ref, top_ref, i, vbs, acc_s, tot_s)
+        return 0
+
+    lax.fori_loop(0, half, step, 0)
     flat = (req_dev * sub, LANES)
-    tots = class_reduce(tot_s[...].reshape(flat), jnp.add, heads)
-    top, ftop = top_ref[...].reshape(flat), ftop_ref[...].reshape(flat)
+    tots = jnp.concatenate(
+        [reduce_rows(ref, jnp.add, heads) for ref in (first_tot_ref, tot_s)], axis=0)
+    top = jnp.concatenate(
+        [ref[...].reshape(half * sub, LANES) for ref in (first_top_ref, top_ref)], axis=0)
+    ftop = ftop_ref[...].reshape(flat)
     both = jnp.maximum(top, ftop)
     fade, ffade = jnp.exp2(top - both), jnp.exp2(ftop - both)
     tots = tots * fade + ftot_ref[...].reshape(flat) * ffade
     fade, ffade = fade / tots, ffade / tots
     lses = both + jnp.log2(tots)
     for i in range(req_dev):
+        acc_ref = first_acc_ref if i < half else acc_s
         rows = slice(i * sub, (i + 1) * sub)
         for h in range(heads):
             part = slice(h * sub, (h + 1) * sub)
-            some = acc_s[i, part, :] * rows_of(fade[rows], h)
-            some = some + acc_ref[i, part, :] * rows_of(ffade[rows], h)
+            some = acc_ref[i % half, part, :] * rows_of(fade[rows], h)
+            some = some + facc_ref[i, part, :] * rows_of(ffade[rows], h)
             put_rows(keep_ref, send_ref, (0, i * heads + h), some)
     lse = by_request(lses, heads, sub, range(req_dev))
     put_rows(keep_ref, send_ref, (0, req_dev * heads), lse, heads)
@@ -225,27 +273,31 @@
     return out
 
 
-def fresh_kernel(
-    dims, slots_ref, counts_ref, *refs,
-):
-    heads, page_rows, slots, sub, req_dev = dims
-    *q_refs, kf, vf, keep_ref, send_ref, acc_ref, top_ref, tot_ref, t_s, p_s = refs
+def fresh_kernel(dims, pieces, slots_ref, counts_ref, q_ref, kf, vf, *refs):
+    heads, page_rows, slots, sub = dims
+    n_req, req_dev = q_ref.shape[:2]
+    refs = list(refs)
+    pool = [refs.pop(0)] if pieces else []
+    keep_ref, send_ref, acc_ref, top_ref, tot_ref, *refs = refs
+    target = [refs.pop(0)] if pieces else []
+    t_s, p_s, *sem = refs
+    copies = ValueCopies(pool + target + sem, 0, pieces)
+    copies.start()
     lane = lax.broadcasted_iota(jnp.int32, (sub, LANES), 1)
     onehots = [(lane % heads == h).astype(jnp.bfloat16) for h in range(heads)]
     columns = slots * page_rows
     wide = min(SCORE_WIDE, columns)
     per = wide // page_rows
     own = lax.axis_index("req")
-    requests = [(own ^ k) * req_dev + i for k in range(len(q_refs)) for i in range(req_dev)]
+    requests = [(own ^ k) * req_dev + i for k in range(n_req) for i in range(req_dev)]
     n_reqs = len(requests)
     tops = []
     for n, request in enumerate(requests):
         limit = counts_ref[request] * page_rows
         top = jnp.full((sub, LANES), NEG, jnp.float32)
         for c in range(columns // wide):
-            keys = pages_of(kf, slots_ref, request * slots + c * per, per)
-            q = q_refs[n // req_dev][n % req_dev]
-            parts = score_parts(q, keys, lane, limit, c * wide, heads, sub)
+            keys = pages_of([kf], slots_ref, request * slots + c * per, per)
+            parts = score_parts(q_ref[n // req_dev, n % req_dev], keys, lane, limit, c * wide, heads, sub)
             for j, part in enumerate(parts):
                 t_s[n, :, c * wide + j * LANES:c * wide + (j + 1) * LANES] = part
             top = jnp.maximum(top, fold_max(parts))
@@ -264,7 +316,7 @@
     whole = 1.0 / tots
     lses = tops + jnp.log2(tots)
     for n, request in enumerate(requests):
-        values = pages_of(vf, slots_ref, request * slots, slots)
+        values = pages_of([vf], slots_ref, request * slots, slots)
         acc = jnp.dot(p_s[n], values, preferred_element_type=jnp.float32)
         rows = slice(n * sub, (n + 1) * sub)
         block, i = n // req_dev - 1, n % req_dev
@@ -276,10 +328,11 @@
         for h in range(heads):
             some = acc[h * sub:(h + 1) * sub] * rows_of(whole[rows], h)
             put_rows(keep_ref, send_ref, (block, i * heads + h), some)
-    for block in range(len(q_refs) - 1):
+    for block in range(n_req - 1):
         first = (block + 1) * req_dev
         lse = by_request(lses, heads, sub, range(first, first + req_dev))
         put_rows(keep_ref, send_ref, (block, req_dev * heads), lse, heads)
+    copies.wait()
 
 
 def pieces_of(lse, heads):
@@ -377,9 +430,8 @@
     split = heads % 4 == 0
     pieces = 8 if split else 0
 
-    near = query[None]
+    reqs = [swap(query, "req", k) for k in range(n_req - 1, 0, -1)][::-1]
     first, *others = bits_of("ctx")
-    arrived = swap(near, "ctx", first)
     if split:
         in_hbm = lambda a: pltpu.with_memory_space_constraint(a, pltpu.HBM)
         pool = in_hbm(kv_pool)
@@ -395,7 +447,9 @@
                 flops=0, transcendentals=0, bytes_accessed=4 * fresh_kv.size),
             name="stage_fresh",
         )(in_hbm(fresh_kv))
-        arrived, kf = lax.optimization_barrier((arrived, kf))
+        bucket, kf, *reqs = lax.optimization_barrier((in_hbm(fresh_bucket), kf, *reqs))
+        near = jnp.stack([query] + reqs)[None]
+        arrived = swap(near, "ctx", first)
         kb, slot_table, counts = pl.pallas_call(
             functools.partial(stage_keys_kernel, n_ctx, slots),
             out_shape=(half(pool_slots), smem(n_reqs * slots), smem(n_reqs)),
@@ -408,10 +462,12 @@
             cost_estimate=pl.CostEstimate(
                 flops=0, transcendentals=0, bytes_accessed=2 * kv_pool.size),
             name="stage_keys",
-        )(in_hbm(fresh_bucket), pool)
+        )(in_hbm(bucket), pool)
+        arrived, counts = lax.optimization_barrier((arrived, counts))
         kb, kf, vf = (a.reshape(a.shape[0], page_rows, LANES) for a in (kb, kf, vf))
-        score_in, score_specs, score_out = (pool,), [HBM], (half(pool_slots),)
-        score_scratch = [pltpu.SemaphoreType.DMA((pieces,))]
+        value_in, value_specs = (pool,), [HBM]
+        value_out = (bf16(pool_slots, page // 2, heads, LANES),)
+        value_scratch = [pltpu.SemaphoreType.DMA((pieces,))]
     else:
         kb, vb, kf, vf = (
             a[..., h * LANES:(h + 1) * LANES].reshape(a.shape[0], page_rows, LANES)
@@ -424,33 +480,35 @@
             out_specs=(SMEM,) * 2,
             name="list",
         )(fresh_bucket)
-        score_in, score_specs, score_out, score_scratch = (), [], (), []
+        value_in, value_specs, value_out, value_scratch = (), [], (), []
+        near = jnp.stack([query] + reqs)[None]
+        arrived = swap(near, "ctx", first)
 
     near = jnp.concatenate([near, arrived])
     for bit in others:
         near = jnp.concatenate([near, swap(near, "ctx", bit)])
-    q_own = near.transpose(1, 2, 0, 3, 4).reshape(req_dev, rows, head_dim)
-    far = [q_own] + [swap(q_own, "req", k) for k in range(n_req - 1, 0, -1)][::-1]
+    queries = near.transpose(1, 2, 3, 0, 4, 5).reshape(n_req, req_dev, rows, head_dim)
 
     slabs = req_dev * heads + 1
     left = sub // 2
-    keep, send, acc, ftop, ftot = pl.pallas_call(
-        functools.partial(fresh_kernel, (heads, page_rows, slots, sub, req_dev)),
+    keep, send, facc, ftop, ftot, *vbs = pl.pallas_call(
+        functools.partial(fresh_kernel, (heads, page_rows, slots, sub), pieces),
         out_shape=(
             f32(n_req - 1, slabs, left, LANES), bf16(n_req - 1, slabs, left, LANES),
-            f32(req_dev, rows, LANES), f32(req_dev, sub, LANES), f32(req_dev, sub, LANES)),
-        in_specs=[SMEM] * 2 + [VMEM] * (2 + n_req),
-        out_specs=(VMEM,) * 5,
+            f32(req_dev, rows, LANES), f32(req_dev, sub, LANES), f32(req_dev, sub, LANES),
+        ) + value_out,
+        in_specs=[SMEM] * 2 + [VMEM] * 3 + value_specs,
+        out_specs=(VMEM,) * (5 + len(value_out)),
         scratch_shapes=[
             pltpu.VMEM((n_reqs, sub, slots * page_rows), jnp.float32),
             pltpu.VMEM((n_reqs, rows, slots * page_rows), jnp.bfloat16),
-        ],
+        ] + value_scratch,
         compiler_params=params(8),
         cost_estimate=pl.CostEstimate(
             flops=4 * n_reqs * rows * slots * page_rows * LANES,
             transcendentals=n_reqs * sub * slots * page_rows, bytes_accessed=2 * fresh_kv.size),
         name="fresh",
-    )(slot_table, counts, *far, kf, vf)
+    )(slot_table, counts, queries, kf, vf, *value_in)
 
     def merge(keep, got, skip, goals, shapes):
         return pl.pallas_call(
@@ -477,56 +535,69 @@
 
     ctx_bits = list(bits_of("ctx"))[::-1]
     req_bits = list(bits_of("req"))[::-1]
+    dims = (heads, page_rows, pages_dev, sub)
     table = page_table.reshape(-1)
-    send, q_own = lax.optimization_barrier((send, q_own))
+    part = req_dev // 2
+    cost = lambda scores, values: pl.CostEstimate(
+        flops=2 * (scores + values) * rows * columns * LANES,
+        transcendentals=values * sub * columns,
+        bytes_accessed=(scores + values) * columns * LANES * 2)
+    send, queries = lax.optimization_barrier((send, queries))
     got = swap(send, "ctx", ctx_bits[0])
-    t, top, *staged = pl.pallas_call(
-        functools.partial(score_kernel, (heads, page_rows, pages_dev, sub, pieces)),
-        out_shape=(f32(req_dev, sub, columns), f32(req_dev, sub, LANES)) + score_out,
-        in_specs=[SMEM] * 2 + [VMEM] * 2 + score_specs,
-        out_specs=(VMEM,) * (2 + len(score_out)),
-        scratch_shapes=score_scratch,
+    t, top, *more = pl.pallas_call(
+        functools.partial(first_kernel, dims, pieces),
+        out_shape=(f32(part, sub, columns), f32(part, sub, LANES)) + value_out,
+        in_specs=[SMEM] * 2 + [VMEM] * 2 + value_specs,
+        out_specs=(VMEM,) * (2 + len(value_out)),
+        scratch_shapes=value_scratch,
         compiler_params=params(4),
-        cost_estimate=pl.CostEstimate(
-            flops=2 * req_dev * rows * columns * LANES, transcendentals=0,
-            bytes_accessed=kv_pool.size),
-        name="scores",
-    )(table, context_len, q_own, kb, *score_in)
-    if staged:
-        vb = staged[0].reshape(pool_slots, page_rows, LANES)
+        cost_estimate=cost(part, 0),
+        name="first",
+    )(table, context_len, queries, kb, *value_in)
+    vbs = [a.reshape(a.shape[0], -1, LANES) for a in vbs + more] if split else [vb]
     got, top = lax.optimization_barrier((got, top))
     for bit in ctx_bits[1:]:
         keep, send = halved(keep, got)
         send, top = lax.optimization_barrier((send, top))
         got = swap(send, "ctx", bit)
+    later, later_top, acc, tot = pl.pallas_call(
+        functools.partial(middle_kernel, dims),
+        out_shape=(
+            f32(part, sub, columns), f32(part, sub, LANES), f32(part, rows, LANES),
+            f32(part, sub, LANES)),
+        in_specs=[SMEM] * 2 + [VMEM] * (4 + len(vbs)),
+        out_specs=(VMEM,) * 4,
+        compiler_params=params(4),
+        cost_estimate=cost(part, part),
+        name="middle",
+    )(table, context_len, queries, kb, t, top, *vbs)
+    got, later_top = lax.optimization_barrier((got, later_top))
+    offsets = list(range(1, n_req))
+    (send, *kept), offsets = sorted_by(keep, got, 0, offsets, req_bits[0])
+    send, later_top = lax.optimization_barrier((send, later_top))
+    got = swap(send, "req", req_bits[0])
+    arrived = [got]
     own_keep, own_send = pl.pallas_call(
-        functools.partial(value_kernel, (heads, page_rows, pages_dev, sub)),
+        functools.partial(second_kernel, dims),
         out_shape=(f32(1, slabs, left, LANES), bf16(1, slabs, left, LANES)),
-        in_specs=[SMEM] + [VMEM] * 6,
+        in_specs=[SMEM] + [VMEM] * (8 + len(vbs)),
         out_specs=(VMEM,) * 2,
         scratch_shapes=[
-            pltpu.VMEM((req_dev, rows, LANES), jnp.float32),
-            pltpu.VMEM((req_dev, sub, LANES), jnp.float32)],
+            pltpu.VMEM((part, rows, LANES), jnp.float32),
+            pltpu.VMEM((part, sub, LANES), jnp.float32)],
         compiler_params=params(4),
-        cost_estimate=pl.CostEstimate(
-            flops=2 * req_dev * rows * columns * LANES, transcendentals=req_dev * sub * columns,
-            bytes_accessed=kv_pool.size),
-        name="values",
-    )(table, t, top, vb, acc, ftop, ftot)
+        cost_estimate=cost(0, part),
+        name="second",
+    )(table, later, later_top, top, acc, tot, facc, ftop, ftot, *vbs)
+    got, own_send = lax.optimization_barrier((got, own_send))
     own_got = swap(own_send, "ctx", ctx_bits[0])
-    got, own_keep = lax.optimization_barrier((got, own_keep))
-    offsets, skip, arrived = list(range(1, n_req)), 0, []
-    for bit in req_bits:
-        if offsets:
-            (send, *kept), offsets = sorted_by(keep, got, skip, offsets, bit)
-        keep = kept[0] if kept else None
-        if bit == req_bits[0]:
-            for ctx_bit in ctx_bits[1:]:
-                own_keep, own_send = halved(own_keep, own_got)
-                own_got = swap(own_send, "ctx", ctx_bit)
+    for bit in req_bits[1:]:
+        (send, *kept), offsets = sorted_by(kept[0], got, 1, offsets, bit)
         got = swap(send, "req", bit)
         arrived.append(got)
-        skip = 1
+    for bit in ctx_bits[1:]:
+        own_keep, own_send = halved(own_keep, own_got)
+        own_got = swap(own_send, "ctx", bit)
     return pl.pallas_call(
         last_kernel,
         out_shape=bf16(req_dev, heads, group, LANES),

time: 38.9 us -> 40.8 us (1.049)
  starting transfers between devices: 13.2 us -> 9.4 us
  waiting for transfers between devices: 7.14 us -> 10.8 us
  other arithmetic: 0.08 us -> 1.05 us
  Pallas kernels: 18.1 us -> 19 us
    ppermute x11, starting transfers between devices: 13.2 us -> 9.4 us  [swap(): lax.ppermute(value, axis, [(n, n ^ bit) for n in range(lax.axis_size(axis...]
    ppermute x11, waiting for transfers between devices: 7.14 us -> 10.8 us  [swap(): lax.ppermute(value, axis, [(n, n ^ bit) for n in range(lax.axis_size(axis...]
    broadcast_in_dim x0 -> x1, other arithmetic: none -> 0.77 us  [local(): near = jnp.stack([query] + reqs)[None]]
    pallas_call x2 -> x3, Pallas kernels: 7.38 us -> 8.03 us  [the longest x1 3.2 us: local(): pl.pallas_call(functools.partial(middle_kernel, dims), out_shape=(f32(par...]
  transfers between devices with their start and end apart: 11 -> 11, of which waited for: 4 -> 8; matrix products, arithmetic and copies ran while one was open for 0% -> 0% of each run, Pallas kernels for 37% -> 36%
where the time goes in v8:
time: 40.8 us; the launch traced here: 40.6 us
  Pallas kernels  19 us (47%)
  waiting for transfers between devices  10.8 us (26%)
  starting transfers between devices  9.4 us (23%)
  other arithmetic  1.05 us (3%)
    ppermute x11, waiting for transfers between devices, swap(): lax.ppermute(value, axis, [(n, n ^ bit) for n in range(lax.axis_size(axis...  10.8 us
    ppermute x11, starting transfers between devices, swap(): lax.ppermute(value, axis, [(n, n ^ bit) for n in range(lax.axis_size(axis...  9.4 us
    pallas_call x1, Pallas kernels, local(): pl.pallas_call(functools.partial(stage_keys_kernel, n_ctx, slots), out_sh...  4.08 us
    pallas_call x1, Pallas kernels, local(): pl.pallas_call(functools.partial(middle_kernel, dims), out_shape=(f32(par...  3.2 us
    pallas_call x1, Pallas kernels, local(): pl.pallas_call(functools.partial(first_kernel, dims, pieces), out_shape=(...  2.83 us
    pallas_call x1, Pallas kernels, local(): pl.pallas_call(functools.partial(fresh_kernel, (heads, page_rows, slots,...  2.81 us
    pallas_call x1, Pallas kernels, local(): pl.pallas_call(stage_fresh_kernel, out_shape=(half(new_dev), half(new_dev...  2.05 us
    pallas_call x1, Pallas kernels, local(): pl.pallas_call(functools.partial(second_kernel, dims), out_shape=(f32(1,...  1.99 us
  transfers between devices with their start and end apart: 11, of which 8 were waited for; matrix products, arithmetic and copies ran while one was open for 0% of the time, Pallas kernels for 36%

profile of v8, /device:TPU:0, one launch (start us, length us, event | category | flops | bytes accessed | tf_op | source)
XLA Modules:
  0.0 40.6 jit_solution(7444504305023835609)
XLA Ops:
  0.0 4.0 %collective-permute-start.1 = (bf16[4,4,4,128]{3,2,1,0:T(4,128)(2,1)}, bf16[4,4,4,128]{3,2,1,0:T(4,128)(2,1)S(1)}, u32[]{:S(2)}, u32[]{:S(2)}) collective-permute-start(bf16[4,4,4,128]{3,2,1,0:T(4,128)(2,1)} %param.6), channel_id=1, source_target_pairs={{0,16},{8,24},{16,0},{24,8},{1,17},{9,25},{17,1},{25,9},{2,18},{10... | collective-permute-start | bytes 49160 | tf_op jit(solution)/shard_map/ppermute | solution.py:23
  4.0 1.6 %collective-permute-start = (bf16[4,4,4,128]{3,2,1,0:T(4,128)(2,1)}, bf16[4,4,4,128]{3,2,1,0:T(4,128)(2,1)S(1)}, u32[]{:S(2)}, u32[]{:S(2)}) collective-permute-start(bf16[4,4,4,128]{3,2,1,0:T(4,128)(2,1)} %param.6), channel_id=1, source_target_pairs={{0,8},{8,0},{16,24},{24,16},{1,9},{9,1},{17,25},{25,17},{2,10},{10... | collective-permute-start | bytes 49160 | tf_op jit(solution)/shard_map/ppermute | solution.py:23
  5.6 2.1 %stage_fresh.1 = (bf16[112,16,4,128]{3,2,1,0:T(4,128)(2,1)S(1)}, bf16[112,16,4,128]{3,2,1,0:T(4,128)(2,1)S(1)}) custom-call(bf16[112,16,4,256]{3,2,1,0:T(4,128)(2,1)} %fresh_ref.1), custom_call_target="tpu_custom_call" | custom-call | bytes 7340032 | tf_op jit(solution)/shard_map/stage_fresh/pallas_call | solution.py:439
  7.7 0.3 collective-permute-done
  8.0 3.4 %collective-permute-done.2 = bf16[4,4,4,128]{3,2,1,0:T(4,128)(2,1)S(1)} collective-permute-done((bf16[4,4,4,128]{3,2,1,0:T(4,128)(2,1)}, bf16[4,4,4,128]{3,2,1,0:T(4,128)(2,1)S(1)}, u32[]{:S(2)}, u32[]{:S(2)}) %collective-permute-start.2) | collective-permute-done | bytes 16416 | tf_op jit(solution)/shard_map/ppermute | solution.py:23
  11.4 0.8 %maximum_bitcast_fusion.1 = bf16[1,4,4,4,4,128]{5,4,3,2,1,0:T(4,128)(2,1)S(1)} fusion(bf16[1,4,4,4,128]{4,3,2,1,0:T(4,128)(2,1)S(1)} %bitcast.32, bf16[1,4,4,4,128]{4,3,2,1,0:T(4,128)(2,1)S(1)} %bitcast.30, bf16[1,4,4,4,128]{4,3,2,1,0:T(4,128)(2,1)S(1)} %bitcast.31, bf16[1,4,4,4,128]{4,3,2,1,0:T(4,128)(2,1)} %bitcast.29), kind=kLoop, calls=%fused_computation.2 | loop fusion | flops 98304 | bytes 131072 | tf_op jit(solution)/shard_map/broadcast_in_dim | solution.py:451
  12.1 1.6 %collective-permute-start.3 = (bf16[1,4,4,4,4,128]{5,4,3,2,1,0:T(4,128)(2,1)S(1)}, bf16[1,4,4,4,4,128]{5,4,3,2,1,0:T(4,128)(2,1)S(1)}, u32[]{:S(2)}, u32[]{:S(2)}) collective-permute-start(bf16[1,4,4,4,4,128]{5,4,3,2,1,0:T(4,128)(2,1)S(1)} %maximum_bitcast_fusion.1), channel_id=1, source_target_pairs={{0,4},{2,6},{4,0},{6,2},{1,5},{3,7},{5,1},{7,3},{8,12},{10,14},{12... | collective-permute-start | bytes 196616 | tf_op jit(solution)/shard_map/ppermute | solution.py:23
  13.7 4.1 %stage_keys.1 = (bf16[512,16,4,128]{3,2,1,0:T(4,128)(2,1)S(1)}, s32[128]{0:T(128)S(1)}, s32[16]{0:T(128)S(1)}) custom-call(s32[112]{0:T(128)} %bucket_hbm, bf16[512,16,4,256]{3,2,1,0:T(4,128)(2,1)} %refs_0_.3), custom_call_target="tpu_custom_call" | custom-call | bytes 16777216 | tf_op jit(solution)/shard_map/stage_keys/pallas_call | solution.py:453
  18.0 1.3 %collective-permute-done.4 = bf16[2,4,4,4,4,128]{5,4,3,2,1,0:T(4,128)(2,1)S(1)} collective-permute-done((bf16[2,4,4,4,4,128]{5,4,3,2,1,0:T(4,128)(2,1)S(1)}, bf16[2,4,4,4,4,128]{5,4,3,2,1,0:T(4,128)(2,1)S(1)}, u32[]{:S(2)}, u32[]{:S(2)}) %collective-permute-start.4) | collective-permute-done | bytes 131104 | tf_op jit(solution)/shard_map/ppermute | solution.py:23
  19.6 2.8 %fresh.1 = (f32[3,17,8,128]{3,2,1,0:T(8,128)S(1)}, bf16[3,17,8,128]{3,2,1,0:T(8,128)(2,1)S(1)}, f32[4,64,128]{2,1,0:T(8,128)S(1)}, f32[4,16,128]{2,1,0:T(8,128)S...) custom-call(s32[128]{0:T(128)S(1)} %get-tuple-element.52.slots_ref, ...), custom_call_target="tpu_custom_call" | custom-call | flops 268435456 | bytes 3670016 | tf_op jit(solution)/shard_map/fresh/pallas_call | solution.py:494
  22.7 2.8 %first.1 = (f32[2,16,8192]{2,1,0:T(8,128)S(1)}, f32[2,16,128]{2,1,0:T(8,128)S(1)}, bf16[512,8,4,128]{3,2,1,0:T(4,128)(2,1)S(1)}) custom-call(s32[512]{0:T(512)S(1)} %bitcast.26, s32[4]{0:T(128)S(1)} %copy-done.1, bf16[4,4,64,128]{3,2,1,0:T(8,128)(2,1)S(1)} %bitcast.22, bf16[512,64,128]{2,1,0:T(8,128)(2,1)S(1)} %bitcast.15, bf16[512,16,4,256]{3,2,1,0:T(4,128)(2,1)} %refs_0_.3), custom_call_target="tpu_custom_call" | custom-call | flops 268435456 | bytes 4194304 | tf_op jit(solution)/shard_map/first/pallas_call | solution.py:547
  25.5 0.3 merge.4
  25.9 0.6 %collective-permute-start.6 = (bf16[3,17,4,128]{3,2,1,0:T(4,128)(2,1)S(1)}, bf16[3,17,4,128]{3,2,1,0:T(4,128)(2,1)S(1)}, u32[]{:S(2)}, u32[]{:S(2)}) collective-permute-start(bf16[3,17,4,128]{3,2,1,0:T(4,128)(2,1)S(1)} %get-tuple-element.76), channel_id=1, source_target_pairs={{0,4},{2,6},{4,0},{6,2},{1,5},{3,7},{5,1},{7,3},{8,12},{10,14},{12... | collective-permute-start | bytes 156680 | tf_op jit(solution)/shard_map/ppermute | solution.py:23
  26.5 3.2 %middle.1 = (f32[2,16,8192]{2,1,0:T(8,128)S(1)}, f32[2,16,128]{2,1,0:T(8,128)S(1)}, f32[2,64,128]{2,1,0:T(8,128)S(1)}, f32[2,16,128]{2,1,0:T(8,128)S(1)}) custom-call(s32[512]{0:T(512)S(1)} %bitcast.27, s32[4]{0:T(128)S(1)} %copy-done.1, bf16[4,4,64,128]{3,2,1,0:T(8,128)(2,1)S(1)} %bitcast.23, bf16[512,64,128]{2,1,0:T(8,128)(2,1)S(1)} %bitcast.16, ...), custom_call_target="tpu_custom_call" | custom-call | flops 536870912 | bytes 8388608 | tf_op jit(solution)/shard_map/middle/pallas_call | solution.py:563
  29.7 0.4 collective-permute-done.6.got_ref
  30.1 0.3 merge.5
  30.4 2.0 %second.1 = (f32[1,17,8,128]{3,2,1,0:T(8,128)S(1)}, bf16[1,17,8,128]{3,2,1,0:T(8,128)(2,1)S(1)}) custom-call(s32[512]{0:T(512)S(1)} %bitcast.28, f32[2,16,8192]{2,1,0:T(8,128)S(1)} %get-tuple-element.74.t_ref, f32[2,16,128]{2,1,0:T(8,128)S(1)} %get-tuple-element.81.top_ref, f32[2,16,128]{2,1,0:T(8,128)S(1)} %get-tuple-element.71.top_ref.first_top_ref, ...), custom_call_target="tpu_custom_call" | custom-call | flops 268435456 | bytes 4194304 | tf_op jit(solution)/shard_map/second/pallas_call | solution.py:580
  32.4 1.9 %collective-permute-done.7.got_ref.refs_1_ = bf16[2,17,4,128]{3,2,1,0:T(4,128)(2,1)S(1)} collective-permute-done((bf16[2,17,4,128]{3,2,1,0:T(4,128)(2,1)S(1)}, bf16[2,17,4,128]{3,2,1,0:T(4,128)(2,1)S(1)}, u32[]{:S(2)}, u32[]{:S(2)}) %collective-permute-start.7) | collective-permute-done | bytes 34848 | tf_op jit(solution)/shard_map/ppermute | solution.py:23
  34.7 0.9 %collective-permute-done.8.got_ref = bf16[1,17,8,128]{3,2,1,0:T(8,128)(2,1)S(1)} collective-permute-done((bf16[1,17,8,128]{3,2,1,0:T(8,128)(2,1)S(1)}, bf16[1,17,8,128]{3,2,1,0:T(8,128)(2,1)S(1)}, u32[]{:S(2)}, u32[]{:S(2)}) %collective-permute-start.8) | collective-permute-done | bytes 34848 | tf_op jit(solution)/shard_map/ppermute | solution.py:23
  35.6 0.3 merge.6
  35.8 1.2 %collective-permute-start.9 = (bf16[1,17,4,128]{3,2,1,0:T(4,128)(2,1)S(1)}, bf16[1,17,4,128]{3,2,1,0:T(4,128)(2,1)S(1)}, u32[]{:S(2)}, u32[]{:S(2)}) collective-permute-start(bf16[1,17,4,128]{3,2,1,0:T(4,128)(2,1)S(1)} %get-tuple-element.92), channel_id=1, source_target_pairs={{0,4},{2,6},{4,0},{6,2},{1,5},{3,7},{5,1},{7,3},{8,12},{10,14},{12... | collective-permute-start | bytes 52232 | tf_op jit(solution)/shard_map/ppermute | solution.py:23
  37.0 2.3 %collective-permute-done.10.refs_2_ = bf16[1,17,4,128]{3,2,1,0:T(4,128)(2,1)S(1)} collective-permute-done((bf16[1,17,4,128]{3,2,1,0:T(4,128)(2,1)S(1)}, bf16[1,17,4,128]{3,2,1,0:T(4,128)(2,1)S(1)}, u32[]{:S(2)}, u32[]{:S(2)}) %collective-permute-start.10) | collective-permute-done | bytes 17440 | tf_op jit(solution)/shard_map/ppermute | solution.py:23
  39.3 0.3 collective-permute-done.9.refs_0_
  39.7 0.9 %last.1 = bf16[4,4,4,128]{3,2,1,0:T(4,128)(2,1)} custom-call(f32[1,17,4,128]{3,2,1,0:T(4,128)S(1)} %get-tuple-element.91.keep_ref, bf16[1,17,4,128]{3,2,1,0:T(4,128)(2,1)S(1)} %collective-permute-done.9.refs_0_, bf16[2,17,4,128]{3,2,1,0:T(4,128)(2,1)S(1)} %collective-permute-done.7.got_ref.refs_1_, bf16[1,17,4,128]{3,2,1,0:T(4,128)(2,1)S(1)} %collective-permute-done.10.refs_2_), custom_call_target="tpu_custom_call" | custom-call | tf_op jit(solution)/shard_map/last/pallas_call | solution.py:601
  (17 shorter events, 1.1 us)
Async XLA Ops:
  0.0 7.7 %collective-permute-start.1 = (bf16[4,4,4,128]{3,2,1,0:T(4,128)(2,1)}, bf16[4,4,4,128]{3,2,1,0:T(4,128)(2,1)S(1)}, u32[]{:S(2)}, u32[]{:S(2)}) collective-permute-start(bf16[4,4,4,128]{3,2,1,0:T(4,128)(2,1)} %param.6), channel_id=1, source_target_pairs={{0,16},{8,24},{16,0},{24,8},{1,17},{9,25},{17,1},{25,9},{2,18},{10... | collective-permute-start | bytes 49160 | tf_op jit(solution)/shard_map/ppermute | solution.py:23
  4.0 3.9 %collective-permute-start = (bf16[4,4,4,128]{3,2,1,0:T(4,128)(2,1)}, bf16[4,4,4,128]{3,2,1,0:T(4,128)(2,1)S(1)}, u32[]{:S(2)}, u32[]{:S(2)}) collective-permute-start(bf16[4,4,4,128]{3,2,1,0:T(4,128)(2,1)} %param.6), channel_id=1, source_target_pairs={{0,8},{8,0},{16,24},{24,16},{1,9},{9,1},{17,25},{25,17},{2,10},{10... | collective-permute-start | bytes 49160 | tf_op jit(solution)/shard_map/ppermute | solution.py:23
  5.6 5.7 %collective-permute-start.2 = (bf16[4,4,4,128]{3,2,1,0:T(4,128)(2,1)}, bf16[4,4,4,128]{3,2,1,0:T(4,128)(2,1)S(1)}, u32[]{:S(2)}, u32[]{:S(2)}) collective-permute-start(bf16[4,4,4,128]{3,2,1,0:T(4,128)(2,1)} %param.6), channel_id=1, source_target_pairs={{0,24},{8,16},{16,8},{24,0},{1,25},{9,17},{17,9},{25,1},{2,26},{10... | collective-permute-start | bytes 49160 | tf_op jit(solution)/shard_map/ppermute | solution.py:23
  12.1 5.6 %collective-permute-start.3 = (bf16[1,4,4,4,4,128]{5,4,3,2,1,0:T(4,128)(2,1)S(1)}, bf16[1,4,4,4,4,128]{5,4,3,2,1,0:T(4,128)(2,1)S(1)}, u32[]{:S(2)}, u32[]{:S(2)}) collective-permute-start(bf16[1,4,4,4,4,128]{5,4,3,2,1,0:T(4,128)(2,1)S(1)} %maximum_bitcast_fusion.1), channel_id=1, source_target_pairs={{0,4},{2,6},{4,0},{6,2},{1,5},{3,7},{5,1},{7,3},{8,12},{10,14},{12... | collective-permute-start | bytes 196616 | tf_op jit(solution)/shard_map/ppermute | solution.py:23
  17.9 1.4 %collective-permute-start.4 = (bf16[2,4,4,4,4,128]{5,4,3,2,1,0:T(4,128)(2,1)S(1)}, bf16[2,4,4,4,4,128]{5,4,3,2,1,0:T(4,128)(2,1)S(1)}, u32[]{:S(2)}, u32[]{:S(2)}) collective-permute-start(bf16[2,4,4,4,4,128]{5,4,3,2,1,0:T(4,128)(2,1)S(1)} %pad_maximum_fusion), channel_id=1, source_target_pairs={{0,2},{2,0},{4,6},{6,4},{1,3},{3,1},{5,7},{7,5},{8,10},{10,8},{12,... | collective-permute-start | bytes 393224 | tf_op jit(solution)/shard_map/ppermute | solution.py:23
  19.6 3.1 %copy-start = (s32[4,128]{1,0:T(4,128)S(1)}, s32[4,128]{1,0:T(4,128)}, u32[]{:S(2)}) copy-start(s32[4,128]{1,0:T(4,128)} %param.8) | copy-start | bytes 6148
  19.6 3.1 %copy-start.1 = (s32[4]{0:T(128)S(1)}, s32[4]{0:T(128)}, u32[]{:S(2)}) copy-start(s32[4]{0:T(128)} %len_ref.3) | copy-start | bytes 52
  22.5 3.1 %collective-permute-start.5 = (bf16[3,17,8,128]{3,2,1,0:T(8,128)(2,1)S(1)}, bf16[3,17,8,128]{3,2,1,0:T(8,128)(2,1)S(1)}, u32[]{:S(2)}, u32[]{:S(2)}) collective-permute-start(bf16[3,17,8,128]{3,2,1,0:T(8,128)(2,1)S(1)} %get-tuple-element.66), channel_id=1, source_target_pairs={{0,2},{2,0},{4,6},{6,4},{1,3},{3,1},{5,7},{7,5},{8,10},{10,8},{12,... | collective-permute-start | bytes 313352 | tf_op jit(solution)/shard_map/ppermute | solution.py:23
  25.9 4.2 %collective-permute-start.6 = (bf16[3,17,4,128]{3,2,1,0:T(4,128)(2,1)S(1)}, bf16[3,17,4,128]{3,2,1,0:T(4,128)(2,1)S(1)}, u32[]{:S(2)}, u32[]{:S(2)}) collective-permute-start(bf16[3,17,4,128]{3,2,1,0:T(4,128)(2,1)S(1)} %get-tuple-element.76), channel_id=1, source_target_pairs={{0,4},{2,6},{4,0},{6,2},{1,5},{3,7},{5,1},{7,3},{8,12},{10,14},{12... | collective-permute-start | bytes 156680 | tf_op jit(solution)/shard_map/ppermute | solution.py:23
  30.4 4.0 %collective-permute-start.7 = (bf16[2,17,4,128]{3,2,1,0:T(4,128)(2,1)S(1)}, bf16[2,17,4,128]{3,2,1,0:T(4,128)(2,1)S(1)}, u32[]{:S(2)}, u32[]{:S(2)}) collective-permute-start(bf16[2,17,4,128]{3,2,1,0:T(4,128)(2,1)S(1)} %get-tuple-element.88), channel_id=1, source_target_pairs={{0,8},{8,0},{16,24},{24,16},{1,9},{9,1},{17,25},{25,17},{2,10},{10... | collective-permute-start | bytes 104456 | tf_op jit(solution)/shard_map/ppermute | solution.py:23
  34.4 1.2 %collective-permute-start.8 = (bf16[1,17,8,128]{3,2,1,0:T(8,128)(2,1)S(1)}, bf16[1,17,8,128]{3,2,1,0:T(8,128)(2,1)S(1)}, u32[]{:S(2)}, u32[]{:S(2)}) collective-permute-start(bf16[1,17,8,128]{3,2,1,0:T(8,128)(2,1)S(1)} %get-tuple-element.90), channel_id=1, source_target_pairs={{0,2},{2,0},{4,6},{6,4},{1,3},{3,1},{5,7},{7,5},{8,10},{10,8},{12,... | collective-permute-start | bytes 104456 | tf_op jit(solution)/shard_map/ppermute | solution.py:23
  34.6 4.7 %collective-permute-start.10 = (bf16[1,17,4,128]{3,2,1,0:T(4,128)(2,1)S(1)}, bf16[1,17,4,128]{3,2,1,0:T(4,128)(2,1)S(1)}, u32[]{:S(2)}, u32[]{:S(2)}) collective-permute-start(bf16[1,17,4,128]{3,2,1,0:T(4,128)(2,1)S(1)} %merge.7), channel_id=1, source_target_pairs={{0,16},{8,24},{16,0},{24,8},{1,17},{9,25},{17,1},{25,9},{2,18},{10... | collective-permute-start | bytes 52232 | tf_op jit(solution)/shard_map/ppermute | solution.py:23
  35.8 3.8 %collective-permute-start.9 = (bf16[1,17,4,128]{3,2,1,0:T(4,128)(2,1)S(1)}, bf16[1,17,4,128]{3,2,1,0:T(4,128)(2,1)S(1)}, u32[]{:S(2)}, u32[]{:S(2)}) collective-permute-start(bf16[1,17,4,128]{3,2,1,0:T(4,128)(2,1)S(1)} %get-tuple-element.92), channel_id=1, source_target_pairs={{0,4},{2,6},{4,0},{6,2},{1,5},{3,7},{5,1},{7,3},{8,12},{10,14},{12... | collective-permute-start | bytes 52232 | tf_op jit(solution)/shard_map/ppermute | solution.py:23

commit v9 on v8

--- a/solution.py
+++ b/solution.py
@@ -154,7 +154,7 @@
     limit = len_ref[i] * heads - lax.axis_index("ctx") * columns
     for c in range(columns // wide):
         keys = pages_of([kb], table_ref, i * pages_dev + c * per, per)
-        parts = score_parts(q_ref[0, i], keys, lane, limit, c * wide, heads, sub)
+        parts = score_parts(q_ref[i], keys, lane, limit, c * wide, heads, sub)
         for j, part in enumerate(parts):
             t_ref[at, :, c * wide + j * LANES:c * wide + (j + 1) * LANES] = part
         top = jnp.maximum(top, fold_max(parts))
@@ -273,10 +273,10 @@
     return out
 
 
-def fresh_kernel(dims, pieces, slots_ref, counts_ref, q_ref, kf, vf, *refs):
+def fresh_kernel(dims, pieces, n_req, slots_ref, counts_ref, kf, vf, *refs):
     heads, page_rows, slots, sub = dims
-    n_req, req_dev = q_ref.shape[:2]
-    refs = list(refs)
+    q_refs, refs = refs[:n_req], list(refs[n_req:])
+    req_dev = q_refs[0].shape[0]
     pool = [refs.pop(0)] if pieces else []
     keep_ref, send_ref, acc_ref, top_ref, tot_ref, *refs = refs
     target = [refs.pop(0)] if pieces else []
@@ -297,7 +297,8 @@
         top = jnp.full((sub, LANES), NEG, jnp.float32)
         for c in range(columns // wide):
             keys = pages_of([kf], slots_ref, request * slots + c * per, per)
-            parts = score_parts(q_ref[n // req_dev, n % req_dev], keys, lane, limit, c * wide, heads, sub)
+            parts = score_parts(
+                q_refs[n // req_dev][n % req_dev], keys, lane, limit, c * wide, heads, sub)
             for j, part in enumerate(parts):
                 t_s[n, :, c * wide + j * LANES:c * wide + (j + 1) * LANES] = part
             top = jnp.maximum(top, fold_max(parts))
@@ -430,8 +431,9 @@
     split = heads % 4 == 0
     pieces = 8 if split else 0
 
-    reqs = [swap(query, "req", k) for k in range(n_req - 1, 0, -1)][::-1]
+    near = query[None]
     first, *others = bits_of("ctx")
+    arrived = swap(near, "ctx", first)
     if split:
         in_hbm = lambda a: pltpu.with_memory_space_constraint(a, pltpu.HBM)
         pool = in_hbm(kv_pool)
@@ -447,9 +449,7 @@
                 flops=0, transcendentals=0, bytes_accessed=4 * fresh_kv.size),
             name="stage_fresh",
         )(in_hbm(fresh_kv))
-        bucket, kf, *reqs = lax.optimization_barrier((in_hbm(fresh_bucket), kf, *reqs))
-        near = jnp.stack([query] + reqs)[None]
-        arrived = swap(near, "ctx", first)
+        arrived, kf = lax.optimization_barrier((arrived, kf))
         kb, slot_table, counts = pl.pallas_call(
             functools.partial(stage_keys_kernel, n_ctx, slots),
             out_shape=(half(pool_slots), smem(n_reqs * slots), smem(n_reqs)),
@@ -462,8 +462,7 @@
             cost_estimate=pl.CostEstimate(
                 flops=0, transcendentals=0, bytes_accessed=2 * kv_pool.size),
             name="stage_keys",
-        )(in_hbm(bucket), pool)
-        arrived, counts = lax.optimization_barrier((arrived, counts))
+        )(in_hbm(fresh_bucket), pool)
         kb, kf, vf = (a.reshape(a.shape[0], page_rows, LANES) for a in (kb, kf, vf))
         value_in, value_specs = (pool,), [HBM]
         value_out = (bf16(pool_slots, page // 2, heads, LANES),)
@@ -481,23 +480,22 @@
             name="list",
         )(fresh_bucket)
         value_in, value_specs, value_out, value_scratch = (), [], (), []
-        near = jnp.stack([query] + reqs)[None]
-        arrived = swap(near, "ctx", first)
 
     near = jnp.concatenate([near, arrived])
     for bit in others:
         near = jnp.concatenate([near, swap(near, "ctx", bit)])
-    queries = near.transpose(1, 2, 3, 0, 4, 5).reshape(n_req, req_dev, rows, head_dim)
+    queries = near.transpose(1, 2, 0, 3, 4).reshape(req_dev, rows, head_dim)
+    far = [swap(queries, "req", k) for k in range(n_req - 1, 0, -1)][::-1]
 
     slabs = req_dev * heads + 1
     left = sub // 2
     keep, send, facc, ftop, ftot, *vbs = pl.pallas_call(
-        functools.partial(fresh_kernel, (heads, page_rows, slots, sub), pieces),
+        functools.partial(fresh_kernel, (heads, page_rows, slots, sub), pieces, n_req),
         out_shape=(
             f32(n_req - 1, slabs, left, LANES), bf16(n_req - 1, slabs, left, LANES),
             f32(req_dev, rows, LANES), f32(req_dev, sub, LANES), f32(req_dev, sub, LANES),
         ) + value_out,
-        in_specs=[SMEM] * 2 + [VMEM] * 3 + value_specs,
+        in_specs=[SMEM] * 2 + [VMEM] * (2 + n_req) + value_specs,
         out_specs=(VMEM,) * (5 + len(value_out)),
         scratch_shapes=[
             pltpu.VMEM((n_reqs, sub, slots * page_rows), jnp.float32),
@@ -508,7 +506,7 @@
             flops=4 * n_reqs * rows * slots * page_rows * LANES,
             transcendentals=n_reqs * sub * slots * page_rows, bytes_accessed=2 * fresh_kv.size),
         name="fresh",
-    )(slot_table, counts, queries, kf, vf, *value_in)
+    )(slot_table, counts, kf, vf, queries, *far, *value_in)
 
     def merge(keep, got, skip, goals, shapes):
         return pl.pallas_call(
@@ -589,10 +587,11 @@
         cost_estimate=cost(0, part),
         name="second",
     )(table, later, later_top, top, acc, tot, facc, ftop, ftot, *vbs)
-    got, own_send = lax.optimization_barrier((got, own_send))
+    got, own_keep = lax.optimization_barrier((got, own_keep))
     own_got = swap(own_send, "ctx", ctx_bits[0])
     for bit in req_bits[1:]:
         (send, *kept), offsets = sorted_by(kept[0], got, 1, offsets, bit)
+        send, own_got = lax.optimization_barrier((send, own_got))
         got = swap(send, "req", bit)
         arrived.append(got)
     for bit in ctx_bits[1:]:

time: 40.8 us -> 40.6 us (level)
  waiting for transfers between devices: 10.8 us -> 5.85 us
  starting transfers between devices: 9.4 us -> 13.7 us
  other arithmetic: 1.05 us -> 1.51 us
    ppermute x11, waiting for transfers between devices: 10.8 us -> 5.85 us  [swap(): lax.ppermute(value, axis, [(n, n ^ bit) for n in range(lax.axis_size(axis...]
    ppermute x11, starting transfers between devices: 9.4 us -> 13.7 us  [swap(): lax.ppermute(value, axis, [(n, n ^ bit) for n in range(lax.axis_size(axis...]
    broadcast_in_dim x1 -> x0, other arithmetic: 0.77 us -> none  [local(): near = jnp.stack([query] + reqs)[None]]
    concatenate x1, other arithmetic: 0.09 us -> 0.75 us  [local(): near = jnp.concatenate([near, arrived])]
    transpose x1, other arithmetic: 0.19 us -> 0.77 us  [local(): queries = near.transpose(1, 2, 0, 3, 4).reshape(req_dev, rows, head_dim)]
  transfers between devices with their start and end apart: 11 -> 11, of which waited for: 8 -> 6; matrix products, arithmetic and copies ran while one was open for 0% -> 0% of each run, Pallas kernels for 36% -> 36%
where the time goes in v9:
time: 40.6 us; the launch traced here: 40.3 us
  Pallas kernels  19.1 us (47%)
  starting transfers between devices  13.7 us (34%)
  waiting for transfers between devices  5.85 us (14%)
  other arithmetic  1.51 us (4%)
    ppermute x11, starting transfers between devices, swap(): lax.ppermute(value, axis, [(n, n ^ bit) for n in range(lax.axis_size(axis...  13.7 us
    ppermute x11, waiting for transfers between devices, swap(): lax.ppermute(value, axis, [(n, n ^ bit) for n in range(lax.axis_size(axis...  5.85 us
    pallas_call x1, Pallas kernels, local(): pl.pallas_call(functools.partial(stage_keys_kernel, n_ctx, slots), out_sh...  4.08 us
    pallas_call x1, Pallas kernels, local(): pl.pallas_call(functools.partial(middle_kernel, dims), out_shape=(f32(par...  3.22 us
    pallas_call x1, Pallas kernels, local(): pl.pallas_call(functools.partial(first_kernel, dims, pieces), out_shape=(...  2.83 us
    pallas_call x1, Pallas kernels, local(): pl.pallas_call(functools.partial(fresh_kernel, (heads, page_rows, slots,...  2.81 us
    pallas_call x1, Pallas kernels, local(): pl.pallas_call(stage_fresh_kernel, out_shape=(half(new_dev), half(new_dev...  2.05 us
    pallas_call x1, Pallas kernels, local(): pl.pallas_call(functools.partial(second_kernel, dims), out_shape=(f32(1,...  2 us
  transfers between devices with their start and end apart: 11, of which 6 were waited for; matrix products, arithmetic and copies ran while one was open for 0% of the time, Pallas kernels for 36%

profile of v9, /device:TPU:0, one launch (start us, length us, event | category | flops | bytes accessed | tf_op | source)
XLA Modules:
  0.0 40.3 jit_solution(16482556334802159280)
XLA Ops:
  0.0 2.9 %collective-permute-start = (bf16[1,4,4,4,128]{4,3,2,1,0:T(4,128)(2,1)}, bf16[1,4,4,4,128]{4,3,2,1,0:T(4,128)(2,1)S(1)}, u32[]{:S(2)}, u32[]{:S(2)}) collective-permute-start(bf16[1,4,4,4,128]{4,3,2,1,0:T(4,128)(2,1)} %bitcast.27), channel_id=1, source_target_pairs={{0,4},{2,6},{4,0},{6,2},{1,5},{3,7},{5,1},{7,3},{8,12},{10,14},{12... | collective-permute-start | bytes 49160 | tf_op jit(solution)/shard_map/ppermute | solution.py:23
  2.9 2.1 %stage_fresh.1 = (bf16[112,16,4,128]{3,2,1,0:T(4,128)(2,1)S(1)}, bf16[112,16,4,128]{3,2,1,0:T(4,128)(2,1)S(1)}) custom-call(bf16[112,16,4,256]{3,2,1,0:T(4,128)(2,1)} %fresh_ref.1), custom_call_target="tpu_custom_call" | custom-call | bytes 7340032 | tf_op jit(solution)/shard_map/stage_fresh/pallas_call | solution.py:441
  5.0 0.7 %pad_maximum_fusion = bf16[2,4,4,4,128]{4,3,2,1,0:T(4,128)(2,1)S(1)} fusion(bf16[1,4,4,4,128]{4,3,2,1,0:T(4,128)(2,1)S(1)} %collective-permute-done, bf16[1,4,4,4,128]{4,3,2,1,0:T(4,128)(2,1)} %bitcast.28), kind=kLoop, calls=%fused_computation.1 | loop fusion | flops 16384 | bytes 65536 | tf_op jit(solution)/shard_map/concatenate | solution.py:484
  5.8 1.2 %collective-permute-done.1 = bf16[2,4,4,4,128]{4,3,2,1,0:T(4,128)(2,1)S(1)} collective-permute-done((bf16[2,4,4,4,128]{4,3,2,1,0:T(4,128)(2,1)S(1)}, bf16[2,4,4,4,128]{4,3,2,1,0:T(4,128)(2,1)S(1)}, u32[]{:S(2)}, u32[]{:S(2)}) %collective-permute-start.1) | collective-permute-done | bytes 32800 | tf_op jit(solution)/shard_map/ppermute | solution.py:23
  7.0 0.8 %maximum_bitcast_fusion = bf16[4,4,4,4,128]{4,3,1,0,2:T(4,128)(2,1)S(1)} fusion(bf16[2,4,4,4,128]{4,3,2,1,0:T(4,128)(2,1)S(1)} %collective-permute-done.1, bf16[1,4,4,4,128]{4,3,2,1,0:T(4,128)(2,1)S(1)} %collective-permute-done, bf16[1,4,4,4,128]{4,3,2,1,0:T(4,128)(2,1)} %bitcast.29), kind=kLoop, calls=%fused_computation | loop fusion | flops 65536 | bytes 131072 | tf_op jit(solution)/shard_map/transpose | solution.py:487
  7.8 4.0 %collective-permute-start.4 = (bf16[4,64,128]{2,1,0:T(8,128)(2,1)S(1)}, bf16[4,64,128]{2,1,0:T(8,128)(2,1)S(1)}, u32[]{:S(2)}, u32[]{:S(2)}) collective-permute-start(bf16[4,64,128]{2,1,0:T(8,128)(2,1)S(1)} %bitcast.18), channel_id=1, source_target_pairs={{0,24},{8,16},{16,8},{24,0},{1,25},{9,17},{17,9},{25,1},{2,26},{10... | collective-permute-start | bytes 196616 | tf_op jit(solution)/shard_map/ppermute | solution.py:23
  11.9 0.6 %collective-permute-start.2 = (bf16[4,64,128]{2,1,0:T(8,128)(2,1)S(1)}, bf16[4,64,128]{2,1,0:T(8,128)(2,1)S(1)}, u32[]{:S(2)}, u32[]{:S(2)}) collective-permute-start(bf16[4,64,128]{2,1,0:T(8,128)(2,1)S(1)} %bitcast.20), channel_id=1, source_target_pairs={{0,8},{8,0},{16,24},{24,16},{1,9},{9,1},{17,25},{25,17},{2,10},{10... | collective-permute-start | bytes 196616 | tf_op jit(solution)/shard_map/ppermute | solution.py:23
  12.5 4.1 %stage_keys.1 = (bf16[512,16,4,128]{3,2,1,0:T(4,128)(2,1)S(1)}, s32[128]{0:T(128)S(1)}, s32[16]{0:T(128)S(1)}) custom-call(s32[112]{0:T(128)} %bucket_hbm.1, bf16[512,16,4,256]{3,2,1,0:T(4,128)(2,1)} %refs_0_.1), custom_call_target="tpu_custom_call" | custom-call | bytes 16777216 | tf_op jit(solution)/shard_map/stage_keys/pallas_call | solution.py:453
  16.6 1.1 %collective-permute-done.3.refs_2_ = bf16[4,64,128]{2,1,0:T(8,128)(2,1)S(1)} collective-permute-done((bf16[4,64,128]{2,1,0:T(8,128)(2,1)S(1)}, bf16[4,64,128]{2,1,0:T(8,128)(2,1)S(1)}, u32[]{:S(2)}, u32[]{:S(2)}) %collective-permute-start.3) | collective-permute-done | bytes 65568 | tf_op jit(solution)/shard_map/ppermute | solution.py:23
  17.8 2.8 %fresh.1 = (f32[3,17,8,128]{3,2,1,0:T(8,128)S(1)}, bf16[3,17,8,128]{3,2,1,0:T(8,128)(2,1)S(1)}, f32[4,64,128]{2,1,0:T(8,128)S(1)}, f32[4,16,128]{2,1,0:T(8,128)S...) custom-call(s32[128]{0:T(128)S(1)} %get-tuple-element.47.slots_ref, ...), custom_call_target="tpu_custom_call" | custom-call | flops 268435456 | bytes 3670016 | tf_op jit(solution)/shard_map/fresh/pallas_call | solution.py:492
  20.7 2.8 %first.1 = (f32[2,16,8192]{2,1,0:T(8,128)S(1)}, f32[2,16,128]{2,1,0:T(8,128)S(1)}, bf16[512,8,4,128]{3,2,1,0:T(4,128)(2,1)S(1)}) custom-call(s32[512]{0:T(512)S(1)} %bitcast.24, s32[4]{0:T(128)S(1)} %copy-done.1, bf16[4,64,128]{2,1,0:T(8,128)(2,1)S(1)} %bitcast.22, bf16[512,64,128]{2,1,0:T(8,128)(2,1)S(1)} %bitcast.10, bf16[512,16,4,256]{3,2,1,0:T(4,128)(2,1)} %refs_0_.1), custom_call_target="tpu_custom_call" | custom-call | flops 268435456 | bytes 4194304 | tf_op jit(solution)/shard_map/first/pallas_call | solution.py:545
  23.6 0.3 merge.4
  23.9 1.6 %collective-permute-start.6 = (bf16[3,17,4,128]{3,2,1,0:T(4,128)(2,1)S(1)}, bf16[3,17,4,128]{3,2,1,0:T(4,128)(2,1)S(1)}, u32[]{:S(2)}, u32[]{:S(2)}) collective-permute-start(bf16[3,17,4,128]{3,2,1,0:T(4,128)(2,1)S(1)} %get-tuple-element.63), channel_id=1, source_target_pairs={{0,4},{2,6},{4,0},{6,2},{1,5},{3,7},{5,1},{7,3},{8,12},{10,14},{12... | collective-permute-start | bytes 156680 | tf_op jit(solution)/shard_map/ppermute | solution.py:23
  25.4 3.2 %middle.1 = (f32[2,16,8192]{2,1,0:T(8,128)S(1)}, f32[2,16,128]{2,1,0:T(8,128)S(1)}, f32[2,64,128]{2,1,0:T(8,128)S(1)}, f32[2,16,128]{2,1,0:T(8,128)S(1)}) custom-call(s32[512]{0:T(512)S(1)} %bitcast.25, s32[4]{0:T(128)S(1)} %copy-done.1, bf16[4,64,128]{2,1,0:T(8,128)(2,1)S(1)} %bitcast.23, bf16[512,64,128]{2,1,0:T(8,128)(2,1)S(1)} %bitcast.11, ...), custom_call_target="tpu_custom_call" | custom-call | flops 536870912 | bytes 8388608 | tf_op jit(solution)/shard_map/middle/pallas_call | solution.py:561
  28.6 0.3 merge.5
  29.0 1.2 %collective-permute-start.7 = (bf16[2,17,4,128]{3,2,1,0:T(4,128)(2,1)S(1)}, bf16[2,17,4,128]{3,2,1,0:T(4,128)(2,1)S(1)}, u32[]{:S(2)}, u32[]{:S(2)}) collective-permute-start(bf16[2,17,4,128]{3,2,1,0:T(4,128)(2,1)S(1)} %get-tuple-element.72), channel_id=1, source_target_pairs={{0,8},{8,0},{16,24},{24,16},{1,9},{9,1},{17,25},{25,17},{2,10},{10... | collective-permute-start | bytes 104456 | tf_op jit(solution)/shard_map/ppermute | solution.py:23
  30.2 2.0 %second.1 = (f32[1,17,8,128]{3,2,1,0:T(8,128)S(1)}, bf16[1,17,8,128]{3,2,1,0:T(8,128)(2,1)S(1)}) custom-call(s32[512]{0:T(512)S(1)} %bitcast.26, f32[2,16,8192]{2,1,0:T(8,128)S(1)} %get-tuple-element.73.t_ref, f32[2,16,128]{2,1,0:T(8,128)S(1)} %get-tuple-element.74.top_ref, f32[2,16,128]{2,1,0:T(8,128)S(1)} %get-tuple-element.65.top_ref.first_top_ref, ...), custom_call_target="tpu_custom_call" | custom-call | flops 268435456 | bytes 4194304 | tf_op jit(solution)/shard_map/second/pallas_call | solution.py:578
  32.2 0.7 %collective-permute-done.7.got_ref.refs_1_ = bf16[2,17,4,128]{3,2,1,0:T(4,128)(2,1)S(1)} collective-permute-done((bf16[2,17,4,128]{3,2,1,0:T(4,128)(2,1)S(1)}, bf16[2,17,4,128]{3,2,1,0:T(4,128)(2,1)S(1)}, u32[]{:S(2)}, u32[]{:S(2)}) %collective-permute-start.7) | collective-permute-done | bytes 34848 | tf_op jit(solution)/shard_map/ppermute | solution.py:23
  33.4 0.3 merge.7
  33.7 1.0 %collective-permute-start.9 = (bf16[1,17,4,128]{3,2,1,0:T(4,128)(2,1)S(1)}, bf16[1,17,4,128]{3,2,1,0:T(4,128)(2,1)S(1)}, u32[]{:S(2)}, u32[]{:S(2)}) collective-permute-start(bf16[1,17,4,128]{3,2,1,0:T(4,128)(2,1)S(1)} %get-tuple-element.87), channel_id=1, source_target_pairs={{0,4},{2,6},{4,0},{6,2},{1,5},{3,7},{5,1},{7,3},{8,12},{10,14},{12... | collective-permute-start | bytes 52232 | tf_op jit(solution)/shard_map/ppermute | solution.py:23
  34.7 2.1 %collective-permute-start.10 = (bf16[1,17,4,128]{3,2,1,0:T(4,128)(2,1)S(1)}, bf16[1,17,4,128]{3,2,1,0:T(4,128)(2,1)S(1)}, u32[]{:S(2)}, u32[]{:S(2)}) collective-permute-start(bf16[1,17,4,128]{3,2,1,0:T(4,128)(2,1)S(1)} %merge.6), channel_id=1, source_target_pairs={{0,16},{8,24},{16,0},{24,8},{1,17},{9,25},{17,1},{25,9},{2,18},{10... | collective-permute-start | bytes 52232 | tf_op jit(solution)/shard_map/ppermute | solution.py:23
  36.8 0.7 %collective-permute-done.9.refs_0_ = bf16[1,17,4,128]{3,2,1,0:T(4,128)(2,1)S(1)} collective-permute-done((bf16[1,17,4,128]{3,2,1,0:T(4,128)(2,1)S(1)}, bf16[1,17,4,128]{3,2,1,0:T(4,128)(2,1)S(1)}, u32[]{:S(2)}, u32[]{:S(2)}) %collective-permute-start.9) | collective-permute-done | bytes 17440 | tf_op jit(solution)/shard_map/ppermute | solution.py:23
  37.5 1.8 %collective-permute-done.10.refs_2_ = bf16[1,17,4,128]{3,2,1,0:T(4,128)(2,1)S(1)} collective-permute-done((bf16[1,17,4,128]{3,2,1,0:T(4,128)(2,1)S(1)}, bf16[1,17,4,128]{3,2,1,0:T(4,128)(2,1)S(1)}, u32[]{:S(2)}, u32[]{:S(2)}) %collective-permute-start.10) | collective-permute-done | bytes 17440 | tf_op jit(solution)/shard_map/ppermute | solution.py:23
  39.4 0.9 %last.1 = bf16[4,4,4,128]{3,2,1,0:T(4,128)(2,1)} custom-call(f32[1,17,4,128]{3,2,1,0:T(4,128)S(1)} %get-tuple-element.86.keep_ref, bf16[1,17,4,128]{3,2,1,0:T(4,128)(2,1)S(1)} %collective-permute-done.9.refs_0_, bf16[2,17,4,128]{3,2,1,0:T(4,128)(2,1)S(1)} %collective-permute-done.7.got_ref.refs_1_, bf16[1,17,4,128]{3,2,1,0:T(4,128)(2,1)S(1)} %collective-permute-done.10.refs_2_), custom_call_target="tpu_custom_call" | custom-call | tf_op jit(solution)/shard_map/last/pallas_call | solution.py:600
  (16 shorter events, 0.7 us)
Async XLA Ops:
  0.0 5.0 %collective-permute-start = (bf16[1,4,4,4,128]{4,3,2,1,0:T(4,128)(2,1)}, bf16[1,4,4,4,128]{4,3,2,1,0:T(4,128)(2,1)S(1)}, u32[]{:S(2)}, u32[]{:S(2)}) collective-permute-start(bf16[1,4,4,4,128]{4,3,2,1,0:T(4,128)(2,1)} %bitcast.27), channel_id=1, source_target_pairs={{0,4},{2,6},{4,0},{6,2},{1,5},{3,7},{5,1},{7,3},{8,12},{10,14},{12... | collective-permute-start | bytes 49160 | tf_op jit(solution)/shard_map/ppermute | solution.py:23
  5.8 1.3 %collective-permute-start.1 = (bf16[2,4,4,4,128]{4,3,2,1,0:T(4,128)(2,1)S(1)}, bf16[2,4,4,4,128]{4,3,2,1,0:T(4,128)(2,1)S(1)}, u32[]{:S(2)}, u32[]{:S(2)}) collective-permute-start(bf16[2,4,4,4,128]{4,3,2,1,0:T(4,128)(2,1)S(1)} %pad_maximum_fusion), channel_id=1, source_target_pairs={{0,2},{2,0},{4,6},{6,4},{1,3},{3,1},{5,7},{7,5},{8,10},{10,8},{12,... | collective-permute-start | bytes 98312 | tf_op jit(solution)/shard_map/ppermute | solution.py:23
  7.8 8.8 %collective-permute-start.4 = (bf16[4,64,128]{2,1,0:T(8,128)(2,1)S(1)}, bf16[4,64,128]{2,1,0:T(8,128)(2,1)S(1)}, u32[]{:S(2)}, u32[]{:S(2)}) collective-permute-start(bf16[4,64,128]{2,1,0:T(8,128)(2,1)S(1)} %bitcast.18), channel_id=1, source_target_pairs={{0,24},{8,16},{16,8},{24,0},{1,25},{9,17},{17,9},{25,1},{2,26},{10... | collective-permute-start | bytes 196616 | tf_op jit(solution)/shard_map/ppermute | solution.py:23
  11.9 5.9 %collective-permute-start.3 = (bf16[4,64,128]{2,1,0:T(8,128)(2,1)S(1)}, bf16[4,64,128]{2,1,0:T(8,128)(2,1)S(1)}, u32[]{:S(2)}, u32[]{:S(2)}) collective-permute-start(bf16[4,64,128]{2,1,0:T(8,128)(2,1)S(1)} %bitcast.19), channel_id=1, source_target_pairs={{0,16},{8,24},{16,0},{24,8},{1,17},{9,25},{17,1},{25,9},{2,18},{10... | collective-permute-start | bytes 196616 | tf_op jit(solution)/shard_map/ppermute | solution.py:23
  11.9 5.9 %collective-permute-start.2 = (bf16[4,64,128]{2,1,0:T(8,128)(2,1)S(1)}, bf16[4,64,128]{2,1,0:T(8,128)(2,1)S(1)}, u32[]{:S(2)}, u32[]{:S(2)}) collective-permute-start(bf16[4,64,128]{2,1,0:T(8,128)(2,1)S(1)} %bitcast.20), channel_id=1, source_target_pairs={{0,8},{8,0},{16,24},{24,16},{1,9},{9,1},{17,25},{25,17},{2,10},{10... | collective-permute-start | bytes 196616 | tf_op jit(solution)/shard_map/ppermute | solution.py:23
  17.8 2.9 %copy-start = (s32[4,128]{1,0:T(4,128)S(1)}, s32[4,128]{1,0:T(4,128)}, u32[]{:S(2)}) copy-start(s32[4,128]{1,0:T(4,128)} %param.8) | copy-start | bytes 6148
  17.8 2.9 %copy-start.1 = (s32[4]{0:T(128)S(1)}, s32[4]{0:T(128)}, u32[]{:S(2)}) copy-start(s32[4]{0:T(128)} %len_ref.3) | copy-start | bytes 52
  20.6 2.9 %collective-permute-start.5 = (bf16[3,17,8,128]{3,2,1,0:T(8,128)(2,1)S(1)}, bf16[3,17,8,128]{3,2,1,0:T(8,128)(2,1)S(1)}, u32[]{:S(2)}, u32[]{:S(2)}) collective-permute-start(bf16[3,17,8,128]{3,2,1,0:T(8,128)(2,1)S(1)} %get-tuple-element.55), channel_id=1, source_target_pairs={{0,2},{2,0},{4,6},{6,4},{1,3},{3,1},{5,7},{7,5},{8,10},{10,8},{12,... | collective-permute-start | bytes 313352 | tf_op jit(solution)/shard_map/ppermute | solution.py:23
  23.9 4.8 %collective-permute-start.6 = (bf16[3,17,4,128]{3,2,1,0:T(4,128)(2,1)S(1)}, bf16[3,17,4,128]{3,2,1,0:T(4,128)(2,1)S(1)}, u32[]{:S(2)}, u32[]{:S(2)}) collective-permute-start(bf16[3,17,4,128]{3,2,1,0:T(4,128)(2,1)S(1)} %get-tuple-element.63), channel_id=1, source_target_pairs={{0,4},{2,6},{4,0},{6,2},{1,5},{3,7},{5,1},{7,3},{8,12},{10,14},{12... | collective-permute-start | bytes 156680 | tf_op jit(solution)/shard_map/ppermute | solution.py:23
  29.0 4.0 %collective-permute-start.7 = (bf16[2,17,4,128]{3,2,1,0:T(4,128)(2,1)S(1)}, bf16[2,17,4,128]{3,2,1,0:T(4,128)(2,1)S(1)}, u32[]{:S(2)}, u32[]{:S(2)}) collective-permute-start(bf16[2,17,4,128]{3,2,1,0:T(4,128)(2,1)S(1)} %get-tuple-element.72), channel_id=1, source_target_pairs={{0,8},{8,0},{16,24},{24,16},{1,9},{9,1},{17,25},{25,17},{2,10},{10... | collective-permute-start | bytes 104456 | tf_op jit(solution)/shard_map/ppermute | solution.py:23
  32.2 1.3 %collective-permute-start.8 = (bf16[1,17,8,128]{3,2,1,0:T(8,128)(2,1)S(1)}, bf16[1,17,8,128]{3,2,1,0:T(8,128)(2,1)S(1)}, u32[]{:S(2)}, u32[]{:S(2)}) collective-permute-start(bf16[1,17,8,128]{3,2,1,0:T(8,128)(2,1)S(1)} %get-tuple-element.84), channel_id=1, source_target_pairs={{0,2},{2,0},{4,6},{6,4},{1,3},{3,1},{5,7},{7,5},{8,10},{10,8},{12,... | collective-permute-start | bytes 104456 | tf_op jit(solution)/shard_map/ppermute | solution.py:23
  33.7 3.8 %collective-permute-start.9 = (bf16[1,17,4,128]{3,2,1,0:T(4,128)(2,1)S(1)}, bf16[1,17,4,128]{3,2,1,0:T(4,128)(2,1)S(1)}, u32[]{:S(2)}, u32[]{:S(2)}) collective-permute-start(bf16[1,17,4,128]{3,2,1,0:T(4,128)(2,1)S(1)} %get-tuple-element.87), channel_id=1, source_target_pairs={{0,4},{2,6},{4,0},{6,2},{1,5},{3,7},{5,1},{7,3},{8,12},{10,14},{12... | collective-permute-start | bytes 52232 | tf_op jit(solution)/shard_map/ppermute | solution.py:23
  34.7 4.6 %collective-permute-start.10 = (bf16[1,17,4,128]{3,2,1,0:T(4,128)(2,1)S(1)}, bf16[1,17,4,128]{3,2,1,0:T(4,128)(2,1)S(1)}, u32[]{:S(2)}, u32[]{:S(2)}) collective-permute-start(bf16[1,17,4,128]{3,2,1,0:T(4,128)(2,1)S(1)} %merge.6), channel_id=1, source_target_pairs={{0,16},{8,24},{16,0},{24,8},{1,17},{9,25},{17,1},{25,9},{2,18},{10... | collective-permute-start | bytes 52232 | tf_op jit(solution)/shard_map/ppermute | solution.py:23

commit v10 on v9

--- a/solution.py
+++ b/solution.py
@@ -59,8 +59,8 @@
             one.wait()
 
 
-def stage_fresh_kernel(fresh_ref, kf, vf, sem):
-    copies = []
+def stage_fresh_kernel(query_hbm, fresh_ref, query_ref, kf, vf, sem, query_sem):
+    copies = [pltpu.make_async_copy(query_hbm, query_ref, query_sem)]
     for half, to in enumerate((kf, vf)):
         copies += half_copies(fresh_ref, to, sem.at[half], half, sem.shape[1])
     for one in copies:
@@ -222,13 +222,20 @@
 
 
 def second_kernel(
-    dims, table_ref, t_ref, top_ref, first_top_ref, first_acc_ref, first_tot_ref, facc_ref,
+    dims, n_vbs, table_ref, t_ref, top_ref, first_top_ref, first_acc_ref, first_tot_ref, facc_ref,
     ftop_ref, ftot_ref, *refs,
 ):
-    *vbs, keep_ref, send_ref, acc_s, tot_s = refs
     heads, page_rows, pages_dev, sub = dims
     half = t_ref.shape[0]
     req_dev = ftop_ref.shape[0]
+    vbs, (keep_ref, *send_refs, acc_s, tot_s) = refs[:n_vbs], refs[n_vbs:]
+    group = keep_ref.shape[2]
+
+    def put(slab, value, coded=0):
+        keep_ref[0, slab] = value[:group]
+        for place, ref in enumerate(send_refs):
+            send = value[(place + 1) * group:(place + 2) * group]
+            ref[0, slab] = pieces_of(send, coded) if coded else send.astype(jnp.bfloat16)
 
     def step(i, _):
         value_request(dims, half + i, table_ref, t_ref, top_ref, i, vbs, acc_s, tot_s)
@@ -253,9 +260,8 @@
             part = slice(h * sub, (h + 1) * sub)
             some = acc_ref[i % half, part, :] * rows_of(fade[rows], h)
             some = some + facc_ref[i, part, :] * rows_of(ffade[rows], h)
-            put_rows(keep_ref, send_ref, (0, i * heads + h), some)
-    lse = by_request(lses, heads, sub, range(req_dev))
-    put_rows(keep_ref, send_ref, (0, req_dev * heads), lse, heads)
+            put(i * heads + h, some)
+    put(req_dev * heads, by_request(lses, heads, sub, range(req_dev)), heads)
 
 
 def put_rows(keep_ref, send_ref, place, value, heads=0):
@@ -431,25 +437,26 @@
     split = heads % 4 == 0
     pieces = 8 if split else 0
 
-    near = query[None]
-    first, *others = bits_of("ctx")
-    arrived = swap(near, "ctx", first)
+    ctx_offsets = [0]
+    for bit in bits_of("ctx"):
+        ctx_offsets += [offset ^ bit for offset in ctx_offsets]
+    near = [swap(query, "ctx", offset) for offset in ctx_offsets[1:]]
     if split:
         in_hbm = lambda a: pltpu.with_memory_space_constraint(a, pltpu.HBM)
         pool = in_hbm(kv_pool)
         half = lambda count: bf16(count, page, heads, LANES)
-        kf, vf = pl.pallas_call(
+        query, kf, vf = pl.pallas_call(
             stage_fresh_kernel,
-            out_shape=(half(new_dev), half(new_dev)),
-            in_specs=[HBM],
-            out_specs=(VMEM,) * 2,
-            scratch_shapes=[pltpu.SemaphoreType.DMA((2, 4))],
+            out_shape=(bf16(*query.shape), half(new_dev), half(new_dev)),
+            in_specs=[HBM] * 2,
+            out_specs=(VMEM,) * 3,
+            scratch_shapes=[pltpu.SemaphoreType.DMA((2, 4)), pltpu.SemaphoreType.DMA],
             compiler_params=params(2),
             cost_estimate=pl.CostEstimate(
                 flops=0, transcendentals=0, bytes_accessed=4 * fresh_kv.size),
             name="stage_fresh",
-        )(in_hbm(fresh_kv))
-        arrived, kf = lax.optimization_barrier((arrived, kf))
+        )(in_hbm(query), in_hbm(fresh_kv))
+        kf, *near = lax.optimization_barrier((kf, *near))
         kb, slot_table, counts = pl.pallas_call(
             functools.partial(stage_keys_kernel, n_ctx, slots),
             out_shape=(half(pool_slots), smem(n_reqs * slots), smem(n_reqs)),
@@ -481,10 +488,7 @@
         )(fresh_bucket)
         value_in, value_specs, value_out, value_scratch = (), [], (), []
 
-    near = jnp.concatenate([near, arrived])
-    for bit in others:
-        near = jnp.concatenate([near, swap(near, "ctx", bit)])
-    queries = near.transpose(1, 2, 0, 3, 4).reshape(req_dev, rows, head_dim)
+    queries = jnp.stack([query] + near).transpose(1, 2, 0, 3, 4).reshape(req_dev, rows, head_dim)
     far = [swap(queries, "req", k) for k in range(n_req - 1, 0, -1)][::-1]
 
     slabs = req_dev * heads + 1
@@ -575,11 +579,12 @@
     send, later_top = lax.optimization_barrier((send, later_top))
     got = swap(send, "req", req_bits[0])
     arrived = [got]
-    own_keep, own_send = pl.pallas_call(
-        functools.partial(second_kernel, dims),
-        out_shape=(f32(1, slabs, left, LANES), bf16(1, slabs, left, LANES)),
+    own_keep, *own_sends = pl.pallas_call(
+        functools.partial(second_kernel, dims, len(vbs)),
+        out_shape=(f32(1, slabs, group, LANES),)
+        + (bf16(1, slabs, group, LANES),) * (n_ctx - 1),
         in_specs=[SMEM] + [VMEM] * (8 + len(vbs)),
-        out_specs=(VMEM,) * 2,
+        out_specs=(VMEM,) * n_ctx,
         scratch_shapes=[
             pltpu.VMEM((part, rows, LANES), jnp.float32),
             pltpu.VMEM((part, sub, LANES), jnp.float32)],
@@ -588,23 +593,20 @@
         name="second",
     )(table, later, later_top, top, acc, tot, facc, ftop, ftot, *vbs)
     got, own_keep = lax.optimization_barrier((got, own_keep))
-    own_got = swap(own_send, "ctx", ctx_bits[0])
+    arrived += [
+        swap(one, "ctx", offset) for one, offset in zip(own_sends, ctx_offsets[1:])]
     for bit in req_bits[1:]:
         (send, *kept), offsets = sorted_by(kept[0], got, 1, offsets, bit)
-        send, own_got = lax.optimization_barrier((send, own_got))
         got = swap(send, "req", bit)
         arrived.append(got)
-    for bit in ctx_bits[1:]:
-        own_keep, own_send = halved(own_keep, own_got)
-        own_got = swap(own_send, "ctx", bit)
     return pl.pallas_call(
         last_kernel,
         out_shape=bf16(req_dev, heads, group, LANES),
-        in_specs=[VMEM] * (2 + len(arrived)),
+        in_specs=[VMEM] * (1 + len(arrived)),
         out_specs=VMEM,
         compiler_params=params(8),
         name="last",
-    )(own_keep, own_got, *arrived)
+    )(own_keep, *arrived)
 
 
 def solution(mesh):

time: 40.6 us -> 37.9 us (0.933)
  waiting for transfers between devices: 5.85 us -> 4 us
  other arithmetic: 1.51 us -> 0.05 us
  starting transfers between devices: 13.7 us -> 14.6 us
    ppermute x11 -> x13, waiting for transfers between devices: 5.85 us -> 4 us  [swap(): lax.ppermute(value, axis, [(n, n ^ bit) for n in range(lax.axis_size(axis...]
    ppermute x11 -> x13, starting transfers between devices: 13.7 us -> 14.6 us  [swap(): lax.ppermute(value, axis, [(n, n ^ bit) for n in range(lax.axis_size(axis...]
    concatenate x1 -> x0, other arithmetic: 0.75 us -> none  [local(): near = jnp.concatenate([near, arrived])]
    transpose x1, other arithmetic: 0.77 us -> 0.05 us  [local(): jnp.stack([query] + near).transpose(1, 2, 0, 3, 4)]
    pallas_call x4 -> x3, Pallas kernels: 1.13 us -> 0.87 us  [merge(): pl.pallas_call(functools.partial(merge_kernel, heads, skip, goals), out_s...]
  transfers between devices with their start and end apart: 11 -> 13, of which waited for: 6 -> 4; matrix products, arithmetic and copies ran while one was open for 0% -> 0% of each run, Pallas kernels for 36% -> 38%
where the time goes in v10:
time: 37.9 us; the launch traced here: 37.7 us
  Pallas kernels  18.9 us (50%)
  starting transfers between devices  14.6 us (39%)
  waiting for transfers between devices  4 us (11%)
    ppermute x13, starting transfers between devices, swap(): lax.ppermute(value, axis, [(n, n ^ bit) for n in range(lax.axis_size(axis...  14.6 us
    pallas_call x1, Pallas kernels, local(): pl.pallas_call(functools.partial(stage_keys_kernel, n_ctx, slots), out_sh...  4.08 us
    ppermute x13, waiting for transfers between devices, swap(): lax.ppermute(value, axis, [(n, n ^ bit) for n in range(lax.axis_size(axis...  4 us
    pallas_call x1, Pallas kernels, local(): pl.pallas_call(functools.partial(middle_kernel, dims), out_shape=(f32(par...  3.22 us
    pallas_call x1, Pallas kernels, local(): pl.pallas_call(functools.partial(first_kernel, dims, pieces), out_shape=(...  2.83 us
    pallas_call x1, Pallas kernels, local(): pl.pallas_call(functools.partial(fresh_kernel, (heads, page_rows, slots,...  2.81 us
    pallas_call x1, Pallas kernels, local(): pl.pallas_call(stage_fresh_kernel, out_shape=(bf16(*query.shape), half(ne...  2.08 us
    pallas_call x1, Pallas kernels, local(): pl.pallas_call(functools.partial(second_kernel, dims, len(vbs)), out_shap...  1.99 us
  transfers between devices with their start and end apart: 13, of which 4 were waited for; matrix products, arithmetic and copies ran while one was open for 0% of the time, Pallas kernels for 38%

profile of v10, /device:TPU:0, one launch (start us, length us, event | category | flops | bytes accessed | tf_op | source)
XLA Modules:
  0.0 37.7 jit_solution(8918646065993913889)
XLA Ops:
  0.0 2.9 %collective-permute-start = (bf16[4,4,4,128]{3,2,1,0:T(4,128)(2,1)}, bf16[4,4,4,128]{3,2,1,0:T(4,128)(2,1)S(1)}, u32[]{:S(2)}, u32[]{:S(2)}) collective-permute-start(bf16[4,4,4,128]{3,2,1,0:T(4,128)(2,1)} %query_hbm.1), channel_id=1, source_target_pairs={{0,4},{2,6},{4,0},{6,2},{1,5},{3,7},{5,1},{7,3},{8,12},{10,14},{12... | collective-permute-start | bytes 49160 | tf_op jit(solution)/shard_map/ppermute | solution.py:23
  2.9 0.1 collective-permute-start.1
  3.1 2.1 %stage_fresh.1 = (bf16[4,4,4,128]{3,2,1,0:T(4,128)(2,1)S(1)}, bf16[112,16,4,128]{3,2,1,0:T(4,128)(2,1)S(1)}, bf16[112,16,4,128]{3,2,1,0:T(4,128)(2,1)S(1)}) custom-call(bf16[4,4,4,128]{3,2,1,0:T(4,128)(2,1)} %query_hbm.1, bf16[112,16,4,256]{3,2,1,0:T(4,128)(2,1)} %fresh_ref.1), custom_call_target="tpu_custom_call" | custom-call | bytes 7340032 | tf_op jit(solution)/shard_map/stage_fresh/pallas_call | solution.py:448
  5.2 1.1 %collective-permute-done.2 = bf16[4,4,4,128]{3,2,1,0:T(4,128)(2,1)S(1)} collective-permute-done((bf16[4,4,4,128]{3,2,1,0:T(4,128)(2,1)}, bf16[4,4,4,128]{3,2,1,0:T(4,128)(2,1)S(1)}, u32[]{:S(2)}, u32[]{:S(2)}) %collective-permute-start.2) | collective-permute-done | bytes 16416 | tf_op jit(solution)/shard_map/ppermute | solution.py:23
  6.3 0.1 maximum_bitcast_fusion
  6.4 3.7 %collective-permute-start.5 = (bf16[4,64,128]{2,1,0:T(8,128)(2,1)S(1)}, bf16[4,64,128]{2,1,0:T(8,128)(2,1)S(1)}, u32[]{:S(2)}, u32[]{:S(2)}) collective-permute-start(bf16[4,64,128]{2,1,0:T(8,128)(2,1)S(1)} %bitcast.21), channel_id=1, source_target_pairs={{0,24},{8,16},{16,8},{24,0},{1,25},{9,17},{17,9},{25,1},{2,26},{10... | collective-permute-start | bytes 196616 | tf_op jit(solution)/shard_map/ppermute | solution.py:23
  10.1 0.8 %collective-permute-start.3 = (bf16[4,64,128]{2,1,0:T(8,128)(2,1)S(1)}, bf16[4,64,128]{2,1,0:T(8,128)(2,1)S(1)}, u32[]{:S(2)}, u32[]{:S(2)}) collective-permute-start(bf16[4,64,128]{2,1,0:T(8,128)(2,1)S(1)} %bitcast.23), channel_id=1, source_target_pairs={{0,8},{8,0},{16,24},{24,16},{1,9},{9,1},{17,25},{25,17},{2,10},{10... | collective-permute-start | bytes 196616 | tf_op jit(solution)/shard_map/ppermute | solution.py:23
  10.9 4.1 %stage_keys.1 = (bf16[512,16,4,128]{3,2,1,0:T(4,128)(2,1)S(1)}, s32[128]{0:T(128)S(1)}, s32[16]{0:T(128)S(1)}) custom-call(s32[112]{0:T(128)} %bucket_hbm.1, bf16[512,16,4,256]{3,2,1,0:T(4,128)(2,1)} %refs_0_.1), custom_call_target="tpu_custom_call" | custom-call | bytes 16777216 | tf_op jit(solution)/shard_map/stage_keys/pallas_call | solution.py:460
  15.0 0.5 %collective-permute-done.4.refs_2_ = bf16[4,64,128]{2,1,0:T(8,128)(2,1)S(1)} collective-permute-done((bf16[4,64,128]{2,1,0:T(8,128)(2,1)S(1)}, bf16[4,64,128]{2,1,0:T(8,128)(2,1)S(1)}, u32[]{:S(2)}, u32[]{:S(2)}) %collective-permute-start.4) | collective-permute-done | bytes 65568 | tf_op jit(solution)/shard_map/ppermute | solution.py:23
  15.5 2.8 %fresh.1 = (f32[3,17,8,128]{3,2,1,0:T(8,128)S(1)}, bf16[3,17,8,128]{3,2,1,0:T(8,128)(2,1)S(1)}, f32[4,64,128]{2,1,0:T(8,128)S(1)}, f32[4,16,128]{2,1,0:T(8,128)S...) custom-call(s32[128]{0:T(128)S(1)} %get-tuple-element.48.slots_ref, ...), custom_call_target="tpu_custom_call" | custom-call | flops 268435456 | bytes 3670016 | tf_op jit(solution)/shard_map/fresh/pallas_call | solution.py:496
  18.3 0.1 collective-permute-start.6
  18.4 2.8 %first.1 = (f32[2,16,8192]{2,1,0:T(8,128)S(1)}, f32[2,16,128]{2,1,0:T(8,128)S(1)}, bf16[512,8,4,128]{3,2,1,0:T(4,128)(2,1)S(1)}) custom-call(s32[512]{0:T(512)S(1)} %bitcast.27, s32[4]{0:T(128)S(1)} %copy-done.1, bf16[4,64,128]{2,1,0:T(8,128)(2,1)S(1)} %bitcast.25, bf16[512,64,128]{2,1,0:T(8,128)(2,1)S(1)} %bitcast.13, bf16[512,16,4,256]{3,2,1,0:T(4,128)(2,1)} %refs_0_.1), custom_call_target="tpu_custom_call" | custom-call | flops 268435456 | bytes 4194304 | tf_op jit(solution)/shard_map/first/pallas_call | solution.py:549
  21.3 0.3 merge.3
  21.6 1.3 %collective-permute-start.7 = (bf16[3,17,4,128]{3,2,1,0:T(4,128)(2,1)S(1)}, bf16[3,17,4,128]{3,2,1,0:T(4,128)(2,1)S(1)}, u32[]{:S(2)}, u32[]{:S(2)}) collective-permute-start(bf16[3,17,4,128]{3,2,1,0:T(4,128)(2,1)S(1)} %get-tuple-element.67), channel_id=1, source_target_pairs={{0,4},{2,6},{4,0},{6,2},{1,5},{3,7},{5,1},{7,3},{8,12},{10,14},{12... | collective-permute-start | bytes 156680 | tf_op jit(solution)/shard_map/ppermute | solution.py:23
  22.9 3.2 %middle.1 = (f32[2,16,8192]{2,1,0:T(8,128)S(1)}, f32[2,16,128]{2,1,0:T(8,128)S(1)}, f32[2,64,128]{2,1,0:T(8,128)S(1)}, f32[2,16,128]{2,1,0:T(8,128)S(1)}) custom-call(s32[512]{0:T(512)S(1)} %bitcast.28, s32[4]{0:T(128)S(1)} %copy-done.1, bf16[4,64,128]{2,1,0:T(8,128)(2,1)S(1)} %bitcast.26, bf16[512,64,128]{2,1,0:T(8,128)(2,1)S(1)} %bitcast.14, ...), custom_call_target="tpu_custom_call" | custom-call | flops 536870912 | bytes 8388608 | tf_op jit(solution)/shard_map/middle/pallas_call | solution.py:565
  26.1 0.3 merge.4
  26.4 1.1 %collective-permute-start.8 = (bf16[2,17,4,128]{3,2,1,0:T(4,128)(2,1)S(1)}, bf16[2,17,4,128]{3,2,1,0:T(4,128)(2,1)S(1)}, u32[]{:S(2)}, u32[]{:S(2)}) collective-permute-start(bf16[2,17,4,128]{3,2,1,0:T(4,128)(2,1)S(1)} %get-tuple-element.76), channel_id=1, source_target_pairs={{0,8},{8,0},{16,24},{24,16},{1,9},{9,1},{17,25},{25,17},{2,10},{10... | collective-permute-start | bytes 104456 | tf_op jit(solution)/shard_map/ppermute | solution.py:23
  27.6 2.0 %second.1 = (f32[1,17,4,128]{3,2,1,0:T(4,128)S(1)}, bf16[1,17,4,128]{3,2,1,0:T(4,128)(2,1)S(1)}, bf16[1,17,4,128]{3,2,1,0:T(4,128)(2,1)S(1)}, bf16[1,17,4,128]{3,2,1,0:T(4,128)(2,1)S(1)}) custom-call(s32[512]{0:T(512)S(1)} %bitcast.29, f32[2,16,8192]{2,1,0:T(8,128)S(1)} %get-tuple-element.77.t_ref, f32[2,16,128]{2,1,0:T(8,128)S(1)} %get-tuple-element.78.top_ref, ...), custom_call_target="tpu_custom_call" | custom-call | flops 268435456 | bytes 4194304 | tf_op jit(solution)/shard_map/second/pallas_call | solution.py:582
  29.6 1.0 %collective-permute-start.9 = (bf16[1,17,4,128]{3,2,1,0:T(4,128)(2,1)S(1)}, bf16[1,17,4,128]{3,2,1,0:T(4,128)(2,1)S(1)}, u32[]{:S(2)}, u32[]{:S(2)}) collective-permute-start(bf16[1,17,4,128]{3,2,1,0:T(4,128)(2,1)S(1)} %get-tuple-element.86), channel_id=1, source_target_pairs={{0,4},{2,6},{4,0},{6,2},{1,5},{3,7},{5,1},{7,3},{8,12},{10,14},{12... | collective-permute-start | bytes 52232 | tf_op jit(solution)/shard_map/ppermute | solution.py:23
  30.6 1.2 %collective-permute-start.11 = (bf16[1,17,4,128]{3,2,1,0:T(4,128)(2,1)S(1)}, bf16[1,17,4,128]{3,2,1,0:T(4,128)(2,1)S(1)}, u32[]{:S(2)}, u32[]{:S(2)}) collective-permute-start(bf16[1,17,4,128]{3,2,1,0:T(4,128)(2,1)S(1)} %get-tuple-element.88), channel_id=1, source_target_pairs={{0,6},{2,4},{4,2},{6,0},{1,7},{3,5},{5,3},{7,1},{8,14},{10,12},{12... | collective-permute-start | bytes 52232 | tf_op jit(solution)/shard_map/ppermute | solution.py:23
  31.8 0.3 merge.5
  32.0 2.4 %collective-permute-start.12 = (bf16[1,17,4,128]{3,2,1,0:T(4,128)(2,1)S(1)}, bf16[1,17,4,128]{3,2,1,0:T(4,128)(2,1)S(1)}, u32[]{:S(2)}, u32[]{:S(2)}) collective-permute-start(bf16[1,17,4,128]{3,2,1,0:T(4,128)(2,1)S(1)} %merge.5), channel_id=1, source_target_pairs={{0,16},{8,24},{16,0},{24,8},{1,17},{9,25},{17,1},{25,9},{2,18},{10... | collective-permute-start | bytes 52232 | tf_op jit(solution)/shard_map/ppermute | solution.py:23
  34.4 2.3 %collective-permute-done.12.refs_4_ = bf16[1,17,4,128]{3,2,1,0:T(4,128)(2,1)S(1)} collective-permute-done((bf16[1,17,4,128]{3,2,1,0:T(4,128)(2,1)S(1)}, bf16[1,17,4,128]{3,2,1,0:T(4,128)(2,1)S(1)}, u32[]{:S(2)}, u32[]{:S(2)}) %collective-permute-start.12) | collective-permute-done | bytes 17440 | tf_op jit(solution)/shard_map/ppermute | solution.py:23
  36.8 1.0 %last.1 = bf16[4,4,4,128]{3,2,1,0:T(4,128)(2,1)} custom-call(f32[1,17,4,128]{3,2,1,0:T(4,128)S(1)} %get-tuple-element.85.keep_ref, bf16[2,17,4,128]{3,2,1,0:T(4,128)(2,1)S(1)} %collective-permute-done.8.got_ref.refs_0_, bf16[1,17,4,128]{3,2,1,0:T(4,128)(2,1)S(1)} %collective-permute-done.9.refs_1_, ...), custom_call_target="tpu_custom_call" | custom-call | tf_op jit(solution)/shard_map/last/pallas_call | solution.py:602
  (18 shorter events, 0.1 us)
Async XLA Ops:
  0.0 5.2 %collective-permute-start = (bf16[4,4,4,128]{3,2,1,0:T(4,128)(2,1)}, bf16[4,4,4,128]{3,2,1,0:T(4,128)(2,1)S(1)}, u32[]{:S(2)}, u32[]{:S(2)}) collective-permute-start(bf16[4,4,4,128]{3,2,1,0:T(4,128)(2,1)} %query_hbm.1), channel_id=1, source_target_pairs={{0,4},{2,6},{4,0},{6,2},{1,5},{3,7},{5,1},{7,3},{8,12},{10,14},{12... | collective-permute-start | bytes 49160 | tf_op jit(solution)/shard_map/ppermute | solution.py:23
  2.9 3.4 %collective-permute-start.2 = (bf16[4,4,4,128]{3,2,1,0:T(4,128)(2,1)}, bf16[4,4,4,128]{3,2,1,0:T(4,128)(2,1)S(1)}, u32[]{:S(2)}, u32[]{:S(2)}) collective-permute-start(bf16[4,4,4,128]{3,2,1,0:T(4,128)(2,1)} %query_hbm.1), channel_id=1, source_target_pairs={{0,6},{2,4},{4,2},{6,0},{1,7},{3,5},{5,3},{7,1},{8,14},{10,12},{12... | collective-permute-start | bytes 49160 | tf_op jit(solution)/shard_map/ppermute | solution.py:23
  2.9 3.4 %collective-permute-start.1 = (bf16[4,4,4,128]{3,2,1,0:T(4,128)(2,1)}, bf16[4,4,4,128]{3,2,1,0:T(4,128)(2,1)S(1)}, u32[]{:S(2)}, u32[]{:S(2)}) collective-permute-start(bf16[4,4,4,128]{3,2,1,0:T(4,128)(2,1)} %query_hbm.1), channel_id=1, source_target_pairs={{0,2},{2,0},{4,6},{6,4},{1,3},{3,1},{5,7},{7,5},{8,10},{10,8},{12,... | collective-permute-start | bytes 49160 | tf_op jit(solution)/shard_map/ppermute | solution.py:23
  6.4 8.5 %collective-permute-start.5 = (bf16[4,64,128]{2,1,0:T(8,128)(2,1)S(1)}, bf16[4,64,128]{2,1,0:T(8,128)(2,1)S(1)}, u32[]{:S(2)}, u32[]{:S(2)}) collective-permute-start(bf16[4,64,128]{2,1,0:T(8,128)(2,1)S(1)} %bitcast.21), channel_id=1, source_target_pairs={{0,24},{8,16},{16,8},{24,0},{1,25},{9,17},{17,9},{25,1},{2,26},{10... | collective-permute-start | bytes 196616 | tf_op jit(solution)/shard_map/ppermute | solution.py:23
  10.1 5.4 %collective-permute-start.4 = (bf16[4,64,128]{2,1,0:T(8,128)(2,1)S(1)}, bf16[4,64,128]{2,1,0:T(8,128)(2,1)S(1)}, u32[]{:S(2)}, u32[]{:S(2)}) collective-permute-start(bf16[4,64,128]{2,1,0:T(8,128)(2,1)S(1)} %bitcast.22), channel_id=1, source_target_pairs={{0,16},{8,24},{16,0},{24,8},{1,17},{9,25},{17,1},{25,9},{2,18},{10... | collective-permute-start | bytes 196616 | tf_op jit(solution)/shard_map/ppermute | solution.py:23
  10.1 5.4 %collective-permute-start.3 = (bf16[4,64,128]{2,1,0:T(8,128)(2,1)S(1)}, bf16[4,64,128]{2,1,0:T(8,128)(2,1)S(1)}, u32[]{:S(2)}, u32[]{:S(2)}) collective-permute-start(bf16[4,64,128]{2,1,0:T(8,128)(2,1)S(1)} %bitcast.23), channel_id=1, source_target_pairs={{0,8},{8,0},{16,24},{24,16},{1,9},{9,1},{17,25},{25,17},{2,10},{10... | collective-permute-start | bytes 196616 | tf_op jit(solution)/shard_map/ppermute | solution.py:23
  15.5 2.9 %copy-start = (s32[4,128]{1,0:T(4,128)S(1)}, s32[4,128]{1,0:T(4,128)}, u32[]{:S(2)}) copy-start(s32[4,128]{1,0:T(4,128)} %param.8) | copy-start | bytes 6148
  15.5 2.9 %copy-start.1 = (s32[4]{0:T(128)S(1)}, s32[4]{0:T(128)}, u32[]{:S(2)}) copy-start(s32[4]{0:T(128)} %len_ref.3) | copy-start | bytes 52
  18.3 2.9 %collective-permute-start.6 = (bf16[3,17,8,128]{3,2,1,0:T(8,128)(2,1)S(1)}, bf16[3,17,8,128]{3,2,1,0:T(8,128)(2,1)S(1)}, u32[]{:S(2)}, u32[]{:S(2)}) collective-permute-start(bf16[3,17,8,128]{3,2,1,0:T(8,128)(2,1)S(1)} %get-tuple-element.59), channel_id=1, source_target_pairs={{0,2},{2,0},{4,6},{6,4},{1,3},{3,1},{5,7},{7,5},{8,10},{10,8},{12,... | collective-permute-start | bytes 313352 | tf_op jit(solution)/shard_map/ppermute | solution.py:23
  21.6 4.5 %collective-permute-start.7 = (bf16[3,17,4,128]{3,2,1,0:T(4,128)(2,1)S(1)}, bf16[3,17,4,128]{3,2,1,0:T(4,128)(2,1)S(1)}, u32[]{:S(2)}, u32[]{:S(2)}) collective-permute-start(bf16[3,17,4,128]{3,2,1,0:T(4,128)(2,1)S(1)} %get-tuple-element.67), channel_id=1, source_target_pairs={{0,4},{2,6},{4,0},{6,2},{1,5},{3,7},{5,1},{7,3},{8,12},{10,14},{12... | collective-permute-start | bytes 156680 | tf_op jit(solution)/shard_map/ppermute | solution.py:23
  26.4 5.3 %collective-permute-start.8 = (bf16[2,17,4,128]{3,2,1,0:T(4,128)(2,1)S(1)}, bf16[2,17,4,128]{3,2,1,0:T(4,128)(2,1)S(1)}, u32[]{:S(2)}, u32[]{:S(2)}) collective-permute-start(bf16[2,17,4,128]{3,2,1,0:T(4,128)(2,1)S(1)} %get-tuple-element.76), channel_id=1, source_target_pairs={{0,8},{8,0},{16,24},{24,16},{1,9},{9,1},{17,25},{25,17},{2,10},{10... | collective-permute-start | bytes 104456 | tf_op jit(solution)/shard_map/ppermute | solution.py:23
  29.6 4.9 %collective-permute-start.9 = (bf16[1,17,4,128]{3,2,1,0:T(4,128)(2,1)S(1)}, bf16[1,17,4,128]{3,2,1,0:T(4,128)(2,1)S(1)}, u32[]{:S(2)}, u32[]{:S(2)}) collective-permute-start(bf16[1,17,4,128]{3,2,1,0:T(4,128)(2,1)S(1)} %get-tuple-element.86), channel_id=1, source_target_pairs={{0,4},{2,6},{4,0},{6,2},{1,5},{3,7},{5,1},{7,3},{8,12},{10,14},{12... | collective-permute-start | bytes 52232 | tf_op jit(solution)/shard_map/ppermute | solution.py:23
  30.6 3.8 %collective-permute-start.10 = (bf16[1,17,4,128]{3,2,1,0:T(4,128)(2,1)S(1)}, bf16[1,17,4,128]{3,2,1,0:T(4,128)(2,1)S(1)}, u32[]{:S(2)}, u32[]{:S(2)}) collective-permute-start(bf16[1,17,4,128]{3,2,1,0:T(4,128)(2,1)S(1)} %get-tuple-element.87), channel_id=1, source_target_pairs={{0,2},{2,0},{4,6},{6,4},{1,3},{3,1},{5,7},{7,5},{8,10},{10,8},{12,... | collective-permute-start | bytes 52232 | tf_op jit(solution)/shard_map/ppermute | solution.py:23
  30.6 3.8 %collective-permute-start.11 = (bf16[1,17,4,128]{3,2,1,0:T(4,128)(2,1)S(1)}, bf16[1,17,4,128]{3,2,1,0:T(4,128)(2,1)S(1)}, u32[]{:S(2)}, u32[]{:S(2)}) collective-permute-start(bf16[1,17,4,128]{3,2,1,0:T(4,128)(2,1)S(1)} %get-tuple-element.88), channel_id=1, source_target_pairs={{0,6},{2,4},{4,2},{6,0},{1,7},{3,5},{5,3},{7,1},{8,14},{10,12},{12... | collective-permute-start | bytes 52232 | tf_op jit(solution)/shard_map/ppermute | solution.py:23
  32.0 4.7 %collective-permute-start.12 = (bf16[1,17,4,128]{3,2,1,0:T(4,128)(2,1)S(1)}, bf16[1,17,4,128]{3,2,1,0:T(4,128)(2,1)S(1)}, u32[]{:S(2)}, u32[]{:S(2)}) collective-permute-start(bf16[1,17,4,128]{3,2,1,0:T(4,128)(2,1)S(1)} %merge.5), channel_id=1, source_target_pairs={{0,16},{8,24},{16,0},{24,8},{1,17},{9,25},{17,1},{25,9},{2,18},{10... | collective-permute-start | bytes 52232 | tf_op jit(solution)/shard_map/ppermute | solution.py:23

commit v11 on v10

--- a/solution.py
+++ b/solution.py
@@ -190,7 +190,7 @@
     return class_reduce(flat, op, heads)
 
 
-def first_kernel(dims, pieces, table_ref, len_ref, q_ref, kb, *refs):
+def score_kernel(dims, first, pieces, table_ref, len_ref, q_ref, kb, *refs):
     refs = list(refs)
     pool = [refs.pop(0)] if pieces else []
     t_ref, top_ref, *refs = refs
@@ -198,7 +198,7 @@
     copies.start()
 
     def step(i, _):
-        score_request(dims, i, table_ref, len_ref, q_ref, kb, t_ref, top_ref, i)
+        score_request(dims, first + i, table_ref, len_ref, q_ref, kb, t_ref, top_ref, i)
         return 0
 
     lax.fori_loop(0, t_ref.shape[0], step, 0)
@@ -206,29 +206,14 @@
     copies.wait()
 
 
-def middle_kernel(dims, table_ref, len_ref, q_ref, kb, t_ref, top_ref, *refs):
-    *vbs, later_ref, later_top_ref, acc_ref, tot_ref = refs
-    half = t_ref.shape[0]
-
-    def step(i, _):
-        score_request(
-            dims, half + i, table_ref, len_ref, q_ref, kb, later_ref, later_top_ref, i)
-        value_request(dims, i, table_ref, t_ref, top_ref, i, vbs, acc_ref, tot_ref)
-        return 0
-
-    lax.fori_loop(0, half, step, 0)
-    later_top_ref[...] = reduce_rows(
-        later_top_ref, jnp.maximum, dims[0]).reshape(later_top_ref.shape)
-
-
-def second_kernel(
-    dims, n_vbs, table_ref, t_ref, top_ref, first_top_ref, first_acc_ref, first_tot_ref, facc_ref,
-    ftop_ref, ftot_ref, *refs,
+def value_kernel(
+    dims, n_vbs, table_ref, first_t_ref, first_top_ref, t_ref, top_ref, facc_ref, ftop_ref,
+    ftot_ref, *refs,
 ):
     heads, page_rows, pages_dev, sub = dims
     half = t_ref.shape[0]
     req_dev = ftop_ref.shape[0]
-    vbs, (keep_ref, *send_refs, acc_s, tot_s) = refs[:n_vbs], refs[n_vbs:]
+    vbs, (keep_ref, *send_refs, first_acc, first_tot, acc_s, tot_s) = refs[:n_vbs], refs[n_vbs:]
     group = keep_ref.shape[2]
 
     def put(slab, value, coded=0):
@@ -238,13 +223,15 @@
             ref[0, slab] = pieces_of(send, coded) if coded else send.astype(jnp.bfloat16)
 
     def step(i, _):
+        value_request(
+            dims, i, table_ref, first_t_ref, first_top_ref, i, vbs, first_acc, first_tot)
         value_request(dims, half + i, table_ref, t_ref, top_ref, i, vbs, acc_s, tot_s)
         return 0
 
     lax.fori_loop(0, half, step, 0)
     flat = (req_dev * sub, LANES)
     tots = jnp.concatenate(
-        [reduce_rows(ref, jnp.add, heads) for ref in (first_tot_ref, tot_s)], axis=0)
+        [reduce_rows(ref, jnp.add, heads) for ref in (first_tot, tot_s)], axis=0)
     top = jnp.concatenate(
         [ref[...].reshape(half * sub, LANES) for ref in (first_top_ref, top_ref)], axis=0)
     ftop = ftop_ref[...].reshape(flat)
@@ -254,7 +241,7 @@
     fade, ffade = fade / tots, ffade / tots
     lses = both + jnp.log2(tots)
     for i in range(req_dev):
-        acc_ref = first_acc_ref if i < half else acc_s
+        acc_ref = first_acc if i < half else acc_s
         rows = slice(i * sub, (i + 1) * sub)
         for h in range(heads):
             part = slice(h * sub, (h + 1) * sub)
@@ -435,7 +422,7 @@
     f32 = lambda *shape: jax.ShapeDtypeStruct(shape, jnp.float32)
     columns = pages_dev * page_rows
     split = heads % 4 == 0
-    pieces = 8 if split else 0
+    pieces = 16 if split else 0
 
     ctx_offsets = [0]
     for bit in bits_of("ctx"):
@@ -546,33 +533,28 @@
         bytes_accessed=(scores + values) * columns * LANES * 2)
     send, queries = lax.optimization_barrier((send, queries))
     got = swap(send, "ctx", ctx_bits[0])
-    t, top, *more = pl.pallas_call(
-        functools.partial(first_kernel, dims, pieces),
-        out_shape=(f32(part, sub, columns), f32(part, sub, LANES)) + value_out,
-        in_specs=[SMEM] * 2 + [VMEM] * 2 + value_specs,
-        out_specs=(VMEM,) * (2 + len(value_out)),
-        scratch_shapes=value_scratch,
-        compiler_params=params(4),
-        cost_estimate=cost(part, 0),
-        name="first",
-    )(table, context_len, queries, kb, *value_in)
-    vbs = [a.reshape(a.shape[0], -1, LANES) for a in vbs + more] if split else [vb]
+
+    def score_call(first, copied):
+        return pl.pallas_call(
+            functools.partial(score_kernel, dims, first, pieces if copied else 0),
+            out_shape=(f32(part, sub, columns), f32(part, sub, LANES))
+            + (value_out if copied else ()),
+            in_specs=[SMEM] * 2 + [VMEM] * 2 + (value_specs if copied else []),
+            out_specs=(VMEM,) * (2 + len(value_out) * copied),
+            scratch_shapes=value_scratch if copied else [],
+            compiler_params=params(4),
+            cost_estimate=cost(part, 0),
+            name="scores",
+        )(table, context_len, queries, kb, *(value_in if copied else ()))
+
+    t, top = score_call(0, False)
     got, top = lax.optimization_barrier((got, top))
     for bit in ctx_bits[1:]:
         keep, send = halved(keep, got)
-        send, top = lax.optimization_barrier((send, top))
+        send, queries = lax.optimization_barrier((send, queries))
         got = swap(send, "ctx", bit)
-    later, later_top, acc, tot = pl.pallas_call(
-        functools.partial(middle_kernel, dims),
-        out_shape=(
-            f32(part, sub, columns), f32(part, sub, LANES), f32(part, rows, LANES),
-            f32(part, sub, LANES)),
-        in_specs=[SMEM] * 2 + [VMEM] * (4 + len(vbs)),
-        out_specs=(VMEM,) * 4,
-        compiler_params=params(4),
-        cost_estimate=cost(part, part),
-        name="middle",
-    )(table, context_len, queries, kb, t, top, *vbs)
+    later, later_top, *more = score_call(part, True)
+    vbs = [a.reshape(a.shape[0], -1, LANES) for a in vbs + more] if split else [vb]
     got, later_top = lax.optimization_barrier((got, later_top))
     offsets = list(range(1, n_req))
     (send, *kept), offsets = sorted_by(keep, got, 0, offsets, req_bits[0])
@@ -580,25 +562,26 @@
     got = swap(send, "req", req_bits[0])
     arrived = [got]
     own_keep, *own_sends = pl.pallas_call(
-        functools.partial(second_kernel, dims, len(vbs)),
+        functools.partial(value_kernel, dims, len(vbs)),
         out_shape=(f32(1, slabs, group, LANES),)
         + (bf16(1, slabs, group, LANES),) * (n_ctx - 1),
-        in_specs=[SMEM] + [VMEM] * (8 + len(vbs)),
+        in_specs=[SMEM] + [VMEM] * (7 + len(vbs)),
         out_specs=(VMEM,) * n_ctx,
         scratch_shapes=[
             pltpu.VMEM((part, rows, LANES), jnp.float32),
-            pltpu.VMEM((part, sub, LANES), jnp.float32)],
+            pltpu.VMEM((part, sub, LANES), jnp.float32)] * 2,
         compiler_params=params(4),
-        cost_estimate=cost(0, part),
-        name="second",
-    )(table, later, later_top, top, acc, tot, facc, ftop, ftot, *vbs)
+        cost_estimate=cost(0, req_dev),
+        name="values",
+    )(table, t, top, later, later_top, facc, ftop, ftot, *vbs)
     got, own_keep = lax.optimization_barrier((got, own_keep))
+    for bit in req_bits[1:]:
+        (send, *kept), offsets = sorted_by(kept[0], got, 1, offsets, bit)
+        send, *own_sends = lax.optimization_barrier((send, *own_sends))
+        got = swap(send, "req", bit)
+        arrived.append(got)
     arrived += [
         swap(one, "ctx", offset) for one, offset in zip(own_sends, ctx_offsets[1:])]
-    for bit in req_bits[1:]:
-        (send, *kept), offsets = sorted_by(kept[0], got, 1, offsets, bit)
-        got = swap(send, "req", bit)
-        arrived.append(got)
     return pl.pallas_call(
         last_kernel,
         out_shape=bf16(req_dev, heads, group, LANES),

time: 37.9 us -> 38 us (level)
  transfers between devices with their start and end apart: 13 -> 13, of which waited for: 4 -> 8; matrix products, arithmetic and copies ran while one was open for 0% -> 0% of each run, Pallas kernels for 38% -> 38%
where the time goes in v11:
time: 38 us; the launch traced here: 37.8 us
  Pallas kernels  19 us (50%)
  starting transfers between devices  14.6 us (38%)
  waiting for transfers between devices  3.97 us (10%)
    ppermute x13, starting transfers between devices, swap(): lax.ppermute(value, axis, [(n, n ^ bit) for n in range(lax.axis_size(axis...  14.6 us
    pallas_call x2, Pallas kernels, score_call(): pl.pallas_call(functools.partial(score_kernel, dims, first, pieces if cop...  5.51 us
    pallas_call x1, Pallas kernels, local(): pl.pallas_call(functools.partial(stage_keys_kernel, n_ctx, slots), out_sh...  4.13 us
    ppermute x13, waiting for transfers between devices, swap(): lax.ppermute(value, axis, [(n, n ^ bit) for n in range(lax.axis_size(axis...  3.97 us
    pallas_call x1, Pallas kernels, local(): pl.pallas_call(functools.partial(fresh_kernel, (heads, page_rows, slots,...  2.87 us
    pallas_call x1, Pallas kernels, local(): pl.pallas_call(functools.partial(value_kernel, dims, len(vbs)), out_shape...  2.6 us
    pallas_call x1, Pallas kernels, local(): pl.pallas_call(stage_fresh_kernel, out_shape=(bf16(*query.shape), half(ne...  2.08 us
    pallas_call x1, Pallas kernels, local(): pl.pallas_call(last_kernel, out_shape=bf16(req_dev, heads, group, LANES),...  0.98 us
  transfers between devices with their start and end apart: 13, of which 8 were waited for; matrix products, arithmetic and copies ran while one was open for 0% of the time, Pallas kernels for 38%

profile of v11, /device:TPU:0, one launch (start us, length us, event | category | flops | bytes accessed | tf_op | source)
XLA Modules:
  0.0 37.8 jit_solution(4710998322336169057)
XLA Ops:
  0.0 2.9 %collective-permute-start = (bf16[4,4,4,128]{3,2,1,0:T(4,128)(2,1)}, bf16[4,4,4,128]{3,2,1,0:T(4,128)(2,1)S(1)}, u32[]{:S(2)}, u32[]{:S(2)}) collective-permute-start(bf16[4,4,4,128]{3,2,1,0:T(4,128)(2,1)} %query_hbm.1), channel_id=1, source_target_pairs={{0,4},{2,6},{4,0},{6,2},{1,5},{3,7},{5,1},{7,3},{8,12},{10,14},{12... | collective-permute-start | bytes 49160 | tf_op jit(solution)/shard_map/ppermute | solution.py:23
  2.9 0.1 collective-permute-start.1
  3.1 2.1 %stage_fresh.1 = (bf16[4,4,4,128]{3,2,1,0:T(4,128)(2,1)S(1)}, bf16[112,16,4,128]{3,2,1,0:T(4,128)(2,1)S(1)}, bf16[112,16,4,128]{3,2,1,0:T(4,128)(2,1)S(1)}) custom-call(bf16[4,4,4,128]{3,2,1,0:T(4,128)(2,1)} %query_hbm.1, bf16[112,16,4,256]{3,2,1,0:T(4,128)(2,1)} %fresh_ref.1), custom_call_target="tpu_custom_call" | custom-call | bytes 7340032 | tf_op jit(solution)/shard_map/stage_fresh/pallas_call | solution.py:435
  5.2 1.1 %collective-permute-done.2 = bf16[4,4,4,128]{3,2,1,0:T(4,128)(2,1)S(1)} collective-permute-done((bf16[4,4,4,128]{3,2,1,0:T(4,128)(2,1)}, bf16[4,4,4,128]{3,2,1,0:T(4,128)(2,1)S(1)}, u32[]{:S(2)}, u32[]{:S(2)}) %collective-permute-start.2) | collective-permute-done | bytes 16416 | tf_op jit(solution)/shard_map/ppermute | solution.py:23
  6.4 3.7 %collective-permute-start.5 = (bf16[4,64,128]{2,1,0:T(8,128)(2,1)S(1)}, bf16[4,64,128]{2,1,0:T(8,128)(2,1)S(1)}, u32[]{:S(2)}, u32[]{:S(2)}) collective-permute-start(bf16[4,64,128]{2,1,0:T(8,128)(2,1)S(1)} %bitcast.19), channel_id=1, source_target_pairs={{0,24},{8,16},{16,8},{24,0},{1,25},{9,17},{17,9},{25,1},{2,26},{10... | collective-permute-start | bytes 196616 | tf_op jit(solution)/shard_map/ppermute | solution.py:23
  10.1 0.8 %collective-permute-start.3 = (bf16[4,64,128]{2,1,0:T(8,128)(2,1)S(1)}, bf16[4,64,128]{2,1,0:T(8,128)(2,1)S(1)}, u32[]{:S(2)}, u32[]{:S(2)}) collective-permute-start(bf16[4,64,128]{2,1,0:T(8,128)(2,1)S(1)} %bitcast.21), channel_id=1, source_target_pairs={{0,8},{8,0},{16,24},{24,16},{1,9},{9,1},{17,25},{25,17},{2,10},{10... | collective-permute-start | bytes 196616 | tf_op jit(solution)/shard_map/ppermute | solution.py:23
  10.9 4.1 %stage_keys.1 = (bf16[512,16,4,128]{3,2,1,0:T(4,128)(2,1)S(1)}, s32[128]{0:T(128)S(1)}, s32[16]{0:T(128)S(1)}) custom-call(s32[112]{0:T(128)} %bucket_hbm.1, bf16[512,16,4,256]{3,2,1,0:T(4,128)(2,1)} %refs_0_.1), custom_call_target="tpu_custom_call" | custom-call | bytes 16777216 | tf_op jit(solution)/shard_map/stage_keys/pallas_call | solution.py:447
  15.0 0.4 %collective-permute-done.4.refs_2_ = bf16[4,64,128]{2,1,0:T(8,128)(2,1)S(1)} collective-permute-done((bf16[4,64,128]{2,1,0:T(8,128)(2,1)S(1)}, bf16[4,64,128]{2,1,0:T(8,128)(2,1)S(1)}, u32[]{:S(2)}, u32[]{:S(2)}) %collective-permute-start.4) | collective-permute-done | bytes 65568 | tf_op jit(solution)/shard_map/ppermute | solution.py:23
  15.5 2.9 %fresh.1 = (f32[3,17,8,128]{3,2,1,0:T(8,128)S(1)}, bf16[3,17,8,128]{3,2,1,0:T(8,128)(2,1)S(1)}, f32[4,64,128]{2,1,0:T(8,128)S(1)}, f32[4,16,128]{2,1,0:T(8,128)S...) custom-call(s32[128]{0:T(128)S(1)} %get-tuple-element.50.slots_ref, ...), custom_call_target="tpu_custom_call" | custom-call | flops 268435456 | bytes 3670016 | tf_op jit(solution)/shard_map/fresh/pallas_call | solution.py:483
  18.5 2.6 %scores.2 = (f32[2,16,8192]{2,1,0:T(8,128)S(1)}, f32[2,16,128]{2,1,0:T(8,128)S(1)}) custom-call(s32[512]{0:T(512)S(1)} %bitcast.25, s32[4]{0:T(128)S(1)} %copy-done.1, bf16[4,64,128]{2,1,0:T(8,128)(2,1)S(1)} %bitcast.23, bf16[512,64,128]{2,1,0:T(8,128)(2,1)S(1)} %bitcast.13), custom_call_target="tpu_custom_call" | custom-call | flops 268435456 | bytes 4194304 | tf_op jit(solution)/shard_map/scores/pallas_call | solution.py:538
  21.1 0.3 merge.3
  21.4 1.3 %collective-permute-start.7 = (bf16[3,17,4,128]{3,2,1,0:T(4,128)(2,1)S(1)}, bf16[3,17,4,128]{3,2,1,0:T(4,128)(2,1)S(1)}, u32[]{:S(2)}, u32[]{:S(2)}) collective-permute-start(bf16[3,17,4,128]{3,2,1,0:T(4,128)(2,1)S(1)} %get-tuple-element.68), channel_id=1, source_target_pairs={{0,4},{2,6},{4,0},{6,2},{1,5},{3,7},{5,1},{7,3},{8,12},{10,14},{12... | collective-permute-start | bytes 156680 | tf_op jit(solution)/shard_map/ppermute | solution.py:23
  22.8 2.9 %scores.3 = (f32[2,16,8192]{2,1,0:T(8,128)S(1)}, f32[2,16,128]{2,1,0:T(8,128)S(1)}, bf16[512,8,4,128]{3,2,1,0:T(4,128)(2,1)S(1)}) custom-call(s32[512]{0:T(512)S(1)} %bitcast.26, s32[4]{0:T(128)S(1)} %copy-done.1, bf16[4,64,128]{2,1,0:T(8,128)(2,1)S(1)} %bitcast.24, bf16[512,64,128]{2,1,0:T(8,128)(2,1)S(1)} %bitcast.14, bf16[512,16,4,256]{3,2,1,0:T(4,128)(2,1)} %refs_0_.1), custom_call_target="tpu_custom_call" | custom-call | flops 268435456 | bytes 4194304 | tf_op jit(solution)/shard_map/scores/pallas_call | solution.py:538
  25.7 0.3 merge.4
  26.0 1.1 %collective-permute-start.8 = (bf16[2,17,4,128]{3,2,1,0:T(4,128)(2,1)S(1)}, bf16[2,17,4,128]{3,2,1,0:T(4,128)(2,1)S(1)}, u32[]{:S(2)}, u32[]{:S(2)}) collective-permute-start(bf16[2,17,4,128]{3,2,1,0:T(4,128)(2,1)S(1)} %get-tuple-element.74), channel_id=1, source_target_pairs={{0,8},{8,0},{16,24},{24,16},{1,9},{9,1},{17,25},{25,17},{2,10},{10... | collective-permute-start | bytes 104456 | tf_op jit(solution)/shard_map/ppermute | solution.py:23
  27.1 2.6 %values.1 = (f32[1,17,4,128]{3,2,1,0:T(4,128)S(1)}, bf16[1,17,4,128]{3,2,1,0:T(4,128)(2,1)S(1)}, bf16[1,17,4,128]{3,2,1,0:T(4,128)(2,1)S(1)}, bf16[1,17,4,128]{3,2,1,0:T(4,128)(2,1)S(1)}) custom-call(s32[512]{0:T(512)S(1)} %bitcast.27, f32[2,16,8192]{2,1,0:T(8,128)S(1)} %get-tuple-element.75.first_t_ref, f32[2,16,128]{2,1,0:T(8,128)S(1)} %get-tuple-element.76.first_top_ref, ...), custom_call_target="tpu_custom_call" | custom-call | flops 536870912 | bytes 8388608 | tf_op jit(solution)/shard_map/values/pallas_call | solution.py:564
  29.7 0.3 collective-permute-done.8.got_ref.refs_0_
  30.0 0.3 merge.5
  30.3 2.4 %collective-permute-start.9 = (bf16[1,17,4,128]{3,2,1,0:T(4,128)(2,1)S(1)}, bf16[1,17,4,128]{3,2,1,0:T(4,128)(2,1)S(1)}, u32[]{:S(2)}, u32[]{:S(2)}) collective-permute-start(bf16[1,17,4,128]{3,2,1,0:T(4,128)(2,1)S(1)} %merge.5), channel_id=1, source_target_pairs={{0,16},{8,24},{16,0},{24,8},{1,17},{9,25},{17,1},{25,9},{2,18},{10... | collective-permute-start | bytes 52232 | tf_op jit(solution)/shard_map/ppermute | solution.py:23
  32.7 0.9 %collective-permute-start.10 = (bf16[1,17,4,128]{3,2,1,0:T(4,128)(2,1)S(1)}, bf16[1,17,4,128]{3,2,1,0:T(4,128)(2,1)S(1)}, u32[]{:S(2)}, u32[]{:S(2)}) collective-permute-start(bf16[1,17,4,128]{3,2,1,0:T(4,128)(2,1)S(1)} %get-tuple-element.92), channel_id=1, source_target_pairs={{0,4},{2,6},{4,0},{6,2},{1,5},{3,7},{5,1},{7,3},{8,12},{10,14},{12... | collective-permute-start | bytes 52232 | tf_op jit(solution)/shard_map/ppermute | solution.py:23
  33.6 1.2 %collective-permute-start.12 = (bf16[1,17,4,128]{3,2,1,0:T(4,128)(2,1)S(1)}, bf16[1,17,4,128]{3,2,1,0:T(4,128)(2,1)S(1)}, u32[]{:S(2)}, u32[]{:S(2)}) collective-permute-start(bf16[1,17,4,128]{3,2,1,0:T(4,128)(2,1)S(1)} %get-tuple-element.94), channel_id=1, source_target_pairs={{0,6},{2,4},{4,2},{6,0},{1,7},{3,5},{5,3},{7,1},{8,14},{10,12},{12... | collective-permute-start | bytes 52232 | tf_op jit(solution)/shard_map/ppermute | solution.py:23
  35.0 1.5 %collective-permute-done.10.refs_2_ = bf16[1,17,4,128]{3,2,1,0:T(4,128)(2,1)S(1)} collective-permute-done((bf16[1,17,4,128]{3,2,1,0:T(4,128)(2,1)S(1)}, bf16[1,17,4,128]{3,2,1,0:T(4,128)(2,1)S(1)}, u32[]{:S(2)}, u32[]{:S(2)}) %collective-permute-start.10) | collective-permute-done | bytes 17440 | tf_op jit(solution)/shard_map/ppermute | solution.py:23
  36.5 0.3 collective-permute-done.12.refs_4_
  36.8 1.0 %last.1 = bf16[4,4,4,128]{3,2,1,0:T(4,128)(2,1)} custom-call(f32[1,17,4,128]{3,2,1,0:T(4,128)S(1)} %get-tuple-element.85.keep_ref, bf16[2,17,4,128]{3,2,1,0:T(4,128)(2,1)S(1)} %collective-permute-done.8.got_ref.refs_0_, bf16[1,17,4,128]{3,2,1,0:T(4,128)(2,1)S(1)} %collective-permute-done.9.refs_1_, ...), custom_call_target="tpu_custom_call" | custom-call | tf_op jit(solution)/shard_map/last/pallas_call | solution.py:585
  (18 shorter events, 0.4 us)
Async XLA Ops:
  0.0 5.2 %collective-permute-start = (bf16[4,4,4,128]{3,2,1,0:T(4,128)(2,1)}, bf16[4,4,4,128]{3,2,1,0:T(4,128)(2,1)S(1)}, u32[]{:S(2)}, u32[]{:S(2)}) collective-permute-start(bf16[4,4,4,128]{3,2,1,0:T(4,128)(2,1)} %query_hbm.1), channel_id=1, source_target_pairs={{0,4},{2,6},{4,0},{6,2},{1,5},{3,7},{5,1},{7,3},{8,12},{10,14},{12... | collective-permute-start | bytes 49160 | tf_op jit(solution)/shard_map/ppermute | solution.py:23
  2.9 3.4 %collective-permute-start.2 = (bf16[4,4,4,128]{3,2,1,0:T(4,128)(2,1)}, bf16[4,4,4,128]{3,2,1,0:T(4,128)(2,1)S(1)}, u32[]{:S(2)}, u32[]{:S(2)}) collective-permute-start(bf16[4,4,4,128]{3,2,1,0:T(4,128)(2,1)} %query_hbm.1), channel_id=1, source_target_pairs={{0,6},{2,4},{4,2},{6,0},{1,7},{3,5},{5,3},{7,1},{8,14},{10,12},{12... | collective-permute-start | bytes 49160 | tf_op jit(solution)/shard_map/ppermute | solution.py:23
  2.9 3.4 %collective-permute-start.1 = (bf16[4,4,4,128]{3,2,1,0:T(4,128)(2,1)}, bf16[4,4,4,128]{3,2,1,0:T(4,128)(2,1)S(1)}, u32[]{:S(2)}, u32[]{:S(2)}) collective-permute-start(bf16[4,4,4,128]{3,2,1,0:T(4,128)(2,1)} %query_hbm.1), channel_id=1, source_target_pairs={{0,2},{2,0},{4,6},{6,4},{1,3},{3,1},{5,7},{7,5},{8,10},{10,8},{12,... | collective-permute-start | bytes 49160 | tf_op jit(solution)/shard_map/ppermute | solution.py:23
  6.4 8.6 %collective-permute-start.5 = (bf16[4,64,128]{2,1,0:T(8,128)(2,1)S(1)}, bf16[4,64,128]{2,1,0:T(8,128)(2,1)S(1)}, u32[]{:S(2)}, u32[]{:S(2)}) collective-permute-start(bf16[4,64,128]{2,1,0:T(8,128)(2,1)S(1)} %bitcast.19), channel_id=1, source_target_pairs={{0,24},{8,16},{16,8},{24,0},{1,25},{9,17},{17,9},{25,1},{2,26},{10... | collective-permute-start | bytes 196616 | tf_op jit(solution)/shard_map/ppermute | solution.py:23
  10.1 5.4 %collective-permute-start.4 = (bf16[4,64,128]{2,1,0:T(8,128)(2,1)S(1)}, bf16[4,64,128]{2,1,0:T(8,128)(2,1)S(1)}, u32[]{:S(2)}, u32[]{:S(2)}) collective-permute-start(bf16[4,64,128]{2,1,0:T(8,128)(2,1)S(1)} %bitcast.20), channel_id=1, source_target_pairs={{0,16},{8,24},{16,0},{24,8},{1,17},{9,25},{17,1},{25,9},{2,18},{10... | collective-permute-start | bytes 196616 | tf_op jit(solution)/shard_map/ppermute | solution.py:23
  10.1 5.4 %collective-permute-start.3 = (bf16[4,64,128]{2,1,0:T(8,128)(2,1)S(1)}, bf16[4,64,128]{2,1,0:T(8,128)(2,1)S(1)}, u32[]{:S(2)}, u32[]{:S(2)}) collective-permute-start(bf16[4,64,128]{2,1,0:T(8,128)(2,1)S(1)} %bitcast.21), channel_id=1, source_target_pairs={{0,8},{8,0},{16,24},{24,16},{1,9},{9,1},{17,25},{25,17},{2,10},{10... | collective-permute-start | bytes 196616 | tf_op jit(solution)/shard_map/ppermute | solution.py:23
  15.5 3.0 %copy-start = (s32[4,128]{1,0:T(4,128)S(1)}, s32[4,128]{1,0:T(4,128)}, u32[]{:S(2)}) copy-start(s32[4,128]{1,0:T(4,128)} %param.8) | copy-start | bytes 6148
  15.5 3.0 %copy-start.1 = (s32[4]{0:T(128)S(1)}, s32[4]{0:T(128)}, u32[]{:S(2)}) copy-start(s32[4]{0:T(128)} %len_ref.3) | copy-start | bytes 52
  18.4 2.7 %collective-permute-start.6 = (bf16[3,17,8,128]{3,2,1,0:T(8,128)(2,1)S(1)}, bf16[3,17,8,128]{3,2,1,0:T(8,128)(2,1)S(1)}, u32[]{:S(2)}, u32[]{:S(2)}) collective-permute-start(bf16[3,17,8,128]{3,2,1,0:T(8,128)(2,1)S(1)} %get-tuple-element.61), channel_id=1, source_target_pairs={{0,2},{2,0},{4,6},{6,4},{1,3},{3,1},{5,7},{7,5},{8,10},{10,8},{12,... | collective-permute-start | bytes 313352 | tf_op jit(solution)/shard_map/ppermute | solution.py:23
  21.4 4.3 %collective-permute-start.7 = (bf16[3,17,4,128]{3,2,1,0:T(4,128)(2,1)S(1)}, bf16[3,17,4,128]{3,2,1,0:T(4,128)(2,1)S(1)}, u32[]{:S(2)}, u32[]{:S(2)}) collective-permute-start(bf16[3,17,4,128]{3,2,1,0:T(4,128)(2,1)S(1)} %get-tuple-element.68), channel_id=1, source_target_pairs={{0,4},{2,6},{4,0},{6,2},{1,5},{3,7},{5,1},{7,3},{8,12},{10,14},{12... | collective-permute-start | bytes 156680 | tf_op jit(solution)/shard_map/ppermute | solution.py:23
  26.0 4.0 %collective-permute-start.8 = (bf16[2,17,4,128]{3,2,1,0:T(4,128)(2,1)S(1)}, bf16[2,17,4,128]{3,2,1,0:T(4,128)(2,1)S(1)}, u32[]{:S(2)}, u32[]{:S(2)}) collective-permute-start(bf16[2,17,4,128]{3,2,1,0:T(4,128)(2,1)S(1)} %get-tuple-element.74), channel_id=1, source_target_pairs={{0,8},{8,0},{16,24},{24,16},{1,9},{9,1},{17,25},{25,17},{2,10},{10... | collective-permute-start | bytes 104456 | tf_op jit(solution)/shard_map/ppermute | solution.py:23
  30.3 4.7 %collective-permute-start.9 = (bf16[1,17,4,128]{3,2,1,0:T(4,128)(2,1)S(1)}, bf16[1,17,4,128]{3,2,1,0:T(4,128)(2,1)S(1)}, u32[]{:S(2)}, u32[]{:S(2)}) collective-permute-start(bf16[1,17,4,128]{3,2,1,0:T(4,128)(2,1)S(1)} %merge.5), channel_id=1, source_target_pairs={{0,16},{8,24},{16,0},{24,8},{1,17},{9,25},{17,1},{25,9},{2,18},{10... | collective-permute-start | bytes 52232 | tf_op jit(solution)/shard_map/ppermute | solution.py:23
  32.7 3.8 %collective-permute-start.10 = (bf16[1,17,4,128]{3,2,1,0:T(4,128)(2,1)S(1)}, bf16[1,17,4,128]{3,2,1,0:T(4,128)(2,1)S(1)}, u32[]{:S(2)}, u32[]{:S(2)}) collective-permute-start(bf16[1,17,4,128]{3,2,1,0:T(4,128)(2,1)S(1)} %get-tuple-element.92), channel_id=1, source_target_pairs={{0,4},{2,6},{4,0},{6,2},{1,5},{3,7},{5,1},{7,3},{8,12},{10,14},{12... | collective-permute-start | bytes 52232 | tf_op jit(solution)/shard_map/ppermute | solution.py:23
  33.6 2.9 %collective-permute-start.11 = (bf16[1,17,4,128]{3,2,1,0:T(4,128)(2,1)S(1)}, bf16[1,17,4,128]{3,2,1,0:T(4,128)(2,1)S(1)}, u32[]{:S(2)}, u32[]{:S(2)}) collective-permute-start(bf16[1,17,4,128]{3,2,1,0:T(4,128)(2,1)S(1)} %get-tuple-element.93), channel_id=1, source_target_pairs={{0,2},{2,0},{4,6},{6,4},{1,3},{3,1},{5,7},{7,5},{8,10},{10,8},{12,... | collective-permute-start | bytes 52232 | tf_op jit(solution)/shard_map/ppermute | solution.py:23
  33.6 3.2 %collective-permute-start.12 = (bf16[1,17,4,128]{3,2,1,0:T(4,128)(2,1)S(1)}, bf16[1,17,4,128]{3,2,1,0:T(4,128)(2,1)S(1)}, u32[]{:S(2)}, u32[]{:S(2)}) collective-permute-start(bf16[1,17,4,128]{3,2,1,0:T(4,128)(2,1)S(1)} %get-tuple-element.94), channel_id=1, source_target_pairs={{0,6},{2,4},{4,2},{6,0},{1,7},{3,5},{5,3},{7,1},{8,14},{10,12},{12... | collective-permute-start | bytes 52232 | tf_op jit(solution)/shard_map/ppermute | solution.py:23

commit v12 on v10

--- a/solution.py
+++ b/solution.py
@@ -12,7 +12,7 @@
 CAP = 2
 LANES = 128
 SCALE = math.log2(math.e) / math.sqrt(LANES)
-SCORE_WIDE = 256
+SCORE_WIDE = 512
 VALUE_WIDE = 512
 VMEM = pl.BlockSpec(memory_space=pltpu.VMEM)
 SMEM = pl.BlockSpec(memory_space=pltpu.SMEM)
@@ -117,10 +117,18 @@
 
 
 def score_parts(q, keys, lane, limit, first, heads, sub):
-    s = lax.dot_general(q, keys, (((1,), (1,)), ((), ())), preferred_element_type=jnp.float32)
+    half = keys.shape[0] // 2
+    none = jnp.zeros_like(q)
+    pair = jnp.concatenate(
+        [jnp.concatenate([q, none], axis=1), jnp.concatenate([none, q], axis=1)], axis=0)
+    s = lax.dot_general(
+        pair, jnp.concatenate([keys[:half], keys[half:]], axis=1), (((1,), (1,)), ((), ())),
+        preferred_element_type=jnp.float32)
     out = []
-    for j in range(s.shape[1] // LANES):
-        part = s[:, j * LANES:(j + 1) * LANES]
+    for j in range(2 * half // LANES):
+        base = 0 if j * LANES < half else q.shape[0]
+        at = j * LANES % half
+        part = s[base:base + q.shape[0], at:at + LANES]
         one = part[:sub]
         for h in range(1, heads):
             one = jnp.where(lane % heads == h, part[h * sub:(h + 1) * sub], one)

time: 37.9 us -> 37.8 us (level)
  no operation moved by 1% of the time
where the time goes in v12:
time: 37.8 us; the launch traced here: 37.7 us
  Pallas kernels  18.8 us (50%)
  starting transfers between devices  14.7 us (39%)
  waiting for transfers between devices  3.95 us (10%)
    ppermute x13, starting transfers between devices, swap(): lax.ppermute(value, axis, [(n, n ^ bit) for n in range(lax.axis_size(axis...  14.7 us
    pallas_call x1, Pallas kernels, local(): pl.pallas_call(functools.partial(stage_keys_kernel, n_ctx, slots), out_sh...  4.08 us
    ppermute x13, waiting for transfers between devices, swap(): lax.ppermute(value, axis, [(n, n ^ bit) for n in range(lax.axis_size(axis...  3.95 us
    pallas_call x1, Pallas kernels, local(): pl.pallas_call(functools.partial(middle_kernel, dims), out_shape=(f32(par...  3.15 us
    pallas_call x1, Pallas kernels, local(): pl.pallas_call(functools.partial(first_kernel, dims, pieces), out_shape=(...  2.83 us
    pallas_call x1, Pallas kernels, local(): pl.pallas_call(functools.partial(fresh_kernel, (heads, page_rows, slots,...  2.81 us
    pallas_call x1, Pallas kernels, local(): pl.pallas_call(stage_fresh_kernel, out_shape=(bf16(*query.shape), half(ne...  2.08 us
    pallas_call x1, Pallas kernels, local(): pl.pallas_call(functools.partial(second_kernel, dims, len(vbs)), out_shap...  2 us
  transfers between devices with their start and end apart: 13, of which 4 were waited for; matrix products, arithmetic and copies ran while one was open for 0% of the time, Pallas kernels for 38%

profile of v12, /device:TPU:0, one launch (start us, length us, event | category | flops | bytes accessed | tf_op | source)
XLA Modules:
  0.0 37.7 jit_solution(14968461247032577723)
XLA Ops:
  0.0 2.9 %collective-permute-start = (bf16[4,4,4,128]{3,2,1,0:T(4,128)(2,1)}, bf16[4,4,4,128]{3,2,1,0:T(4,128)(2,1)S(1)}, u32[]{:S(2)}, u32[]{:S(2)}) collective-permute-start(bf16[4,4,4,128]{3,2,1,0:T(4,128)(2,1)} %query_hbm.1), channel_id=1, source_target_pairs={{0,4},{2,6},{4,0},{6,2},{1,5},{3,7},{5,1},{7,3},{8,12},{10,14},{12... | collective-permute-start | bytes 49160 | tf_op jit(solution)/shard_map/ppermute | solution.py:23
  2.9 0.1 collective-permute-start.1
  3.1 2.1 %stage_fresh.1 = (bf16[4,4,4,128]{3,2,1,0:T(4,128)(2,1)S(1)}, bf16[112,16,4,128]{3,2,1,0:T(4,128)(2,1)S(1)}, bf16[112,16,4,128]{3,2,1,0:T(4,128)(2,1)S(1)}) custom-call(bf16[4,4,4,128]{3,2,1,0:T(4,128)(2,1)} %query_hbm.1, bf16[112,16,4,256]{3,2,1,0:T(4,128)(2,1)} %fresh_ref.1), custom_call_target="tpu_custom_call" | custom-call | bytes 7340032 | tf_op jit(solution)/shard_map/stage_fresh/pallas_call | solution.py:456
  5.2 1.1 %collective-permute-done.2 = bf16[4,4,4,128]{3,2,1,0:T(4,128)(2,1)S(1)} collective-permute-done((bf16[4,4,4,128]{3,2,1,0:T(4,128)(2,1)}, bf16[4,4,4,128]{3,2,1,0:T(4,128)(2,1)S(1)}, u32[]{:S(2)}, u32[]{:S(2)}) %collective-permute-start.2) | collective-permute-done | bytes 16416 | tf_op jit(solution)/shard_map/ppermute | solution.py:23
  6.3 0.1 maximum_bitcast_fusion
  6.4 3.7 %collective-permute-start.5 = (bf16[4,64,128]{2,1,0:T(8,128)(2,1)S(1)}, bf16[4,64,128]{2,1,0:T(8,128)(2,1)S(1)}, u32[]{:S(2)}, u32[]{:S(2)}) collective-permute-start(bf16[4,64,128]{2,1,0:T(8,128)(2,1)S(1)} %bitcast.21), channel_id=1, source_target_pairs={{0,24},{8,16},{16,8},{24,0},{1,25},{9,17},{17,9},{25,1},{2,26},{10... | collective-permute-start | bytes 196616 | tf_op jit(solution)/shard_map/ppermute | solution.py:23
  10.1 0.8 %collective-permute-start.3 = (bf16[4,64,128]{2,1,0:T(8,128)(2,1)S(1)}, bf16[4,64,128]{2,1,0:T(8,128)(2,1)S(1)}, u32[]{:S(2)}, u32[]{:S(2)}) collective-permute-start(bf16[4,64,128]{2,1,0:T(8,128)(2,1)S(1)} %bitcast.23), channel_id=1, source_target_pairs={{0,8},{8,0},{16,24},{24,16},{1,9},{9,1},{17,25},{25,17},{2,10},{10... | collective-permute-start | bytes 196616 | tf_op jit(solution)/shard_map/ppermute | solution.py:23
  10.9 4.1 %stage_keys.1 = (bf16[512,16,4,128]{3,2,1,0:T(4,128)(2,1)S(1)}, s32[128]{0:T(128)S(1)}, s32[16]{0:T(128)S(1)}) custom-call(s32[112]{0:T(128)} %bucket_hbm.1, bf16[512,16,4,256]{3,2,1,0:T(4,128)(2,1)} %refs_0_.1), custom_call_target="tpu_custom_call" | custom-call | bytes 16777216 | tf_op jit(solution)/shard_map/stage_keys/pallas_call | solution.py:468
  15.0 0.5 %collective-permute-done.4.refs_2_ = bf16[4,64,128]{2,1,0:T(8,128)(2,1)S(1)} collective-permute-done((bf16[4,64,128]{2,1,0:T(8,128)(2,1)S(1)}, bf16[4,64,128]{2,1,0:T(8,128)(2,1)S(1)}, u32[]{:S(2)}, u32[]{:S(2)}) %collective-permute-start.4) | collective-permute-done | bytes 65568 | tf_op jit(solution)/shard_map/ppermute | solution.py:23
  15.5 2.8 %fresh.1 = (f32[3,17,8,128]{3,2,1,0:T(8,128)S(1)}, bf16[3,17,8,128]{3,2,1,0:T(8,128)(2,1)S(1)}, f32[4,64,128]{2,1,0:T(8,128)S(1)}, f32[4,16,128]{2,1,0:T(8,128)S...) custom-call(s32[128]{0:T(128)S(1)} %get-tuple-element.48.slots_ref, ...), custom_call_target="tpu_custom_call" | custom-call | flops 268435456 | bytes 3670016 | tf_op jit(solution)/shard_map/fresh/pallas_call | solution.py:504
  18.3 0.1 collective-permute-start.6
  18.4 2.8 %first.1 = (f32[2,16,8192]{2,1,0:T(8,128)S(1)}, f32[2,16,128]{2,1,0:T(8,128)S(1)}, bf16[512,8,4,128]{3,2,1,0:T(4,128)(2,1)S(1)}) custom-call(s32[512]{0:T(512)S(1)} %bitcast.27, s32[4]{0:T(128)S(1)} %copy-done.1, bf16[4,64,128]{2,1,0:T(8,128)(2,1)S(1)} %bitcast.25, bf16[512,64,128]{2,1,0:T(8,128)(2,1)S(1)} %bitcast.13, bf16[512,16,4,256]{3,2,1,0:T(4,128)(2,1)} %refs_0_.1), custom_call_target="tpu_custom_call" | custom-call | flops 268435456 | bytes 4194304 | tf_op jit(solution)/shard_map/first/pallas_call | solution.py:557
  21.3 0.3 merge.3
  21.6 1.3 %collective-permute-start.7 = (bf16[3,17,4,128]{3,2,1,0:T(4,128)(2,1)S(1)}, bf16[3,17,4,128]{3,2,1,0:T(4,128)(2,1)S(1)}, u32[]{:S(2)}, u32[]{:S(2)}) collective-permute-start(bf16[3,17,4,128]{3,2,1,0:T(4,128)(2,1)S(1)} %get-tuple-element.67), channel_id=1, source_target_pairs={{0,4},{2,6},{4,0},{6,2},{1,5},{3,7},{5,1},{7,3},{8,12},{10,14},{12... | collective-permute-start | bytes 156680 | tf_op jit(solution)/shard_map/ppermute | solution.py:23
  22.9 3.1 %middle.1 = (f32[2,16,8192]{2,1,0:T(8,128)S(1)}, f32[2,16,128]{2,1,0:T(8,128)S(1)}, f32[2,64,128]{2,1,0:T(8,128)S(1)}, f32[2,16,128]{2,1,0:T(8,128)S(1)}) custom-call(s32[512]{0:T(512)S(1)} %bitcast.28, s32[4]{0:T(128)S(1)} %copy-done.1, bf16[4,64,128]{2,1,0:T(8,128)(2,1)S(1)} %bitcast.26, bf16[512,64,128]{2,1,0:T(8,128)(2,1)S(1)} %bitcast.14, ...), custom_call_target="tpu_custom_call" | custom-call | flops 536870912 | bytes 8388608 | tf_op jit(solution)/shard_map/middle/pallas_call | solution.py:573
  26.0 0.3 merge.4
  26.4 1.1 %collective-permute-start.8 = (bf16[2,17,4,128]{3,2,1,0:T(4,128)(2,1)S(1)}, bf16[2,17,4,128]{3,2,1,0:T(4,128)(2,1)S(1)}, u32[]{:S(2)}, u32[]{:S(2)}) collective-permute-start(bf16[2,17,4,128]{3,2,1,0:T(4,128)(2,1)S(1)} %get-tuple-element.76), channel_id=1, source_target_pairs={{0,8},{8,0},{16,24},{24,16},{1,9},{9,1},{17,25},{25,17},{2,10},{10... | collective-permute-start | bytes 104456 | tf_op jit(solution)/shard_map/ppermute | solution.py:23
  27.5 2.0 %second.1 = (f32[1,17,4,128]{3,2,1,0:T(4,128)S(1)}, bf16[1,17,4,128]{3,2,1,0:T(4,128)(2,1)S(1)}, bf16[1,17,4,128]{3,2,1,0:T(4,128)(2,1)S(1)}, bf16[1,17,4,128]{3,2,1,0:T(4,128)(2,1)S(1)}) custom-call(s32[512]{0:T(512)S(1)} %bitcast.29, f32[2,16,8192]{2,1,0:T(8,128)S(1)} %get-tuple-element.77.t_ref, f32[2,16,128]{2,1,0:T(8,128)S(1)} %get-tuple-element.78.top_ref, ...), custom_call_target="tpu_custom_call" | custom-call | flops 268435456 | bytes 4194304 | tf_op jit(solution)/shard_map/second/pallas_call | solution.py:590
  29.5 1.1 %collective-permute-start.9 = (bf16[1,17,4,128]{3,2,1,0:T(4,128)(2,1)S(1)}, bf16[1,17,4,128]{3,2,1,0:T(4,128)(2,1)S(1)}, u32[]{:S(2)}, u32[]{:S(2)}) collective-permute-start(bf16[1,17,4,128]{3,2,1,0:T(4,128)(2,1)S(1)} %get-tuple-element.86), channel_id=1, source_target_pairs={{0,4},{2,6},{4,0},{6,2},{1,5},{3,7},{5,1},{7,3},{8,12},{10,14},{12... | collective-permute-start | bytes 52232 | tf_op jit(solution)/shard_map/ppermute | solution.py:23
  30.6 1.1 %collective-permute-start.11 = (bf16[1,17,4,128]{3,2,1,0:T(4,128)(2,1)S(1)}, bf16[1,17,4,128]{3,2,1,0:T(4,128)(2,1)S(1)}, u32[]{:S(2)}, u32[]{:S(2)}) collective-permute-start(bf16[1,17,4,128]{3,2,1,0:T(4,128)(2,1)S(1)} %get-tuple-element.88), channel_id=1, source_target_pairs={{0,6},{2,4},{4,2},{6,0},{1,7},{3,5},{5,3},{7,1},{8,14},{10,12},{12... | collective-permute-start | bytes 52232 | tf_op jit(solution)/shard_map/ppermute | solution.py:23
  31.7 0.3 merge.5
  32.0 2.5 %collective-permute-start.12 = (bf16[1,17,4,128]{3,2,1,0:T(4,128)(2,1)S(1)}, bf16[1,17,4,128]{3,2,1,0:T(4,128)(2,1)S(1)}, u32[]{:S(2)}, u32[]{:S(2)}) collective-permute-start(bf16[1,17,4,128]{3,2,1,0:T(4,128)(2,1)S(1)} %merge.5), channel_id=1, source_target_pairs={{0,16},{8,24},{16,0},{24,8},{1,17},{9,25},{17,1},{25,9},{2,18},{10... | collective-permute-start | bytes 52232 | tf_op jit(solution)/shard_map/ppermute | solution.py:23
  34.4 2.2 %collective-permute-done.12.refs_4_ = bf16[1,17,4,128]{3,2,1,0:T(4,128)(2,1)S(1)} collective-permute-done((bf16[1,17,4,128]{3,2,1,0:T(4,128)(2,1)S(1)}, bf16[1,17,4,128]{3,2,1,0:T(4,128)(2,1)S(1)}, u32[]{:S(2)}, u32[]{:S(2)}) %collective-permute-start.12) | collective-permute-done | bytes 17440 | tf_op jit(solution)/shard_map/ppermute | solution.py:23
  36.7 1.0 %last.1 = bf16[4,4,4,128]{3,2,1,0:T(4,128)(2,1)} custom-call(f32[1,17,4,128]{3,2,1,0:T(4,128)S(1)} %get-tuple-element.85.keep_ref, bf16[2,17,4,128]{3,2,1,0:T(4,128)(2,1)S(1)} %collective-permute-done.8.got_ref.refs_0_, bf16[1,17,4,128]{3,2,1,0:T(4,128)(2,1)S(1)} %collective-permute-done.9.refs_1_, ...), custom_call_target="tpu_custom_call" | custom-call | tf_op jit(solution)/shard_map/last/pallas_call | solution.py:610
  (18 shorter events, 0.1 us)
Async XLA Ops:
  0.0 5.2 %collective-permute-start = (bf16[4,4,4,128]{3,2,1,0:T(4,128)(2,1)}, bf16[4,4,4,128]{3,2,1,0:T(4,128)(2,1)S(1)}, u32[]{:S(2)}, u32[]{:S(2)}) collective-permute-start(bf16[4,4,4,128]{3,2,1,0:T(4,128)(2,1)} %query_hbm.1), channel_id=1, source_target_pairs={{0,4},{2,6},{4,0},{6,2},{1,5},{3,7},{5,1},{7,3},{8,12},{10,14},{12... | collective-permute-start | bytes 49160 | tf_op jit(solution)/shard_map/ppermute | solution.py:23
  2.9 3.4 %collective-permute-start.2 = (bf16[4,4,4,128]{3,2,1,0:T(4,128)(2,1)}, bf16[4,4,4,128]{3,2,1,0:T(4,128)(2,1)S(1)}, u32[]{:S(2)}, u32[]{:S(2)}) collective-permute-start(bf16[4,4,4,128]{3,2,1,0:T(4,128)(2,1)} %query_hbm.1), channel_id=1, source_target_pairs={{0,6},{2,4},{4,2},{6,0},{1,7},{3,5},{5,3},{7,1},{8,14},{10,12},{12... | collective-permute-start | bytes 49160 | tf_op jit(solution)/shard_map/ppermute | solution.py:23
  2.9 3.4 %collective-permute-start.1 = (bf16[4,4,4,128]{3,2,1,0:T(4,128)(2,1)}, bf16[4,4,4,128]{3,2,1,0:T(4,128)(2,1)S(1)}, u32[]{:S(2)}, u32[]{:S(2)}) collective-permute-start(bf16[4,4,4,128]{3,2,1,0:T(4,128)(2,1)} %query_hbm.1), channel_id=1, source_target_pairs={{0,2},{2,0},{4,6},{6,4},{1,3},{3,1},{5,7},{7,5},{8,10},{10,8},{12,... | collective-permute-start | bytes 49160 | tf_op jit(solution)/shard_map/ppermute | solution.py:23
  6.4 8.5 %collective-permute-start.5 = (bf16[4,64,128]{2,1,0:T(8,128)(2,1)S(1)}, bf16[4,64,128]{2,1,0:T(8,128)(2,1)S(1)}, u32[]{:S(2)}, u32[]{:S(2)}) collective-permute-start(bf16[4,64,128]{2,1,0:T(8,128)(2,1)S(1)} %bitcast.21), channel_id=1, source_target_pairs={{0,24},{8,16},{16,8},{24,0},{1,25},{9,17},{17,9},{25,1},{2,26},{10... | collective-permute-start | bytes 196616 | tf_op jit(solution)/shard_map/ppermute | solution.py:23
  10.1 5.4 %collective-permute-start.4 = (bf16[4,64,128]{2,1,0:T(8,128)(2,1)S(1)}, bf16[4,64,128]{2,1,0:T(8,128)(2,1)S(1)}, u32[]{:S(2)}, u32[]{:S(2)}) collective-permute-start(bf16[4,64,128]{2,1,0:T(8,128)(2,1)S(1)} %bitcast.22), channel_id=1, source_target_pairs={{0,16},{8,24},{16,0},{24,8},{1,17},{9,25},{17,1},{25,9},{2,18},{10... | collective-permute-start | bytes 196616 | tf_op jit(solution)/shard_map/ppermute | solution.py:23
  10.1 5.4 %collective-permute-start.3 = (bf16[4,64,128]{2,1,0:T(8,128)(2,1)S(1)}, bf16[4,64,128]{2,1,0:T(8,128)(2,1)S(1)}, u32[]{:S(2)}, u32[]{:S(2)}) collective-permute-start(bf16[4,64,128]{2,1,0:T(8,128)(2,1)S(1)} %bitcast.23), channel_id=1, source_target_pairs={{0,8},{8,0},{16,24},{24,16},{1,9},{9,1},{17,25},{25,17},{2,10},{10... | collective-permute-start | bytes 196616 | tf_op jit(solution)/shard_map/ppermute | solution.py:23
  15.5 2.9 %copy-start = (s32[4,128]{1,0:T(4,128)S(1)}, s32[4,128]{1,0:T(4,128)}, u32[]{:S(2)}) copy-start(s32[4,128]{1,0:T(4,128)} %param.8) | copy-start | bytes 6148
  15.5 2.9 %copy-start.1 = (s32[4]{0:T(128)S(1)}, s32[4]{0:T(128)}, u32[]{:S(2)}) copy-start(s32[4]{0:T(128)} %len_ref.3) | copy-start | bytes 52
  18.3 2.9 %collective-permute-start.6 = (bf16[3,17,8,128]{3,2,1,0:T(8,128)(2,1)S(1)}, bf16[3,17,8,128]{3,2,1,0:T(8,128)(2,1)S(1)}, u32[]{:S(2)}, u32[]{:S(2)}) collective-permute-start(bf16[3,17,8,128]{3,2,1,0:T(8,128)(2,1)S(1)} %get-tuple-element.59), channel_id=1, source_target_pairs={{0,2},{2,0},{4,6},{6,4},{1,3},{3,1},{5,7},{7,5},{8,10},{10,8},{12,... | collective-permute-start | bytes 313352 | tf_op jit(solution)/shard_map/ppermute | solution.py:23
  21.6 4.4 %collective-permute-start.7 = (bf16[3,17,4,128]{3,2,1,0:T(4,128)(2,1)S(1)}, bf16[3,17,4,128]{3,2,1,0:T(4,128)(2,1)S(1)}, u32[]{:S(2)}, u32[]{:S(2)}) collective-permute-start(bf16[3,17,4,128]{3,2,1,0:T(4,128)(2,1)S(1)} %get-tuple-element.67), channel_id=1, source_target_pairs={{0,4},{2,6},{4,0},{6,2},{1,5},{3,7},{5,1},{7,3},{8,12},{10,14},{12... | collective-permute-start | bytes 156680 | tf_op jit(solution)/shard_map/ppermute | solution.py:23
  26.4 5.3 %collective-permute-start.8 = (bf16[2,17,4,128]{3,2,1,0:T(4,128)(2,1)S(1)}, bf16[2,17,4,128]{3,2,1,0:T(4,128)(2,1)S(1)}, u32[]{:S(2)}, u32[]{:S(2)}) collective-permute-start(bf16[2,17,4,128]{3,2,1,0:T(4,128)(2,1)S(1)} %get-tuple-element.76), channel_id=1, source_target_pairs={{0,8},{8,0},{16,24},{24,16},{1,9},{9,1},{17,25},{25,17},{2,10},{10... | collective-permute-start | bytes 104456 | tf_op jit(solution)/shard_map/ppermute | solution.py:23
  29.5 4.9 %collective-permute-start.9 = (bf16[1,17,4,128]{3,2,1,0:T(4,128)(2,1)S(1)}, bf16[1,17,4,128]{3,2,1,0:T(4,128)(2,1)S(1)}, u32[]{:S(2)}, u32[]{:S(2)}) collective-permute-start(bf16[1,17,4,128]{3,2,1,0:T(4,128)(2,1)S(1)} %get-tuple-element.86), channel_id=1, source_target_pairs={{0,4},{2,6},{4,0},{6,2},{1,5},{3,7},{5,1},{7,3},{8,12},{10,14},{12... | collective-permute-start | bytes 52232 | tf_op jit(solution)/shard_map/ppermute | solution.py:23
  30.6 3.8 %collective-permute-start.10 = (bf16[1,17,4,128]{3,2,1,0:T(4,128)(2,1)S(1)}, bf16[1,17,4,128]{3,2,1,0:T(4,128)(2,1)S(1)}, u32[]{:S(2)}, u32[]{:S(2)}) collective-permute-start(bf16[1,17,4,128]{3,2,1,0:T(4,128)(2,1)S(1)} %get-tuple-element.87), channel_id=1, source_target_pairs={{0,2},{2,0},{4,6},{6,4},{1,3},{3,1},{5,7},{7,5},{8,10},{10,8},{12,... | collective-permute-start | bytes 52232 | tf_op jit(solution)/shard_map/ppermute | solution.py:23
  30.6 3.8 %collective-permute-start.11 = (bf16[1,17,4,128]{3,2,1,0:T(4,128)(2,1)S(1)}, bf16[1,17,4,128]{3,2,1,0:T(4,128)(2,1)S(1)}, u32[]{:S(2)}, u32[]{:S(2)}) collective-permute-start(bf16[1,17,4,128]{3,2,1,0:T(4,128)(2,1)S(1)} %get-tuple-element.88), channel_id=1, source_target_pairs={{0,6},{2,4},{4,2},{6,0},{1,7},{3,5},{5,3},{7,1},{8,14},{10,12},{12... | collective-permute-start | bytes 52232 | tf_op jit(solution)/shard_map/ppermute | solution.py:23
  32.0 4.7 %collective-permute-start.12 = (bf16[1,17,4,128]{3,2,1,0:T(4,128)(2,1)S(1)}, bf16[1,17,4,128]{3,2,1,0:T(4,128)(2,1)S(1)}, u32[]{:S(2)}, u32[]{:S(2)}) collective-permute-start(bf16[1,17,4,128]{3,2,1,0:T(4,128)(2,1)S(1)} %merge.5), channel_id=1, source_target_pairs={{0,16},{8,24},{16,0},{24,8},{1,17},{9,25},{17,1},{25,9},{2,18},{10... | collective-permute-start | bytes 52232 | tf_op jit(solution)/shard_map/ppermute | solution.py:23

commit v13 on v10

--- a/solution.py
+++ b/solution.py
@@ -201,7 +201,7 @@
         score_request(dims, i, table_ref, len_ref, q_ref, kb, t_ref, top_ref, i)
         return 0
 
-    lax.fori_loop(0, t_ref.shape[0], step, 0)
+    lax.fori_loop(0, t_ref.shape[0], step, 0, unroll=True)
     top_ref[...] = reduce_rows(top_ref, jnp.maximum, dims[0]).reshape(top_ref.shape)
     copies.wait()
 
@@ -216,7 +216,7 @@
         value_request(dims, i, table_ref, t_ref, top_ref, i, vbs, acc_ref, tot_ref)
         return 0
 
-    lax.fori_loop(0, half, step, 0)
+    lax.fori_loop(0, half, step, 0, unroll=True)
     later_top_ref[...] = reduce_rows(
         later_top_ref, jnp.maximum, dims[0]).reshape(later_top_ref.shape)
 
@@ -241,7 +241,7 @@
         value_request(dims, half + i, table_ref, t_ref, top_ref, i, vbs, acc_s, tot_s)
         return 0
 
-    lax.fori_loop(0, half, step, 0)
+    lax.fori_loop(0, half, step, 0, unroll=True)
     flat = (req_dev * sub, LANES)
     tots = jnp.concatenate(
         [reduce_rows(ref, jnp.add, heads) for ref in (first_tot_ref, tot_s)], axis=0)

time: 37.9 us -> 37 us (0.976)
  Pallas kernels: 18.9 us -> 18 us
    pallas_call x1, Pallas kernels: 1.99 us -> 1.48 us  [local(): pl.pallas_call(functools.partial(second_kernel, dims, len(vbs)), out_shap...]
  transfers between devices with their start and end apart: 13 -> 13, of which waited for: 4 -> 5; matrix products, arithmetic and copies ran while one was open for 0% -> 0% of each run, Pallas kernels for 38% -> 37%
where the time goes in v13:
time: 37 us; the launch traced here: 36.9 us
  Pallas kernels  18 us (49%)
  starting transfers between devices  14.9 us (40%)
  waiting for transfers between devices  3.75 us (10%)
    ppermute x13, starting transfers between devices, swap(): lax.ppermute(value, axis, [(n, n ^ bit) for n in range(lax.axis_size(axis...  14.9 us
    pallas_call x1, Pallas kernels, local(): pl.pallas_call(functools.partial(stage_keys_kernel, n_ctx, slots), out_sh...  4.08 us
    ppermute x13, waiting for transfers between devices, swap(): lax.ppermute(value, axis, [(n, n ^ bit) for n in range(lax.axis_size(axis...  3.75 us
    pallas_call x1, Pallas kernels, local(): pl.pallas_call(functools.partial(middle_kernel, dims), out_shape=(f32(par...  2.85 us
    pallas_call x1, Pallas kernels, local(): pl.pallas_call(functools.partial(first_kernel, dims, pieces), out_shape=(...  2.83 us
    pallas_call x1, Pallas kernels, local(): pl.pallas_call(functools.partial(fresh_kernel, (heads, page_rows, slots,...  2.81 us
    pallas_call x1, Pallas kernels, local(): pl.pallas_call(stage_fresh_kernel, out_shape=(bf16(*query.shape), half(ne...  2.08 us
    pallas_call x1, Pallas kernels, local(): pl.pallas_call(functools.partial(second_kernel, dims, len(vbs)), out_shap...  1.48 us
  transfers between devices with their start and end apart: 13, of which 5 were waited for; matrix products, arithmetic and copies ran while one was open for 0% of the time, Pallas kernels for 37%

profile of v13, /device:TPU:0, one launch (start us, length us, event | category | flops | bytes accessed | tf_op | source)
XLA Modules:
  0.0 36.9 jit_solution(2776398734530131989)
XLA Ops:
  0.0 2.9 %collective-permute-start = (bf16[4,4,4,128]{3,2,1,0:T(4,128)(2,1)}, bf16[4,4,4,128]{3,2,1,0:T(4,128)(2,1)S(1)}, u32[]{:S(2)}, u32[]{:S(2)}) collective-permute-start(bf16[4,4,4,128]{3,2,1,0:T(4,128)(2,1)} %query_hbm.1), channel_id=1, source_target_pairs={{0,4},{2,6},{4,0},{6,2},{1,5},{3,7},{5,1},{7,3},{8,12},{10,14},{12... | collective-permute-start | bytes 49160 | tf_op jit(solution)/shard_map/ppermute | solution.py:23
  2.9 0.1 collective-permute-start.1
  3.1 2.1 %stage_fresh.1 = (bf16[4,4,4,128]{3,2,1,0:T(4,128)(2,1)S(1)}, bf16[112,16,4,128]{3,2,1,0:T(4,128)(2,1)S(1)}, bf16[112,16,4,128]{3,2,1,0:T(4,128)(2,1)S(1)}) custom-call(bf16[4,4,4,128]{3,2,1,0:T(4,128)(2,1)} %query_hbm.1, bf16[112,16,4,256]{3,2,1,0:T(4,128)(2,1)} %fresh_ref.1), custom_call_target="tpu_custom_call" | custom-call | bytes 7340032 | tf_op jit(solution)/shard_map/stage_fresh/pallas_call | solution.py:448
  5.2 1.1 %collective-permute-done.2 = bf16[4,4,4,128]{3,2,1,0:T(4,128)(2,1)S(1)} collective-permute-done((bf16[4,4,4,128]{3,2,1,0:T(4,128)(2,1)}, bf16[4,4,4,128]{3,2,1,0:T(4,128)(2,1)S(1)}, u32[]{:S(2)}, u32[]{:S(2)}) %collective-permute-start.2) | collective-permute-done | bytes 16416 | tf_op jit(solution)/shard_map/ppermute | solution.py:23
  6.4 3.7 %collective-permute-start.5 = (bf16[4,64,128]{2,1,0:T(8,128)(2,1)S(1)}, bf16[4,64,128]{2,1,0:T(8,128)(2,1)S(1)}, u32[]{:S(2)}, u32[]{:S(2)}) collective-permute-start(bf16[4,64,128]{2,1,0:T(8,128)(2,1)S(1)} %bitcast.21), channel_id=1, source_target_pairs={{0,24},{8,16},{16,8},{24,0},{1,25},{9,17},{17,9},{25,1},{2,26},{10... | collective-permute-start | bytes 196616 | tf_op jit(solution)/shard_map/ppermute | solution.py:23
  10.1 0.8 %collective-permute-start.3 = (bf16[4,64,128]{2,1,0:T(8,128)(2,1)S(1)}, bf16[4,64,128]{2,1,0:T(8,128)(2,1)S(1)}, u32[]{:S(2)}, u32[]{:S(2)}) collective-permute-start(bf16[4,64,128]{2,1,0:T(8,128)(2,1)S(1)} %bitcast.23), channel_id=1, source_target_pairs={{0,8},{8,0},{16,24},{24,16},{1,9},{9,1},{17,25},{25,17},{2,10},{10... | collective-permute-start | bytes 196616 | tf_op jit(solution)/shard_map/ppermute | solution.py:23
  10.9 4.1 %stage_keys.1 = (bf16[512,16,4,128]{3,2,1,0:T(4,128)(2,1)S(1)}, s32[128]{0:T(128)S(1)}, s32[16]{0:T(128)S(1)}) custom-call(s32[112]{0:T(128)} %bucket_hbm.1, bf16[512,16,4,256]{3,2,1,0:T(4,128)(2,1)} %refs_0_.1), custom_call_target="tpu_custom_call" | custom-call | bytes 16777216 | tf_op jit(solution)/shard_map/stage_keys/pallas_call | solution.py:460
  15.0 0.5 %collective-permute-done.4.refs_2_ = bf16[4,64,128]{2,1,0:T(8,128)(2,1)S(1)} collective-permute-done((bf16[4,64,128]{2,1,0:T(8,128)(2,1)S(1)}, bf16[4,64,128]{2,1,0:T(8,128)(2,1)S(1)}, u32[]{:S(2)}, u32[]{:S(2)}) %collective-permute-start.4) | collective-permute-done | bytes 65568 | tf_op jit(solution)/shard_map/ppermute | solution.py:23
  15.5 2.8 %fresh.1 = (f32[3,17,8,128]{3,2,1,0:T(8,128)S(1)}, bf16[3,17,8,128]{3,2,1,0:T(8,128)(2,1)S(1)}, f32[4,64,128]{2,1,0:T(8,128)S(1)}, f32[4,16,128]{2,1,0:T(8,128)S...) custom-call(s32[128]{0:T(128)S(1)} %get-tuple-element.48.slots_ref, ...), custom_call_target="tpu_custom_call" | custom-call | flops 268435456 | bytes 3670016 | tf_op jit(solution)/shard_map/fresh/pallas_call | solution.py:496
  18.3 0.1 collective-permute-start.6
  18.4 2.8 %first.1 = (f32[2,16,8192]{2,1,0:T(8,128)S(1)}, f32[2,16,128]{2,1,0:T(8,128)S(1)}, bf16[512,8,4,128]{3,2,1,0:T(4,128)(2,1)S(1)}) custom-call(s32[512]{0:T(512)S(1)} %bitcast.27, s32[4]{0:T(128)S(1)} %copy-done.1, bf16[4,64,128]{2,1,0:T(8,128)(2,1)S(1)} %bitcast.25, bf16[512,64,128]{2,1,0:T(8,128)(2,1)S(1)} %bitcast.13, bf16[512,16,4,256]{3,2,1,0:T(4,128)(2,1)} %refs_0_.1), custom_call_target="tpu_custom_call" | custom-call | flops 268435456 | bytes 4194304 | tf_op jit(solution)/shard_map/first/pallas_call | solution.py:549
  21.3 0.3 merge.3
  21.6 1.3 %collective-permute-start.7 = (bf16[3,17,4,128]{3,2,1,0:T(4,128)(2,1)S(1)}, bf16[3,17,4,128]{3,2,1,0:T(4,128)(2,1)S(1)}, u32[]{:S(2)}, u32[]{:S(2)}) collective-permute-start(bf16[3,17,4,128]{3,2,1,0:T(4,128)(2,1)S(1)} %get-tuple-element.67), channel_id=1, source_target_pairs={{0,4},{2,6},{4,0},{6,2},{1,5},{3,7},{5,1},{7,3},{8,12},{10,14},{12... | collective-permute-start | bytes 156680 | tf_op jit(solution)/shard_map/ppermute | solution.py:23
  22.9 2.8 %middle.1 = (f32[2,16,8192]{2,1,0:T(8,128)S(1)}, f32[2,16,128]{2,1,0:T(8,128)S(1)}, f32[2,64,128]{2,1,0:T(8,128)S(1)}, f32[2,16,128]{2,1,0:T(8,128)S(1)}) custom-call(s32[512]{0:T(512)S(1)} %bitcast.28, s32[4]{0:T(128)S(1)} %copy-done.1, bf16[4,64,128]{2,1,0:T(8,128)(2,1)S(1)} %bitcast.26, bf16[512,64,128]{2,1,0:T(8,128)(2,1)S(1)} %bitcast.14, ...), custom_call_target="tpu_custom_call" | custom-call | flops 536870912 | bytes 8388608 | tf_op jit(solution)/shard_map/middle/pallas_call | solution.py:565
  25.7 0.1 collective-permute-done.7.got_ref
  25.9 0.3 merge.4
  26.2 1.0 %collective-permute-start.8 = (bf16[2,17,4,128]{3,2,1,0:T(4,128)(2,1)S(1)}, bf16[2,17,4,128]{3,2,1,0:T(4,128)(2,1)S(1)}, u32[]{:S(2)}, u32[]{:S(2)}) collective-permute-start(bf16[2,17,4,128]{3,2,1,0:T(4,128)(2,1)S(1)} %get-tuple-element.76), channel_id=1, source_target_pairs={{0,8},{8,0},{16,24},{24,16},{1,9},{9,1},{17,25},{25,17},{2,10},{10... | collective-permute-start | bytes 104456 | tf_op jit(solution)/shard_map/ppermute | solution.py:23
  27.2 1.5 %second.1 = (f32[1,17,4,128]{3,2,1,0:T(4,128)S(1)}, bf16[1,17,4,128]{3,2,1,0:T(4,128)(2,1)S(1)}, bf16[1,17,4,128]{3,2,1,0:T(4,128)(2,1)S(1)}, bf16[1,17,4,128]{3,2,1,0:T(4,128)(2,1)S(1)}) custom-call(s32[512]{0:T(512)S(1)} %bitcast.29, f32[2,16,8192]{2,1,0:T(8,128)S(1)} %get-tuple-element.77.t_ref, f32[2,16,128]{2,1,0:T(8,128)S(1)} %get-tuple-element.78.top_ref, ...), custom_call_target="tpu_custom_call" | custom-call | flops 268435456 | bytes 4194304 | tf_op jit(solution)/shard_map/second/pallas_call | solution.py:582
  28.7 1.4 %collective-permute-start.9 = (bf16[1,17,4,128]{3,2,1,0:T(4,128)(2,1)S(1)}, bf16[1,17,4,128]{3,2,1,0:T(4,128)(2,1)S(1)}, u32[]{:S(2)}, u32[]{:S(2)}) collective-permute-start(bf16[1,17,4,128]{3,2,1,0:T(4,128)(2,1)S(1)} %get-tuple-element.86), channel_id=1, source_target_pairs={{0,4},{2,6},{4,0},{6,2},{1,5},{3,7},{5,1},{7,3},{8,12},{10,14},{12... | collective-permute-start | bytes 52232 | tf_op jit(solution)/shard_map/ppermute | solution.py:23
  30.1 0.8 %collective-permute-start.11 = (bf16[1,17,4,128]{3,2,1,0:T(4,128)(2,1)S(1)}, bf16[1,17,4,128]{3,2,1,0:T(4,128)(2,1)S(1)}, u32[]{:S(2)}, u32[]{:S(2)}) collective-permute-start(bf16[1,17,4,128]{3,2,1,0:T(4,128)(2,1)S(1)} %get-tuple-element.88), channel_id=1, source_target_pairs={{0,6},{2,4},{4,2},{6,0},{1,7},{3,5},{5,3},{7,1},{8,14},{10,12},{12... | collective-permute-start | bytes 52232 | tf_op jit(solution)/shard_map/ppermute | solution.py:23
  30.9 0.3 merge.5
  31.2 2.8 %collective-permute-start.12 = (bf16[1,17,4,128]{3,2,1,0:T(4,128)(2,1)S(1)}, bf16[1,17,4,128]{3,2,1,0:T(4,128)(2,1)S(1)}, u32[]{:S(2)}, u32[]{:S(2)}) collective-permute-start(bf16[1,17,4,128]{3,2,1,0:T(4,128)(2,1)S(1)} %merge.5), channel_id=1, source_target_pairs={{0,16},{8,24},{16,0},{24,8},{1,17},{9,25},{17,1},{25,9},{2,18},{10... | collective-permute-start | bytes 52232 | tf_op jit(solution)/shard_map/ppermute | solution.py:23
  33.9 1.9 %collective-permute-done.12.refs_4_ = bf16[1,17,4,128]{3,2,1,0:T(4,128)(2,1)S(1)} collective-permute-done((bf16[1,17,4,128]{3,2,1,0:T(4,128)(2,1)S(1)}, bf16[1,17,4,128]{3,2,1,0:T(4,128)(2,1)S(1)}, u32[]{:S(2)}, u32[]{:S(2)}) %collective-permute-start.12) | collective-permute-done | bytes 17440 | tf_op jit(solution)/shard_map/ppermute | solution.py:23
  35.9 1.0 %last.1 = bf16[4,4,4,128]{3,2,1,0:T(4,128)(2,1)} custom-call(f32[1,17,4,128]{3,2,1,0:T(4,128)S(1)} %get-tuple-element.85.keep_ref, bf16[2,17,4,128]{3,2,1,0:T(4,128)(2,1)S(1)} %collective-permute-done.8.got_ref.refs_0_, bf16[1,17,4,128]{3,2,1,0:T(4,128)(2,1)S(1)} %collective-permute-done.9.refs_1_, ...), custom_call_target="tpu_custom_call" | custom-call | tf_op jit(solution)/shard_map/last/pallas_call | solution.py:602
  (18 shorter events, 0.2 us)
Async XLA Ops:
  0.0 5.2 %collective-permute-start = (bf16[4,4,4,128]{3,2,1,0:T(4,128)(2,1)}, bf16[4,4,4,128]{3,2,1,0:T(4,128)(2,1)S(1)}, u32[]{:S(2)}, u32[]{:S(2)}) collective-permute-start(bf16[4,4,4,128]{3,2,1,0:T(4,128)(2,1)} %query_hbm.1), channel_id=1, source_target_pairs={{0,4},{2,6},{4,0},{6,2},{1,5},{3,7},{5,1},{7,3},{8,12},{10,14},{12... | collective-permute-start | bytes 49160 | tf_op jit(solution)/shard_map/ppermute | solution.py:23
  2.9 3.4 %collective-permute-start.2 = (bf16[4,4,4,128]{3,2,1,0:T(4,128)(2,1)}, bf16[4,4,4,128]{3,2,1,0:T(4,128)(2,1)S(1)}, u32[]{:S(2)}, u32[]{:S(2)}) collective-permute-start(bf16[4,4,4,128]{3,2,1,0:T(4,128)(2,1)} %query_hbm.1), channel_id=1, source_target_pairs={{0,6},{2,4},{4,2},{6,0},{1,7},{3,5},{5,3},{7,1},{8,14},{10,12},{12... | collective-permute-start | bytes 49160 | tf_op jit(solution)/shard_map/ppermute | solution.py:23
  2.9 3.4 %collective-permute-start.1 = (bf16[4,4,4,128]{3,2,1,0:T(4,128)(2,1)}, bf16[4,4,4,128]{3,2,1,0:T(4,128)(2,1)S(1)}, u32[]{:S(2)}, u32[]{:S(2)}) collective-permute-start(bf16[4,4,4,128]{3,2,1,0:T(4,128)(2,1)} %query_hbm.1), channel_id=1, source_target_pairs={{0,2},{2,0},{4,6},{6,4},{1,3},{3,1},{5,7},{7,5},{8,10},{10,8},{12,... | collective-permute-start | bytes 49160 | tf_op jit(solution)/shard_map/ppermute | solution.py:23
  6.4 8.5 %collective-permute-start.5 = (bf16[4,64,128]{2,1,0:T(8,128)(2,1)S(1)}, bf16[4,64,128]{2,1,0:T(8,128)(2,1)S(1)}, u32[]{:S(2)}, u32[]{:S(2)}) collective-permute-start(bf16[4,64,128]{2,1,0:T(8,128)(2,1)S(1)} %bitcast.21), channel_id=1, source_target_pairs={{0,24},{8,16},{16,8},{24,0},{1,25},{9,17},{17,9},{25,1},{2,26},{10... | collective-permute-start | bytes 196616 | tf_op jit(solution)/shard_map/ppermute | solution.py:23
  10.1 5.4 %collective-permute-start.4 = (bf16[4,64,128]{2,1,0:T(8,128)(2,1)S(1)}, bf16[4,64,128]{2,1,0:T(8,128)(2,1)S(1)}, u32[]{:S(2)}, u32[]{:S(2)}) collective-permute-start(bf16[4,64,128]{2,1,0:T(8,128)(2,1)S(1)} %bitcast.22), channel_id=1, source_target_pairs={{0,16},{8,24},{16,0},{24,8},{1,17},{9,25},{17,1},{25,9},{2,18},{10... | collective-permute-start | bytes 196616 | tf_op jit(solution)/shard_map/ppermute | solution.py:23
  10.1 5.4 %collective-permute-start.3 = (bf16[4,64,128]{2,1,0:T(8,128)(2,1)S(1)}, bf16[4,64,128]{2,1,0:T(8,128)(2,1)S(1)}, u32[]{:S(2)}, u32[]{:S(2)}) collective-permute-start(bf16[4,64,128]{2,1,0:T(8,128)(2,1)S(1)} %bitcast.23), channel_id=1, source_target_pairs={{0,8},{8,0},{16,24},{24,16},{1,9},{9,1},{17,25},{25,17},{2,10},{10... | collective-permute-start | bytes 196616 | tf_op jit(solution)/shard_map/ppermute | solution.py:23
  15.5 2.9 %copy-start = (s32[4,128]{1,0:T(4,128)S(1)}, s32[4,128]{1,0:T(4,128)}, u32[]{:S(2)}) copy-start(s32[4,128]{1,0:T(4,128)} %param.8) | copy-start | bytes 6148
  15.5 2.9 %copy-start.1 = (s32[4]{0:T(128)S(1)}, s32[4]{0:T(128)}, u32[]{:S(2)}) copy-start(s32[4]{0:T(128)} %len_ref.3) | copy-start | bytes 52
  18.3 2.9 %collective-permute-start.6 = (bf16[3,17,8,128]{3,2,1,0:T(8,128)(2,1)S(1)}, bf16[3,17,8,128]{3,2,1,0:T(8,128)(2,1)S(1)}, u32[]{:S(2)}, u32[]{:S(2)}) collective-permute-start(bf16[3,17,8,128]{3,2,1,0:T(8,128)(2,1)S(1)} %get-tuple-element.59), channel_id=1, source_target_pairs={{0,2},{2,0},{4,6},{6,4},{1,3},{3,1},{5,7},{7,5},{8,10},{10,8},{12,... | collective-permute-start | bytes 313352 | tf_op jit(solution)/shard_map/ppermute | solution.py:23
  21.6 4.3 %collective-permute-start.7 = (bf16[3,17,4,128]{3,2,1,0:T(4,128)(2,1)S(1)}, bf16[3,17,4,128]{3,2,1,0:T(4,128)(2,1)S(1)}, u32[]{:S(2)}, u32[]{:S(2)}) collective-permute-start(bf16[3,17,4,128]{3,2,1,0:T(4,128)(2,1)S(1)} %get-tuple-element.67), channel_id=1, source_target_pairs={{0,4},{2,6},{4,0},{6,2},{1,5},{3,7},{5,1},{7,3},{8,12},{10,14},{12... | collective-permute-start | bytes 156680 | tf_op jit(solution)/shard_map/ppermute | solution.py:23
  26.2 4.7 %collective-permute-start.8 = (bf16[2,17,4,128]{3,2,1,0:T(4,128)(2,1)S(1)}, bf16[2,17,4,128]{3,2,1,0:T(4,128)(2,1)S(1)}, u32[]{:S(2)}, u32[]{:S(2)}) collective-permute-start(bf16[2,17,4,128]{3,2,1,0:T(4,128)(2,1)S(1)} %get-tuple-element.76), channel_id=1, source_target_pairs={{0,8},{8,0},{16,24},{24,16},{1,9},{9,1},{17,25},{25,17},{2,10},{10... | collective-permute-start | bytes 104456 | tf_op jit(solution)/shard_map/ppermute | solution.py:23
  28.7 5.2 %collective-permute-start.9 = (bf16[1,17,4,128]{3,2,1,0:T(4,128)(2,1)S(1)}, bf16[1,17,4,128]{3,2,1,0:T(4,128)(2,1)S(1)}, u32[]{:S(2)}, u32[]{:S(2)}) collective-permute-start(bf16[1,17,4,128]{3,2,1,0:T(4,128)(2,1)S(1)} %get-tuple-element.86), channel_id=1, source_target_pairs={{0,4},{2,6},{4,0},{6,2},{1,5},{3,7},{5,1},{7,3},{8,12},{10,14},{12... | collective-permute-start | bytes 52232 | tf_op jit(solution)/shard_map/ppermute | solution.py:23
  30.1 3.8 %collective-permute-start.10 = (bf16[1,17,4,128]{3,2,1,0:T(4,128)(2,1)S(1)}, bf16[1,17,4,128]{3,2,1,0:T(4,128)(2,1)S(1)}, u32[]{:S(2)}, u32[]{:S(2)}) collective-permute-start(bf16[1,17,4,128]{3,2,1,0:T(4,128)(2,1)S(1)} %get-tuple-element.87), channel_id=1, source_target_pairs={{0,2},{2,0},{4,6},{6,4},{1,3},{3,1},{5,7},{7,5},{8,10},{10,8},{12,... | collective-permute-start | bytes 52232 | tf_op jit(solution)/shard_map/ppermute | solution.py:23
  30.1 3.8 %collective-permute-start.11 = (bf16[1,17,4,128]{3,2,1,0:T(4,128)(2,1)S(1)}, bf16[1,17,4,128]{3,2,1,0:T(4,128)(2,1)S(1)}, u32[]{:S(2)}, u32[]{:S(2)}) collective-permute-start(bf16[1,17,4,128]{3,2,1,0:T(4,128)(2,1)S(1)} %get-tuple-element.88), channel_id=1, source_target_pairs={{0,6},{2,4},{4,2},{6,0},{1,7},{3,5},{5,3},{7,1},{8,14},{10,12},{12... | collective-permute-start | bytes 52232 | tf_op jit(solution)/shard_map/ppermute | solution.py:23
  31.2 4.7 %collective-permute-start.12 = (bf16[1,17,4,128]{3,2,1,0:T(4,128)(2,1)S(1)}, bf16[1,17,4,128]{3,2,1,0:T(4,128)(2,1)S(1)}, u32[]{:S(2)}, u32[]{:S(2)}) collective-permute-start(bf16[1,17,4,128]{3,2,1,0:T(4,128)(2,1)S(1)} %merge.5), channel_id=1, source_target_pairs={{0,16},{8,24},{16,0},{24,8},{1,17},{9,25},{17,1},{25,9},{2,18},{10... | collective-permute-start | bytes 52232 | tf_op jit(solution)/shard_map/ppermute | solution.py:23

commit v14 on v13

--- a/solution.py
+++ b/solution.py
@@ -281,7 +281,7 @@
 
 def fresh_kernel(dims, pieces, n_req, slots_ref, counts_ref, kf, vf, *refs):
     heads, page_rows, slots, sub = dims
-    q_refs, refs = refs[:n_req], list(refs[n_req:])
+    q_refs, refs = refs[:1] + refs[1:n_req][::-1], list(refs[n_req:])
     req_dev = q_refs[0].shape[0]
     pool = [refs.pop(0)] if pieces else []
     keep_ref, send_ref, acc_ref, top_ref, tot_ref, *refs = refs
@@ -510,7 +510,7 @@
             flops=4 * n_reqs * rows * slots * page_rows * LANES,
             transcendentals=n_reqs * sub * slots * page_rows, bytes_accessed=2 * fresh_kv.size),
         name="fresh",
-    )(slot_table, counts, kf, vf, queries, *far, *value_in)
+    )(slot_table, counts, kf, vf, queries, *far[::-1], *value_in)
 
     def merge(keep, got, skip, goals, shapes):
         return pl.pallas_call(

time: 37 us -> 37.6 us (1.016)
  waiting for transfers between devices: 3.75 us -> 5.76 us
  starting transfers between devices: 14.9 us -> 13.5 us
    ppermute x13, waiting for transfers between devices: 3.75 us -> 5.76 us  [swap(): lax.ppermute(value, axis, [(n, n ^ bit) for n in range(lax.axis_size(axis...]
    ppermute x13, starting transfers between devices: 14.9 us -> 13.5 us  [swap(): lax.ppermute(value, axis, [(n, n ^ bit) for n in range(lax.axis_size(axis...]
  transfers between devices with their start and end apart: 13 -> 13, of which waited for: 5 -> 5; matrix products, arithmetic and copies ran while one was open for 0% -> 0% of each run, Pallas kernels for 37% -> 36%
where the time goes in v14:
time: 37.6 us; the launch traced here: 37.4 us
  Pallas kernels  18 us (48%)
  starting transfers between devices  13.5 us (36%)
  waiting for transfers between devices  5.76 us (15%)
    ppermute x13, starting transfers between devices, swap(): lax.ppermute(value, axis, [(n, n ^ bit) for n in range(lax.axis_size(axis...  13.5 us
    ppermute x13, waiting for transfers between devices, swap(): lax.ppermute(value, axis, [(n, n ^ bit) for n in range(lax.axis_size(axis...  5.76 us
    pallas_call x1, Pallas kernels, local(): pl.pallas_call(functools.partial(stage_keys_kernel, n_ctx, slots), out_sh...  4.08 us
    pallas_call x1, Pallas kernels, local(): pl.pallas_call(functools.partial(middle_kernel, dims), out_shape=(f32(par...  2.84 us
    pallas_call x1, Pallas kernels, local(): pl.pallas_call(functools.partial(first_kernel, dims, pieces), out_shape=(...  2.83 us
    pallas_call x1, Pallas kernels, local(): pl.pallas_call(functools.partial(fresh_kernel, (heads, page_rows, slots,...  2.81 us
    pallas_call x1, Pallas kernels, local(): pl.pallas_call(stage_fresh_kernel, out_shape=(bf16(*query.shape), half(ne...  2.08 us
    pallas_call x1, Pallas kernels, local(): pl.pallas_call(functools.partial(second_kernel, dims, len(vbs)), out_shap...  1.48 us
  transfers between devices with their start and end apart: 13, of which 5 were waited for; matrix products, arithmetic and copies ran while one was open for 0% of the time, Pallas kernels for 36%

profile of v14, /device:TPU:0, one launch (start us, length us, event | category | flops | bytes accessed | tf_op | source)
XLA Modules:
  0.0 37.4 jit_solution(5737361389060809118)
XLA Ops:
  0.0 2.9 %collective-permute-start = (bf16[4,4,4,128]{3,2,1,0:T(4,128)(2,1)}, bf16[4,4,4,128]{3,2,1,0:T(4,128)(2,1)S(1)}, u32[]{:S(2)}, u32[]{:S(2)}) collective-permute-start(bf16[4,4,4,128]{3,2,1,0:T(4,128)(2,1)} %query_hbm.1), channel_id=1, source_target_pairs={{0,4},{2,6},{4,0},{6,2},{1,5},{3,7},{5,1},{7,3},{8,12},{10,14},{12... | collective-permute-start | bytes 49160 | tf_op jit(solution)/shard_map/ppermute | solution.py:23
  2.9 0.1 collective-permute-start.1
  3.1 2.1 %stage_fresh.1 = (bf16[4,4,4,128]{3,2,1,0:T(4,128)(2,1)S(1)}, bf16[112,16,4,128]{3,2,1,0:T(4,128)(2,1)S(1)}, bf16[112,16,4,128]{3,2,1,0:T(4,128)(2,1)S(1)}) custom-call(bf16[4,4,4,128]{3,2,1,0:T(4,128)(2,1)} %query_hbm.1, bf16[112,16,4,256]{3,2,1,0:T(4,128)(2,1)} %fresh_ref.1), custom_call_target="tpu_custom_call" | custom-call | bytes 7340032 | tf_op jit(solution)/shard_map/stage_fresh/pallas_call | solution.py:448
  5.2 1.1 %collective-permute-done.2 = bf16[4,4,4,128]{3,2,1,0:T(4,128)(2,1)S(1)} collective-permute-done((bf16[4,4,4,128]{3,2,1,0:T(4,128)(2,1)}, bf16[4,4,4,128]{3,2,1,0:T(4,128)(2,1)S(1)}, u32[]{:S(2)}, u32[]{:S(2)}) %collective-permute-start.2) | collective-permute-done | bytes 16416 | tf_op jit(solution)/shard_map/ppermute | solution.py:23
  6.4 1.6 %collective-permute-start.5 = (bf16[4,64,128]{2,1,0:T(8,128)(2,1)S(1)}, bf16[4,64,128]{2,1,0:T(8,128)(2,1)S(1)}, u32[]{:S(2)}, u32[]{:S(2)}) collective-permute-start(bf16[4,64,128]{2,1,0:T(8,128)(2,1)S(1)} %bitcast.21), channel_id=1, source_target_pairs={{0,8},{8,0},{16,24},{24,16},{1,9},{9,1},{17,25},{25,17},{2,10},{10... | collective-permute-start | bytes 196616 | tf_op jit(solution)/shard_map/ppermute | solution.py:23
  8.1 2.6 %collective-permute-start.4 = (bf16[4,64,128]{2,1,0:T(8,128)(2,1)S(1)}, bf16[4,64,128]{2,1,0:T(8,128)(2,1)S(1)}, u32[]{:S(2)}, u32[]{:S(2)}) collective-permute-start(bf16[4,64,128]{2,1,0:T(8,128)(2,1)S(1)} %bitcast.22), channel_id=1, source_target_pairs={{0,16},{8,24},{16,0},{24,8},{1,17},{9,25},{17,1},{25,9},{2,18},{10... | collective-permute-start | bytes 196616 | tf_op jit(solution)/shard_map/ppermute | solution.py:23
  10.6 0.2 collective-permute-start.3
  10.9 4.1 %stage_keys.1 = (bf16[512,16,4,128]{3,2,1,0:T(4,128)(2,1)S(1)}, s32[128]{0:T(128)S(1)}, s32[16]{0:T(128)S(1)}) custom-call(s32[112]{0:T(128)} %bucket_hbm.1, bf16[512,16,4,256]{3,2,1,0:T(4,128)(2,1)} %refs_0_.1), custom_call_target="tpu_custom_call" | custom-call | bytes 16777216 | tf_op jit(solution)/shard_map/stage_keys/pallas_call | solution.py:460
  15.0 1.7 %collective-permute-done.3.refs_1_ = bf16[4,64,128]{2,1,0:T(8,128)(2,1)S(1)} collective-permute-done((bf16[4,64,128]{2,1,0:T(8,128)(2,1)S(1)}, bf16[4,64,128]{2,1,0:T(8,128)(2,1)S(1)}, u32[]{:S(2)}, u32[]{:S(2)}) %collective-permute-start.3) | collective-permute-done | bytes 65568 | tf_op jit(solution)/shard_map/ppermute | solution.py:23
  16.7 2.8 %fresh.1 = (f32[3,17,8,128]{3,2,1,0:T(8,128)S(1)}, bf16[3,17,8,128]{3,2,1,0:T(8,128)(2,1)S(1)}, f32[4,64,128]{2,1,0:T(8,128)S(1)}, f32[4,16,128]{2,1,0:T(8,128)S...) custom-call(s32[128]{0:T(128)S(1)} %get-tuple-element.48.slots_ref, ...), custom_call_target="tpu_custom_call" | custom-call | flops 268435456 | bytes 3670016 | tf_op jit(solution)/shard_map/fresh/pallas_call | solution.py:496
  19.6 2.8 %first.1 = (f32[2,16,8192]{2,1,0:T(8,128)S(1)}, f32[2,16,128]{2,1,0:T(8,128)S(1)}, bf16[512,8,4,128]{3,2,1,0:T(4,128)(2,1)S(1)}) custom-call(s32[512]{0:T(512)S(1)} %bitcast.27, s32[4]{0:T(128)S(1)} %copy-done.1, bf16[4,64,128]{2,1,0:T(8,128)(2,1)S(1)} %bitcast.25, bf16[512,64,128]{2,1,0:T(8,128)(2,1)S(1)} %bitcast.13, bf16[512,16,4,256]{3,2,1,0:T(4,128)(2,1)} %refs_0_.1), custom_call_target="tpu_custom_call" | custom-call | flops 268435456 | bytes 4194304 | tf_op jit(solution)/shard_map/first/pallas_call | solution.py:549
  22.5 0.3 merge.3
  22.8 1.1 %collective-permute-start.7 = (bf16[3,17,4,128]{3,2,1,0:T(4,128)(2,1)S(1)}, bf16[3,17,4,128]{3,2,1,0:T(4,128)(2,1)S(1)}, u32[]{:S(2)}, u32[]{:S(2)}) collective-permute-start(bf16[3,17,4,128]{3,2,1,0:T(4,128)(2,1)S(1)} %get-tuple-element.67), channel_id=1, source_target_pairs={{0,4},{2,6},{4,0},{6,2},{1,5},{3,7},{5,1},{7,3},{8,12},{10,14},{12... | collective-permute-start | bytes 156680 | tf_op jit(solution)/shard_map/ppermute | solution.py:23
  23.8 2.8 %middle.1 = (f32[2,16,8192]{2,1,0:T(8,128)S(1)}, f32[2,16,128]{2,1,0:T(8,128)S(1)}, f32[2,64,128]{2,1,0:T(8,128)S(1)}, f32[2,16,128]{2,1,0:T(8,128)S(1)}) custom-call(s32[512]{0:T(512)S(1)} %bitcast.28, s32[4]{0:T(128)S(1)} %copy-done.1, bf16[4,64,128]{2,1,0:T(8,128)(2,1)S(1)} %bitcast.26, bf16[512,64,128]{2,1,0:T(8,128)(2,1)S(1)} %bitcast.14, ...), custom_call_target="tpu_custom_call" | custom-call | flops 536870912 | bytes 8388608 | tf_op jit(solution)/shard_map/middle/pallas_call | solution.py:565
  26.7 0.4 collective-permute-done.7.got_ref
  27.0 0.3 merge.4
  27.4 0.4 %collective-permute-start.8 = (bf16[2,17,4,128]{3,2,1,0:T(4,128)(2,1)S(1)}, bf16[2,17,4,128]{3,2,1,0:T(4,128)(2,1)S(1)}, u32[]{:S(2)}, u32[]{:S(2)}) collective-permute-start(bf16[2,17,4,128]{3,2,1,0:T(4,128)(2,1)S(1)} %get-tuple-element.76), channel_id=1, source_target_pairs={{0,8},{8,0},{16,24},{24,16},{1,9},{9,1},{17,25},{25,17},{2,10},{10... | collective-permute-start | bytes 104456 | tf_op jit(solution)/shard_map/ppermute | solution.py:23
  27.8 1.5 %second.1 = (f32[1,17,4,128]{3,2,1,0:T(4,128)S(1)}, bf16[1,17,4,128]{3,2,1,0:T(4,128)(2,1)S(1)}, bf16[1,17,4,128]{3,2,1,0:T(4,128)(2,1)S(1)}, bf16[1,17,4,128]{3,2,1,0:T(4,128)(2,1)S(1)}) custom-call(s32[512]{0:T(512)S(1)} %bitcast.29, f32[2,16,8192]{2,1,0:T(8,128)S(1)} %get-tuple-element.77.t_ref, f32[2,16,128]{2,1,0:T(8,128)S(1)} %get-tuple-element.78.top_ref, ...), custom_call_target="tpu_custom_call" | custom-call | flops 268435456 | bytes 4194304 | tf_op jit(solution)/shard_map/second/pallas_call | solution.py:582
  29.3 1.4 %collective-permute-start.9 = (bf16[1,17,4,128]{3,2,1,0:T(4,128)(2,1)S(1)}, bf16[1,17,4,128]{3,2,1,0:T(4,128)(2,1)S(1)}, u32[]{:S(2)}, u32[]{:S(2)}) collective-permute-start(bf16[1,17,4,128]{3,2,1,0:T(4,128)(2,1)S(1)} %get-tuple-element.86), channel_id=1, source_target_pairs={{0,4},{2,6},{4,0},{6,2},{1,5},{3,7},{5,1},{7,3},{8,12},{10,14},{12... | collective-permute-start | bytes 52232 | tf_op jit(solution)/shard_map/ppermute | solution.py:23
  30.7 0.8 %collective-permute-start.11 = (bf16[1,17,4,128]{3,2,1,0:T(4,128)(2,1)S(1)}, bf16[1,17,4,128]{3,2,1,0:T(4,128)(2,1)S(1)}, u32[]{:S(2)}, u32[]{:S(2)}) collective-permute-start(bf16[1,17,4,128]{3,2,1,0:T(4,128)(2,1)S(1)} %get-tuple-element.88), channel_id=1, source_target_pairs={{0,6},{2,4},{4,2},{6,0},{1,7},{3,5},{5,3},{7,1},{8,14},{10,12},{12... | collective-permute-start | bytes 52232 | tf_op jit(solution)/shard_map/ppermute | solution.py:23
  31.5 0.3 merge.5
  31.7 2.2 %collective-permute-start.12 = (bf16[1,17,4,128]{3,2,1,0:T(4,128)(2,1)S(1)}, bf16[1,17,4,128]{3,2,1,0:T(4,128)(2,1)S(1)}, u32[]{:S(2)}, u32[]{:S(2)}) collective-permute-start(bf16[1,17,4,128]{3,2,1,0:T(4,128)(2,1)S(1)} %merge.5), channel_id=1, source_target_pairs={{0,16},{8,24},{16,0},{24,8},{1,17},{9,25},{17,1},{25,9},{2,18},{10... | collective-permute-start | bytes 52232 | tf_op jit(solution)/shard_map/ppermute | solution.py:23
  33.9 2.5 %collective-permute-done.12.refs_4_ = bf16[1,17,4,128]{3,2,1,0:T(4,128)(2,1)S(1)} collective-permute-done((bf16[1,17,4,128]{3,2,1,0:T(4,128)(2,1)S(1)}, bf16[1,17,4,128]{3,2,1,0:T(4,128)(2,1)S(1)}, u32[]{:S(2)}, u32[]{:S(2)}) %collective-permute-start.12) | collective-permute-done | bytes 17440 | tf_op jit(solution)/shard_map/ppermute | solution.py:23
  36.4 1.0 %last.1 = bf16[4,4,4,128]{3,2,1,0:T(4,128)(2,1)} custom-call(f32[1,17,4,128]{3,2,1,0:T(4,128)S(1)} %get-tuple-element.85.keep_ref, bf16[2,17,4,128]{3,2,1,0:T(4,128)(2,1)S(1)} %collective-permute-done.8.got_ref.refs_0_, bf16[1,17,4,128]{3,2,1,0:T(4,128)(2,1)S(1)} %collective-permute-done.9.refs_1_, ...), custom_call_target="tpu_custom_call" | custom-call | tf_op jit(solution)/shard_map/last/pallas_call | solution.py:602
  (18 shorter events, 0.3 us)
Async XLA Ops:
  0.0 5.2 %collective-permute-start = (bf16[4,4,4,128]{3,2,1,0:T(4,128)(2,1)}, bf16[4,4,4,128]{3,2,1,0:T(4,128)(2,1)S(1)}, u32[]{:S(2)}, u32[]{:S(2)}) collective-permute-start(bf16[4,4,4,128]{3,2,1,0:T(4,128)(2,1)} %query_hbm.1), channel_id=1, source_target_pairs={{0,4},{2,6},{4,0},{6,2},{1,5},{3,7},{5,1},{7,3},{8,12},{10,14},{12... | collective-permute-start | bytes 49160 | tf_op jit(solution)/shard_map/ppermute | solution.py:23
  2.9 3.4 %collective-permute-start.2 = (bf16[4,4,4,128]{3,2,1,0:T(4,128)(2,1)}, bf16[4,4,4,128]{3,2,1,0:T(4,128)(2,1)S(1)}, u32[]{:S(2)}, u32[]{:S(2)}) collective-permute-start(bf16[4,4,4,128]{3,2,1,0:T(4,128)(2,1)} %query_hbm.1), channel_id=1, source_target_pairs={{0,6},{2,4},{4,2},{6,0},{1,7},{3,5},{5,3},{7,1},{8,14},{10,12},{12... | collective-permute-start | bytes 49160 | tf_op jit(solution)/shard_map/ppermute | solution.py:23
  2.9 3.4 %collective-permute-start.1 = (bf16[4,4,4,128]{3,2,1,0:T(4,128)(2,1)}, bf16[4,4,4,128]{3,2,1,0:T(4,128)(2,1)S(1)}, u32[]{:S(2)}, u32[]{:S(2)}) collective-permute-start(bf16[4,4,4,128]{3,2,1,0:T(4,128)(2,1)} %query_hbm.1), channel_id=1, source_target_pairs={{0,2},{2,0},{4,6},{6,4},{1,3},{3,1},{5,7},{7,5},{8,10},{10,8},{12,... | collective-permute-start | bytes 49160 | tf_op jit(solution)/shard_map/ppermute | solution.py:23
  6.4 8.5 %collective-permute-start.5 = (bf16[4,64,128]{2,1,0:T(8,128)(2,1)S(1)}, bf16[4,64,128]{2,1,0:T(8,128)(2,1)S(1)}, u32[]{:S(2)}, u32[]{:S(2)}) collective-permute-start(bf16[4,64,128]{2,1,0:T(8,128)(2,1)S(1)} %bitcast.21), channel_id=1, source_target_pairs={{0,8},{8,0},{16,24},{24,16},{1,9},{9,1},{17,25},{25,17},{2,10},{10... | collective-permute-start | bytes 196616 | tf_op jit(solution)/shard_map/ppermute | solution.py:23
  8.1 7.0 %collective-permute-start.4 = (bf16[4,64,128]{2,1,0:T(8,128)(2,1)S(1)}, bf16[4,64,128]{2,1,0:T(8,128)(2,1)S(1)}, u32[]{:S(2)}, u32[]{:S(2)}) collective-permute-start(bf16[4,64,128]{2,1,0:T(8,128)(2,1)S(1)} %bitcast.22), channel_id=1, source_target_pairs={{0,16},{8,24},{16,0},{24,8},{1,17},{9,25},{17,1},{25,9},{2,18},{10... | collective-permute-start | bytes 196616 | tf_op jit(solution)/shard_map/ppermute | solution.py:23
  10.6 6.1 %collective-permute-start.3 = (bf16[4,64,128]{2,1,0:T(8,128)(2,1)S(1)}, bf16[4,64,128]{2,1,0:T(8,128)(2,1)S(1)}, u32[]{:S(2)}, u32[]{:S(2)}) collective-permute-start(bf16[4,64,128]{2,1,0:T(8,128)(2,1)S(1)} %bitcast.23), channel_id=1, source_target_pairs={{0,24},{8,16},{16,8},{24,0},{1,25},{9,17},{17,9},{25,1},{2,26},{10... | collective-permute-start | bytes 196616 | tf_op jit(solution)/shard_map/ppermute | solution.py:23
  16.7 2.9 %copy-start = (s32[4,128]{1,0:T(4,128)S(1)}, s32[4,128]{1,0:T(4,128)}, u32[]{:S(2)}) copy-start(s32[4,128]{1,0:T(4,128)} %param.8) | copy-start | bytes 6148
  16.7 2.9 %copy-start.1 = (s32[4]{0:T(128)S(1)}, s32[4]{0:T(128)}, u32[]{:S(2)}) copy-start(s32[4]{0:T(128)} %len_ref.3) | copy-start | bytes 52
  19.5 2.9 %collective-permute-start.6 = (bf16[3,17,8,128]{3,2,1,0:T(8,128)(2,1)S(1)}, bf16[3,17,8,128]{3,2,1,0:T(8,128)(2,1)S(1)}, u32[]{:S(2)}, u32[]{:S(2)}) collective-permute-start(bf16[3,17,8,128]{3,2,1,0:T(8,128)(2,1)S(1)} %get-tuple-element.59), channel_id=1, source_target_pairs={{0,2},{2,0},{4,6},{6,4},{1,3},{3,1},{5,7},{7,5},{8,10},{10,8},{12,... | collective-permute-start | bytes 313352 | tf_op jit(solution)/shard_map/ppermute | solution.py:23
  22.8 4.3 %collective-permute-start.7 = (bf16[3,17,4,128]{3,2,1,0:T(4,128)(2,1)S(1)}, bf16[3,17,4,128]{3,2,1,0:T(4,128)(2,1)S(1)}, u32[]{:S(2)}, u32[]{:S(2)}) collective-permute-start(bf16[3,17,4,128]{3,2,1,0:T(4,128)(2,1)S(1)} %get-tuple-element.67), channel_id=1, source_target_pairs={{0,4},{2,6},{4,0},{6,2},{1,5},{3,7},{5,1},{7,3},{8,12},{10,14},{12... | collective-permute-start | bytes 156680 | tf_op jit(solution)/shard_map/ppermute | solution.py:23
  27.4 4.1 %collective-permute-start.8 = (bf16[2,17,4,128]{3,2,1,0:T(4,128)(2,1)S(1)}, bf16[2,17,4,128]{3,2,1,0:T(4,128)(2,1)S(1)}, u32[]{:S(2)}, u32[]{:S(2)}) collective-permute-start(bf16[2,17,4,128]{3,2,1,0:T(4,128)(2,1)S(1)} %get-tuple-element.76), channel_id=1, source_target_pairs={{0,8},{8,0},{16,24},{24,16},{1,9},{9,1},{17,25},{25,17},{2,10},{10... | collective-permute-start | bytes 104456 | tf_op jit(solution)/shard_map/ppermute | solution.py:23
  29.3 4.7 %collective-permute-start.9 = (bf16[1,17,4,128]{3,2,1,0:T(4,128)(2,1)S(1)}, bf16[1,17,4,128]{3,2,1,0:T(4,128)(2,1)S(1)}, u32[]{:S(2)}, u32[]{:S(2)}) collective-permute-start(bf16[1,17,4,128]{3,2,1,0:T(4,128)(2,1)S(1)} %get-tuple-element.86), channel_id=1, source_target_pairs={{0,4},{2,6},{4,0},{6,2},{1,5},{3,7},{5,1},{7,3},{8,12},{10,14},{12... | collective-permute-start | bytes 52232 | tf_op jit(solution)/shard_map/ppermute | solution.py:23
  30.7 3.3 %collective-permute-start.10 = (bf16[1,17,4,128]{3,2,1,0:T(4,128)(2,1)S(1)}, bf16[1,17,4,128]{3,2,1,0:T(4,128)(2,1)S(1)}, u32[]{:S(2)}, u32[]{:S(2)}) collective-permute-start(bf16[1,17,4,128]{3,2,1,0:T(4,128)(2,1)S(1)} %get-tuple-element.87), channel_id=1, source_target_pairs={{0,2},{2,0},{4,6},{6,4},{1,3},{3,1},{5,7},{7,5},{8,10},{10,8},{12,... | collective-permute-start | bytes 52232 | tf_op jit(solution)/shard_map/ppermute | solution.py:23
  30.7 3.3 %collective-permute-start.11 = (bf16[1,17,4,128]{3,2,1,0:T(4,128)(2,1)S(1)}, bf16[1,17,4,128]{3,2,1,0:T(4,128)(2,1)S(1)}, u32[]{:S(2)}, u32[]{:S(2)}) collective-permute-start(bf16[1,17,4,128]{3,2,1,0:T(4,128)(2,1)S(1)} %get-tuple-element.88), channel_id=1, source_target_pairs={{0,6},{2,4},{4,2},{6,0},{1,7},{3,5},{5,3},{7,1},{8,14},{10,12},{12... | collective-permute-start | bytes 52232 | tf_op jit(solution)/shard_map/ppermute | solution.py:23
  31.7 4.7 %collective-permute-start.12 = (bf16[1,17,4,128]{3,2,1,0:T(4,128)(2,1)S(1)}, bf16[1,17,4,128]{3,2,1,0:T(4,128)(2,1)S(1)}, u32[]{:S(2)}, u32[]{:S(2)}) collective-permute-start(bf16[1,17,4,128]{3,2,1,0:T(4,128)(2,1)S(1)} %merge.5), channel_id=1, source_target_pairs={{0,16},{8,24},{16,0},{24,8},{1,17},{9,25},{17,1},{25,9},{2,18},{10... | collective-permute-start | bytes 52232 | tf_op jit(solution)/shard_map/ppermute | solution.py:23

commit v15 on v13

--- a/solution.py
+++ b/solution.py
@@ -13,7 +13,7 @@
 LANES = 128
 SCALE = math.log2(math.e) / math.sqrt(LANES)
 SCORE_WIDE = 256
-VALUE_WIDE = 512
+VALUE_WIDE = 1024
 VMEM = pl.BlockSpec(memory_space=pltpu.VMEM)
 SMEM = pl.BlockSpec(memory_space=pltpu.SMEM)
 HBM = pl.BlockSpec(memory_space=pltpu.HBM)

time: 37 us -> 37 us (level)
  no operation moved by 1% of the time
where the time goes in v15:
time: 37 us; the launch traced here: 36.8 us
  Pallas kernels  18 us (49%)
  starting transfers between devices  14.9 us (40%)
  waiting for transfers between devices  3.76 us (10%)
    ppermute x13, starting transfers between devices, swap(): lax.ppermute(value, axis, [(n, n ^ bit) for n in range(lax.axis_size(axis...  14.9 us
    pallas_call x1, Pallas kernels, local(): pl.pallas_call(functools.partial(stage_keys_kernel, n_ctx, slots), out_sh...  4.08 us
    ppermute x13, waiting for transfers between devices, swap(): lax.ppermute(value, axis, [(n, n ^ bit) for n in range(lax.axis_size(axis...  3.76 us
    pallas_call x1, Pallas kernels, local(): pl.pallas_call(functools.partial(first_kernel, dims, pieces), out_shape=(...  2.83 us
    pallas_call x1, Pallas kernels, local(): pl.pallas_call(functools.partial(middle_kernel, dims), out_shape=(f32(par...  2.83 us
    pallas_call x1, Pallas kernels, local(): pl.pallas_call(functools.partial(fresh_kernel, (heads, page_rows, slots,...  2.81 us
    pallas_call x1, Pallas kernels, local(): pl.pallas_call(stage_fresh_kernel, out_shape=(bf16(*query.shape), half(ne...  2.08 us
    pallas_call x1, Pallas kernels, local(): pl.pallas_call(functools.partial(second_kernel, dims, len(vbs)), out_shap...  1.47 us
  transfers between devices with their start and end apart: 13, of which 5 were waited for; matrix products, arithmetic and copies ran while one was open for 0% of the time, Pallas kernels for 37%

profile of v15, /device:TPU:0, one launch (start us, length us, event | category | flops | bytes accessed | tf_op | source)
XLA Modules:
  0.0 36.8 jit_solution(6940086143875585553)
XLA Ops:
  0.0 2.9 %collective-permute-start = (bf16[4,4,4,128]{3,2,1,0:T(4,128)(2,1)}, bf16[4,4,4,128]{3,2,1,0:T(4,128)(2,1)S(1)}, u32[]{:S(2)}, u32[]{:S(2)}) collective-permute-start(bf16[4,4,4,128]{3,2,1,0:T(4,128)(2,1)} %query_hbm.1), channel_id=1, source_target_pairs={{0,4},{2,6},{4,0},{6,2},{1,5},{3,7},{5,1},{7,3},{8,12},{10,14},{12... | collective-permute-start | bytes 49160 | tf_op jit(solution)/shard_map/ppermute | solution.py:23
  2.9 0.1 collective-permute-start.1
  3.1 2.1 %stage_fresh.1 = (bf16[4,4,4,128]{3,2,1,0:T(4,128)(2,1)S(1)}, bf16[112,16,4,128]{3,2,1,0:T(4,128)(2,1)S(1)}, bf16[112,16,4,128]{3,2,1,0:T(4,128)(2,1)S(1)}) custom-call(bf16[4,4,4,128]{3,2,1,0:T(4,128)(2,1)} %query_hbm.1, bf16[112,16,4,256]{3,2,1,0:T(4,128)(2,1)} %fresh_ref.1), custom_call_target="tpu_custom_call" | custom-call | bytes 7340032 | tf_op jit(solution)/shard_map/stage_fresh/pallas_call | solution.py:448
  5.2 1.1 %collective-permute-done.2 = bf16[4,4,4,128]{3,2,1,0:T(4,128)(2,1)S(1)} collective-permute-done((bf16[4,4,4,128]{3,2,1,0:T(4,128)(2,1)}, bf16[4,4,4,128]{3,2,1,0:T(4,128)(2,1)S(1)}, u32[]{:S(2)}, u32[]{:S(2)}) %collective-permute-start.2) | collective-permute-done | bytes 16416 | tf_op jit(solution)/shard_map/ppermute | solution.py:23
  6.4 3.7 %collective-permute-start.5 = (bf16[4,64,128]{2,1,0:T(8,128)(2,1)S(1)}, bf16[4,64,128]{2,1,0:T(8,128)(2,1)S(1)}, u32[]{:S(2)}, u32[]{:S(2)}) collective-permute-start(bf16[4,64,128]{2,1,0:T(8,128)(2,1)S(1)} %bitcast.21), channel_id=1, source_target_pairs={{0,24},{8,16},{16,8},{24,0},{1,25},{9,17},{17,9},{25,1},{2,26},{10... | collective-permute-start | bytes 196616 | tf_op jit(solution)/shard_map/ppermute | solution.py:23
  10.1 0.8 %collective-permute-start.3 = (bf16[4,64,128]{2,1,0:T(8,128)(2,1)S(1)}, bf16[4,64,128]{2,1,0:T(8,128)(2,1)S(1)}, u32[]{:S(2)}, u32[]{:S(2)}) collective-permute-start(bf16[4,64,128]{2,1,0:T(8,128)(2,1)S(1)} %bitcast.23), channel_id=1, source_target_pairs={{0,8},{8,0},{16,24},{24,16},{1,9},{9,1},{17,25},{25,17},{2,10},{10... | collective-permute-start | bytes 196616 | tf_op jit(solution)/shard_map/ppermute | solution.py:23
  10.9 4.1 %stage_keys.1 = (bf16[512,16,4,128]{3,2,1,0:T(4,128)(2,1)S(1)}, s32[128]{0:T(128)S(1)}, s32[16]{0:T(128)S(1)}) custom-call(s32[112]{0:T(128)} %bucket_hbm.1, bf16[512,16,4,256]{3,2,1,0:T(4,128)(2,1)} %refs_0_.1), custom_call_target="tpu_custom_call" | custom-call | bytes 16777216 | tf_op jit(solution)/shard_map/stage_keys/pallas_call | solution.py:460
  15.0 0.5 %collective-permute-done.4.refs_2_ = bf16[4,64,128]{2,1,0:T(8,128)(2,1)S(1)} collective-permute-done((bf16[4,64,128]{2,1,0:T(8,128)(2,1)S(1)}, bf16[4,64,128]{2,1,0:T(8,128)(2,1)S(1)}, u32[]{:S(2)}, u32[]{:S(2)}) %collective-permute-start.4) | collective-permute-done | bytes 65568 | tf_op jit(solution)/shard_map/ppermute | solution.py:23
  15.5 2.8 %fresh.1 = (f32[3,17,8,128]{3,2,1,0:T(8,128)S(1)}, bf16[3,17,8,128]{3,2,1,0:T(8,128)(2,1)S(1)}, f32[4,64,128]{2,1,0:T(8,128)S(1)}, f32[4,16,128]{2,1,0:T(8,128)S...) custom-call(s32[128]{0:T(128)S(1)} %get-tuple-element.48.slots_ref, ...), custom_call_target="tpu_custom_call" | custom-call | flops 268435456 | bytes 3670016 | tf_op jit(solution)/shard_map/fresh/pallas_call | solution.py:496
  18.3 0.1 collective-permute-start.6
  18.4 2.8 %first.1 = (f32[2,16,8192]{2,1,0:T(8,128)S(1)}, f32[2,16,128]{2,1,0:T(8,128)S(1)}, bf16[512,8,4,128]{3,2,1,0:T(4,128)(2,1)S(1)}) custom-call(s32[512]{0:T(512)S(1)} %bitcast.27, s32[4]{0:T(128)S(1)} %copy-done.1, bf16[4,64,128]{2,1,0:T(8,128)(2,1)S(1)} %bitcast.25, bf16[512,64,128]{2,1,0:T(8,128)(2,1)S(1)} %bitcast.13, bf16[512,16,4,256]{3,2,1,0:T(4,128)(2,1)} %refs_0_.1), custom_call_target="tpu_custom_call" | custom-call | flops 268435456 | bytes 4194304 | tf_op jit(solution)/shard_map/first/pallas_call | solution.py:549
  21.3 0.3 merge.3
  21.6 1.3 %collective-permute-start.7 = (bf16[3,17,4,128]{3,2,1,0:T(4,128)(2,1)S(1)}, bf16[3,17,4,128]{3,2,1,0:T(4,128)(2,1)S(1)}, u32[]{:S(2)}, u32[]{:S(2)}) collective-permute-start(bf16[3,17,4,128]{3,2,1,0:T(4,128)(2,1)S(1)} %get-tuple-element.67), channel_id=1, source_target_pairs={{0,4},{2,6},{4,0},{6,2},{1,5},{3,7},{5,1},{7,3},{8,12},{10,14},{12... | collective-permute-start | bytes 156680 | tf_op jit(solution)/shard_map/ppermute | solution.py:23
  22.9 2.8 %middle.1 = (f32[2,16,8192]{2,1,0:T(8,128)S(1)}, f32[2,16,128]{2,1,0:T(8,128)S(1)}, f32[2,64,128]{2,1,0:T(8,128)S(1)}, f32[2,16,128]{2,1,0:T(8,128)S(1)}) custom-call(s32[512]{0:T(512)S(1)} %bitcast.28, s32[4]{0:T(128)S(1)} %copy-done.1, bf16[4,64,128]{2,1,0:T(8,128)(2,1)S(1)} %bitcast.26, bf16[512,64,128]{2,1,0:T(8,128)(2,1)S(1)} %bitcast.14, ...), custom_call_target="tpu_custom_call" | custom-call | flops 536870912 | bytes 8388608 | tf_op jit(solution)/shard_map/middle/pallas_call | solution.py:565
  25.7 0.1 collective-permute-done.7.got_ref
  25.9 0.3 merge.4
  26.2 1.0 %collective-permute-start.8 = (bf16[2,17,4,128]{3,2,1,0:T(4,128)(2,1)S(1)}, bf16[2,17,4,128]{3,2,1,0:T(4,128)(2,1)S(1)}, u32[]{:S(2)}, u32[]{:S(2)}) collective-permute-start(bf16[2,17,4,128]{3,2,1,0:T(4,128)(2,1)S(1)} %get-tuple-element.76), channel_id=1, source_target_pairs={{0,8},{8,0},{16,24},{24,16},{1,9},{9,1},{17,25},{25,17},{2,10},{10... | collective-permute-start | bytes 104456 | tf_op jit(solution)/shard_map/ppermute | solution.py:23
  27.2 1.5 %second.1 = (f32[1,17,4,128]{3,2,1,0:T(4,128)S(1)}, bf16[1,17,4,128]{3,2,1,0:T(4,128)(2,1)S(1)}, bf16[1,17,4,128]{3,2,1,0:T(4,128)(2,1)S(1)}, bf16[1,17,4,128]{3,2,1,0:T(4,128)(2,1)S(1)}) custom-call(s32[512]{0:T(512)S(1)} %bitcast.29, f32[2,16,8192]{2,1,0:T(8,128)S(1)} %get-tuple-element.77.t_ref, f32[2,16,128]{2,1,0:T(8,128)S(1)} %get-tuple-element.78.top_ref, ...), custom_call_target="tpu_custom_call" | custom-call | flops 268435456 | bytes 4194304 | tf_op jit(solution)/shard_map/second/pallas_call | solution.py:582
  28.7 1.4 %collective-permute-start.9 = (bf16[1,17,4,128]{3,2,1,0:T(4,128)(2,1)S(1)}, bf16[1,17,4,128]{3,2,1,0:T(4,128)(2,1)S(1)}, u32[]{:S(2)}, u32[]{:S(2)}) collective-permute-start(bf16[1,17,4,128]{3,2,1,0:T(4,128)(2,1)S(1)} %get-tuple-element.86), channel_id=1, source_target_pairs={{0,4},{2,6},{4,0},{6,2},{1,5},{3,7},{5,1},{7,3},{8,12},{10,14},{12... | collective-permute-start | bytes 52232 | tf_op jit(solution)/shard_map/ppermute | solution.py:23
  30.1 0.8 %collective-permute-start.11 = (bf16[1,17,4,128]{3,2,1,0:T(4,128)(2,1)S(1)}, bf16[1,17,4,128]{3,2,1,0:T(4,128)(2,1)S(1)}, u32[]{:S(2)}, u32[]{:S(2)}) collective-permute-start(bf16[1,17,4,128]{3,2,1,0:T(4,128)(2,1)S(1)} %get-tuple-element.88), channel_id=1, source_target_pairs={{0,6},{2,4},{4,2},{6,0},{1,7},{3,5},{5,3},{7,1},{8,14},{10,12},{12... | collective-permute-start | bytes 52232 | tf_op jit(solution)/shard_map/ppermute | solution.py:23
  30.9 0.3 merge.5
  31.1 2.8 %collective-permute-start.12 = (bf16[1,17,4,128]{3,2,1,0:T(4,128)(2,1)S(1)}, bf16[1,17,4,128]{3,2,1,0:T(4,128)(2,1)S(1)}, u32[]{:S(2)}, u32[]{:S(2)}) collective-permute-start(bf16[1,17,4,128]{3,2,1,0:T(4,128)(2,1)S(1)} %merge.5), channel_id=1, source_target_pairs={{0,16},{8,24},{16,0},{24,8},{1,17},{9,25},{17,1},{25,9},{2,18},{10... | collective-permute-start | bytes 52232 | tf_op jit(solution)/shard_map/ppermute | solution.py:23
  33.9 1.9 %collective-permute-done.12.refs_4_ = bf16[1,17,4,128]{3,2,1,0:T(4,128)(2,1)S(1)} collective-permute-done((bf16[1,17,4,128]{3,2,1,0:T(4,128)(2,1)S(1)}, bf16[1,17,4,128]{3,2,1,0:T(4,128)(2,1)S(1)}, u32[]{:S(2)}, u32[]{:S(2)}) %collective-permute-start.12) | collective-permute-done | bytes 17440 | tf_op jit(solution)/shard_map/ppermute | solution.py:23
  35.9 1.0 %last.1 = bf16[4,4,4,128]{3,2,1,0:T(4,128)(2,1)} custom-call(f32[1,17,4,128]{3,2,1,0:T(4,128)S(1)} %get-tuple-element.85.keep_ref, bf16[2,17,4,128]{3,2,1,0:T(4,128)(2,1)S(1)} %collective-permute-done.8.got_ref.refs_0_, bf16[1,17,4,128]{3,2,1,0:T(4,128)(2,1)S(1)} %collective-permute-done.9.refs_1_, ...), custom_call_target="tpu_custom_call" | custom-call | tf_op jit(solution)/shard_map/last/pallas_call | solution.py:602
  (18 shorter events, 0.2 us)
Async XLA Ops:
  0.0 5.2 %collective-permute-start = (bf16[4,4,4,128]{3,2,1,0:T(4,128)(2,1)}, bf16[4,4,4,128]{3,2,1,0:T(4,128)(2,1)S(1)}, u32[]{:S(2)}, u32[]{:S(2)}) collective-permute-start(bf16[4,4,4,128]{3,2,1,0:T(4,128)(2,1)} %query_hbm.1), channel_id=1, source_target_pairs={{0,4},{2,6},{4,0},{6,2},{1,5},{3,7},{5,1},{7,3},{8,12},{10,14},{12... | collective-permute-start | bytes 49160 | tf_op jit(solution)/shard_map/ppermute | solution.py:23
  2.9 3.4 %collective-permute-start.2 = (bf16[4,4,4,128]{3,2,1,0:T(4,128)(2,1)}, bf16[4,4,4,128]{3,2,1,0:T(4,128)(2,1)S(1)}, u32[]{:S(2)}, u32[]{:S(2)}) collective-permute-start(bf16[4,4,4,128]{3,2,1,0:T(4,128)(2,1)} %query_hbm.1), channel_id=1, source_target_pairs={{0,6},{2,4},{4,2},{6,0},{1,7},{3,5},{5,3},{7,1},{8,14},{10,12},{12... | collective-permute-start | bytes 49160 | tf_op jit(solution)/shard_map/ppermute | solution.py:23
  2.9 3.4 %collective-permute-start.1 = (bf16[4,4,4,128]{3,2,1,0:T(4,128)(2,1)}, bf16[4,4,4,128]{3,2,1,0:T(4,128)(2,1)S(1)}, u32[]{:S(2)}, u32[]{:S(2)}) collective-permute-start(bf16[4,4,4,128]{3,2,1,0:T(4,128)(2,1)} %query_hbm.1), channel_id=1, source_target_pairs={{0,2},{2,0},{4,6},{6,4},{1,3},{3,1},{5,7},{7,5},{8,10},{10,8},{12,... | collective-permute-start | bytes 49160 | tf_op jit(solution)/shard_map/ppermute | solution.py:23
  6.4 8.5 %collective-permute-start.5 = (bf16[4,64,128]{2,1,0:T(8,128)(2,1)S(1)}, bf16[4,64,128]{2,1,0:T(8,128)(2,1)S(1)}, u32[]{:S(2)}, u32[]{:S(2)}) collective-permute-start(bf16[4,64,128]{2,1,0:T(8,128)(2,1)S(1)} %bitcast.21), channel_id=1, source_target_pairs={{0,24},{8,16},{16,8},{24,0},{1,25},{9,17},{17,9},{25,1},{2,26},{10... | collective-permute-start | bytes 196616 | tf_op jit(solution)/shard_map/ppermute | solution.py:23
  10.1 5.4 %collective-permute-start.4 = (bf16[4,64,128]{2,1,0:T(8,128)(2,1)S(1)}, bf16[4,64,128]{2,1,0:T(8,128)(2,1)S(1)}, u32[]{:S(2)}, u32[]{:S(2)}) collective-permute-start(bf16[4,64,128]{2,1,0:T(8,128)(2,1)S(1)} %bitcast.22), channel_id=1, source_target_pairs={{0,16},{8,24},{16,0},{24,8},{1,17},{9,25},{17,1},{25,9},{2,18},{10... | collective-permute-start | bytes 196616 | tf_op jit(solution)/shard_map/ppermute | solution.py:23
  10.1 5.4 %collective-permute-start.3 = (bf16[4,64,128]{2,1,0:T(8,128)(2,1)S(1)}, bf16[4,64,128]{2,1,0:T(8,128)(2,1)S(1)}, u32[]{:S(2)}, u32[]{:S(2)}) collective-permute-start(bf16[4,64,128]{2,1,0:T(8,128)(2,1)S(1)} %bitcast.23), channel_id=1, source_target_pairs={{0,8},{8,0},{16,24},{24,16},{1,9},{9,1},{17,25},{25,17},{2,10},{10... | collective-permute-start | bytes 196616 | tf_op jit(solution)/shard_map/ppermute | solution.py:23
  15.5 2.9 %copy-start = (s32[4,128]{1,0:T(4,128)S(1)}, s32[4,128]{1,0:T(4,128)}, u32[]{:S(2)}) copy-start(s32[4,128]{1,0:T(4,128)} %param.8) | copy-start | bytes 6148
  15.5 2.9 %copy-start.1 = (s32[4]{0:T(128)S(1)}, s32[4]{0:T(128)}, u32[]{:S(2)}) copy-start(s32[4]{0:T(128)} %len_ref.3) | copy-start | bytes 52
  18.3 2.9 %collective-permute-start.6 = (bf16[3,17,8,128]{3,2,1,0:T(8,128)(2,1)S(1)}, bf16[3,17,8,128]{3,2,1,0:T(8,128)(2,1)S(1)}, u32[]{:S(2)}, u32[]{:S(2)}) collective-permute-start(bf16[3,17,8,128]{3,2,1,0:T(8,128)(2,1)S(1)} %get-tuple-element.59), channel_id=1, source_target_pairs={{0,2},{2,0},{4,6},{6,4},{1,3},{3,1},{5,7},{7,5},{8,10},{10,8},{12,... | collective-permute-start | bytes 313352 | tf_op jit(solution)/shard_map/ppermute | solution.py:23
  21.6 4.3 %collective-permute-start.7 = (bf16[3,17,4,128]{3,2,1,0:T(4,128)(2,1)S(1)}, bf16[3,17,4,128]{3,2,1,0:T(4,128)(2,1)S(1)}, u32[]{:S(2)}, u32[]{:S(2)}) collective-permute-start(bf16[3,17,4,128]{3,2,1,0:T(4,128)(2,1)S(1)} %get-tuple-element.67), channel_id=1, source_target_pairs={{0,4},{2,6},{4,0},{6,2},{1,5},{3,7},{5,1},{7,3},{8,12},{10,14},{12... | collective-permute-start | bytes 156680 | tf_op jit(solution)/shard_map/ppermute | solution.py:23
  26.2 4.7 %collective-permute-start.8 = (bf16[2,17,4,128]{3,2,1,0:T(4,128)(2,1)S(1)}, bf16[2,17,4,128]{3,2,1,0:T(4,128)(2,1)S(1)}, u32[]{:S(2)}, u32[]{:S(2)}) collective-permute-start(bf16[2,17,4,128]{3,2,1,0:T(4,128)(2,1)S(1)} %get-tuple-element.76), channel_id=1, source_target_pairs={{0,8},{8,0},{16,24},{24,16},{1,9},{9,1},{17,25},{25,17},{2,10},{10... | collective-permute-start | bytes 104456 | tf_op jit(solution)/shard_map/ppermute | solution.py:23
  28.7 5.2 %collective-permute-start.9 = (bf16[1,17,4,128]{3,2,1,0:T(4,128)(2,1)S(1)}, bf16[1,17,4,128]{3,2,1,0:T(4,128)(2,1)S(1)}, u32[]{:S(2)}, u32[]{:S(2)}) collective-permute-start(bf16[1,17,4,128]{3,2,1,0:T(4,128)(2,1)S(1)} %get-tuple-element.86), channel_id=1, source_target_pairs={{0,4},{2,6},{4,0},{6,2},{1,5},{3,7},{5,1},{7,3},{8,12},{10,14},{12... | collective-permute-start | bytes 52232 | tf_op jit(solution)/shard_map/ppermute | solution.py:23
  30.1 3.8 %collective-permute-start.10 = (bf16[1,17,4,128]{3,2,1,0:T(4,128)(2,1)S(1)}, bf16[1,17,4,128]{3,2,1,0:T(4,128)(2,1)S(1)}, u32[]{:S(2)}, u32[]{:S(2)}) collective-permute-start(bf16[1,17,4,128]{3,2,1,0:T(4,128)(2,1)S(1)} %get-tuple-element.87), channel_id=1, source_target_pairs={{0,2},{2,0},{4,6},{6,4},{1,3},{3,1},{5,7},{7,5},{8,10},{10,8},{12,... | collective-permute-start | bytes 52232 | tf_op jit(solution)/shard_map/ppermute | solution.py:23
  30.1 3.8 %collective-permute-start.11 = (bf16[1,17,4,128]{3,2,1,0:T(4,128)(2,1)S(1)}, bf16[1,17,4,128]{3,2,1,0:T(4,128)(2,1)S(1)}, u32[]{:S(2)}, u32[]{:S(2)}) collective-permute-start(bf16[1,17,4,128]{3,2,1,0:T(4,128)(2,1)S(1)} %get-tuple-element.88), channel_id=1, source_target_pairs={{0,6},{2,4},{4,2},{6,0},{1,7},{3,5},{5,3},{7,1},{8,14},{10,12},{12... | collective-permute-start | bytes 52232 | tf_op jit(solution)/shard_map/ppermute | solution.py:23
  31.1 4.7 %collective-permute-start.12 = (bf16[1,17,4,128]{3,2,1,0:T(4,128)(2,1)S(1)}, bf16[1,17,4,128]{3,2,1,0:T(4,128)(2,1)S(1)}, u32[]{:S(2)}, u32[]{:S(2)}) collective-permute-start(bf16[1,17,4,128]{3,2,1,0:T(4,128)(2,1)S(1)} %merge.5), channel_id=1, source_target_pairs={{0,16},{8,24},{16,0},{24,8},{1,17},{9,25},{17,1},{25,9},{2,18},{10... | collective-permute-start | bytes 52232 | tf_op jit(solution)/shard_map/ppermute | solution.py:23
